TPU v7x, 32 devices: a whole 2x2x4 slice. The times are simulated.
32 devices in a mesh: row: 4 (over y, x), col: 8 (over z, core).
Axes of the slice: x: 2, y: 2, z: 4, core: 2. Of those that a mesh axis runs over, the one named last changes fastest.
Arguments:
- density_block_entries: bfloat16 [32, 16, 128, 128], P('row', 'col'), as said below
- density_cols: int32 [32, 16], P('row', 'col'), may hold values from 0 to 31, as said below
- hamilton_values: bfloat16 [32, 16, 128, 128], P('row', 'col'), as said below
- hamilton_cols: int32 [32, 16], P('row', 'col'), may hold values from 0 to 31, as said below
- filter_cols: int32 [32, 32], P('row', 'col'), may hold values from 0 to 31, as said below
Outputs:
- squared_density: bfloat16 [32, 32, 128, 128], P('row', 'col')
- mixed_product: bfloat16 [32, 32, 128, 128], P('row', 'col')
- gradient: bfloat16 [32, 16, 128, 128], P('row', 'col')
Inputs may be any that keep to these rules, and one draw needn't show every extreme that they name: `density_cols`: in every block row, slots c * 2 to (c + 1) * 2 - 1 hold distinct block columns of c * 4 to (c + 1) * 4 - 1. The pattern is symmetric: j is listed in row i exactly when i is listed in row j. `hamilton_cols`: in every block row, slots c * 2 to (c + 1) * 2 - 1 hold distinct block columns of c * 4 to (c + 1) * 4 - 1. The pattern is symmetric: j is listed in row i exactly when i is listed in row j. `filter_cols`: in every block row, slots c * 4 to (c + 1) * 4 - 1 hold distinct block columns of c * 4 to (c + 1) * 4 - 1. `density_block_entries`: the density matrix is symmetric: the block of row i and column j is the transpose of the block of row j and column i. `hamilton_values`: the Hamiltonian is symmetric: the block of row i and column j is the transpose of the block of row j and column i.
All inputs are finite; a program needn't handle non-finite values.
Results may differ from a plain program's by a relative error of at most 0.015.
Values may be sent and summed in bfloat16 or wider, within the bound.
No kernel may reach another device: no remote copies, remote signals or barrier semaphores. Data moves between devices by JAX's collectives and lax.ppermute only.
A program may use at most 128 MiB of HBM per device.

v0:
```python
import jax
import jax.numpy as jnp
from jax import lax
from jax.sharding import PartitionSpec as P


def block_products(left_vals, left_cols, right_vals, right_cols):
    chosen = right_vals[left_cols]
    block_product_list = jnp.einsum(
        "sab,stbc->stac", left_vals, chosen, preferred_element_type=jnp.float32
    )
    block_size = left_vals.shape[-1]
    return (
        block_product_list.reshape(-1, block_size, block_size),
        right_cols[left_cols].reshape(-1),
    )


def to_slots(block_product_list, product_cols, targets):
    filter_picker = (targets[:, None] == product_cols[None, :]).astype(jnp.float32)
    return jnp.einsum(
        "wv,vug->wug", filter_picker, block_product_list, precision=lax.Precision.HIGHEST
    )


def local(density_block_entries, density_cols, hamilton_values, hamilton_cols, filter_cols):
    density_panel, density_panel_cols, hamilton_panel, hamilton_panel_cols = (
        lax.all_gather(density_block_entries, "row", axis=0, tiled=True),
        lax.all_gather(density_cols, "row", axis=0, tiled=True),
        lax.all_gather(hamilton_values, "row", axis=0, tiled=True),
        lax.all_gather(hamilton_cols, "row", axis=0, tiled=True),
    )
    piece_values = lax.all_gather(density_block_entries, "col", axis=1, tiled=True)
    piece_cols = lax.all_gather(density_cols, "col", axis=1, tiled=True)

    def left_row(row_data):
        left_vals, left_cols, square_targets, pattern_targets = row_data
        square_terms, square_cols = block_products(
            left_vals, left_cols, density_panel, density_panel_cols
        )
        mixed_terms, mixed_cols = block_products(
            left_vals, left_cols, hamilton_panel, hamilton_panel_cols
        )
        return (
            to_slots(square_terms, square_cols, square_targets),
            to_slots(mixed_terms, mixed_cols, square_targets),
            to_slots(mixed_terms, mixed_cols, pattern_targets),
        )

    additions = lax.map(left_row, (piece_values, piece_cols, filter_cols, density_cols))
    square_sum = additions[0]
    mixed_sum = additions[1]
    direct_term = additions[2]
    square_term = square_sum.astype(jnp.bfloat16)
    mixed_term = mixed_sum.astype(jnp.bfloat16)
    piece_values = lax.all_gather(square_term, "col", axis=1, tiled=True)
    piece_cols = lax.all_gather(filter_cols, "col", axis=1, tiled=True)

    def square_row(row_data):
        left_vals, left_cols, pattern_targets = row_data
        cubic_terms, cubic_cols = block_products(
            left_vals, left_cols, hamilton_panel, hamilton_panel_cols
        )
        return to_slots(cubic_terms, cubic_cols, pattern_targets)

    cubic_term = lax.map(square_row, (piece_values, piece_cols, density_cols))
    gradient = (3.0 * direct_term - 2.0 * cubic_term).astype(jnp.bfloat16)
    return (square_term, mixed_term, gradient)


def solution(mesh):
    in_specs = (
        P("row", "col", None, None),
        P("row", "col"),
        P("row", "col", None, None),
        P("row", "col"),
        P("row", "col"),
    )
    out_specs = (
        P("row", "col", None, None),
        P("row", "col", None, None),
        P("row", "col", None, None),
    )
    return jax.shard_map(local, mesh=mesh, in_specs=in_specs, out_specs=out_specs, check_vma=False)
```

profile of v0, /device:TPU:0, one launch (start us, length us, event | category | flops | bytes accessed | tf_op | source)
XLA Modules:
  0.0 516.1 jit_solution(15394701395576931865)
XLA Ops:
  9.4 9.6 %all-gather.2 = s32[4,8,2]{1,2,0:T(2,128)S(1)} all-gather(s32[1,8,2]{1,2,0:T(2,128)} %bitcast.154), channel_id=1, replica_groups=mesh['row'=4,'col'=8] {'row'}, dimensions={0}, use_global_device_ids=true | all-gather | bytes 320 | tf_op jit(solution)/shard_map/all_gather | solution.py:31
  19.1 7.9 %all-gather.1 = s32[4,8,2]{1,2,0:T(2,128)S(1)} all-gather(s32[1,8,2]{1,2,0:T(2,128)} %bitcast.150), channel_id=1, replica_groups=mesh['row'=4,'col'=8] {'row'}, dimensions={0}, use_global_device_ids=true | all-gather | bytes 320 | tf_op jit(solution)/shard_map/all_gather | solution.py:29
  28.5 12.2 %all-gather = s32[8,2,8]{2,1,0:T(2,128)S(1)} all-gather(s32[1,2,8]{2,1,0:T(2,128)} %bitcast.151), channel_id=1, replica_groups=mesh['row'=4,'col'=8] {'col'}, dimensions={0}, use_global_device_ids=true | all-gather | bytes 576 | tf_op jit(solution)/shard_map/all_gather | solution.py:34
  41.0 6.9 %all-gather.13.cloned.1.call-done = bf16[32,2,128,128]{3,2,1,0:T(8,128)(2,1)} async-done(((bf16[8,2,128,128]{3,2,1,0:T(8,128)(2,1)}), bf16[32,2,128,128]{3,2,1,0:T(8,128)(2,1)}) %all-gather.13.cloned.1.call-update) | async-done | bytes 2097168 | tf_op jit(solution)/shard_map/all_gather | solution.py:30
  47.9 37.2 %all-gather.9.cloned.1.call-done = bf16[32,2,128,128]{3,2,1,0:T(8,128)(2,1)} async-done(((bf16[8,2,128,128]{3,2,1,0:T(8,128)(2,1)}), bf16[32,2,128,128]{3,2,1,0:T(8,128)(2,1)}) %all-gather.9.cloned.1.call-update) | async-done | bytes 2097168 | tf_op jit(solution)/shard_map/all_gather | solution.py:28
  85.1 48.8 %all-gather.11.cloned.1.call-done = bf16[8,16,128,128]{3,2,1,0:T(8,128)(2,1)} async-done(((bf16[8,2,128,128]{3,2,1,0:T(8,128)(2,1)}), bf16[8,16,128,128]{3,2,1,0:T(8,128)(2,1)}) %all-gather.11.cloned.1.call-update) | async-done | bytes 4194320 | tf_op jit(solution)/shard_map/all_gather | solution.py:33
  135.0 160.9 %while.24 = (s32[]{:T(128)}, bf16[8,4,128,128]{3,2,1,0:T(8,128)(2,1)}, bf16[8,4,128,128]{3,2,1,0:T(8,128)(2,1)}, f32[8,2,128,128]{3,2,1,0:T(8,128)}, s32[8,4]{1,...) while((s32[]{:T(128)}, ...), condition=%wide.region_1.2_spmd, body=%wide.region_0.1_spmd.sunk | while | flops 331351424 | bytes 35788884 | solution.py:50
  295.9 12.8 %all-gather.3 = s32[8,4,8]{2,1,0:T(4,128)S(1)} all-gather(s32[1,4,8]{2,1,0:T(4,128)S(1)} %bitcast.152), channel_id=1, replica_groups=mesh['row'=4,'col'=8] {'col'}, dimensions={0}, use_global_device_ids=true | all-gather | bytes 1152 | tf_op jit(solution)/shard_map/all_gather | solution.py:57
  308.8 68.1 %all-gather.15.cloned.1.call-done = bf16[8,32,128,128]{3,2,1,0:T(8,128)(2,1)} async-done(((bf16[8,4,128,128]{3,2,1,0:T(8,128)(2,1)}), bf16[8,32,128,128]{3,2,1,0:T(8,128)(2,1)}) %all-gather.15.cloned.1.call-update) | async-done | bytes 8388624 | tf_op jit(solution)/shard_map/all_gather | solution.py:56
  376.9 130.5 %while.25 = (s32[]{:T(128)}, f32[8,2,128,128]{3,2,1,0:T(8,128)S(1)}, s32[8,2]{1,0:T(8,128)S(1)}, s32[8,32]{1,0:T(8,128)S(1)}, s32[32,2]{1,0:T(8,128)S(1)}, /*ind...) while((s32[]{:T(128)}, f32[8,2,128,128]{3,2,1,0:T(8,128)S(1)}, ...), condition=%wide.region_3.4_spmd, body=%wide.region_2.3_spmd.sunk | while | flops 293602528 | bytes 24516612 | solution.py:66
  380.2 4.0 fusion.84
  384.2 5.4 %copy.103 = f32[64,128,128]{2,0,1:T(8,128)} copy(f32[64,128,128]{1,2,0:T(8,128)} %bitcast.143) | data formatting | bytes 8388608 | tf_op jit(solution)/shard_map/while/body/eval_jaxpr/reshape | solution.py:14
  389.6 3.6 convolution_bitcast_fusion.11
  396.5 4.0 fusion.84
  400.5 5.4 %copy.103 = f32[64,128,128]{2,0,1:T(8,128)} copy(f32[64,128,128]{1,2,0:T(8,128)} %bitcast.143) | data formatting | bytes 8388608 | tf_op jit(solution)/shard_map/while/body/eval_jaxpr/reshape | solution.py:14
  405.9 3.6 convolution_bitcast_fusion.11
  412.8 4.0 fusion.84
  416.8 5.4 %copy.103 = f32[64,128,128]{2,0,1:T(8,128)} copy(f32[64,128,128]{1,2,0:T(8,128)} %bitcast.143) | data formatting | bytes 8388608 | tf_op jit(solution)/shard_map/while/body/eval_jaxpr/reshape | solution.py:14
  422.2 3.6 convolution_bitcast_fusion.11
  429.1 4.0 fusion.84
  433.1 5.4 %copy.103 = f32[64,128,128]{2,0,1:T(8,128)} copy(f32[64,128,128]{1,2,0:T(8,128)} %bitcast.143) | data formatting | bytes 8388608 | tf_op jit(solution)/shard_map/while/body/eval_jaxpr/reshape | solution.py:14
  438.5 3.6 convolution_bitcast_fusion.11
  445.5 4.0 fusion.84
  449.4 5.4 %copy.103 = f32[64,128,128]{2,0,1:T(8,128)} copy(f32[64,128,128]{1,2,0:T(8,128)} %bitcast.143) | data formatting | bytes 8388608 | tf_op jit(solution)/shard_map/while/body/eval_jaxpr/reshape | solution.py:14
  454.8 3.6 convolution_bitcast_fusion.11
  461.8 4.0 fusion.84
  465.7 5.4 %copy.103 = f32[64,128,128]{2,0,1:T(8,128)} copy(f32[64,128,128]{1,2,0:T(8,128)} %bitcast.143) | data formatting | bytes 8388608 | tf_op jit(solution)/shard_map/while/body/eval_jaxpr/reshape | solution.py:14
  471.1 3.6 convolution_bitcast_fusion.11
  478.1 4.0 fusion.84
  482.0 5.4 %copy.103 = f32[64,128,128]{2,0,1:T(8,128)} copy(f32[64,128,128]{1,2,0:T(8,128)} %bitcast.143) | data formatting | bytes 8388608 | tf_op jit(solution)/shard_map/while/body/eval_jaxpr/reshape | solution.py:14
  494.4 4.0 fusion.84
  498.4 5.4 %copy.103 = f32[64,128,128]{2,0,1:T(8,128)} copy(f32[64,128,128]{1,2,0:T(8,128)} %bitcast.143) | data formatting | bytes 8388608 | tf_op jit(solution)/shard_map/while/body/eval_jaxpr/reshape | solution.py:14
  (247 shorter events, 201.0 us)
Async XLA Ops:
  7.2 40.7 %all-gather.13.cloned.1.call-start = ((), (), s32[]{:S(2)}) async-start(), calls=%async_computation.2 | async-start | bytes 2621440 | tf_op jit(solution)/shard_map/all_gather | solution.py:30
  7.9 77.2 %all-gather.9.cloned.1.call-start = ((), (), s32[]{:S(2)}) async-start(), calls=%async_computation | async-start | bytes 2621440 | tf_op jit(solution)/shard_map/all_gather | solution.py:28
  8.6 125.2 %all-gather.11.cloned.1.call-start = ((), (), s32[]{:S(2)}) async-start(), calls=%async_computation.1 | async-start | bytes 4718592 | tf_op jit(solution)/shard_map/all_gather | solution.py:33
  9.4 367.4 %all-gather.15.cloned.1.call-start = ((), (), s32[]{:S(2)}) async-start(), calls=%async_computation.3 | async-start | bytes 9437184 | tf_op jit(solution)/shard_map/all_gather | solution.py:56
  135.0 160.9 %copy-start.1 = (s32[8,4]{0,1:T(4,128)S(1)}, s32[8,4]{0,1:T(4,128)}, u32[]{:S(2)}) copy-start(s32[8,4]{0,1:T(4,128)} %param.13) | copy-start | bytes 388
  135.0 3.7 copy-start
  155.1 3.7 copy-start
  175.2 3.7 copy-start
  195.3 3.7 copy-start
  215.4 3.7 copy-start
  235.5 3.7 copy-start
  255.6 3.7 copy-start
  275.7 3.7 copy-start
Sparse Core Ops, SparseCore 0:
  9.8 38.0 all-gather.12
  49.7 35.2 all-gather.8
  86.7 47.1 all-gather.10
  296.0 80.7 all-gather.14
where the time goes:
time: 519 us; the launch traced here: 516 us
  local copies, waits for them, and re-layouts  165 us (32%)
  waiting for transfers between devices  163 us (31%)
  matrix products  128 us (25%)
  blocking collectives  42.6 us (8%)
  between operations  13.8 us (3%)
    reshape x24, local copies, waits for them, and re-layouts, block_products(): block_product_list.reshape(-1, block_size, block_size)  81.1 us
    dot_general x24, matrix products, block_products(): jnp.einsum('sab,stbc->stac', left_vals, chosen, preferred_element_type=jn...  80.2 us
    all_gather x1, waiting for transfers between devices, local(): piece_values = lax.all_gather(square_term, 'col', axis=1, tiled=True)  68.1 us
    gather x24, local copies, waits for them, and re-layouts, block_products(): chosen = right_vals[left_cols]  53 us
    all_gather x1, waiting for transfers between devices, local(): lax.all_gather(density_block_entries, 'col', axis=1, tiled=True)  48.8 us
    dot_general x32, matrix products, to_slots(): jnp.einsum('wv,vug->wug', filter_picker, block_product_list, precision=la...  48.3 us
    all_gather x1, waiting for transfers between devices, local(): lax.all_gather(density_block_entries, 'row', axis=0, tiled=True)  37.2 us
    gather x24, local copies, waits for them, and re-layouts, block_products(): right_cols[left_cols].reshape(-1)  13.6 us
  transfers between devices with their start and end apart: 4, of which 4 were waited for; matrix products, arithmetic and copies ran while one was open for 0% of the time, Pallas kernels for 0%

commit v1 on v0

v1 whole, which is shorter than its diff:
```python
import functools

import jax
import jax.numpy as jnp
from jax import lax
from jax.experimental import pallas as pl
from jax.experimental.pallas import tpu as pltpu
from jax.sharding import PartitionSpec as P

VMEM_LIMIT = 56 * 1024 * 1024
DENSE_LIMIT = 16 * 1024 * 1024


class Sizes:
    def __init__(self, n_row, n_col, density, hamilton, filt):
        self.n_row, self.n_col = n_row, n_col
        self.rows, self.ka, self.bs = density.shape[0], density.shape[1], density.shape[2]
        self.kh, self.kf = hamilton.shape[1], filt.shape[1]
        self.nb = self.rows * n_row
        self.bc = self.nb // n_col
        self.wide = self.bc * self.bs
        self.groups = 2 if n_col % (2 * n_row) == 0 else 1
        self.chunks = n_col // self.groups
        chunk_bytes = self.rows * self.bs * self.groups * self.wide * 2
        self.dense_slots = self.chunks if chunk_bytes * self.chunks <= DENSE_LIMIT else 1


def density_col(z, idx, row, col, i, s):
    return idx[((row * z.n_col + col) * z.rows + i) * (z.ka + z.kh) + s]


def hamilton_col(z, idx, row, col, i, s):
    return idx[((row * z.n_col + col) * z.rows + i) * (z.ka + z.kh) + z.ka + s]


def lanes(z, block):
    return pl.ds(pl.multiple_of(block * z.bs, z.bs), z.bs)


def start_pieces(z, pos, left_in, right_in, left_buf, right_buf, left_sem, right_sem):
    copies = []
    for n, ref in enumerate(right_in):
        copies.append(pltpu.make_async_copy(ref, right_buf.at[pos[0] ^ n], right_sem.at[pos[0] ^ n]))
    n_chip = z.n_col // 2
    for n, ref in enumerate(left_in):
        chip = lax.rem(pos[1] // 2 + n_chip - n // 2, n_chip)
        col = chip * 2 + (lax.rem(pos[1], 2) ^ (n % 2))
        copies.append(pltpu.make_async_copy(ref, left_buf.at[col], left_sem.at[col]))
    for copy in copies:
        copy.start()


def fill_right(z, pos, idx, col_of, count, right_buf, right_sem, right_dense):
    right_dense[...] = jnp.zeros_like(right_dense)

    def one_row(row, _):
        pltpu.make_async_copy(right_buf.at[row], right_buf.at[row], right_sem.at[row]).wait()
        for i in range(z.rows):
            for s in range(count):
                j = col_of(z, idx, row, pos[1], i, s) - pos[1] * z.bc
                right_dense[row * z.rows + i, :, lanes(z, j)] = right_buf[row, i, s]
        return 0

    lax.fori_loop(0, z.n_row, one_row, 0)


def fill_left(z, pos, idx, chunk, left_buf, left_dense, left_sem):
    slot = chunk if z.dense_slots > 1 else 0
    left_dense[slot] = jnp.zeros(left_dense.shape[1:], left_dense.dtype)
    for g in range(z.groups):
        col = chunk * z.groups + g
        if left_sem is not None:
            pltpu.make_async_copy(left_buf.at[col], left_buf.at[col], left_sem.at[col]).wait()
        for i in range(z.rows):
            for s in range(z.ka):
                k = density_col(z, idx, pos[0], col, i, s) - col * z.bc
                left_dense[slot, i * z.bs:(i + 1) * z.bs, lanes(z, k + g * z.bc)] = left_buf[col, i, s]
    return slot


def multiply_panels(z, pos, idx, left_buf, left_sem, left_dense, right_dense, total):
    def one_chunk(chunk, _):
        slot = fill_left(z, pos, idx, chunk, left_buf, left_dense, left_sem)
        blocks = z.groups * z.bc
        right = right_dense[pl.ds(chunk * blocks, blocks)].reshape(blocks * z.bs, z.wide)
        term = jnp.dot(left_dense[slot], right, preferred_element_type=jnp.float32)

        @pl.when(chunk == 0)
        def _():
            total[...] = term

        @pl.when(chunk > 0)
        def _():
            total[...] += term
        return 0

    lax.fori_loop(0, z.chunks, one_chunk, 0)


def write_filtered(z, pos, total, filt, out):
    for i in range(z.rows):
        for s in range(z.kf):
            j = filt[i * z.kf + s] - pos[1] * z.bc
            out[i, s] = total[i * z.bs:(i + 1) * z.bs, lanes(z, j)].astype(out.dtype)


def mixed_kernel(z, *refs):
    pos, idx, filt = refs[:3]
    left_in = refs[3:3 + z.n_col]
    right_in = refs[3 + z.n_col:3 + z.n_col + z.n_row]
    rest = refs[3 + z.n_col + z.n_row:]
    mixed, direct = rest[:2]
    parts = rest[2:2 + z.n_row]
    left_buf, right_buf, left_dense, right_dense, total, turned, column, left_sem, right_sem = rest[2 + z.n_row:]
    start_pieces(z, pos, left_in, right_in, left_buf, right_buf, left_sem, right_sem)
    fill_right(z, pos, idx, hamilton_col, z.kh, right_buf, right_sem, right_dense)
    multiply_panels(z, pos, idx, left_buf, left_sem, left_dense, right_dense, total)

    for i in range(z.rows):
        rows = slice(i * z.bs, (i + 1) * z.bs)
        for j in range(z.bc):
            cols = slice(j * z.bs, (j + 1) * z.bs)
            turned[cols, rows] = total[rows, cols].T.astype(turned.dtype)

    step = 2
    for n in range(z.n_row):
        row = pos[0] ^ n
        first = row * (z.chunks // z.n_row)

        def one_chunk(chunk, _, n=n, row=row, first=first):
            if z.dense_slots > 1:
                slot = first + chunk
            else:
                slot = fill_left(z, pos, idx, first + chunk, left_buf, left_dense, None)

            def one_step(t, _):
                here = pl.ds(pl.multiple_of(t * step * z.bs, step * z.bs), step * z.bs)
                column[...] = jnp.dot(turned[...], left_dense[slot, :, here], preferred_element_type=jnp.float32)
                for b in range(step):
                    i = chunk * z.groups * z.bc + t * step + b
                    for s in range(z.ka):
                        j = density_col(z, idx, row, pos[1], i, s) - pos[1] * z.bc
                        parts[n][i, s] = column[lanes(z, j), b * z.bs:(b + 1) * z.bs].astype(parts[n].dtype)
                return 0

            lax.fori_loop(0, z.groups * z.bc // step, one_step, 0)
            return 0

        lax.fori_loop(0, z.chunks // z.n_row, one_chunk, 0)

    write_filtered(z, pos, total, filt, mixed)
    for i in range(z.rows):
        for s in range(z.ka):
            j = density_col(z, idx, pos[0], pos[1], i, s) - pos[1] * z.bc
            direct[i, s] = total[i * z.bs:(i + 1) * z.bs, lanes(z, j)]


def square_kernel(z, *refs):
    pos, idx, filt = refs[:3]
    left_in = refs[3:3 + z.n_col]
    right_in = refs[3 + z.n_col:3 + z.n_col + z.n_row]
    squared = refs[4 + z.n_col + z.n_row]
    left_buf, right_buf, left_dense, right_dense, total, left_sem, right_sem = refs[5 + z.n_col + z.n_row:]
    start_pieces(z, pos, left_in, right_in, left_buf, right_buf, left_sem, right_sem)
    fill_right(z, pos, idx, density_col, z.ka, right_buf, right_sem, right_dense)
    multiply_panels(z, pos, idx, left_buf, left_sem, left_dense, right_dense, total)
    write_filtered(z, pos, total, filt, squared)


def gradient_kernel(z, *refs):
    direct, parts, out = refs[0], refs[1:1 + z.n_row], refs[1 + z.n_row]
    for i in range(z.rows):
        for s in range(z.ka):
            cubic = parts[0][i, s].astype(jnp.float32)
            for n in range(1, z.n_row):
                cubic += parts[n][i, s].astype(jnp.float32)
            out[i, s] = (3.0 * direct[i, s] - 2.0 * cubic.T).astype(out.dtype)


def common_scratch(z, count):
    bf16, block = jnp.bfloat16, (z.bs, z.bs)
    return [
        pltpu.VMEM((z.n_col, z.rows, z.ka) + block, bf16),
        pltpu.VMEM((z.n_row, z.rows, count) + block, bf16),
        pltpu.VMEM((z.dense_slots, z.rows * z.bs, z.groups * z.wide), bf16),
        pltpu.VMEM((z.nb, z.bs, z.wide), bf16),
        pltpu.VMEM((z.rows * z.bs, z.wide), jnp.float32),
    ]


def local(n_row, n_col, density, density_cols, hamilton, hamilton_cols, filter_cols):
    z = Sizes(n_row, n_col, density, hamilton, filter_cols)
    n_chip = n_col // 2
    block = (z.bs, z.bs)

    def over_row(x, flip):
        return lax.ppermute(x, "row", [(r, r ^ flip) for r in range(n_row)])

    def next_chip(x):
        return lax.ppermute(x, "col", [(c, (c + 2) % n_col) for c in range(n_col)])

    def other_core(x):
        return lax.ppermute(x, "col", [(c, c ^ 1) for c in range(n_col)])

    left = []
    piece = density
    for step in range(n_chip):
        if step:
            piece = next_chip(piece)
        left += [piece, other_core(piece)]
    d_right, h_right = [density], [hamilton]
    for flip in range(1, n_row):
        high, low = 1 << (flip.bit_length() - 1), flip & -flip
        d_right.append(over_row(d_right[flip - high], high))
        h_right.append(over_row(h_right[flip - low], low))

    cols = jnp.concatenate([density_cols, hamilton_cols], axis=1).reshape(-1)
    idx = lax.all_gather(cols, ("row", "col"), axis=0, tiled=True)
    pos = jnp.stack([lax.axis_index("row"), lax.axis_index("col")]).astype(jnp.int32)
    filt = filter_cols.reshape(-1)

    smem = pl.BlockSpec(memory_space=pltpu.SMEM)
    vmem = pl.BlockSpec(memory_space=pltpu.VMEM)
    anywhere = pl.BlockSpec(memory_space=pl.ANY)
    params = pltpu.CompilerParams(vmem_limit_bytes=VMEM_LIMIT)
    flops = 2 * z.rows * z.bs * z.nb * z.bs * z.wide
    sems = [pltpu.SemaphoreType.DMA((n_col,)), pltpu.SemaphoreType.DMA((n_row,))]
    part = jax.ShapeDtypeStruct((z.rows, z.ka) + block, jnp.bfloat16)
    mixed, direct, *parts = pl.pallas_call(
        functools.partial(mixed_kernel, z),
        out_shape=[
            jax.ShapeDtypeStruct((z.rows, z.kf) + block, jnp.bfloat16),
            jax.ShapeDtypeStruct((z.rows, z.ka) + block, jnp.float32),
        ] + [part] * n_row,
        in_specs=[smem] * 3 + [anywhere] * (n_col + n_row),
        out_specs=[vmem] * (2 + n_row),
        scratch_shapes=common_scratch(z, z.kh) + [
            pltpu.VMEM((z.wide, z.rows * z.bs), jnp.bfloat16),
            pltpu.VMEM((z.wide, 2 * z.bs), jnp.float32),
        ] + sems,
        compiler_params=params,
        cost_estimate=pl.CostEstimate(flops=2 * flops, bytes_accessed=12 << 20, transcendentals=0),
        name="mixed",
    )(pos, idx, filt, *left, *h_right)
    received = [over_row(parts[n], n) for n in range(1, n_row)]
    squared = pl.pallas_call(
        functools.partial(square_kernel, z),
        out_shape=jax.ShapeDtypeStruct((z.rows, z.kf) + block, jnp.bfloat16),
        in_specs=[smem] * 3 + [anywhere] * (n_col + n_row + 1),
        out_specs=vmem,
        scratch_shapes=common_scratch(z, z.ka) + sems,
        compiler_params=params,
        cost_estimate=pl.CostEstimate(flops=flops, bytes_accessed=8 << 20, transcendentals=0),
        name="squared",
    )(pos, idx, filt, *left, *d_right, direct)
    gradient = pl.pallas_call(
        functools.partial(gradient_kernel, z),
        out_shape=jax.ShapeDtypeStruct((z.rows, z.ka) + block, jnp.bfloat16),
        in_specs=[vmem] * (1 + n_row),
        out_specs=vmem,
        compiler_params=params,
        name="gradient",
    )(direct, parts[0], *received)
    return squared, mixed, gradient


def solution(mesh):
    spec4 = P("row", "col", None, None)
    spec2 = P("row", "col")
    body = functools.partial(local, mesh.shape["row"], mesh.shape["col"])
    return jax.shard_map(
        body,
        mesh=mesh,
        in_specs=(spec4, spec2, spec4, spec2, spec2),
        out_specs=(spec4, spec4, spec4),
        check_vma=False,
    )
```

time: 519 us -> 145 us (0.28)
  local copies, waits for them, and re-layouts: 165 us -> 4.96 us
  matrix products: 128 us -> 0 us
  waiting for transfers between devices: 163 us -> 45.6 us
  Pallas kernels: 0 us -> 36.4 us
  starting transfers between devices: 0.15 us -> 14.5 us
  between operations: 13.8 us -> 0.79 us
    all_gather x4 -> x0, waiting for transfers between devices: 161 us -> none  [the longest x1 68.1 us: local(): piece_values = lax.all_gather(square_term, 'col', axis=1, tiled=True)]
    dot_general x56 -> x0, matrix products: 128 us -> none  [the longest x24 80.2 us: block_products(): jnp.einsum('sab,stbc->stac', left_vals, chosen, preferred_element_type=jn...]
    reshape x24 -> x2, local copies, waits for them, and re-layouts: 81.1 us -> 0.65 us  [the longest x1 0.57 us: local(): filt = filter_cols.reshape(-1)]
    gather x48 -> x0, local copies, waits for them, and re-layouts: 66.6 us -> none  [the longest x24 53 us: block_products(): chosen = right_vals[left_cols]]
    ppermute x0 -> x16, waiting for transfers between devices: none -> 45.6 us  [the longest x3 37.7 us: next_chip(): return lax.ppermute(x, 'col', [(c, (c + 2) % n_col) for c in range(n_col)])]
    all_gather x4 -> x0, blocking collectives: 42.6 us -> none  [the longest x1 12.8 us: local(): piece_cols = lax.all_gather(filter_cols, 'col', axis=1, tiled=True)]
    unnamed x0 -> x1, blocking collectives: none -> 42 us
    pallas_call x0 -> x3, Pallas kernels: none -> 36.4 us  [the longest x1 21.2 us: local(): pl.pallas_call(functools.partial(mixed_kernel, z), out_shape=[jax.ShapeDt...]
  transfers between devices with their start and end apart: 4 -> 16, of which waited for: 4 -> 4; matrix products, arithmetic and copies ran while one was open for 0% -> 1% of each run, Pallas kernels for 0% -> 23%
where the time goes in v1:
time: 145 us
  waiting for transfers between devices  45.6 us (31%)
  blocking collectives  42 us (29%)
  Pallas kernels  36.4 us (25%)
  starting transfers between devices  14.5 us (10%)
  local copies, waits for them, and re-layouts  4.96 us (3%)
    unnamed x1, blocking collectives  42 us
    ppermute x3, waiting for transfers between devices, next_chip(): return lax.ppermute(x, 'col', [(c, (c + 2) % n_col) for c in range(n_col)])  37.7 us
    pallas_call x1, Pallas kernels, local(): pl.pallas_call(functools.partial(mixed_kernel, z), out_shape=[jax.ShapeDt...  21.2 us
    pallas_call x1, Pallas kernels, local(): pl.pallas_call(functools.partial(square_kernel, z), out_shape=jax.ShapeDt...  12.2 us
    ppermute x9, starting transfers between devices, over_row(): return lax.ppermute(x, 'row', [(r, r ^ flip) for r in range(n_row)])  11.3 us
    ppermute x9, waiting for transfers between devices, over_row(): return lax.ppermute(x, 'row', [(r, r ^ flip) for r in range(n_row)])  7.79 us
    unnamed x33, local copies, waits for them, and re-layouts  4.23 us
    ppermute x3, starting transfers between devices, next_chip(): return lax.ppermute(x, 'col', [(c, (c + 2) % n_col) for c in range(n_col)])  3.08 us
  transfers between devices with their start and end apart: 16, of which 4 were waited for; matrix products, arithmetic and copies ran while one was open for 1% of the time, Pallas kernels for 23%

profile of v1, /device:TPU:0, one launch (start us, length us, event | category | flops | bytes accessed | tf_op | source)
XLA Modules:
  0.0 144.8 jit_solution(13353525388285641669)
XLA Ops:
  0.6 3.1 %collective-permute-start.1 = (bf16[8,2,128,128]{3,2,1,0:T(8,128)(2,1)}, bf16[8,2,128,128]{3,2,1,0:T(8,128)(2,1)S(1)}, u32[]{:S(2)}, u32[]{:S(2)}) collective-permute-start(bf16[8,2,128,128]{3,2,1,0:T(8,128)(2,1)} %refs_11_.3), channel_id=1, source_target_pairs={{0,2},{1,3},{2,4},{3,5},{4,6},{5,7},{6,0},{7,1},{8,10},{9,11},{10,... | collective-permute-start | bytes 1572872 | tf_op jit(solution)/shard_map/ppermute | solution.py:200
  3.7 14.2 %collective-permute-done.1.refs_5_ = bf16[8,2,128,128]{3,2,1,0:T(8,128)(2,1)S(1)} collective-permute-done((bf16[8,2,128,128]{3,2,1,0:T(8,128)(2,1)}, bf16[8,2,128,128]{3,2,1,0:T(8,128)(2,1)S(1)}, u32[]{:S(2)}, u32[]{:S(2)}) %collective-permute-start.1) | collective-permute-done | bytes 524320 | tf_op jit(solution)/shard_map/ppermute | solution.py:200
  17.9 1.5 %collective-permute-start.11 = (bf16[8,2,128,128]{3,2,1,0:T(8,128)(2,1)}, bf16[8,2,128,128]{3,2,1,0:T(8,128)(2,1)}, u32[]{:S(2)}, u32[]{:S(2)}) collective-permute-start(bf16[8,2,128,128]{3,2,1,0:T(8,128)(2,1)} %refs_11_.2), channel_id=1, source_target_pairs={{0,16},{8,24},{16,0},{24,8},{1,17},{9,25},{17,1},{25,9},{2,18},{10... | collective-permute-start | bytes 1572872 | tf_op jit(solution)/shard_map/ppermute | solution.py:197
  19.4 1.5 %collective-permute-start.10 = (bf16[8,2,128,128]{3,2,1,0:T(8,128)(2,1)}, bf16[8,2,128,128]{3,2,1,0:T(8,128)(2,1)S(1)}, u32[]{:S(2)}, u32[]{:S(2)}) collective-permute-start(bf16[8,2,128,128]{3,2,1,0:T(8,128)(2,1)} %refs_11_.2), channel_id=1, source_target_pairs={{0,8},{8,0},{16,24},{24,16},{1,9},{9,1},{17,25},{25,17},{2,10},{10... | collective-permute-start | bytes 1572872 | tf_op jit(solution)/shard_map/ppermute | solution.py:197
  20.9 11.9 %collective-permute-done.3.refs_7_ = bf16[8,2,128,128]{3,2,1,0:T(8,128)(2,1)S(1)} collective-permute-done((bf16[8,2,128,128]{3,2,1,0:T(8,128)(2,1)S(1)}, bf16[8,2,128,128]{3,2,1,0:T(8,128)(2,1)S(1)}, u32[]{:S(2)}, u32[]{:S(2)}) %collective-permute-start.3) | collective-permute-done | bytes 524320 | tf_op jit(solution)/shard_map/ppermute | solution.py:200
  32.8 1.3 collective-permute-start.7
  34.1 0.8 collective-permute-start.12
  34.9 0.2 collective-permute-start.4
  35.1 11.7 %collective-permute-done.5.refs_9_ = bf16[8,2,128,128]{3,2,1,0:T(8,128)(2,1)S(1)} collective-permute-done((bf16[8,2,128,128]{3,2,1,0:T(8,128)(2,1)S(1)}, bf16[8,2,128,128]{3,2,1,0:T(8,128)(2,1)S(1)}, u32[]{:S(2)}, u32[]{:S(2)}) %collective-permute-start.5) | collective-permute-done | bytes 524320 | tf_op jit(solution)/shard_map/ppermute | solution.py:200
  46.8 0.7 copy-done.5
  47.6 0.1 copy.10
  47.6 0.1 reshape.14
  47.7 0.6 copy-done.3
  48.3 0.1 copy.11
  48.4 0.6 reshape.13.refs_2_
  49.0 0.2 dynamic-update-slice
  49.2 42.0 %all-reduce.refs_1_ = s32[1024]{0:T(1024)} all-reduce(s32[1024]{0:T(1024)S(1)} %dynamic-update-slice), channel_id=1, replica_groups=mesh['row'=4,'col'=8] {'row','col'}, use_global_device_ids=true, to_apply=%add | all-reduce | flops 1024 | bytes 8192
  91.1 0.6 pad_add_fusion.1.refs_0_
  91.8 2.5 %collective-permute-start.8 = (bf16[8,2,128,128]{3,2,1,0:T(8,128)(2,1)}, bf16[8,2,128,128]{3,2,1,0:T(8,128)(2,1)S(1)}, u32[]{:S(2)}, u32[]{:S(2)}) collective-permute-start(bf16[8,2,128,128]{3,2,1,0:T(8,128)(2,1)} %refs_11_.3), channel_id=1, source_target_pairs={{0,16},{8,24},{16,0},{24,8},{1,17},{9,25},{17,1},{25,9},{2,18},{10... | collective-permute-start | bytes 1572872 | tf_op jit(solution)/shard_map/ppermute | solution.py:197
  94.3 0.1 collective-permute-start.9
  94.5 0.7 copy-done.11
  95.1 21.2 %mixed.1 = (bf16[8,4,128,128]{3,2,1,0:T(8,128)(2,1)}, f32[8,2,128,128]{3,2,1,0:T(8,128)}, bf16[8,2,128,128]{3,2,1,0:T(8,128)(2,1)}, bf16[8,2,128,128]{3,2,1,0:T(...) custom-call(s32[2]{0:T(128)} %pad_add_fusion.1.refs_0_, s32[1024]{0:T(1024)} %all-reduce.refs_1_, ...), custom_call_target="tpu_custom_call" | custom-call | flops 8589934592 | bytes 12582912 | tf_op jit(solution)/shard_map/mixed/pallas_call | solution.py:229
  116.3 1.2 collective-permute-start.13
  117.6 0.9 collective-permute-start.14
  118.5 1.4 collective-permute-start.15
  119.9 0.8 copy-done.13
  120.7 0.2 copy-done.14
  120.9 12.2 %squared.1 = bf16[8,4,128,128]{3,2,1,0:T(8,128)(2,1)} custom-call(s32[2]{0:T(128)} %pad_add_fusion.1.refs_0_, s32[1024]{0:T(1024)} %all-reduce.refs_1_, s32[32]{0:T(128)} %reshape.13.refs_2_, bf16[8,2,128,128]{3,2,1,0:T(8,128)(2,1)} %refs_11_.3, bf16[8,2,128,128]{3,2,1,0:T(8,128)(2,1)} %copy-done.8, bf16[8,2,128,128]{3,2,1,0:T(8,128)(2,1)} %copy-done.6, ...), custom_call_target="tpu_custom_call" | custom-call | flops 4294967296 | bytes 8388608 | tf_op jit(solution)/shard_map/squared/pallas_call | solution.py:246
  133.0 7.8 %collective-permute-done.14.refs_3_ = bf16[8,2,128,128]{3,2,1,0:T(8,128)(2,1)S(1)} collective-permute-done((bf16[8,2,128,128]{3,2,1,0:T(8,128)(2,1)}, bf16[8,2,128,128]{3,2,1,0:T(8,128)(2,1)S(1)}, u32[]{:S(2)}, u32[]{:S(2)}) %collective-permute-start.14) | collective-permute-done | bytes 524320 | tf_op jit(solution)/shard_map/ppermute | solution.py:197
  140.8 0.8 copy-done.1
  141.6 0.2 copy-done.2
  141.8 3.0 %gradient.1 = bf16[8,2,128,128]{3,2,1,0:T(8,128)(2,1)} custom-call(f32[8,2,128,128]{3,2,1,0:T(8,128)} %get-tuple-element.9.refs_15_.refs_0_, bf16[8,2,128,128]{3,2,1,0:T(8,128)(2,1)} %get-tuple-element.11.refs_1_, bf16[8,2,128,128]{3,2,1,0:T(8,128)(2,1)} %copy-done, bf16[8,2,128,128]{3,2,1,0:T(8,128)(2,1)} %copy-done.1, bf16[8,2,128,128]{3,2,1,0:T(8,128)(2,1)} %copy-done.2), custom_call_target="tpu_custom_call" | custom-call | tf_op jit(solution)/shard_map/gradient/pallas_call | solution.py:256
  (42 shorter events, 0.2 us)
Async XLA Ops:
  0.6 17.2 %collective-permute-start.1 = (bf16[8,2,128,128]{3,2,1,0:T(8,128)(2,1)}, bf16[8,2,128,128]{3,2,1,0:T(8,128)(2,1)S(1)}, u32[]{:S(2)}, u32[]{:S(2)}) collective-permute-start(bf16[8,2,128,128]{3,2,1,0:T(8,128)(2,1)} %refs_11_.3), channel_id=1, source_target_pairs={{0,2},{1,3},{2,4},{3,5},{4,6},{5,7},{6,0},{7,1},{8,10},{9,11},{10,... | collective-permute-start | bytes 1572872 | tf_op jit(solution)/shard_map/ppermute | solution.py:200
  17.9 76.6 %copy-start.6 = (bf16[8,2,128,128]{3,2,1,0:T(8,128)(2,1)}, bf16[8,2,128,128]{3,2,1,0:T(8,128)(2,1)S(1)}, u32[]{:S(2)}) copy-start(bf16[8,2,128,128]{3,2,1,0:T(8,128)(2,1)S(1)} %collective-permute-done.1.refs_5_) | copy-start | bytes 1572868
  17.9 14.9 %collective-permute-start.3 = (bf16[8,2,128,128]{3,2,1,0:T(8,128)(2,1)S(1)}, bf16[8,2,128,128]{3,2,1,0:T(8,128)(2,1)S(1)}, u32[]{:S(2)}, u32[]{:S(2)}) collective-permute-start(bf16[8,2,128,128]{3,2,1,0:T(8,128)(2,1)S(1)} %collective-permute-done.1.refs_5_), channel_id=1, source_target_pairs={{0,2},{1,3},{2,4},{3,5},{4,6},{5,7},{6,0},{7,1},{8,10},{9,11},{10,... | collective-permute-start | bytes 1572872 | tf_op jit(solution)/shard_map/ppermute | solution.py:200
  17.9 16.2 %collective-permute-start.11 = (bf16[8,2,128,128]{3,2,1,0:T(8,128)(2,1)}, bf16[8,2,128,128]{3,2,1,0:T(8,128)(2,1)}, u32[]{:S(2)}, u32[]{:S(2)}) collective-permute-start(bf16[8,2,128,128]{3,2,1,0:T(8,128)(2,1)} %refs_11_.2), channel_id=1, source_target_pairs={{0,16},{8,24},{16,0},{24,8},{1,17},{9,25},{17,1},{25,9},{2,18},{10... | collective-permute-start | bytes 1572872 | tf_op jit(solution)/shard_map/ppermute | solution.py:197
  19.4 14.7 %collective-permute-start = (bf16[8,2,128,128]{3,2,1,0:T(8,128)(2,1)}, bf16[8,2,128,128]{3,2,1,0:T(8,128)(2,1)S(1)}, u32[]{:S(2)}, u32[]{:S(2)}) collective-permute-start(bf16[8,2,128,128]{3,2,1,0:T(8,128)(2,1)} %refs_11_.3), channel_id=1, source_target_pairs={{0,1},{1,0},{2,3},{3,2},{4,5},{5,4},{6,7},{7,6},{8,9},{9,8},{10,11... | collective-permute-start | bytes 1572872 | tf_op jit(solution)/shard_map/ppermute | solution.py:203
  19.4 15.5 %collective-permute-start.10 = (bf16[8,2,128,128]{3,2,1,0:T(8,128)(2,1)}, bf16[8,2,128,128]{3,2,1,0:T(8,128)(2,1)S(1)}, u32[]{:S(2)}, u32[]{:S(2)}) collective-permute-start(bf16[8,2,128,128]{3,2,1,0:T(8,128)(2,1)} %refs_11_.2), channel_id=1, source_target_pairs={{0,8},{8,0},{16,24},{24,16},{1,9},{9,1},{17,25},{25,17},{2,10},{10... | collective-permute-start | bytes 1572872 | tf_op jit(solution)/shard_map/ppermute | solution.py:197
  32.8 61.7 %copy-start.7 = (bf16[8,2,128,128]{3,2,1,0:T(8,128)(2,1)}, bf16[8,2,128,128]{3,2,1,0:T(8,128)(2,1)S(1)}, u32[]{:S(2)}) copy-start(bf16[8,2,128,128]{3,2,1,0:T(8,128)(2,1)S(1)} %collective-permute-done.3.refs_7_) | copy-start | bytes 1572868
  32.8 14.0 %collective-permute-start.5 = (bf16[8,2,128,128]{3,2,1,0:T(8,128)(2,1)S(1)}, bf16[8,2,128,128]{3,2,1,0:T(8,128)(2,1)S(1)}, u32[]{:S(2)}, u32[]{:S(2)}) collective-permute-start(bf16[8,2,128,128]{3,2,1,0:T(8,128)(2,1)S(1)} %collective-permute-done.3.refs_7_), channel_id=1, source_target_pairs={{0,2},{1,3},{2,4},{3,5},{4,6},{5,7},{6,0},{7,1},{8,10},{9,11},{10,... | collective-permute-start | bytes 1572872 | tf_op jit(solution)/shard_map/ppermute | solution.py:200
  32.8 59.0 %collective-permute-start.7 = (bf16[8,2,128,128]{3,2,1,0:T(8,128)(2,1)}, bf16[8,2,128,128]{3,2,1,0:T(8,128)(2,1)S(1)}, u32[]{:S(2)}, u32[]{:S(2)}) collective-permute-start(bf16[8,2,128,128]{3,2,1,0:T(8,128)(2,1)} %refs_11_.3), channel_id=1, source_target_pairs={{0,8},{8,0},{16,24},{24,16},{1,9},{9,1},{17,25},{25,17},{2,10},{10... | collective-permute-start | bytes 1572872 | tf_op jit(solution)/shard_map/ppermute | solution.py:197
  34.0 60.3 %collective-permute-start.2 = (bf16[8,2,128,128]{3,2,1,0:T(8,128)(2,1)S(1)}, bf16[8,2,128,128]{3,2,1,0:T(8,128)(2,1)S(1)}, u32[]{:S(2)}, u32[]{:S(2)}) collective-permute-start(bf16[8,2,128,128]{3,2,1,0:T(8,128)(2,1)S(1)} %collective-permute-done.1.refs_5_), channel_id=1, source_target_pairs={{0,1},{1,0},{2,3},{3,2},{4,5},{5,4},{6,7},{7,6},{8,9},{9,8},{10,11... | collective-permute-start | bytes 1572872 | tf_op jit(solution)/shard_map/ppermute | solution.py:203
  34.0 60.4 %copy-start.8 = (bf16[8,2,128,128]{3,2,1,0:T(8,128)(2,1)}, bf16[8,2,128,128]{3,2,1,0:T(8,128)(2,1)S(1)}, u32[]{:S(2)}) copy-start(bf16[8,2,128,128]{3,2,1,0:T(8,128)(2,1)S(1)} %collective-permute-done.refs_4_) | copy-start | bytes 1572868
  34.1 60.3 %collective-permute-start.12 = (bf16[8,2,128,128]{3,2,1,0:T(8,128)(2,1)}, bf16[8,2,128,128]{3,2,1,0:T(8,128)(2,1)}, u32[]{:S(2)}, u32[]{:S(2)}) collective-permute-start(bf16[8,2,128,128]{3,2,1,0:T(8,128)(2,1)} %collective-permute-done.11.refs_13_), channel_id=1, source_target_pairs={{0,8},{8,0},{16,24},{24,16},{1,9},{9,1},{17,25},{25,17},{2,10},{10... | collective-permute-start | bytes 1572872 | tf_op jit(solution)/shard_map/ppermute | solution.py:197
  34.9 11.9 %copy-start.12 = (bf16[8,2,128,128]{3,2,1,0:T(8,128)(2,1)}, bf16[8,2,128,128]{3,2,1,0:T(8,128)(2,1)S(1)}, u32[]{:S(2)}) copy-start(bf16[8,2,128,128]{3,2,1,0:T(8,128)(2,1)S(1)} %collective-permute-done.10.refs_12_) | copy-start | bytes 1572868
  34.9 59.5 %collective-permute-start.4 = (bf16[8,2,128,128]{3,2,1,0:T(8,128)(2,1)S(1)}, bf16[8,2,128,128]{3,2,1,0:T(8,128)(2,1)}, u32[]{:S(2)}, u32[]{:S(2)}) collective-permute-start(bf16[8,2,128,128]{3,2,1,0:T(8,128)(2,1)S(1)} %collective-permute-done.3.refs_7_), channel_id=1, source_target_pairs={{0,1},{1,0},{2,3},{3,2},{4,5},{5,4},{6,7},{7,6},{8,9},{9,8},{10,11... | collective-permute-start | bytes 1572872 | tf_op jit(solution)/shard_map/ppermute | solution.py:203
  46.8 47.7 %copy-start.9 = (bf16[8,2,128,128]{3,2,1,0:T(8,128)(2,1)}, bf16[8,2,128,128]{3,2,1,0:T(8,128)(2,1)S(1)}, u32[]{:S(2)}) copy-start(bf16[8,2,128,128]{3,2,1,0:T(8,128)(2,1)S(1)} %collective-permute-done.5.refs_9_) | copy-start | bytes 1572868
  46.8 47.6 %collective-permute-start.6 = (bf16[8,2,128,128]{3,2,1,0:T(8,128)(2,1)S(1)}, bf16[8,2,128,128]{3,2,1,0:T(8,128)(2,1)}, u32[]{:S(2)}, u32[]{:S(2)}) collective-permute-start(bf16[8,2,128,128]{3,2,1,0:T(8,128)(2,1)S(1)} %collective-permute-done.5.refs_9_), channel_id=1, source_target_pairs={{0,1},{1,0},{2,3},{3,2},{4,5},{5,4},{6,7},{7,6},{8,9},{9,8},{10,11... | collective-permute-start | bytes 1572872 | tf_op jit(solution)/shard_map/ppermute | solution.py:203
  46.8 0.7 copy-start.5
  46.8 0.8 copy-start.4
  47.6 0.7 copy-start.3
  91.8 24.5 %copy-start.10 = (bf16[8,2,128,128]{3,2,1,0:T(8,128)(2,1)}, bf16[8,2,128,128]{3,2,1,0:T(8,128)(2,1)S(1)}, u32[]{:S(2)}) copy-start(bf16[8,2,128,128]{3,2,1,0:T(8,128)(2,1)S(1)} %collective-permute-done.7.refs_12_) | copy-start | bytes 1572868
  91.8 28.1 %collective-permute-start.8 = (bf16[8,2,128,128]{3,2,1,0:T(8,128)(2,1)}, bf16[8,2,128,128]{3,2,1,0:T(8,128)(2,1)S(1)}, u32[]{:S(2)}, u32[]{:S(2)}) collective-permute-start(bf16[8,2,128,128]{3,2,1,0:T(8,128)(2,1)} %refs_11_.3), channel_id=1, source_target_pairs={{0,16},{8,24},{16,0},{24,8},{1,17},{9,25},{17,1},{25,9},{2,18},{10... | collective-permute-start | bytes 1572872 | tf_op jit(solution)/shard_map/ppermute | solution.py:197
  94.3 0.8 copy-start.11
  94.3 25.6 %collective-permute-start.9 = (bf16[8,2,128,128]{3,2,1,0:T(8,128)(2,1)S(1)}, bf16[8,2,128,128]{3,2,1,0:T(8,128)(2,1)S(1)}, u32[]{:S(2)}, u32[]{:S(2)}) collective-permute-start(bf16[8,2,128,128]{3,2,1,0:T(8,128)(2,1)S(1)} %collective-permute-done.7.refs_12_), channel_id=1, source_target_pairs={{0,16},{8,24},{16,0},{24,8},{1,17},{9,25},{17,1},{25,9},{2,18},{10... | collective-permute-start | bytes 1572872 | tf_op jit(solution)/shard_map/ppermute | solution.py:197
  116.3 16.7 %collective-permute-start.13 = (bf16[8,2,128,128]{3,2,1,0:T(8,128)(2,1)}, bf16[8,2,128,128]{3,2,1,0:T(8,128)(2,1)S(1)}, u32[]{:S(2)}, u32[]{:S(2)}) collective-permute-start(bf16[8,2,128,128]{3,2,1,0:T(8,128)(2,1)} %get-tuple-element.12), channel_id=1, source_target_pairs={{0,8},{8,0},{16,24},{24,16},{1,9},{9,1},{17,25},{25,17},{2,10},{10... | collective-permute-start | bytes 1572872 | tf_op jit(solution)/shard_map/ppermute | solution.py:197
  117.6 23.3 %collective-permute-start.14 = (bf16[8,2,128,128]{3,2,1,0:T(8,128)(2,1)}, bf16[8,2,128,128]{3,2,1,0:T(8,128)(2,1)S(1)}, u32[]{:S(2)}, u32[]{:S(2)}) collective-permute-start(bf16[8,2,128,128]{3,2,1,0:T(8,128)(2,1)} %get-tuple-element.13), channel_id=1, source_target_pairs={{0,16},{8,24},{16,0},{24,8},{1,17},{9,25},{17,1},{25,9},{2,18},{10... | collective-permute-start | bytes 1572872 | tf_op jit(solution)/shard_map/ppermute | solution.py:197
  118.5 22.3 %collective-permute-start.15 = (bf16[8,2,128,128]{3,2,1,0:T(8,128)(2,1)}, bf16[8,2,128,128]{3,2,1,0:T(8,128)(2,1)S(1)}, u32[]{:S(2)}, u32[]{:S(2)}) collective-permute-start(bf16[8,2,128,128]{3,2,1,0:T(8,128)(2,1)} %get-tuple-element.14), channel_id=1, source_target_pairs={{0,24},{8,16},{16,8},{24,0},{1,25},{9,17},{17,9},{25,1},{2,26},{10... | collective-permute-start | bytes 1572872 | tf_op jit(solution)/shard_map/ppermute | solution.py:197
  119.9 0.8 copy-start.13
  119.9 1.0 copy-start.14
  133.0 7.8 %copy-start = (bf16[8,2,128,128]{3,2,1,0:T(8,128)(2,1)}, bf16[8,2,128,128]{3,2,1,0:T(8,128)(2,1)S(1)}, u32[]{:S(2)}) copy-start(bf16[8,2,128,128]{3,2,1,0:T(8,128)(2,1)S(1)} %collective-permute-done.13.refs_2_) | copy-start | bytes 1572868
  140.8 0.8 copy-start.1
  140.8 1.0 copy-start.2

commit v2 on v0

v2 whole, which is shorter than its diff:
```python
import functools

import jax
import jax.numpy as jnp
from jax import lax
from jax.experimental import pallas as pl
from jax.experimental.pallas import tpu as pltpu
from jax.sharding import PartitionSpec as P

VMEM_LIMIT = 52 * 1024 * 1024
TAIL = 16
BF16, F32 = jnp.bfloat16, jnp.float32


class Sizes:
    def __init__(self, n_row, n_col, density, hamilton, filt):
        self.n_row, self.n_col, self.n_chip = n_row, n_col, n_col // 2
        self.rows, self.ka, self.bs = density.shape[0], density.shape[1], density.shape[2]
        self.kh, self.kf = hamilton.shape[1], filt.shape[1]
        self.nb = self.rows * n_row
        self.bc = self.nb // n_col
        self.tall, self.wide = self.rows * self.bs, self.bc * self.bs
        self.n_first = n_col - 2


def lanes(z, block):
    return pl.ds(pl.multiple_of(block * z.bs, z.bs), z.bs)


def block_rows(z, i, s, slots):
    return slice((i * slots + s) * z.bs, (i * slots + s + 1) * z.bs)


def piece_col(z, n):
    me = lax.axis_index("col")
    step, core = n // 2, lax.rem(me, 2) ^ (n % 2)
    up = lax.rem(me // 2 + step, z.n_chip)
    down = lax.rem(me // 2 + z.n_chip - step, z.n_chip)
    return jnp.where(core == 0, down, up) * 2 + core


def piece_of(z, col):
    me = lax.axis_index("col")
    chip, core = col // 2, lax.rem(col, 2)
    ahead = lax.rem(chip - me // 2 + z.n_chip, z.n_chip)
    behind = lax.rem(me // 2 - chip + z.n_chip, z.n_chip)
    return jnp.where(core == 0, behind, ahead) * 2 + (core ^ lax.rem(me, 2))


def pack_kernel(z, d_in, h_in, d_cols, h_cols, d_out, h_out, wide_tail, tail, sems):
    n = d_in.shape[0]
    m = h_in.shape[0]
    copies = [
        pltpu.make_async_copy(d_in, d_out.at[pl.ds(0, n)], sems.at[0]),
        pltpu.make_async_copy(h_in, h_out.at[pl.ds(0, m)], sems.at[1]),
    ]
    for copy in copies:
        copy.start()
    wide_tail[...] = jnp.zeros_like(wide_tail)
    wide_tail[0:z.ka, 0:z.rows] = d_cols[...].astype(F32)
    wide_tail[z.ka:z.ka + z.kh, 0:z.rows] = h_cols[...].astype(F32)
    tail[...] = wide_tail[...].astype(BF16)
    tails = [
        pltpu.make_async_copy(tail, d_out.at[pl.ds(n, TAIL)], sems.at[2]),
        pltpu.make_async_copy(tail, h_out.at[pl.ds(m, TAIL)], sems.at[3]),
    ]
    for copy in tails:
        copy.start()
    for copy in copies + tails:
        copy.wait()


def read_tails(ins, blocks, tails, ints, idx, sems, int_sem):
    copies = [
        pltpu.make_async_copy(ref.at[pl.ds(rows, TAIL)], tails.at[n], sems.at[n])
        for n, (ref, rows) in enumerate(zip(ins, blocks))
    ]
    for copy in copies:
        copy.start()
    for copy in copies:
        copy.wait()
    ints[...] = tails[:, 0:8, :].astype(F32).astype(jnp.int32)
    copy = pltpu.make_async_copy(ints, idx, int_sem)
    copy.start()
    copy.wait()


def fill_left(z, idx, n, col, buf, dense):
    zero = jnp.zeros((z.bs, z.wide), BF16)
    for i in range(z.rows):
        rows = slice(i * z.bs, (i + 1) * z.bs)
        dense[rows, :] = zero
        for s in range(z.ka):
            k = idx[n, s, i] - col * z.bc
            dense[rows, lanes(z, k)] = buf[block_rows(z, i, s, z.ka), :]


def fill_right(z, first_slot, slots, idx, row_of, buf, dense):
    dense[...] = jnp.zeros_like(dense)
    me = lax.axis_index("col")

    def one(p, _):
        for i in range(z.rows):
            k = row_of(p) * z.rows + i
            n = piece_of(z, k // z.bc)
            at = pl.ds(pl.multiple_of((n * z.bc + lax.rem(k, z.bc)) * z.bs, z.bs), z.bs)
            for s in range(slots):
                j = idx[p, first_slot + s, i] - me * z.bc
                dense[at, lanes(z, j)] = buf[p, block_rows(z, i, s, slots), :]
        return 0

    lax.fori_loop(0, z.n_row, one, 0)


def first_kernel(z, *refs):
    left_in, right_in, rest = refs[:z.n_first], refs[z.n_first:z.n_first + z.n_row], refs[z.n_first + z.n_row:]
    total, panel, right_last, table = rest[:4]
    left_buf, right_buf, dense, right, tails, ints, idx, left_sem, right_sem, tail_sem, out_sem, int_sem = rest[4:]
    d_rows, h_rows = z.rows * z.ka * z.bs, z.rows * z.kh * z.bs
    copies = [
        pltpu.make_async_copy(ref.at[pl.ds(0, h_rows)], right_buf.at[n], right_sem.at[n])
        for n, ref in enumerate(right_in)
    ] + [
        pltpu.make_async_copy(ref.at[pl.ds(0, d_rows)], left_buf.at[n], left_sem.at[n])
        for n, ref in enumerate(left_in)
    ]
    for copy in copies:
        copy.start()
    read_tails(right_in + left_in, [h_rows] * z.n_row + [d_rows] * z.n_first, tails, ints, idx, tail_sem, int_sem)
    table[...] = ints[0:z.n_row]
    for copy in copies[:z.n_row]:
        copy.wait()
    fill_right(z, z.ka, z.kh, idx, lambda p: lax.axis_index("row") ^ p, right_buf, right)
    outs = []
    for n in range(z.n_first):
        copies[z.n_row + n].wait()
        here = dense.at[:, n * z.wide:(n + 1) * z.wide]
        fill_left(z, idx, z.n_row + n, piece_col(z, n), left_buf.at[n], here)
        outs.append(pltpu.make_async_copy(here, panel.at[n], out_sem.at[n]))
        outs[-1].start()
    deep = z.n_first * z.wide
    half = z.tall // 2
    for m in range(2):
        rows = slice(m * half, (m + 1) * half)
        total[rows, :] = jnp.dot(dense[rows, :], right[0:deep, :], preferred_element_type=F32)
    right_last[...] = right[deep:, :]
    for copy in outs:
        copy.wait()


def parts_kernel(z, *refs):
    table, left_in, right_in, total_in, panel = refs[0], refs[1:3], refs[3], refs[4], refs[5]
    total_out, turned_out, panel_last = refs[6:9]
    parts = refs[9:9 + z.n_row - 1]
    (left_buf, last, right, total, dense, turned, columns, part_buf, tails, ints, idx,
     sems, dense_sem, tail_sem, out_sem, part_sem, int_sem) = refs[9 + z.n_row - 1:]
    d_rows = z.rows * z.ka * z.bs
    copies = [
        pltpu.make_async_copy(left_in[0].at[pl.ds(0, d_rows)], left_buf.at[0], sems.at[0]),
        pltpu.make_async_copy(left_in[1].at[pl.ds(0, d_rows)], left_buf.at[1], sems.at[1]),
        pltpu.make_async_copy(right_in, right, sems.at[2]),
        pltpu.make_async_copy(total_in, total, sems.at[3]),
    ]
    for copy in copies:
        copy.start()
    loads = [pltpu.make_async_copy(panel.at[n], dense.at[n], dense_sem.at[n]) for n in range(z.n_first)]
    for copy in loads:
        copy.start()
    read_tails(left_in, [d_rows] * 2, tails, ints, idx, tail_sem, int_sem)
    outs = []
    for n in range(2):
        copies[n].wait()
        here = last.at[:, n * z.wide:(n + 1) * z.wide]
        fill_left(z, idx, n, piece_col(z, z.n_first + n), left_buf.at[n], here)
        outs.append(pltpu.make_async_copy(here, panel_last.at[n], out_sem.at[n]))
        outs[-1].start()
        dense[z.n_first + n] = here[...]
    copies[2].wait()
    copies[3].wait()
    half = z.tall // 2
    for m in range(2):
        rows = slice(m * half, (m + 1) * half)
        total[rows, :] += jnp.dot(last[rows, :], right[...], preferred_element_type=F32)
    outs.append(pltpu.make_async_copy(total, total_out, out_sem.at[2]))
    outs[-1].start()
    for i in range(z.rows):
        rows = slice(i * z.bs, (i + 1) * z.bs)
        for j in range(z.bc):
            cols = slice(j * z.bs, (j + 1) * z.bs)
            turned[cols, rows] = total[rows, cols].T.astype(BF16)
    outs.append(pltpu.make_async_copy(turned, turned_out, out_sem.at[3]))
    outs[-1].start()
    for copy in loads:
        copy.wait()
    for n in reversed(range(1, z.n_row)):
        one_part(z, table, n, turned, dense, columns, part_buf.at[n - 1])
        outs.append(pltpu.make_async_copy(part_buf.at[n - 1], parts[n - 1], part_sem.at[n - 1]))
        outs[-1].start()
    for copy in outs:
        copy.wait()


def one_part(z, table, n, turned, dense, columns, out):
    row = lax.axis_index("row") ^ n
    per = z.n_col // z.n_row
    for t in range(per):
        column = columns.at[t % 2]
        column[...] = jnp.dot(turned[...], dense[piece_of(z, row * per + t)], preferred_element_type=F32)
        for b in range(z.bc):
            i = t * z.bc + b
            for s in range(z.ka):
                j = table[n, s, i] - lax.axis_index("col") * z.bc
                out[i, s] = column[lanes(z, j), b * z.bs:(b + 1) * z.bs].astype(out.dtype)


def square_kernel(z, *refs):
    table, filt = refs[:2]
    right_in, panel, panel_last, total_in, turned_in = refs[2:2 + z.n_row], *refs[2 + z.n_row:6 + z.n_row]
    squared, mixed, base = refs[6 + z.n_row:9 + z.n_row]
    right_buf, right, dense, total, turned, columns, own, right_sem, sems, dense_sem = refs[9 + z.n_row:]
    copies = [pltpu.make_async_copy(ref, right_buf.at[n], right_sem.at[n]) for n, ref in enumerate(right_in)]
    small = [
        pltpu.make_async_copy(total_in, total, sems.at[0]),
        pltpu.make_async_copy(turned_in, turned, sems.at[1]),
    ]
    loads = [pltpu.make_async_copy(panel.at[n], dense.at[n], dense_sem.at[n]) for n in range(z.n_first)]
    loads += [
        pltpu.make_async_copy(panel_last.at[n], dense.at[z.n_first + n], dense_sem.at[z.n_first + n]) for n in range(2)
    ]
    for copy in small + copies + loads:
        copy.start()
    me = lax.axis_index("col")
    small[0].wait()
    for i in range(z.rows):
        rows = slice(i * z.bs, (i + 1) * z.bs)
        for s in range(z.kf):
            mixed[i, s] = total[rows, lanes(z, filt[s, i] - me * z.bc)].astype(mixed.dtype)
    small[1].wait()
    for copy in loads:
        copy.wait()
    one_part(z, table, 0, turned, dense, columns, own)
    for i in range(z.rows):
        rows = slice(i * z.bs, (i + 1) * z.bs)
        for s in range(z.ka):
            direct = total[rows, lanes(z, table[0, s, i] - me * z.bc)]
            base[i, s] = 3.0 * direct - 2.0 * own[i, s].T
    for copy in copies:
        copy.wait()
    fill_right(z, 0, z.ka, table, lambda p: lax.axis_index("row") ^ p, right_buf, right)
    half = z.tall // 2
    for m in range(2):
        rows = slice(m * half, (m + 1) * half)
        left = jnp.concatenate([dense[n, rows, :] for n in range(z.n_col)], axis=1)
        total[rows, :] = jnp.dot(left, right[...], preferred_element_type=F32)
    for i in range(z.rows):
        rows = slice(i * z.bs, (i + 1) * z.bs)
        for s in range(z.kf):
            squared[i, s] = total[rows, lanes(z, filt[s, i] - me * z.bc)].astype(squared.dtype)


def gradient_kernel(z, base, *refs):
    parts, out = refs[:z.n_row - 1], refs[z.n_row - 1]
    for i in range(z.rows):
        for s in range(z.ka):
            cubic = parts[0][i, s].astype(F32)
            for n in range(1, z.n_row - 1):
                cubic += parts[n][i, s].astype(F32)
            out[i, s] = (base[i, s] - 2.0 * cubic.T).astype(out.dtype)


def local(n_row, n_col, density, density_cols, hamilton, hamilton_cols, filter_cols):
    z = Sizes(n_row, n_col, density, hamilton, filter_cols)
    block = (z.bs, z.bs)
    shape = jax.ShapeDtypeStruct
    smem = pl.BlockSpec(memory_space=pltpu.SMEM)
    vmem = pl.BlockSpec(memory_space=pltpu.VMEM)
    anywhere = pl.BlockSpec(memory_space=pl.ANY)
    params = pltpu.CompilerParams(vmem_limit_bytes=VMEM_LIMIT)
    dma = pltpu.SemaphoreType.DMA
    d_rows, h_rows = z.rows * z.ka * z.bs, z.rows * z.kh * z.bs
    panel_flops = 2 * z.tall * z.wide * z.nb * z.bs

    def over_row(x, flip):
        return lax.ppermute(x, "row", [(r, r ^ flip) for r in range(n_row)])

    def next_chip(x):
        pairs = [(2 * p, 2 * ((p + 1) % z.n_chip)) for p in range(z.n_chip)]
        pairs += [(2 * p + 1, 2 * ((p - 1) % z.n_chip) + 1) for p in range(z.n_chip)]
        return lax.ppermute(x, "col", pairs)

    def other_core(x):
        return lax.ppermute(x, "col", [(c, c ^ 1) for c in range(n_col)])

    flat = density.reshape(d_rows, z.bs)
    d_pay, h_pay = pl.pallas_call(
        functools.partial(pack_kernel, z),
        out_shape=[shape((d_rows + TAIL, z.bs), BF16), shape((h_rows + TAIL, z.bs), BF16)],
        in_specs=[anywhere, anywhere, vmem, vmem],
        out_specs=[anywhere, anywhere],
        scratch_shapes=[pltpu.VMEM((TAIL, z.bs), F32), pltpu.VMEM((TAIL, z.bs), BF16), dma((4,))],
        name="pack",
    )(flat, hamilton.reshape(h_rows, z.bs), density_cols.T, hamilton_cols.T)

    pieces, d_right, h_right = [d_pay], {0: flat}, {0: h_pay}
    left = [d_pay]
    for step in range(1, z.n_chip):
        pieces.append(next_chip(pieces[-1]))
        for flip in range(1, n_row):
            bits, low = flip.bit_count(), flip & -flip
            if bits == step:
                h_right[flip] = over_row(h_right[flip - low], low)
            if (step == 2 and flip == 1) or (step == 3 and bits == 1 and flip > 1):
                d_right[flip] = over_row(d_right[flip - low], low)
        left.append(other_core(left[-1]))
        if step < z.n_chip - 1:
            pieces[-1], left, d_right, h_right = lax.optimization_barrier((pieces[-1], left, d_right, h_right))
        left.append(pieces[-1])
    h_right = [h_right[flip] for flip in range(n_row)]

    total, panel, right_last, table = pl.pallas_call(
        functools.partial(first_kernel, z),
        out_shape=[
            shape((z.tall, z.wide), F32),
            shape((z.n_first, z.tall, z.wide), BF16),
            shape((2 * z.wide, z.wide), BF16),
            shape((n_row, 8, z.bs), jnp.int32),
        ],
        in_specs=[anywhere] * (z.n_first + n_row),
        out_specs=[vmem, anywhere, vmem, vmem],
        scratch_shapes=[
            pltpu.VMEM((z.n_first, d_rows, z.bs), BF16),
            pltpu.VMEM((n_row, h_rows, z.bs), BF16),
            pltpu.VMEM((z.tall, z.n_first * z.wide), BF16),
            pltpu.VMEM((z.nb * z.bs, z.wide), BF16),
            pltpu.VMEM((z.n_first + n_row, TAIL, z.bs), BF16),
            pltpu.VMEM((z.n_first + n_row, 8, z.bs), jnp.int32),
            pltpu.SMEM((z.n_first + n_row, 8, z.bs), jnp.int32),
            dma((z.n_first,)), dma((n_row,)), dma((z.n_first + n_row,)), dma((z.n_first,)), dma,
        ],
        compiler_params=params,
        cost_estimate=pl.CostEstimate(flops=panel_flops, bytes_accessed=16 << 20, transcendentals=0),
        name="first",
    )(*left[:z.n_first], *h_right)
    last, total, d_right = lax.optimization_barrier((left[-1], total, d_right))
    for flip in range(1, n_row):
        if flip not in d_right:
            d_right[flip] = over_row(d_right[flip & (flip - 1)], flip & -flip)
    d_right = [d_right[flip] for flip in range(n_row)]
    left = [last, other_core(last)]
    part = shape((z.rows, z.ka) + block, BF16)
    total, turned, panel_last, *parts = pl.pallas_call(
        functools.partial(parts_kernel, z),
        out_shape=[
            shape((z.tall, z.wide), F32),
            shape((z.wide, z.tall), BF16),
            shape((2, z.tall, z.wide), BF16),
        ] + [part] * (n_row - 1),
        in_specs=[smem] + [anywhere] * 5,
        out_specs=[anywhere] * (2 + n_row),
        scratch_shapes=[
            pltpu.VMEM((2, d_rows, z.bs), BF16),
            pltpu.VMEM((z.tall, 2 * z.wide), BF16),
            pltpu.VMEM((2 * z.wide, z.wide), BF16),
            pltpu.VMEM((z.tall, z.wide), F32),
            pltpu.VMEM((n_col, z.tall, z.wide), BF16),
            pltpu.VMEM((z.wide, z.tall), BF16),
            pltpu.VMEM((2, z.wide, z.wide), F32),
            pltpu.VMEM((n_row - 1, z.rows, z.ka) + block, BF16),
            pltpu.VMEM((2, TAIL, z.bs), BF16),
            pltpu.VMEM((2, 8, z.bs), jnp.int32),
            pltpu.SMEM((2, 8, z.bs), jnp.int32),
            dma((4,)), dma((z.n_first,)), dma((2,)), dma((4,)), dma((n_row - 1,)), dma,
        ],
        compiler_params=params,
        cost_estimate=pl.CostEstimate(flops=panel_flops, bytes_accessed=16 << 20, transcendentals=0),
        name="parts",
    )(table, *left, right_last, total, panel)
    received = [over_row(parts[n - 1], n) for n in range(1, n_row)]
    squared, mixed, base = pl.pallas_call(
        functools.partial(square_kernel, z),
        out_shape=[
            shape((z.rows, z.kf) + block, BF16),
            shape((z.rows, z.kf) + block, BF16),
            shape((z.rows, z.ka) + block, F32),
        ],
        in_specs=[smem] * 2 + [anywhere] * (n_row + 4),
        out_specs=[vmem] * 3,
        scratch_shapes=[
            pltpu.VMEM((n_row, d_rows, z.bs), BF16),
            pltpu.VMEM((z.nb * z.bs, z.wide), BF16),
            pltpu.VMEM((n_col, z.tall, z.wide), BF16),
            pltpu.VMEM((z.tall, z.wide), F32),
            pltpu.VMEM((z.wide, z.tall), BF16),
            pltpu.VMEM((2, z.wide, z.wide), F32),
            pltpu.VMEM((z.rows, z.ka) + block, F32),
            dma((n_row,)), dma((2,)), dma((n_col,)),
        ],
        compiler_params=params,
        cost_estimate=pl.CostEstimate(flops=2 * panel_flops, bytes_accessed=16 << 20, transcendentals=0),
        name="squared",
    )(table, filter_cols.T, *d_right, panel, panel_last, total, turned)
    gradient = pl.pallas_call(
        functools.partial(gradient_kernel, z),
        out_shape=part,
        in_specs=[vmem] * n_row,
        out_specs=vmem,
        name="gradient",
    )(base, *received)
    return squared, mixed, gradient


def solution(mesh):
    spec4 = P("row", "col", None, None)
    spec2 = P("row", "col")
    body = functools.partial(local, mesh.shape["row"], mesh.shape["col"])
    return jax.shard_map(
        body,
        mesh=mesh,
        in_specs=(spec4, spec2, spec4, spec2, spec2),
        out_specs=(spec4, spec4, spec4),
        check_vma=False,
    )
```

time: 519 us -> 141 us (0.27)
  local copies, waits for them, and re-layouts: 165 us -> 4.43 us
  matrix products: 128 us -> 0 us
  waiting for transfers between devices: 163 us -> 44.4 us
  Pallas kernels: 0 us -> 72.6 us
  blocking collectives: 42.6 us -> 0 us
  starting transfers between devices: 0.15 us -> 18.9 us
  between operations: 13.8 us -> 0.78 us
    all_gather x4 -> x0, waiting for transfers between devices: 161 us -> none  [the longest x1 68.1 us: local(): piece_values = lax.all_gather(square_term, 'col', axis=1, tiled=True)]
    dot_general x56 -> x0, matrix products: 128 us -> none  [the longest x24 80.2 us: block_products(): jnp.einsum('sab,stbc->stac', left_vals, chosen, preferred_element_type=jn...]
    reshape x24 -> x0, local copies, waits for them, and re-layouts: 81.1 us -> none  [block_products(): block_product_list.reshape(-1, block_size, block_size)]
    pallas_call x0 -> x5, Pallas kernels: none -> 72.6 us  [the longest x1 33.6 us: local(): pl.pallas_call(functools.partial(pack_kernel, z), out_shape=[shape((d_row...]
    gather x48 -> x0, local copies, waits for them, and re-layouts: 66.6 us -> none  [the longest x24 53 us: block_products(): chosen = right_vals[left_cols]]
    ppermute x0 -> x16, waiting for transfers between devices: none -> 44.4 us  [the longest x9 33.3 us: over_row(): return lax.ppermute(x, 'row', [(r, r ^ flip) for r in range(n_row)])]
    all_gather x4 -> x0, blocking collectives: 42.6 us -> none  [the longest x1 12.8 us: local(): piece_cols = lax.all_gather(filter_cols, 'col', axis=1, tiled=True)]
    ppermute x0 -> x16, starting transfers between devices: none -> 18.9 us  [the longest x9 10.7 us: over_row(): return lax.ppermute(x, 'row', [(r, r ^ flip) for r in range(n_row)])]
  transfers between devices with their start and end apart: 4 -> 16, of which waited for: 4 -> 7; matrix products, arithmetic and copies ran while one was open for 0% -> 0% of each run, Pallas kernels for 0% -> 26%
where the time goes in v2:
time: 141 us
  Pallas kernels  72.6 us (51%)
  waiting for transfers between devices  44.4 us (31%)
  starting transfers between devices  18.9 us (13%)
  local copies, waits for them, and re-layouts  4.43 us (3%)
    pallas_call x1, Pallas kernels, local(): pl.pallas_call(functools.partial(pack_kernel, z), out_shape=[shape((d_row...  33.6 us
    ppermute x9, waiting for transfers between devices, over_row(): return lax.ppermute(x, 'row', [(r, r ^ flip) for r in range(n_row)])  33.3 us
    pallas_call x1, Pallas kernels, local(): pl.pallas_call(functools.partial(square_kernel, z), out_shape=[shape((z.r...  14.2 us
    pallas_call x1, Pallas kernels, local(): pl.pallas_call(functools.partial(parts_kernel, z), out_shape=[shape((z.ta...  11.4 us
    ppermute x9, starting transfers between devices, over_row(): return lax.ppermute(x, 'row', [(r, r ^ flip) for r in range(n_row)])  10.7 us
    pallas_call x1, Pallas kernels, local(): pl.pallas_call(functools.partial(first_kernel, z), out_shape=[shape((z.ta...  10.7 us
    ppermute x3, waiting for transfers between devices, next_chip(): return lax.ppermute(x, 'col', pairs)  10.1 us
    ppermute x3, starting transfers between devices, next_chip(): return lax.ppermute(x, 'col', pairs)  5.21 us
  transfers between devices with their start and end apart: 16, of which 7 were waited for; matrix products, arithmetic and copies ran while one was open for 0% of the time, Pallas kernels for 26%

profile of v2, /device:TPU:0, one launch (start us, length us, event | category | flops | bytes accessed | tf_op | source)
XLA Modules:
  0.0 141.2 jit_solution(7770537511803020047)
XLA Ops:
  0.6 33.6 %pack.1 = (bf16[2064,128]{1,0:T(8,128)(2,1)}, bf16[2064,128]{1,0:T(8,128)(2,1)}) custom-call(bf16[2048,128]{1,0:T(8,128)(2,1)} %bitcast.5, bf16[2048,128]{1,0:T(8,128)(2,1)} %bitcast.10, s32[2,8]{1,0:T(2,128)} %bitcast.11, s32[2,8]{1,0:T(2,128)} %bitcast.12), custom_call_target="tpu_custom_call" | custom-call | tf_op jit(solution)/shard_map/pack/pallas_call | solution.py:295
  34.2 3.1 %collective-permute-start = (bf16[2064,128]{1,0:T(8,128)(2,1)}, bf16[2064,128]{1,0:T(8,128)(2,1)S(1)}, u32[]{:S(2)}, u32[]{:S(2)}) collective-permute-start(bf16[2064,128]{1,0:T(8,128)(2,1)} %get-tuple-element.50.refs_0_), channel_id=1, source_target_pairs={{0,2},{2,4},{4,6},{6,0},{1,7},{3,1},{5,3},{7,5},{8,10},{10,12},{12... | collective-permute-start | bytes 1585160 | tf_op jit(solution)/shard_map/ppermute | solution.py:289
  37.3 1.6 %collective-permute-start.1 = (bf16[2064,128]{1,0:T(8,128)(2,1)}, bf16[2064,128]{1,0:T(8,128)(2,1)S(1)}, u32[]{:S(2)}, u32[]{:S(2)}) collective-permute-start(bf16[2064,128]{1,0:T(8,128)(2,1)} %get-tuple-element.50.refs_0_), channel_id=1, source_target_pairs={{0,1},{1,0},{2,3},{3,2},{4,5},{5,4},{6,7},{7,6},{8,9},{9,8},{10,11... | collective-permute-start | bytes 1585160 | tf_op jit(solution)/shard_map/ppermute | solution.py:292
  38.9 1.5 %collective-permute-start.2 = (bf16[2064,128]{1,0:T(8,128)(2,1)}, bf16[2064,128]{1,0:T(8,128)(2,1)S(1)}, u32[]{:S(2)}, u32[]{:S(2)}) collective-permute-start(bf16[2064,128]{1,0:T(8,128)(2,1)} %get-tuple-element.55.refs_6_), channel_id=1, source_target_pairs={{0,8},{8,0},{16,24},{24,16},{1,9},{9,1},{17,25},{25,17},{2,10},{10... | collective-permute-start | bytes 1585160 | tf_op jit(solution)/shard_map/ppermute | solution.py:284
  40.4 1.5 %collective-permute-start.3 = (bf16[2064,128]{1,0:T(8,128)(2,1)}, bf16[2064,128]{1,0:T(8,128)(2,1)S(1)}, u32[]{:S(2)}, u32[]{:S(2)}) collective-permute-start(bf16[2064,128]{1,0:T(8,128)(2,1)} %get-tuple-element.55.refs_6_), channel_id=1, source_target_pairs={{0,16},{8,24},{16,0},{24,8},{1,17},{9,25},{17,1},{25,9},{2,18},{10... | collective-permute-start | bytes 1585160 | tf_op jit(solution)/shard_map/ppermute | solution.py:284
  41.9 9.8 %collective-permute-done.refs_2_ = bf16[2064,128]{1,0:T(8,128)(2,1)S(1)} collective-permute-done((bf16[2064,128]{1,0:T(8,128)(2,1)}, bf16[2064,128]{1,0:T(8,128)(2,1)S(1)}, u32[]{:S(2)}, u32[]{:S(2)}) %collective-permute-start) | collective-permute-done | bytes 528416 | tf_op jit(solution)/shard_map/ppermute | solution.py:289
  51.7 1.3 collective-permute-done.2.refs_7_
  53.0 1.2 collective-permute-done.3.refs_8_
  54.2 0.5 collective-permute-start.4
  54.7 0.7 collective-permute-start.7
  55.4 1.3 collective-permute-start.6
  56.8 23.6 %collective-permute-done.6.refs_3_ = bf16[2048,128]{1,0:T(8,128)(2,1)S(1)} collective-permute-done((bf16[2048,128]{1,0:T(8,128)(2,1)}, bf16[2048,128]{1,0:T(8,128)(2,1)S(1)}, u32[]{:S(2)}, u32[]{:S(2)}) %collective-permute-start.6) | collective-permute-done | bytes 524320 | tf_op jit(solution)/shard_map/ppermute | solution.py:284
  80.5 1.6 %collective-permute-start.9 = (bf16[2064,128]{1,0:T(8,128)(2,1)S(1)}, bf16[2064,128]{1,0:T(8,128)(2,1)S(1)}, u32[]{:S(2)}, u32[]{:S(2)}) collective-permute-start(bf16[2064,128]{1,0:T(8,128)(2,1)S(1)} %collective-permute-done.4.refs_4_), channel_id=1, source_target_pairs={{0,2},{2,4},{4,6},{6,0},{1,7},{3,1},{5,3},{7,5},{8,10},{10,12},{12... | collective-permute-start | bytes 1585160 | tf_op jit(solution)/shard_map/ppermute | solution.py:289
  82.2 1.5 %collective-permute-start.10 = (bf16[2048,128]{1,0:T(8,128)(2,1)}, bf16[2048,128]{1,0:T(8,128)(2,1)S(1)}, u32[]{:S(2)}, u32[]{:S(2)}) collective-permute-start(bf16[2048,128]{1,0:T(8,128)(2,1)} %bitcast.7), channel_id=1, source_target_pairs={{0,16},{8,24},{16,0},{24,8},{1,17},{9,25},{17,1},{25,9},{2,18},{10... | collective-permute-start | bytes 1572872 | tf_op jit(solution)/shard_map/ppermute | solution.py:284
  83.7 0.8 copy-done.12
  84.5 1.0 copy-done.1
  85.5 10.7 %first.1 = (f32[1024,512]{1,0:T(8,128)}, bf16[6,1024,512]{2,1,0:T(8,128)(2,1)}, bf16[1024,512]{1,0:T(8,128)(2,1)}, s32[4,8,128]{2,1,0:T(8,128)S(1)}) custom-call(bf16[2064,128]{1,0:T(8,128)(2,1)S(1)} %copy-done.1, bf16[2064,128]{1,0:T(8,128)(2,1)S(1)} %collective-permute-done.1.refs_1_, bf16[2064,128]{1,0:T(8,128)(2,1)S(1)} %collective-permute-done.refs_2_, ...), custom_call_target="tpu_custom_call" | custom-call | flops 4294967296 | bytes 16777216 | tf_op jit(solution)/shard_map/first/pallas_call | solution.py:320
  96.2 0.3 collective-permute-done.9.refs_1_
  96.5 1.4 collective-permute-start.12
  97.9 0.5 collective-permute-start.11
  98.5 1.0 collective-permute-done.12.refs_2_
  99.5 0.8 copy-done.13
  100.3 11.4 %parts.1 = (f32[1024,512]{1,0:T(8,128)}, bf16[512,1024]{1,0:T(8,128)(2,1)}, bf16[2,1024,512]{2,1,0:T(8,128)(2,1)}, bf16[8,2,128,128]{3,2,1,0:T(8,128)(2,1)S(1)},...) custom-call(s32[4,8,128]{2,1,0:T(8,128)S(1)} %get-tuple-element.59.refs_0_, ...), custom_call_target="tpu_custom_call" | custom-call | flops 4294967296 | bytes 16777216 | tf_op jit(solution)/shard_map/parts/pallas_call | solution.py:351
  111.6 0.6 collective-permute-start.13
  112.2 0.6 collective-permute-start.14
  112.8 2.4 %collective-permute-start.15 = (bf16[8,2,128,128]{3,2,1,0:T(8,128)(2,1)S(1)}, bf16[8,2,128,128]{3,2,1,0:T(8,128)(2,1)S(1)}, u32[]{:S(2)}, u32[]{:S(2)}) collective-permute-start(bf16[8,2,128,128]{3,2,1,0:T(8,128)(2,1)S(1)} %get-tuple-element.78), channel_id=1, source_target_pairs={{0,24},{8,16},{16,8},{24,0},{1,25},{9,17},{17,9},{25,1},{2,26},{10... | collective-permute-start | bytes 1572872 | tf_op jit(solution)/shard_map/ppermute | solution.py:284
  115.2 0.8 copy-done.14
  116.0 14.2 %squared.1 = (bf16[8,4,128,128]{3,2,1,0:T(8,128)(2,1)}, bf16[8,4,128,128]{3,2,1,0:T(8,128)(2,1)}, f32[8,2,128,128]{3,2,1,0:T(8,128)}) custom-call(s32[4,8,128]{2,1,0:T(8,128)S(1)} %get-tuple-element.59.refs_0_, s32[4,8]{1,0:T(4,128)S(1)} %bitcast.9, bf16[2048,128]{1,0:T(8,128)(2,1)S(1)} %bitcast.8, bf16[2048,128]{1,0:T(8,128)(2,1)S(1)} %collective-permute-done.6.refs_3_, ...), custom_call_target="tpu_custom_call" | custom-call | flops 8589934592 | bytes 16777216 | tf_op jit(solution)/shard_map/squared/pallas_call | solution.py:379
  130.2 7.1 %collective-permute-done.14.refs_1_ = bf16[8,2,128,128]{3,2,1,0:T(8,128)(2,1)S(1)} collective-permute-done((bf16[8,2,128,128]{3,2,1,0:T(8,128)(2,1)S(1)}, bf16[8,2,128,128]{3,2,1,0:T(8,128)(2,1)S(1)}, u32[]{:S(2)}, u32[]{:S(2)}) %collective-permute-start.14) | collective-permute-done | bytes 524320 | tf_op jit(solution)/shard_map/ppermute | solution.py:284
  137.4 0.8 copy-done.4
  138.2 0.2 copy-done.5
  138.4 2.8 %gradient.1 = bf16[8,2,128,128]{3,2,1,0:T(8,128)(2,1)} custom-call(f32[8,2,128,128]{3,2,1,0:T(8,128)} %get-tuple-element.75.base, bf16[8,2,128,128]{3,2,1,0:T(8,128)(2,1)} %copy-done.3, bf16[8,2,128,128]{3,2,1,0:T(8,128)(2,1)} %copy-done.4, bf16[8,2,128,128]{3,2,1,0:T(8,128)(2,1)} %copy-done.5), custom_call_target="tpu_custom_call" | custom-call | tf_op jit(solution)/shard_map/gradient/pallas_call | solution.py:402
  (35 shorter events, 0.2 us)
Async XLA Ops:
  34.2 17.5 %collective-permute-start = (bf16[2064,128]{1,0:T(8,128)(2,1)}, bf16[2064,128]{1,0:T(8,128)(2,1)S(1)}, u32[]{:S(2)}, u32[]{:S(2)}) collective-permute-start(bf16[2064,128]{1,0:T(8,128)(2,1)} %get-tuple-element.50.refs_0_), channel_id=1, source_target_pairs={{0,2},{2,4},{4,6},{6,0},{1,7},{3,1},{5,3},{7,5},{8,10},{10,12},{12... | collective-permute-start | bytes 1585160 | tf_op jit(solution)/shard_map/ppermute | solution.py:289
  37.3 14.4 %collective-permute-start.1 = (bf16[2064,128]{1,0:T(8,128)(2,1)}, bf16[2064,128]{1,0:T(8,128)(2,1)S(1)}, u32[]{:S(2)}, u32[]{:S(2)}) collective-permute-start(bf16[2064,128]{1,0:T(8,128)(2,1)} %get-tuple-element.50.refs_0_), channel_id=1, source_target_pairs={{0,1},{1,0},{2,3},{3,2},{4,5},{5,4},{6,7},{7,6},{8,9},{9,8},{10,11... | collective-permute-start | bytes 1585160 | tf_op jit(solution)/shard_map/ppermute | solution.py:292
  38.9 14.1 %collective-permute-start.2 = (bf16[2064,128]{1,0:T(8,128)(2,1)}, bf16[2064,128]{1,0:T(8,128)(2,1)S(1)}, u32[]{:S(2)}, u32[]{:S(2)}) collective-permute-start(bf16[2064,128]{1,0:T(8,128)(2,1)} %get-tuple-element.55.refs_6_), channel_id=1, source_target_pairs={{0,8},{8,0},{16,24},{24,16},{1,9},{9,1},{17,25},{25,17},{2,10},{10... | collective-permute-start | bytes 1585160 | tf_op jit(solution)/shard_map/ppermute | solution.py:284
  40.4 13.8 %collective-permute-start.3 = (bf16[2064,128]{1,0:T(8,128)(2,1)}, bf16[2064,128]{1,0:T(8,128)(2,1)S(1)}, u32[]{:S(2)}, u32[]{:S(2)}) collective-permute-start(bf16[2064,128]{1,0:T(8,128)(2,1)} %get-tuple-element.55.refs_6_), channel_id=1, source_target_pairs={{0,16},{8,24},{16,0},{24,8},{1,17},{9,25},{17,1},{25,9},{2,18},{10... | collective-permute-start | bytes 1585160 | tf_op jit(solution)/shard_map/ppermute | solution.py:284
  53.0 30.7 %copy-start.6 = (bf16[2064,128]{1,0:T(8,128)(2,1)}, bf16[2064,128]{1,0:T(8,128)(2,1)S(1)}, u32[]{:S(2)}) copy-start(bf16[2064,128]{1,0:T(8,128)(2,1)S(1)} %collective-permute-done.2.refs_7_) | copy-start | bytes 1585156
  54.2 29.4 %copy-start.7 = (bf16[2064,128]{1,0:T(8,128)(2,1)}, bf16[2064,128]{1,0:T(8,128)(2,1)S(1)}, u32[]{:S(2)}) copy-start(bf16[2064,128]{1,0:T(8,128)(2,1)S(1)} %collective-permute-done.3.refs_8_) | copy-start | bytes 1585156
  54.2 26.2 %collective-permute-start.4 = (bf16[2064,128]{1,0:T(8,128)(2,1)S(1)}, bf16[2064,128]{1,0:T(8,128)(2,1)S(1)}, u32[]{:S(2)}, u32[]{:S(2)}) collective-permute-start(bf16[2064,128]{1,0:T(8,128)(2,1)S(1)} %collective-permute-done.refs_2_), channel_id=1, source_target_pairs={{0,2},{2,4},{4,6},{6,0},{1,7},{3,1},{5,3},{7,5},{8,10},{10,12},{12... | collective-permute-start | bytes 1585160 | tf_op jit(solution)/shard_map/ppermute | solution.py:289
  54.7 25.7 %collective-permute-start.5 = (bf16[2064,128]{1,0:T(8,128)(2,1)S(1)}, bf16[2064,128]{1,0:T(8,128)(2,1)S(1)}, u32[]{:S(2)}, u32[]{:S(2)}) collective-permute-start(bf16[2064,128]{1,0:T(8,128)(2,1)S(1)} %collective-permute-done.refs_2_), channel_id=1, source_target_pairs={{0,1},{1,0},{2,3},{3,2},{4,5},{5,4},{6,7},{7,6},{8,9},{9,8},{10,11... | collective-permute-start | bytes 1585160 | tf_op jit(solution)/shard_map/ppermute | solution.py:292
  54.7 25.7 %collective-permute-start.7 = (bf16[2064,128]{1,0:T(8,128)(2,1)S(1)}, bf16[2064,128]{1,0:T(8,128)(2,1)S(1)}, u32[]{:S(2)}, u32[]{:S(2)}) collective-permute-start(bf16[2064,128]{1,0:T(8,128)(2,1)S(1)} %collective-permute-done.3.refs_8_), channel_id=1, source_target_pairs={{0,8},{8,0},{16,24},{24,16},{1,9},{9,1},{17,25},{25,17},{2,10},{10... | collective-permute-start | bytes 1585160 | tf_op jit(solution)/shard_map/ppermute | solution.py:284
  55.4 25.0 %collective-permute-start.6 = (bf16[2048,128]{1,0:T(8,128)(2,1)}, bf16[2048,128]{1,0:T(8,128)(2,1)S(1)}, u32[]{:S(2)}, u32[]{:S(2)}) collective-permute-start(bf16[2048,128]{1,0:T(8,128)(2,1)} %bitcast.6), channel_id=1, source_target_pairs={{0,8},{8,0},{16,24},{24,16},{1,9},{9,1},{17,25},{25,17},{2,10},{10... | collective-permute-start | bytes 1572872 | tf_op jit(solution)/shard_map/ppermute | solution.py:284
  80.4 3.3 %copy-start.8 = (bf16[2064,128]{1,0:T(8,128)(2,1)}, bf16[2064,128]{1,0:T(8,128)(2,1)S(1)}, u32[]{:S(2)}) copy-start(bf16[2064,128]{1,0:T(8,128)(2,1)S(1)} %collective-permute-done.4.refs_4_) | copy-start | bytes 1585156
  80.4 3.3 %copy-start.10 = (bf16[2064,128]{1,0:T(8,128)(2,1)}, bf16[2064,128]{1,0:T(8,128)(2,1)S(1)}, u32[]{:S(2)}) copy-start(bf16[2064,128]{1,0:T(8,128)(2,1)S(1)} %collective-permute-done.5.refs_3_) | copy-start | bytes 1585156
  80.4 3.3 %copy-start.11 = (bf16[2064,128]{1,0:T(8,128)(2,1)}, bf16[2064,128]{1,0:T(8,128)(2,1)S(1)}, u32[]{:S(2)}) copy-start(bf16[2064,128]{1,0:T(8,128)(2,1)S(1)} %collective-permute-done.7.refs_9_) | copy-start | bytes 1585156
  80.4 3.2 %collective-permute-start.8 = (bf16[2064,128]{1,0:T(8,128)(2,1)S(1)}, bf16[2064,128]{1,0:T(8,128)(2,1)S(1)}, u32[]{:S(2)}, u32[]{:S(2)}) collective-permute-start(bf16[2064,128]{1,0:T(8,128)(2,1)S(1)} %collective-permute-done.4.refs_4_), channel_id=1, source_target_pairs={{0,1},{1,0},{2,3},{3,2},{4,5},{5,4},{6,7},{7,6},{8,9},{9,8},{10,11... | collective-permute-start | bytes 1585160 | tf_op jit(solution)/shard_map/ppermute | solution.py:292
  80.5 16.0 %collective-permute-start.9 = (bf16[2064,128]{1,0:T(8,128)(2,1)S(1)}, bf16[2064,128]{1,0:T(8,128)(2,1)S(1)}, u32[]{:S(2)}, u32[]{:S(2)}) collective-permute-start(bf16[2064,128]{1,0:T(8,128)(2,1)S(1)} %collective-permute-done.4.refs_4_), channel_id=1, source_target_pairs={{0,2},{2,4},{4,6},{6,0},{1,7},{3,1},{5,3},{7,5},{8,10},{10,12},{12... | collective-permute-start | bytes 1585160 | tf_op jit(solution)/shard_map/ppermute | solution.py:289
  82.2 14.1 %collective-permute-start.10 = (bf16[2048,128]{1,0:T(8,128)(2,1)}, bf16[2048,128]{1,0:T(8,128)(2,1)S(1)}, u32[]{:S(2)}, u32[]{:S(2)}) collective-permute-start(bf16[2048,128]{1,0:T(8,128)(2,1)} %bitcast.7), channel_id=1, source_target_pairs={{0,16},{8,24},{16,0},{24,8},{1,17},{9,25},{17,1},{25,9},{2,18},{10... | collective-permute-start | bytes 1572872 | tf_op jit(solution)/shard_map/ppermute | solution.py:284
  83.7 0.8 copy-start.12
  84.5 1.0 copy-start.1
  96.5 3.0 %copy-start.9 = (bf16[2064,128]{1,0:T(8,128)(2,1)}, bf16[2064,128]{1,0:T(8,128)(2,1)S(1)}, u32[]{:S(2)}) copy-start(bf16[2064,128]{1,0:T(8,128)(2,1)S(1)} %collective-permute-done.9.refs_1_) | copy-start | bytes 1585156
  96.5 3.0 %collective-permute-start.12 = (bf16[2064,128]{1,0:T(8,128)(2,1)S(1)}, bf16[2064,128]{1,0:T(8,128)(2,1)S(1)}, u32[]{:S(2)}, u32[]{:S(2)}) collective-permute-start(bf16[2064,128]{1,0:T(8,128)(2,1)S(1)} %collective-permute-done.9.refs_1_), channel_id=1, source_target_pairs={{0,1},{1,0},{2,3},{3,2},{4,5},{5,4},{6,7},{7,6},{8,9},{9,8},{10,11... | collective-permute-start | bytes 1585160 | tf_op jit(solution)/shard_map/ppermute | solution.py:292
  97.9 17.3 %collective-permute-start.11 = (bf16[2048,128]{1,0:T(8,128)(2,1)S(1)}, bf16[2048,128]{1,0:T(8,128)(2,1)S(1)}, u32[]{:S(2)}, u32[]{:S(2)}) collective-permute-start(bf16[2048,128]{1,0:T(8,128)(2,1)S(1)} %collective-permute-done.10.refs_4_), channel_id=1, source_target_pairs={{0,8},{8,0},{16,24},{24,16},{1,9},{9,1},{17,25},{25,17},{2,10},{10... | collective-permute-start | bytes 1572872 | tf_op jit(solution)/shard_map/ppermute | solution.py:284
  99.5 0.8 copy-start.13
  100.3 15.7 %copy-start = (bf16[8,2,128,128]{3,2,1,0:T(8,128)(2,1)S(1)}, bf16[8,2,128,128]{3,2,1,0:T(8,128)(2,1)}, u32[]{:S(2)}) copy-start(bf16[8,2,128,128]{3,2,1,0:T(8,128)(2,1)} %param.5) | copy-start | bytes 1572868
  100.3 15.7 %copy-start.2 = (s32[8,4]{0,1:T(4,128)S(1)}, s32[8,4]{0,1:T(4,128)}, u32[]{:S(2)}) copy-start(s32[8,4]{0,1:T(4,128)} %param.9) | copy-start | bytes 388
  111.6 18.6 %collective-permute-start.13 = (bf16[8,2,128,128]{3,2,1,0:T(8,128)(2,1)S(1)}, bf16[8,2,128,128]{3,2,1,0:T(8,128)(2,1)S(1)}, u32[]{:S(2)}, u32[]{:S(2)}) collective-permute-start(bf16[8,2,128,128]{3,2,1,0:T(8,128)(2,1)S(1)} %get-tuple-element.76), channel_id=1, source_target_pairs={{0,8},{8,0},{16,24},{24,16},{1,9},{9,1},{17,25},{25,17},{2,10},{10... | collective-permute-start | bytes 1572872 | tf_op jit(solution)/shard_map/ppermute | solution.py:284
  112.2 25.1 %collective-permute-start.14 = (bf16[8,2,128,128]{3,2,1,0:T(8,128)(2,1)S(1)}, bf16[8,2,128,128]{3,2,1,0:T(8,128)(2,1)S(1)}, u32[]{:S(2)}, u32[]{:S(2)}) collective-permute-start(bf16[8,2,128,128]{3,2,1,0:T(8,128)(2,1)S(1)} %get-tuple-element.77), channel_id=1, source_target_pairs={{0,16},{8,24},{16,0},{24,8},{1,17},{9,25},{17,1},{25,9},{2,18},{10... | collective-permute-start | bytes 1572872 | tf_op jit(solution)/shard_map/ppermute | solution.py:284
  112.8 24.6 %collective-permute-start.15 = (bf16[8,2,128,128]{3,2,1,0:T(8,128)(2,1)S(1)}, bf16[8,2,128,128]{3,2,1,0:T(8,128)(2,1)S(1)}, u32[]{:S(2)}, u32[]{:S(2)}) collective-permute-start(bf16[8,2,128,128]{3,2,1,0:T(8,128)(2,1)S(1)} %get-tuple-element.78), channel_id=1, source_target_pairs={{0,24},{8,16},{16,8},{24,0},{1,25},{9,17},{17,9},{25,1},{2,26},{10... | collective-permute-start | bytes 1572872 | tf_op jit(solution)/shard_map/ppermute | solution.py:284
  115.2 0.8 copy-start.14
  130.2 7.2 %copy-start.3 = (bf16[8,2,128,128]{3,2,1,0:T(8,128)(2,1)}, bf16[8,2,128,128]{3,2,1,0:T(8,128)(2,1)S(1)}, u32[]{:S(2)}) copy-start(bf16[8,2,128,128]{3,2,1,0:T(8,128)(2,1)S(1)} %collective-permute-done.13.refs_0_) | copy-start | bytes 1572868
  137.4 0.8 copy-start.4
  137.4 1.0 copy-start.5

commit v3 on v2

--- a/solution.py
+++ b/solution.py
@@ -1,4 +1,5 @@
 import functools
+import math
 
 import jax
 import jax.numpy as jnp
@@ -7,7 +8,7 @@
 from jax.experimental.pallas import tpu as pltpu
 from jax.sharding import PartitionSpec as P
 
-VMEM_LIMIT = 52 * 1024 * 1024
+VMEM_ROOM = 6 * 1024 * 1024
 TAIL = 16
 BF16, F32 = jnp.bfloat16, jnp.float32
 
@@ -23,6 +24,22 @@
         self.n_first = n_col - 2
 
 
+def call(kernel, z, ins, outs, scratch, in_specs, out_specs, flops, name):
+    held = [x for x in scratch if getattr(x, "memory_space", None) == pltpu.VMEM]
+    held += [x for x, spec in zip(list(ins) + outs, in_specs + out_specs) if spec.memory_space == pltpu.VMEM]
+    size = sum(math.prod(x.shape) * jnp.dtype(x.dtype).itemsize for x in held)
+    return pl.pallas_call(
+        functools.partial(kernel, z),
+        out_shape=outs,
+        in_specs=in_specs,
+        out_specs=out_specs,
+        scratch_shapes=scratch,
+        compiler_params=pltpu.CompilerParams(vmem_limit_bytes=size + VMEM_ROOM),
+        cost_estimate=pl.CostEstimate(flops=flops, bytes_accessed=16 << 20, transcendentals=0),
+        name=name,
+    )(*ins)
+
+
 def lanes(z, block):
     return pl.ds(pl.multiple_of(block * z.bs, z.bs), z.bs)
 
@@ -47,27 +64,14 @@
     return jnp.where(core == 0, behind, ahead) * 2 + (core ^ lax.rem(me, 2))
 
 
-def pack_kernel(z, d_in, h_in, d_cols, h_cols, d_out, h_out, wide_tail, tail, sems):
-    n = d_in.shape[0]
-    m = h_in.shape[0]
-    copies = [
-        pltpu.make_async_copy(d_in, d_out.at[pl.ds(0, n)], sems.at[0]),
-        pltpu.make_async_copy(h_in, h_out.at[pl.ds(0, m)], sems.at[1]),
-    ]
-    for copy in copies:
-        copy.start()
-    wide_tail[...] = jnp.zeros_like(wide_tail)
-    wide_tail[0:z.ka, 0:z.rows] = d_cols[...].astype(F32)
-    wide_tail[z.ka:z.ka + z.kh, 0:z.rows] = h_cols[...].astype(F32)
-    tail[...] = wide_tail[...].astype(BF16)
-    tails = [
-        pltpu.make_async_copy(tail, d_out.at[pl.ds(n, TAIL)], sems.at[2]),
-        pltpu.make_async_copy(tail, h_out.at[pl.ds(m, TAIL)], sems.at[3]),
-    ]
-    for copy in tails:
-        copy.start()
-    for copy in copies + tails:
-        copy.wait()
+def pack_kernel(z, d_in, h_in, d_cols, h_cols, d_out, h_out, tail):
+    tail[...] = jnp.zeros_like(tail)
+    tail[0:z.ka, 0:z.rows] = d_cols[...].astype(F32)
+    tail[z.ka:z.ka + z.kh, 0:z.rows] = h_cols[...].astype(F32)
+    for ref, out in ((d_in, d_out), (h_in, h_out)):
+        rows = ref.shape[0]
+        out[0:rows, :] = ref[...]
+        out[rows:rows + TAIL, :] = tail[...].astype(BF16)
 
 
 def read_tails(ins, blocks, tails, ints, idx, sems, int_sem):
@@ -275,7 +279,6 @@
     smem = pl.BlockSpec(memory_space=pltpu.SMEM)
     vmem = pl.BlockSpec(memory_space=pltpu.VMEM)
     anywhere = pl.BlockSpec(memory_space=pl.ANY)
-    params = pltpu.CompilerParams(vmem_limit_bytes=VMEM_LIMIT)
     dma = pltpu.SemaphoreType.DMA
     d_rows, h_rows = z.rows * z.ka * z.bs, z.rows * z.kh * z.bs
     panel_flops = 2 * z.tall * z.wide * z.nb * z.bs
@@ -292,23 +295,22 @@
         return lax.ppermute(x, "col", [(c, c ^ 1) for c in range(n_col)])
 
     flat = density.reshape(d_rows, z.bs)
-    d_pay, h_pay = pl.pallas_call(
-        functools.partial(pack_kernel, z),
-        out_shape=[shape((d_rows + TAIL, z.bs), BF16), shape((h_rows + TAIL, z.bs), BF16)],
-        in_specs=[anywhere, anywhere, vmem, vmem],
-        out_specs=[anywhere, anywhere],
-        scratch_shapes=[pltpu.VMEM((TAIL, z.bs), F32), pltpu.VMEM((TAIL, z.bs), BF16), dma((4,))],
-        name="pack",
-    )(flat, hamilton.reshape(h_rows, z.bs), density_cols.T, hamilton_cols.T)
+    d_pay, h_pay = call(
+        pack_kernel, z,
+        [flat, hamilton.reshape(h_rows, z.bs), density_cols.T, hamilton_cols.T],
+        [shape((d_rows + TAIL, z.bs), BF16), shape((h_rows + TAIL, z.bs), BF16)],
+        [pltpu.VMEM((TAIL, z.bs), F32)],
+        [vmem] * 4, [vmem] * 2, 0, "pack",
+    )
 
     pieces, d_right, h_right = [d_pay], {0: flat}, {0: h_pay}
     left = [d_pay]
     for step in range(1, z.n_chip):
         pieces.append(next_chip(pieces[-1]))
         for flip in range(1, n_row):
-            bits, low = flip.bit_count(), flip & -flip
+            bits, low, high = flip.bit_count(), flip & -flip, 1 << (flip.bit_length() - 1)
             if bits == step:
-                h_right[flip] = over_row(h_right[flip - low], low)
+                h_right[flip] = over_row(h_right[flip - high], high)
             if (step == 2 and flip == 1) or (step == 3 and bits == 1 and flip > 1):
                 d_right[flip] = over_row(d_right[flip - low], low)
         left.append(other_core(left[-1]))
@@ -317,47 +319,43 @@
         left.append(pieces[-1])
     h_right = [h_right[flip] for flip in range(n_row)]
 
-    total, panel, right_last, table = pl.pallas_call(
-        functools.partial(first_kernel, z),
-        out_shape=[
+    n_pay = z.n_first + n_row
+    total, panel, right_last, table = call(
+        first_kernel, z,
+        [*left[:z.n_first], *h_right],
+        [
             shape((z.tall, z.wide), F32),
             shape((z.n_first, z.tall, z.wide), BF16),
             shape((2 * z.wide, z.wide), BF16),
             shape((n_row, 8, z.bs), jnp.int32),
         ],
-        in_specs=[anywhere] * (z.n_first + n_row),
-        out_specs=[vmem, anywhere, vmem, vmem],
-        scratch_shapes=[
+        [
             pltpu.VMEM((z.n_first, d_rows, z.bs), BF16),
             pltpu.VMEM((n_row, h_rows, z.bs), BF16),
             pltpu.VMEM((z.tall, z.n_first * z.wide), BF16),
             pltpu.VMEM((z.nb * z.bs, z.wide), BF16),
-            pltpu.VMEM((z.n_first + n_row, TAIL, z.bs), BF16),
-            pltpu.VMEM((z.n_first + n_row, 8, z.bs), jnp.int32),
-            pltpu.SMEM((z.n_first + n_row, 8, z.bs), jnp.int32),
-            dma((z.n_first,)), dma((n_row,)), dma((z.n_first + n_row,)), dma((z.n_first,)), dma,
+            pltpu.VMEM((n_pay, TAIL, z.bs), BF16),
+            pltpu.VMEM((n_pay, 8, z.bs), jnp.int32),
+            pltpu.SMEM((n_pay, 8, z.bs), jnp.int32),
+            dma((z.n_first,)), dma((n_row,)), dma((n_pay,)), dma((z.n_first,)), dma,
         ],
-        compiler_params=params,
-        cost_estimate=pl.CostEstimate(flops=panel_flops, bytes_accessed=16 << 20, transcendentals=0),
-        name="first",
-    )(*left[:z.n_first], *h_right)
+        [anywhere] * n_pay, [vmem, anywhere, vmem, vmem], panel_flops, "first",
+    )
     last, total, d_right = lax.optimization_barrier((left[-1], total, d_right))
     for flip in range(1, n_row):
         if flip not in d_right:
             d_right[flip] = over_row(d_right[flip & (flip - 1)], flip & -flip)
     d_right = [d_right[flip] for flip in range(n_row)]
-    left = [last, other_core(last)]
     part = shape((z.rows, z.ka) + block, BF16)
-    total, turned, panel_last, *parts = pl.pallas_call(
-        functools.partial(parts_kernel, z),
-        out_shape=[
+    total, turned, panel_last, *parts = call(
+        parts_kernel, z,
+        [table, last, other_core(last), right_last, total, panel],
+        [
             shape((z.tall, z.wide), F32),
             shape((z.wide, z.tall), BF16),
             shape((2, z.tall, z.wide), BF16),
         ] + [part] * (n_row - 1),
-        in_specs=[smem] + [anywhere] * 5,
-        out_specs=[anywhere] * (2 + n_row),
-        scratch_shapes=[
+        [
             pltpu.VMEM((2, d_rows, z.bs), BF16),
             pltpu.VMEM((z.tall, 2 * z.wide), BF16),
             pltpu.VMEM((2 * z.wide, z.wide), BF16),
@@ -371,21 +369,18 @@
             pltpu.SMEM((2, 8, z.bs), jnp.int32),
             dma((4,)), dma((z.n_first,)), dma((2,)), dma((4,)), dma((n_row - 1,)), dma,
         ],
-        compiler_params=params,
-        cost_estimate=pl.CostEstimate(flops=panel_flops, bytes_accessed=16 << 20, transcendentals=0),
-        name="parts",
-    )(table, *left, right_last, total, panel)
+        [smem] + [anywhere] * 5, [anywhere] * (2 + n_row), panel_flops, "parts",
+    )
     received = [over_row(parts[n - 1], n) for n in range(1, n_row)]
-    squared, mixed, base = pl.pallas_call(
-        functools.partial(square_kernel, z),
-        out_shape=[
+    squared, mixed, base = call(
+        square_kernel, z,
+        [table, filter_cols.T, *d_right, panel, panel_last, total, turned],
+        [
             shape((z.rows, z.kf) + block, BF16),
             shape((z.rows, z.kf) + block, BF16),
             shape((z.rows, z.ka) + block, F32),
         ],
-        in_specs=[smem] * 2 + [anywhere] * (n_row + 4),
-        out_specs=[vmem] * 3,
-        scratch_shapes=[
+        [
             pltpu.VMEM((n_row, d_rows, z.bs), BF16),
             pltpu.VMEM((z.nb * z.bs, z.wide), BF16),
             pltpu.VMEM((n_col, z.tall, z.wide), BF16),
@@ -395,17 +390,9 @@
             pltpu.VMEM((z.rows, z.ka) + block, F32),
             dma((n_row,)), dma((2,)), dma((n_col,)),
         ],
-        compiler_params=params,
-        cost_estimate=pl.CostEstimate(flops=2 * panel_flops, bytes_accessed=16 << 20, transcendentals=0),
-        name="squared",
-    )(table, filter_cols.T, *d_right, panel, panel_last, total, turned)
-    gradient = pl.pallas_call(
-        functools.partial(gradient_kernel, z),
-        out_shape=part,
-        in_specs=[vmem] * n_row,
-        out_specs=vmem,
-        name="gradient",
-    )(base, *received)
+        [smem] * 2 + [anywhere] * (n_row + 4), [vmem] * 3, 2 * panel_flops, "squared",
+    )
+    gradient, = call(gradient_kernel, z, [base, *received], [part], [], [vmem] * n_row, [vmem], 0, "gradient")
     return squared, mixed, gradient
 
 

time: 141 us -> 94.6 us (0.67)
  Pallas kernels: 72.6 us -> 30.7 us
  local copies, waits for them, and re-layouts: 4.43 us -> 2.4 us
  starting transfers between devices: 18.9 us -> 17.2 us
    pallas_call x5, Pallas kernels: 72.6 us -> 30.7 us  [call(): pl.pallas_call(functools.partial(kernel, z), out_shape=outs, in_specs=in_...]
    unnamed x30 -> x8, local copies, waits for them, and re-layouts: 4.43 us -> 2.4 us
  transfers between devices with their start and end apart: 16 -> 16, of which waited for: 7 -> 9; matrix products, arithmetic and copies ran while one was open for 0% -> 0% of each run, Pallas kernels for 26% -> 30%
where the time goes in v3:
time: 94.6 us; the launch traced here: 94.3 us
  waiting for transfers between devices  43.4 us (46%)
  Pallas kernels  30.7 us (32%)
  starting transfers between devices  17.2 us (18%)
  local copies, waits for them, and re-layouts  2.4 us (3%)
    ppermute x9, waiting for transfers between devices, over_row(): return lax.ppermute(x, 'row', [(r, r ^ flip) for r in range(n_row)])  32.5 us
    pallas_call x5, Pallas kernels, call(): pl.pallas_call(functools.partial(kernel, z), out_shape=outs, in_specs=in_...  30.7 us
    ppermute x3, waiting for transfers between devices, next_chip(): return lax.ppermute(x, 'col', pairs)  9.89 us
    ppermute x9, starting transfers between devices, over_row(): return lax.ppermute(x, 'row', [(r, r ^ flip) for r in range(n_row)])  9.82 us
    ppermute x3, starting transfers between devices, next_chip(): return lax.ppermute(x, 'col', pairs)  5.21 us
    unnamed x8, local copies, waits for them, and re-layouts  2.4 us
    ppermute x4, starting transfers between devices, other_core(): return lax.ppermute(x, 'col', [(c, c ^ 1) for c in range(n_col)])  2.13 us
  transfers between devices with their start and end apart: 16, of which 9 were waited for; matrix products, arithmetic and copies ran while one was open for 0% of the time, Pallas kernels for 30%

profile of v3, /device:TPU:0, one launch (start us, length us, event | category | flops | bytes accessed | tf_op | source)
XLA Modules:
  0.0 94.3 jit_solution(16755300076784060766)
XLA Ops:
  0.6 1.0 %copy-done = bf16[8,2,128,128]{3,2,1,0:T(8,128)(2,1)S(1)} copy-done((bf16[8,2,128,128]{3,2,1,0:T(8,128)(2,1)S(1)}, bf16[8,2,128,128]{3,2,1,0:T(8,128)(2,1)}, u32[]{:S(2)}) %copy-start) | copy-done | bytes 524312
  1.7 0.7 copy-done.1
  2.4 0.7 copy-done.2
  3.0 1.1 %pack.1 = (bf16[2064,128]{1,0:T(8,128)(2,1)S(1)}, bf16[2064,128]{1,0:T(8,128)(2,1)S(1)}) custom-call(bf16[2048,128]{1,0:T(8,128)(2,1)} %bitcast.d_in.refs_2_, bf16[2048,128]{1,0:T(8,128)(2,1)S(1)} %bitcast.5, s32[2,8]{1,0:T(2,128)S(1)} %bitcast.6, s32[2,8]{1,0:T(2,128)S(1)} %bitcast.7), custom_call_target="tpu_custom_call" | custom-call | bytes 16777216 | tf_op jit(solution)/shard_map/pack/pallas_call | solution.py:31
  4.1 3.1 %collective-permute-start = (bf16[2064,128]{1,0:T(8,128)(2,1)S(1)}, bf16[2064,128]{1,0:T(8,128)(2,1)S(1)}, u32[]{:S(2)}, u32[]{:S(2)}) collective-permute-start(bf16[2064,128]{1,0:T(8,128)(2,1)S(1)} %get-tuple-element.50.refs_0_), channel_id=1, source_target_pairs={{0,2},{2,4},{4,6},{6,0},{1,7},{3,1},{5,3},{7,5},{8,10},{10,12},{12... | collective-permute-start | bytes 1585160 | tf_op jit(solution)/shard_map/ppermute | solution.py:292
  7.2 1.6 %collective-permute-start.1 = (bf16[2064,128]{1,0:T(8,128)(2,1)S(1)}, bf16[2064,128]{1,0:T(8,128)(2,1)S(1)}, u32[]{:S(2)}, u32[]{:S(2)}) collective-permute-start(bf16[2064,128]{1,0:T(8,128)(2,1)S(1)} %get-tuple-element.50.refs_0_), channel_id=1, source_target_pairs={{0,1},{1,0},{2,3},{3,2},{4,5},{5,4},{6,7},{7,6},{8,9},{9,8},{10,11... | collective-permute-start | bytes 1585160 | tf_op jit(solution)/shard_map/ppermute | solution.py:295
  8.8 1.5 %collective-permute-start.2 = (bf16[2064,128]{1,0:T(8,128)(2,1)S(1)}, bf16[2064,128]{1,0:T(8,128)(2,1)S(1)}, u32[]{:S(2)}, u32[]{:S(2)}) collective-permute-start(bf16[2064,128]{1,0:T(8,128)(2,1)S(1)} %get-tuple-element.55.refs_6_), channel_id=1, source_target_pairs={{0,8},{8,0},{16,24},{24,16},{1,9},{9,1},{17,25},{25,17},{2,10},{10... | collective-permute-start | bytes 1585160 | tf_op jit(solution)/shard_map/ppermute | solution.py:287
  10.3 1.5 %collective-permute-start.3 = (bf16[2064,128]{1,0:T(8,128)(2,1)S(1)}, bf16[2064,128]{1,0:T(8,128)(2,1)S(1)}, u32[]{:S(2)}, u32[]{:S(2)}) collective-permute-start(bf16[2064,128]{1,0:T(8,128)(2,1)S(1)} %get-tuple-element.55.refs_6_), channel_id=1, source_target_pairs={{0,16},{8,24},{16,0},{24,8},{1,17},{9,25},{17,1},{25,9},{2,18},{10... | collective-permute-start | bytes 1585160 | tf_op jit(solution)/shard_map/ppermute | solution.py:287
  11.8 9.6 %collective-permute-done.refs_2_ = bf16[2064,128]{1,0:T(8,128)(2,1)S(1)} collective-permute-done((bf16[2064,128]{1,0:T(8,128)(2,1)S(1)}, bf16[2064,128]{1,0:T(8,128)(2,1)S(1)}, u32[]{:S(2)}, u32[]{:S(2)}) %collective-permute-start) | collective-permute-done | bytes 528416 | tf_op jit(solution)/shard_map/ppermute | solution.py:292
  21.4 1.3 %collective-permute-done.2.refs_7_ = bf16[2064,128]{1,0:T(8,128)(2,1)S(1)} collective-permute-done((bf16[2064,128]{1,0:T(8,128)(2,1)S(1)}, bf16[2064,128]{1,0:T(8,128)(2,1)S(1)}, u32[]{:S(2)}, u32[]{:S(2)}) %collective-permute-start.2) | collective-permute-done | bytes 528416 | tf_op jit(solution)/shard_map/ppermute | solution.py:287
  22.7 1.2 %collective-permute-done.3.refs_8_ = bf16[2064,128]{1,0:T(8,128)(2,1)S(1)} collective-permute-done((bf16[2064,128]{1,0:T(8,128)(2,1)S(1)}, bf16[2064,128]{1,0:T(8,128)(2,1)S(1)}, u32[]{:S(2)}, u32[]{:S(2)}) %collective-permute-start.3) | collective-permute-done | bytes 528416 | tf_op jit(solution)/shard_map/ppermute | solution.py:287
  23.9 0.5 collective-permute-start.4
  24.4 1.5 %collective-permute-start.7 = (bf16[2064,128]{1,0:T(8,128)(2,1)S(1)}, bf16[2064,128]{1,0:T(8,128)(2,1)S(1)}, u32[]{:S(2)}, u32[]{:S(2)}) collective-permute-start(bf16[2064,128]{1,0:T(8,128)(2,1)S(1)} %collective-permute-done.2.refs_7_), channel_id=1, source_target_pairs={{0,16},{8,24},{16,0},{24,8},{1,17},{9,25},{17,1},{25,9},{2,18},{10... | collective-permute-start | bytes 1585160 | tf_op jit(solution)/shard_map/ppermute | solution.py:287
  26.0 0.7 collective-permute-start.6
  26.6 13.6 %collective-permute-done.6.refs_3_ = bf16[2048,128]{1,0:T(8,128)(2,1)S(1)} collective-permute-done((bf16[2048,128]{1,0:T(8,128)(2,1)}, bf16[2048,128]{1,0:T(8,128)(2,1)S(1)}, u32[]{:S(2)}, u32[]{:S(2)}) %collective-permute-start.6) | collective-permute-done | bytes 524320 | tf_op jit(solution)/shard_map/ppermute | solution.py:287
  40.2 0.1 collective-permute-start.8
  40.3 1.6 %collective-permute-start.9 = (bf16[2064,128]{1,0:T(8,128)(2,1)S(1)}, bf16[2064,128]{1,0:T(8,128)(2,1)S(1)}, u32[]{:S(2)}, u32[]{:S(2)}) collective-permute-start(bf16[2064,128]{1,0:T(8,128)(2,1)S(1)} %collective-permute-done.4.refs_4_), channel_id=1, source_target_pairs={{0,2},{2,4},{4,6},{6,0},{1,7},{3,1},{5,3},{7,5},{8,10},{10,12},{12... | collective-permute-start | bytes 1585160 | tf_op jit(solution)/shard_map/ppermute | solution.py:292
  42.0 0.5 collective-permute-start.10
  42.5 8.4 %first.1 = (f32[1024,512]{1,0:T(8,128)S(1)}, bf16[6,1024,512]{2,1,0:T(8,128)(2,1)S(1)}, bf16[1024,512]{1,0:T(8,128)(2,1)S(1)}, s32[4,8,128]{2,1,0:T(8,128)S(1)}) custom-call(bf16[2064,128]{1,0:T(8,128)(2,1)S(1)} %get-tuple-element.50.refs_0_, bf16[2064,128]{1,0:T(8,128)(2,1)S(1)} %collective-permute-done.1.refs_1_, ...), custom_call_target="tpu_custom_call" | custom-call | flops 4294967296 | bytes 16777216 | tf_op jit(solution)/shard_map/first/pallas_call | solution.py:31
  50.9 5.2 %collective-permute-done.10.refs_4_ = bf16[2048,128]{1,0:T(8,128)(2,1)S(1)} collective-permute-done((bf16[2048,128]{1,0:T(8,128)(2,1)}, bf16[2048,128]{1,0:T(8,128)(2,1)S(1)}, u32[]{:S(2)}, u32[]{:S(2)}) %collective-permute-start.10) | collective-permute-done | bytes 524320 | tf_op jit(solution)/shard_map/ppermute | solution.py:287
  56.0 0.3 collective-permute-done.9.refs_1_
  56.3 0.5 collective-permute-start.12
  56.8 0.5 collective-permute-start.11
  57.3 1.0 %collective-permute-done.12.refs_2_ = bf16[2064,128]{1,0:T(8,128)(2,1)S(1)} collective-permute-done((bf16[2064,128]{1,0:T(8,128)(2,1)S(1)}, bf16[2064,128]{1,0:T(8,128)(2,1)S(1)}, u32[]{:S(2)}, u32[]{:S(2)}) %collective-permute-start.12) | collective-permute-done | bytes 528416 | tf_op jit(solution)/shard_map/ppermute | solution.py:295
  58.3 9.1 %parts.1 = (f32[1024,512]{1,0:T(8,128)S(1)}, bf16[512,1024]{1,0:T(8,128)(2,1)S(1)}, bf16[2,1024,512]{2,1,0:T(8,128)(2,1)S(1)}, bf16[8,2,128,128]{3,2,1,0:T(8,128...) custom-call(s32[4,8,128]{2,1,0:T(8,128)S(1)} %get-tuple-element.59.refs_0_, ...), custom_call_target="tpu_custom_call" | custom-call | flops 4294967296 | bytes 16777216 | tf_op jit(solution)/shard_map/parts/pallas_call | solution.py:31
  67.4 0.6 collective-permute-start.13
  68.1 0.5 collective-permute-start.14
  68.6 2.4 %collective-permute-start.15 = (bf16[8,2,128,128]{3,2,1,0:T(8,128)(2,1)S(1)}, bf16[8,2,128,128]{3,2,1,0:T(8,128)(2,1)S(1)}, u32[]{:S(2)}, u32[]{:S(2)}) collective-permute-start(bf16[8,2,128,128]{3,2,1,0:T(8,128)(2,1)S(1)} %get-tuple-element.78), channel_id=1, source_target_pairs={{0,24},{8,16},{16,8},{24,0},{1,25},{9,17},{17,9},{25,1},{2,26},{10... | collective-permute-start | bytes 1572872 | tf_op jit(solution)/shard_map/ppermute | solution.py:287
  71.0 10.9 %squared.1 = (bf16[8,4,128,128]{3,2,1,0:T(8,128)(2,1)}, bf16[8,4,128,128]{3,2,1,0:T(8,128)(2,1)}, f32[8,2,128,128]{3,2,1,0:T(8,128)S(1)}) custom-call(s32[4,8,128]{2,1,0:T(8,128)S(1)} %get-tuple-element.59.refs_0_, s32[4,8]{1,0:T(4,128)S(1)} %bitcast.8, bf16[2048,128]{1,0:T(8,128)(2,1)} %bitcast.d_in.refs_2_, ...), custom_call_target="tpu_custom_call" | custom-call | flops 8589934592 | bytes 16777216 | tf_op jit(solution)/shard_map/squared/pallas_call | solution.py:31
  82.0 0.3 collective-permute-done.13.refs_0_
  82.3 10.9 %collective-permute-done.14.refs_1_ = bf16[8,2,128,128]{3,2,1,0:T(8,128)(2,1)S(1)} collective-permute-done((bf16[8,2,128,128]{3,2,1,0:T(8,128)(2,1)S(1)}, bf16[8,2,128,128]{3,2,1,0:T(8,128)(2,1)S(1)}, u32[]{:S(2)}, u32[]{:S(2)}) %collective-permute-start.14) | collective-permute-done | bytes 524320 | tf_op jit(solution)/shard_map/ppermute | solution.py:287
  93.2 1.1 %gradient.1 = bf16[8,2,128,128]{3,2,1,0:T(8,128)(2,1)} custom-call(f32[8,2,128,128]{3,2,1,0:T(8,128)S(1)} %get-tuple-element.75.base, bf16[8,2,128,128]{3,2,1,0:T(8,128)(2,1)S(1)} %collective-permute-done.13.refs_0_, bf16[8,2,128,128]{3,2,1,0:T(8,128)(2,1)S(1)} %collective-permute-done.14.refs_1_, bf16[8,2,128,128]{3,2,1,0:T(8,128)(2,1)S(1)} %collective-permute-done.15.refs_2_), custom_call_target="tpu_custom_call" | custom-call | bytes 16777216 | tf_op jit(solution)/shard_map/gradient/pallas_call | solution.py:31
  (13 shorter events, 0.0 us)
Async XLA Ops:
  0.6 1.0 %copy-start = (bf16[8,2,128,128]{3,2,1,0:T(8,128)(2,1)S(1)}, bf16[8,2,128,128]{3,2,1,0:T(8,128)(2,1)}, u32[]{:S(2)}) copy-start(bf16[8,2,128,128]{3,2,1,0:T(8,128)(2,1)} %param.7) | copy-start | bytes 1572868
  1.7 0.7 copy-start.1
  2.4 0.7 copy-start.2
  4.1 17.3 %collective-permute-start = (bf16[2064,128]{1,0:T(8,128)(2,1)S(1)}, bf16[2064,128]{1,0:T(8,128)(2,1)S(1)}, u32[]{:S(2)}, u32[]{:S(2)}) collective-permute-start(bf16[2064,128]{1,0:T(8,128)(2,1)S(1)} %get-tuple-element.50.refs_0_), channel_id=1, source_target_pairs={{0,2},{2,4},{4,6},{6,0},{1,7},{3,1},{5,3},{7,5},{8,10},{10,12},{12... | collective-permute-start | bytes 1585160 | tf_op jit(solution)/shard_map/ppermute | solution.py:292
  7.2 14.2 %collective-permute-start.1 = (bf16[2064,128]{1,0:T(8,128)(2,1)S(1)}, bf16[2064,128]{1,0:T(8,128)(2,1)S(1)}, u32[]{:S(2)}, u32[]{:S(2)}) collective-permute-start(bf16[2064,128]{1,0:T(8,128)(2,1)S(1)} %get-tuple-element.50.refs_0_), channel_id=1, source_target_pairs={{0,1},{1,0},{2,3},{3,2},{4,5},{5,4},{6,7},{7,6},{8,9},{9,8},{10,11... | collective-permute-start | bytes 1585160 | tf_op jit(solution)/shard_map/ppermute | solution.py:295
  8.8 13.9 %collective-permute-start.2 = (bf16[2064,128]{1,0:T(8,128)(2,1)S(1)}, bf16[2064,128]{1,0:T(8,128)(2,1)S(1)}, u32[]{:S(2)}, u32[]{:S(2)}) collective-permute-start(bf16[2064,128]{1,0:T(8,128)(2,1)S(1)} %get-tuple-element.55.refs_6_), channel_id=1, source_target_pairs={{0,8},{8,0},{16,24},{24,16},{1,9},{9,1},{17,25},{25,17},{2,10},{10... | collective-permute-start | bytes 1585160 | tf_op jit(solution)/shard_map/ppermute | solution.py:287
  10.3 13.6 %collective-permute-start.3 = (bf16[2064,128]{1,0:T(8,128)(2,1)S(1)}, bf16[2064,128]{1,0:T(8,128)(2,1)S(1)}, u32[]{:S(2)}, u32[]{:S(2)}) collective-permute-start(bf16[2064,128]{1,0:T(8,128)(2,1)S(1)} %get-tuple-element.55.refs_6_), channel_id=1, source_target_pairs={{0,16},{8,24},{16,0},{24,8},{1,17},{9,25},{17,1},{25,9},{2,18},{10... | collective-permute-start | bytes 1585160 | tf_op jit(solution)/shard_map/ppermute | solution.py:287
  23.9 16.3 %collective-permute-start.4 = (bf16[2064,128]{1,0:T(8,128)(2,1)S(1)}, bf16[2064,128]{1,0:T(8,128)(2,1)S(1)}, u32[]{:S(2)}, u32[]{:S(2)}) collective-permute-start(bf16[2064,128]{1,0:T(8,128)(2,1)S(1)} %collective-permute-done.refs_2_), channel_id=1, source_target_pairs={{0,2},{2,4},{4,6},{6,0},{1,7},{3,1},{5,3},{7,5},{8,10},{10,12},{12... | collective-permute-start | bytes 1585160 | tf_op jit(solution)/shard_map/ppermute | solution.py:292
  24.4 15.8 %collective-permute-start.5 = (bf16[2064,128]{1,0:T(8,128)(2,1)S(1)}, bf16[2064,128]{1,0:T(8,128)(2,1)S(1)}, u32[]{:S(2)}, u32[]{:S(2)}) collective-permute-start(bf16[2064,128]{1,0:T(8,128)(2,1)S(1)} %collective-permute-done.refs_2_), channel_id=1, source_target_pairs={{0,1},{1,0},{2,3},{3,2},{4,5},{5,4},{6,7},{7,6},{8,9},{9,8},{10,11... | collective-permute-start | bytes 1585160 | tf_op jit(solution)/shard_map/ppermute | solution.py:295
  24.4 15.8 %collective-permute-start.7 = (bf16[2064,128]{1,0:T(8,128)(2,1)S(1)}, bf16[2064,128]{1,0:T(8,128)(2,1)S(1)}, u32[]{:S(2)}, u32[]{:S(2)}) collective-permute-start(bf16[2064,128]{1,0:T(8,128)(2,1)S(1)} %collective-permute-done.2.refs_7_), channel_id=1, source_target_pairs={{0,16},{8,24},{16,0},{24,8},{1,17},{9,25},{17,1},{25,9},{2,18},{10... | collective-permute-start | bytes 1585160 | tf_op jit(solution)/shard_map/ppermute | solution.py:287
  26.0 14.3 %collective-permute-start.6 = (bf16[2048,128]{1,0:T(8,128)(2,1)}, bf16[2048,128]{1,0:T(8,128)(2,1)S(1)}, u32[]{:S(2)}, u32[]{:S(2)}) collective-permute-start(bf16[2048,128]{1,0:T(8,128)(2,1)} %bitcast.d_in.refs_2_), channel_id=1, source_target_pairs={{0,8},{8,0},{16,24},{24,16},{1,9},{9,1},{17,25},{25,17},{2,10},{10... | collective-permute-start | bytes 1572872 | tf_op jit(solution)/shard_map/ppermute | solution.py:287
  40.2 2.2 %collective-permute-start.8 = (bf16[2064,128]{1,0:T(8,128)(2,1)S(1)}, bf16[2064,128]{1,0:T(8,128)(2,1)S(1)}, u32[]{:S(2)}, u32[]{:S(2)}) collective-permute-start(bf16[2064,128]{1,0:T(8,128)(2,1)S(1)} %collective-permute-done.4.refs_4_), channel_id=1, source_target_pairs={{0,1},{1,0},{2,3},{3,2},{4,5},{5,4},{6,7},{7,6},{8,9},{9,8},{10,11... | collective-permute-start | bytes 1585160 | tf_op jit(solution)/shard_map/ppermute | solution.py:295
  40.3 16.0 %collective-permute-start.9 = (bf16[2064,128]{1,0:T(8,128)(2,1)S(1)}, bf16[2064,128]{1,0:T(8,128)(2,1)S(1)}, u32[]{:S(2)}, u32[]{:S(2)}) collective-permute-start(bf16[2064,128]{1,0:T(8,128)(2,1)S(1)} %collective-permute-done.4.refs_4_), channel_id=1, source_target_pairs={{0,2},{2,4},{4,6},{6,0},{1,7},{3,1},{5,3},{7,5},{8,10},{10,12},{12... | collective-permute-start | bytes 1585160 | tf_op jit(solution)/shard_map/ppermute | solution.py:292
  42.0 14.1 %collective-permute-start.10 = (bf16[2048,128]{1,0:T(8,128)(2,1)}, bf16[2048,128]{1,0:T(8,128)(2,1)S(1)}, u32[]{:S(2)}, u32[]{:S(2)}) collective-permute-start(bf16[2048,128]{1,0:T(8,128)(2,1)} %bitcast.d_in.refs_2_), channel_id=1, source_target_pairs={{0,16},{8,24},{16,0},{24,8},{1,17},{9,25},{17,1},{25,9},{2,18},{10... | collective-permute-start | bytes 1572872 | tf_op jit(solution)/shard_map/ppermute | solution.py:287
  56.3 2.0 %collective-permute-start.12 = (bf16[2064,128]{1,0:T(8,128)(2,1)S(1)}, bf16[2064,128]{1,0:T(8,128)(2,1)S(1)}, u32[]{:S(2)}, u32[]{:S(2)}) collective-permute-start(bf16[2064,128]{1,0:T(8,128)(2,1)S(1)} %collective-permute-done.9.refs_1_), channel_id=1, source_target_pairs={{0,1},{1,0},{2,3},{3,2},{4,5},{5,4},{6,7},{7,6},{8,9},{9,8},{10,11... | collective-permute-start | bytes 1585160 | tf_op jit(solution)/shard_map/ppermute | solution.py:295
  56.8 14.2 %collective-permute-start.11 = (bf16[2048,128]{1,0:T(8,128)(2,1)S(1)}, bf16[2048,128]{1,0:T(8,128)(2,1)S(1)}, u32[]{:S(2)}, u32[]{:S(2)}) collective-permute-start(bf16[2048,128]{1,0:T(8,128)(2,1)S(1)} %collective-permute-done.10.refs_4_), channel_id=1, source_target_pairs={{0,8},{8,0},{16,24},{24,16},{1,9},{9,1},{17,25},{25,17},{2,10},{10... | collective-permute-start | bytes 1572872 | tf_op jit(solution)/shard_map/ppermute | solution.py:287
  58.3 12.7 %copy-start.3 = (s32[8,4]{0,1:T(4,128)S(1)}, s32[8,4]{0,1:T(4,128)}, u32[]{:S(2)}) copy-start(s32[8,4]{0,1:T(4,128)} %param.9) | copy-start | bytes 388
  67.4 14.8 %collective-permute-start.13 = (bf16[8,2,128,128]{3,2,1,0:T(8,128)(2,1)S(1)}, bf16[8,2,128,128]{3,2,1,0:T(8,128)(2,1)S(1)}, u32[]{:S(2)}, u32[]{:S(2)}) collective-permute-start(bf16[8,2,128,128]{3,2,1,0:T(8,128)(2,1)S(1)} %get-tuple-element.76), channel_id=1, source_target_pairs={{0,8},{8,0},{16,24},{24,16},{1,9},{9,1},{17,25},{25,17},{2,10},{10... | collective-permute-start | bytes 1572872 | tf_op jit(solution)/shard_map/ppermute | solution.py:287
  68.1 25.1 %collective-permute-start.14 = (bf16[8,2,128,128]{3,2,1,0:T(8,128)(2,1)S(1)}, bf16[8,2,128,128]{3,2,1,0:T(8,128)(2,1)S(1)}, u32[]{:S(2)}, u32[]{:S(2)}) collective-permute-start(bf16[8,2,128,128]{3,2,1,0:T(8,128)(2,1)S(1)} %get-tuple-element.77), channel_id=1, source_target_pairs={{0,16},{8,24},{16,0},{24,8},{1,17},{9,25},{17,1},{25,9},{2,18},{10... | collective-permute-start | bytes 1572872 | tf_op jit(solution)/shard_map/ppermute | solution.py:287
  68.6 24.6 %collective-permute-start.15 = (bf16[8,2,128,128]{3,2,1,0:T(8,128)(2,1)S(1)}, bf16[8,2,128,128]{3,2,1,0:T(8,128)(2,1)S(1)}, u32[]{:S(2)}, u32[]{:S(2)}) collective-permute-start(bf16[8,2,128,128]{3,2,1,0:T(8,128)(2,1)S(1)} %get-tuple-element.78), channel_id=1, source_target_pairs={{0,24},{8,16},{16,8},{24,0},{1,25},{9,17},{17,9},{25,1},{2,26},{10... | collective-permute-start | bytes 1572872 | tf_op jit(solution)/shard_map/ppermute | solution.py:287

commit v4 on v3

v4 whole, which is shorter than its diff:
```python
import functools
import math

import jax
import jax.numpy as jnp
from jax import lax
from jax.experimental import pallas as pl
from jax.experimental.pallas import tpu as pltpu
from jax.sharding import PartitionSpec as P

VMEM_ROOM = 6 * 1024 * 1024
TAIL = 16
BF16, F32 = jnp.bfloat16, jnp.float32


class Sizes:
    def __init__(self, n_row, n_col, density, hamilton, filt):
        self.n_row, self.n_col, self.n_chip = n_row, n_col, n_col // 2
        self.rows, self.ka, self.bs = density.shape[0], density.shape[1], density.shape[2]
        self.kh, self.kf = hamilton.shape[1], filt.shape[1]
        self.nb = self.rows * n_row
        self.bc = self.nb // n_col
        self.tall, self.wide = self.rows * self.bs, self.bc * self.bs
        self.n_first = n_col - 2


def call(kernel, z, ins, outs, scratch, in_specs, out_specs, flops, name):
    held = [x for x in scratch if getattr(x, "memory_space", None) == pltpu.VMEM]
    held += [x for x, spec in zip(list(ins) + outs, in_specs + out_specs) if spec.memory_space == pltpu.VMEM]
    size = sum(math.prod(x.shape) * jnp.dtype(x.dtype).itemsize for x in held)
    return pl.pallas_call(
        functools.partial(kernel, z),
        out_shape=outs,
        in_specs=in_specs,
        out_specs=out_specs,
        scratch_shapes=scratch,
        compiler_params=pltpu.CompilerParams(vmem_limit_bytes=size + VMEM_ROOM),
        cost_estimate=pl.CostEstimate(flops=flops, bytes_accessed=16 << 20, transcendentals=0),
        name=name,
    )(*ins)


def lanes(z, block):
    return pl.ds(pl.multiple_of(block * z.bs, z.bs), z.bs)


def block_rows(z, i, s, slots):
    return slice((i * slots + s) * z.bs, (i * slots + s + 1) * z.bs)


def piece_col(z, n):
    me = lax.axis_index("col")
    step, core = n // 2, lax.rem(me, 2) ^ (n % 2)
    up = lax.rem(me // 2 + step, z.n_chip)
    down = lax.rem(me // 2 + z.n_chip - step, z.n_chip)
    return jnp.where(core == 0, down, up) * 2 + core


def piece_of(z, col):
    me = lax.axis_index("col")
    chip, core = col // 2, lax.rem(col, 2)
    ahead = lax.rem(chip - me // 2 + z.n_chip, z.n_chip)
    behind = lax.rem(me // 2 - chip + z.n_chip, z.n_chip)
    return jnp.where(core == 0, behind, ahead) * 2 + (core ^ lax.rem(me, 2))


def pack_kernel(z, vals_in, *refs):
    cols_in, (out, tail) = refs[:-2], refs[-2:]
    tail[...] = jnp.zeros_like(tail)
    first = 0
    for cols in cols_in:
        count = cols.shape[0]
        tail[first:first + count, 0:z.rows] = cols[...].astype(F32)
        first += count
    rows = vals_in.shape[0]
    out[rows:rows + TAIL, :] = tail[...].astype(BF16)
    out[0:rows, :] = vals_in[...]


def read_tails(payloads, ints, idx, sem):
    for n, ref in enumerate(payloads):
        rows = ref.shape[0] - TAIL
        ints[n] = ref[rows:rows + TAIL, :].astype(F32).astype(jnp.int32)[0:8, :]
    copy = pltpu.make_async_copy(ints, idx, sem)
    copy.start()
    copy.wait()


def fill_left(z, idx, n, col, blocks, dense, first):
    zero = jnp.zeros((z.bs, z.wide), BF16)
    for i in range(z.rows):
        rows = slice(i * z.bs, (i + 1) * z.bs)
        dense[rows, first:first + z.wide] = zero
        for s in range(z.ka):
            k = idx[n, s, i] - col * z.bc
            at = pl.ds(pl.multiple_of(first + k * z.bs, z.bs), z.bs)
            dense[rows, at] = blocks[block_rows(z, i, s, z.ka), :]


def fill_right(z, first_slot, slots, idx, payloads, dense):
    dense[...] = jnp.zeros_like(dense)
    me = lax.axis_index("col")
    for p, payload in enumerate(payloads):
        for i in range(z.rows):
            k = (lax.axis_index("row") ^ p) * z.rows + i
            n = piece_of(z, k // z.bc)
            at = pl.ds(pl.multiple_of((n * z.bc + lax.rem(k, z.bc)) * z.bs, z.bs), z.bs)
            for s in range(slots):
                j = idx[p, first_slot + s, i] - me * z.bc
                dense[at, lanes(z, j)] = payload[block_rows(z, i, s, slots), :]


def halves(n):
    return [slice(0, n // 2), slice(n // 2, n)]


def first_kernel(z, *refs):
    left_in, right_in = refs[:z.n_first], refs[z.n_first:z.n_first + z.n_row]
    total, panel, right_last, table, right, ints, idx, sem = refs[z.n_first + z.n_row:]
    read_tails(right_in + left_in, ints, idx, sem)
    table[...] = ints[0:z.n_row]
    fill_right(z, z.ka, z.kh, idx, right_in, right)
    for n in range(z.n_first):
        fill_left(z, idx, z.n_row + n, piece_col(z, n), left_in[n], panel, n * z.wide)
    deep = z.n_first * z.wide
    for rows in halves(z.tall):
        total[rows, :] = jnp.dot(panel[rows, :], right[0:deep, :], preferred_element_type=F32)
    right_last[...] = right[deep:, :]


def last_kernel(z, table, last_0, last_1, right, total_in, panel, *refs):
    total, turned, panel_last, *part, columns, ints, idx, sem = refs
    read_tails([last_0, last_1], ints, idx, sem)
    for n, payload in enumerate((last_0, last_1)):
        fill_left(z, idx, n, piece_col(z, z.n_first + n), payload, panel_last, n * z.wide)
    for rows in halves(z.tall):
        total[rows, :] = total_in[rows, :] + jnp.dot(panel_last[rows, :], right[...], preferred_element_type=F32)
    for i in range(z.rows):
        rows = slice(i * z.bs, (i + 1) * z.bs)
        for j in range(z.bc):
            cols = slice(j * z.bs, (j + 1) * z.bs)
            turned[cols, rows] = total[rows, cols].T.astype(BF16)
    one_part(z, table, z.n_row - 1, turned, panel, panel_last, columns, part)


def parts_kernel(z, table, turned, panel, panel_last, *refs):
    cuts = (len(refs) - 1) // (z.n_row - 2)
    for n in range(1, z.n_row - 1):
        one_part(z, table, n, turned, panel, panel_last, refs[-1], refs[(n - 1) * cuts:n * cuts])


def one_part(z, table, n, turned, panel, panel_last, columns, out):
    per_out = z.rows // len(out)
    row = lax.axis_index("row") ^ n
    per = z.n_col // z.n_row
    for t in range(per):
        column = columns.at[t % 2]
        piece = piece_of(z, row * per + t)

        @pl.when(piece < z.n_first)
        def _():
            at = pl.ds(pl.multiple_of(piece * z.wide, z.wide), z.wide)
            column[...] = jnp.dot(turned[...], panel[:, at], preferred_element_type=F32)

        @pl.when(piece >= z.n_first)
        def _():
            at = pl.ds(pl.multiple_of((piece - z.n_first) * z.wide, z.wide), z.wide)
            column[...] = jnp.dot(turned[...], panel_last[:, at], preferred_element_type=F32)

        for b in range(z.bc):
            i = t * z.bc + b
            for s in range(z.ka):
                j = table[n, s, i] - lax.axis_index("col") * z.bc
                out[i // per_out][i % per_out, s] = column[lanes(z, j), b * z.bs:(b + 1) * z.bs].astype(out[0].dtype)


def base_kernel(z, table, filt, total, turned, panel, panel_last, mixed, base, columns, own):
    me = lax.axis_index("col")
    one_part(z, table, 0, turned, panel, panel_last, columns, [own])
    for i in range(z.rows):
        rows = slice(i * z.bs, (i + 1) * z.bs)
        for s in range(z.kf):
            mixed[i, s] = total[rows, lanes(z, filt[s, i] - me * z.bc)].astype(mixed.dtype)
        for s in range(z.ka):
            direct = total[rows, lanes(z, table[0, s, i] - me * z.bc)]
            base[i, s] = 3.0 * direct - 2.0 * own[i, s].T


def square_kernel(z, *refs):
    table, filt, panel, panel_last = refs[:4]
    squared, right, total = refs[4 + z.n_row:]
    me = lax.axis_index("col")
    fill_right(z, 0, z.ka, table, refs[4:4 + z.n_row], right)
    deep = z.n_first * z.wide
    for rows in halves(z.tall):
        total[rows, :] = jnp.dot(panel[rows, :], right[0:deep, :], preferred_element_type=F32)
        total[rows, :] += jnp.dot(panel_last[rows, :], right[deep:, :], preferred_element_type=F32)
    for i in range(z.rows):
        rows = slice(i * z.bs, (i + 1) * z.bs)
        for s in range(z.kf):
            squared[i, s] = total[rows, lanes(z, filt[s, i] - me * z.bc)].astype(squared.dtype)


def add_kernel(z, x_0, x_1, y_0, y_1, x_out, y_out):
    x_out[...] = (x_0[...].astype(F32) + x_1[...].astype(F32)).astype(x_out.dtype)
    y_out[...] = (y_0[...].astype(F32) + y_1[...].astype(F32)).astype(y_out.dtype)


def gradient_kernel(z, base, *refs):
    terms, out = refs[:-1], refs[-1]
    for i in range(z.rows):
        for s in range(z.ka):
            here = [t for t in terms if t.shape[0] == z.rows]
            cut = [t for t in terms if t.shape[0] < z.rows]
            half = z.rows // 2
            blocks = [t[i, s] for t in here] + [t[i % half, s] for t in cut[i // half::2]]
            cubic = blocks[0].astype(F32)
            for other in blocks[1:]:
                cubic += other.astype(F32)
            out[i, s] = (base[i, s] - 2.0 * cubic.T).astype(out.dtype)


def local(n_row, n_col, density, density_cols, hamilton, hamilton_cols, filter_cols):
    z = Sizes(n_row, n_col, density, hamilton, filter_cols)
    block = (z.bs, z.bs)
    shape = jax.ShapeDtypeStruct
    smem = pl.BlockSpec(memory_space=pltpu.SMEM)
    vmem = pl.BlockSpec(memory_space=pltpu.VMEM)
    dma = pltpu.SemaphoreType.DMA
    d_rows, h_rows = z.rows * z.ka * z.bs, z.rows * z.kh * z.bs
    panel_flops = 2 * z.tall * z.wide * z.nb * z.bs
    part_flops = panel_flops // n_row

    def over_row(x, flip):
        return lax.ppermute(x, "row", [(r, r ^ flip) for r in range(n_row)])

    def next_chip(x):
        pairs = [(2 * p, 2 * ((p + 1) % z.n_chip)) for p in range(z.n_chip)]
        pairs += [(2 * p + 1, 2 * ((p - 1) % z.n_chip) + 1) for p in range(z.n_chip)]
        return lax.ppermute(x, "col", pairs)

    def other_core(x):
        return lax.ppermute(x, "col", [(c, c ^ 1) for c in range(n_col)])

    flat = density.reshape(d_rows, z.bs)

    def pack(vals, cols, name):
        rows = vals.shape[0]
        outs = [shape((rows + TAIL, z.bs), BF16)]
        scratch = [pltpu.VMEM((TAIL, z.bs), F32)]
        return call(pack_kernel, z, [vals, *cols], outs, scratch, [vmem] * (1 + len(cols)), [vmem], 0, name)[0]

    d_pay = pack(flat, [density_cols.T], "pack_d")
    h_pay = pack(hamilton.reshape(h_rows, z.bs), [density_cols.T, hamilton_cols.T], "pack_h")

    def high(flip):
        return 1 << (flip.bit_length() - 1)

    def low(flip):
        return flip & -flip

    d_right, h_right = {0: flat}, {0: h_pay}
    for flip in range(1, n_row):
        if flip.bit_count() == 1:
            h_right[flip] = over_row(h_pay, flip)
    d_right, h_right = lax.optimization_barrier((d_right, h_right))
    d_right[1] = over_row(d_right[0], 1)
    for flip in sorted(range(1, n_row), key=int.bit_count):
        if flip not in h_right:
            h_right[flip] = over_row(h_right[flip - high(flip)], high(flip))
    d_right, h_right = lax.optimization_barrier((d_right, h_right))
    for flip in range(2, n_row):
        if flip.bit_count() == 1:
            d_right[flip] = over_row(d_right[0], flip)
    h_right = [h_right[flip] for flip in range(n_row)]

    left, piece = [], d_pay
    for step in range(z.n_chip):
        if step:
            piece = next_chip(piece)
        left.append(piece)
        if step < z.n_chip - 1:
            left.append(other_core(piece))

    n_pay = z.n_first + n_row
    total, panel, right_last, table = call(
        first_kernel, z,
        [*left[:z.n_first], *h_right],
        [
            shape((z.tall, z.wide), F32),
            shape((z.tall, z.n_first * z.wide), BF16),
            shape((2 * z.wide, z.wide), BF16),
            shape((n_row, 8, z.bs), jnp.int32),
        ],
        [
            pltpu.VMEM((z.nb * z.bs, z.wide), BF16),
            pltpu.VMEM((n_pay, 8, z.bs), jnp.int32),
            pltpu.SMEM((n_pay, 8, z.bs), jnp.int32),
            dma,
        ],
        [vmem] * n_pay, [vmem] * 4, panel_flops, "first",
    )
    last, total, d_right = lax.optimization_barrier((left[-1], total, d_right))
    for flip in range(1, n_row):
        if flip not in d_right:
            d_right[flip] = over_row(d_right[flip - low(flip)], low(flip))
    d_right = [d_right[flip] for flip in range(n_row)]

    part = shape((z.rows, z.ka) + block, BF16)
    columns = pltpu.VMEM((2, z.wide, z.wide), F32)
    cuts = 2 if n_row == 4 and z.rows % 2 == 0 else 1
    cut_part = shape((z.rows // cuts, z.ka) + block, BF16)
    total, turned, panel_last, *far = call(
        last_kernel, z,
        [table, last, other_core(last), right_last, total, panel],
        [shape((z.tall, z.wide), F32), shape((z.wide, z.tall), BF16), shape((z.tall, 2 * z.wide), BF16)]
        + [cut_part] * cuts,
        [
            columns,
            pltpu.VMEM((2, 8, z.bs), jnp.int32),
            pltpu.SMEM((2, 8, z.bs), jnp.int32),
            dma,
        ],
        [smem] + [vmem] * 5, [vmem] * (3 + cuts), panel_flops // 4 + part_flops, "last",
    )
    near = call(
        parts_kernel, z, [table, turned, panel, panel_last], [cut_part] * (cuts * (n_row - 2)), [columns],
        [smem] + [vmem] * 3, [vmem] * (cuts * (n_row - 2)), part_flops * (n_row - 2), "parts",
    )
    if cuts == 2:
        far = over_row(far[0], 1), over_row(far[1], 2)
        x_0, y_1 = over_row(near[0], 1), over_row(near[3], 2)
    else:
        received = [over_row(term, n + 1) for n, term in enumerate([*near, *far])]
    mixed, base = call(
        base_kernel, z,
        [table, filter_cols.T, total, turned, panel, panel_last],
        [shape((z.rows, z.kf) + block, BF16), shape((z.rows, z.ka) + block, F32)],
        [columns, pltpu.VMEM((z.rows, z.ka) + block, F32)],
        [smem] * 2 + [vmem] * 4, [vmem] * 2, part_flops, "base",
    )
    if cuts == 2:
        y_0, x_1 = call(
            add_kernel, z, [near[2], far[0], near[1], far[1]], [cut_part] * 2, [],
            [vmem] * 4, [vmem] * 2, 0, "add",
        )
        received = [x_0, over_row(x_1, 1), over_row(y_0, 2), y_1]
    squared, = call(
        square_kernel, z,
        [table, filter_cols.T, panel, panel_last, *d_right],
        [shape((z.rows, z.kf) + block, BF16)],
        [pltpu.VMEM((z.nb * z.bs, z.wide), BF16), pltpu.VMEM((z.tall, z.wide), F32)],
        [smem] * 2 + [vmem] * (n_row + 2), [vmem], panel_flops, "squared",
    )
    gradient, = call(
        gradient_kernel, z, [base, *received], [part], [],
        [vmem] * (1 + len(received)), [vmem], 0, "gradient",
    )
    return squared, mixed, gradient


def solution(mesh):
    spec4 = P("row", "col", None, None)
    spec2 = P("row", "col")
    body = functools.partial(local, mesh.shape["row"], mesh.shape["col"])
    return jax.shard_map(
        body,
        mesh=mesh,
        in_specs=(spec4, spec2, spec4, spec2, spec2),
        out_specs=(spec4, spec4, spec4),
        check_vma=False,
    )
```

time: 94.6 us -> 84 us (0.89)
  waiting for transfers between devices: 43.4 us -> 33.8 us
  Pallas kernels: 30.7 us -> 28.1 us
  local copies, waits for them, and re-layouts: 2.4 us -> 3.44 us
    ppermute x9 -> x12, waiting for transfers between devices: 32.5 us -> 15.6 us  [over_row(): return lax.ppermute(x, 'row', [(r, r ^ flip) for r in range(n_row)])]
    ppermute x3, waiting for transfers between devices: 9.89 us -> 17.7 us  [next_chip(): return lax.ppermute(x, 'col', pairs)]
    ppermute x9 -> x12, starting transfers between devices: 9.82 us -> 14.1 us  [over_row(): return lax.ppermute(x, 'row', [(r, r ^ flip) for r in range(n_row)])]
    pallas_call x5 -> x9, Pallas kernels: 30.7 us -> 28.1 us  [call(): pl.pallas_call(functools.partial(kernel, z), out_shape=outs, in_specs=in_...]
    ppermute x3, starting transfers between devices: 5.21 us -> 3.08 us  [next_chip(): return lax.ppermute(x, 'col', pairs)]
    ppermute x4, starting transfers between devices: 2.13 us -> 0.62 us  [other_core(): return lax.ppermute(x, 'col', [(c, c ^ 1) for c in range(n_col)])]
    unnamed x8 -> x12, local copies, waits for them, and re-layouts: 2.4 us -> 3.44 us
  transfers between devices with their start and end apart: 16 -> 19, of which waited for: 9 -> 9; matrix products, arithmetic and copies ran while one was open for 0% -> 0% of each run, Pallas kernels for 30% -> 32%
where the time goes in v4:
time: 84 us; the launch traced here: 83.8 us
  waiting for transfers between devices  33.8 us (40%)
  Pallas kernels  28.1 us (33%)
  starting transfers between devices  17.8 us (21%)
  local copies, waits for them, and re-layouts  3.44 us (4%)
    pallas_call x9, Pallas kernels, call(): pl.pallas_call(functools.partial(kernel, z), out_shape=outs, in_specs=in_...  28.1 us
    ppermute x3, waiting for transfers between devices, next_chip(): return lax.ppermute(x, 'col', pairs)  17.7 us
    ppermute x12, waiting for transfers between devices, over_row(): return lax.ppermute(x, 'row', [(r, r ^ flip) for r in range(n_row)])  15.6 us
    ppermute x12, starting transfers between devices, over_row(): return lax.ppermute(x, 'row', [(r, r ^ flip) for r in range(n_row)])  14.1 us
    unnamed x12, local copies, waits for them, and re-layouts  3.44 us
    ppermute x3, starting transfers between devices, next_chip(): return lax.ppermute(x, 'col', pairs)  3.08 us
  transfers between devices with their start and end apart: 19, of which 9 were waited for; matrix products, arithmetic and copies ran while one was open for 0% of the time, Pallas kernels for 32%

profile of v4, /device:TPU:0, one launch (start us, length us, event | category | flops | bytes accessed | tf_op | source)
XLA Modules:
  0.0 83.8 jit_solution(4778426587263761531)
XLA Ops:
  0.6 1.0 %copy-done = bf16[8,2,128,128]{3,2,1,0:T(8,128)(2,1)S(1)} copy-done((bf16[8,2,128,128]{3,2,1,0:T(8,128)(2,1)S(1)}, bf16[8,2,128,128]{3,2,1,0:T(8,128)(2,1)}, u32[]{:S(2)}) %copy-start) | copy-done | bytes 524312
  1.7 0.7 copy-done.3
  2.4 3.1 %collective-permute-start.1 = (bf16[2064,128]{1,0:T(8,128)(2,1)S(1)}, bf16[2064,128]{1,0:T(8,128)(2,1)S(1)}, u32[]{:S(2)}, u32[]{:S(2)}) collective-permute-start(bf16[2064,128]{1,0:T(8,128)(2,1)S(1)} %pack_d.1.refs_0_), channel_id=1, source_target_pairs={{0,2},{2,4},{4,6},{6,0},{1,7},{3,1},{5,3},{7,5},{8,10},{10,12},{12... | collective-permute-start | bytes 1585160 | tf_op jit(solution)/shard_map/ppermute | solution.py:240
  5.5 1.0 %copy-done.2 = bf16[8,2,128,128]{3,2,1,0:T(8,128)(2,1)S(1)} copy-done((bf16[8,2,128,128]{3,2,1,0:T(8,128)(2,1)S(1)}, bf16[8,2,128,128]{3,2,1,0:T(8,128)(2,1)}, u32[]{:S(2)}) %copy-start.2) | copy-done | bytes 524312
  6.5 0.7 copy-done.5
  7.2 1.6 %collective-permute-start.5 = (bf16[2064,128]{1,0:T(8,128)(2,1)S(1)}, bf16[2064,128]{1,0:T(8,128)(2,1)S(1)}, u32[]{:S(2)}, u32[]{:S(2)}) collective-permute-start(bf16[2064,128]{1,0:T(8,128)(2,1)S(1)} %pack_h.1.refs_6_), channel_id=1, source_target_pairs={{0,8},{8,0},{16,24},{24,16},{1,9},{9,1},{17,25},{25,17},{2,10},{10... | collective-permute-start | bytes 1585160 | tf_op jit(solution)/shard_map/ppermute | solution.py:235
  8.8 1.5 %collective-permute-start.6 = (bf16[2064,128]{1,0:T(8,128)(2,1)S(1)}, bf16[2064,128]{1,0:T(8,128)(2,1)S(1)}, u32[]{:S(2)}, u32[]{:S(2)}) collective-permute-start(bf16[2064,128]{1,0:T(8,128)(2,1)S(1)} %pack_h.1.refs_6_), channel_id=1, source_target_pairs={{0,16},{8,24},{16,0},{24,8},{1,17},{9,25},{17,1},{25,9},{2,18},{10... | collective-permute-start | bytes 1585160 | tf_op jit(solution)/shard_map/ppermute | solution.py:235
  10.3 9.4 %collective-permute-done.1.refs_2_ = bf16[2064,128]{1,0:T(8,128)(2,1)S(1)} collective-permute-done((bf16[2064,128]{1,0:T(8,128)(2,1)S(1)}, bf16[2064,128]{1,0:T(8,128)(2,1)S(1)}, u32[]{:S(2)}, u32[]{:S(2)}) %collective-permute-start.1) | collective-permute-done | bytes 528416 | tf_op jit(solution)/shard_map/ppermute | solution.py:240
  19.7 2.0 %collective-permute-done.5.refs_7_ = bf16[2064,128]{1,0:T(8,128)(2,1)S(1)} collective-permute-done((bf16[2064,128]{1,0:T(8,128)(2,1)S(1)}, bf16[2064,128]{1,0:T(8,128)(2,1)S(1)}, u32[]{:S(2)}, u32[]{:S(2)}) %collective-permute-start.5) | collective-permute-done | bytes 528416 | tf_op jit(solution)/shard_map/ppermute | solution.py:235
  21.6 1.7 %collective-permute-done.6.refs_8_ = bf16[2064,128]{1,0:T(8,128)(2,1)S(1)} collective-permute-done((bf16[2064,128]{1,0:T(8,128)(2,1)S(1)}, bf16[2064,128]{1,0:T(8,128)(2,1)S(1)}, u32[]{:S(2)}, u32[]{:S(2)}) %collective-permute-start.6) | collective-permute-done | bytes 528416 | tf_op jit(solution)/shard_map/ppermute | solution.py:235
  23.3 1.5 %collective-permute-start.8 = (bf16[2064,128]{1,0:T(8,128)(2,1)S(1)}, bf16[2064,128]{1,0:T(8,128)(2,1)S(1)}, u32[]{:S(2)}, u32[]{:S(2)}) collective-permute-start(bf16[2064,128]{1,0:T(8,128)(2,1)S(1)} %collective-permute-done.5.refs_7_), channel_id=1, source_target_pairs={{0,16},{8,24},{16,0},{24,8},{1,17},{9,25},{17,1},{25,9},{2,18},{10... | collective-permute-start | bytes 1585160 | tf_op jit(solution)/shard_map/ppermute | solution.py:235
  24.9 0.5 collective-permute-start.7
  25.4 0.5 collective-permute-start.2
  25.9 8.3 %collective-permute-done.3.refs_4_ = bf16[2064,128]{1,0:T(8,128)(2,1)S(1)} collective-permute-done((bf16[2064,128]{1,0:T(8,128)(2,1)S(1)}, bf16[2064,128]{1,0:T(8,128)(2,1)S(1)}, u32[]{:S(2)}, u32[]{:S(2)}) %collective-permute-start.3) | collective-permute-done | bytes 528416 | tf_op jit(solution)/shard_map/ppermute | solution.py:240
  34.3 4.3 %collective-permute-done.7.refs_5_ = bf16[2048,128]{1,0:T(8,128)(2,1)S(1)} collective-permute-done((bf16[2048,128]{1,0:T(8,128)(2,1)S(1)}, bf16[2048,128]{1,0:T(8,128)(2,1)S(1)}, u32[]{:S(2)}, u32[]{:S(2)}) %collective-permute-start.7) | collective-permute-done | bytes 524320 | tf_op jit(solution)/shard_map/ppermute | solution.py:235
  38.6 0.5 collective-permute-start.10
  39.1 6.7 %first.1 = (f32[1024,512]{1,0:T(8,128)S(1)}, bf16[1024,3072]{1,0:T(8,128)(2,1)S(1)}, bf16[1024,512]{1,0:T(8,128)(2,1)S(1)}, s32[4,8,128]{2,1,0:T(8,128)S(1)}) custom-call(bf16[2064,128]{1,0:T(8,128)(2,1)S(1)} %pack_d.1.refs_0_, bf16[2064,128]{1,0:T(8,128)(2,1)S(1)} %collective-permute-done.refs_1_, bf16[2064,128]{1,0:T(8,128)(2,1)S(1)} %collective-permute-done.1.refs_2_, ...), custom_call_target="tpu_custom_call" | custom-call | flops 4294967296 | bytes 16777216 | tf_op jit(solution)/shard_map/first/pallas_call | solution.py:31
  45.8 5.6 %collective-permute-done.10.refs_6_ = bf16[2048,128]{1,0:T(8,128)(2,1)S(1)} collective-permute-done((bf16[2048,128]{1,0:T(8,128)(2,1)S(1)}, bf16[2048,128]{1,0:T(8,128)(2,1)S(1)}, u32[]{:S(2)}, u32[]{:S(2)}) %collective-permute-start.10) | collective-permute-done | bytes 524320 | tf_op jit(solution)/shard_map/ppermute | solution.py:235
  51.5 1.3 %collective-permute-start.12 = (bf16[2048,128]{1,0:T(8,128)(2,1)S(1)}, bf16[2048,128]{1,0:T(8,128)(2,1)S(1)}, u32[]{:S(2)}, u32[]{:S(2)}) collective-permute-start(bf16[2048,128]{1,0:T(8,128)(2,1)S(1)} %collective-permute-done.10.refs_6_), channel_id=1, source_target_pairs={{0,8},{8,0},{16,24},{24,16},{1,9},{9,1},{17,25},{25,17},{2,10},{10... | collective-permute-start | bytes 1572872 | tf_op jit(solution)/shard_map/ppermute | solution.py:235
  52.8 0.5 collective-permute-done.11.last_1
  53.3 4.7 %last.1 = (f32[1024,512]{1,0:T(8,128)S(1)}, bf16[512,1024]{1,0:T(8,128)(2,1)S(1)}, bf16[1024,1024]{1,0:T(8,128)(2,1)S(1)}, bf16[4,2,128,128]{3,2,1,0:T(8,128)(2,1)S(1)}, bf16[4,2,128,128]{3,2,1,0:T(8,128)(2,1)S(1)}) custom-call(s32[4,8,128]{2,1,0:T(8,128)S(1)} %get-tuple-element.43.table.refs_0_, bf16[2064,128]{1,0:T(8,128)(2,1)S(1)} %collective-permute-done.9.last_0, ...), custom_call_target="tpu_custom_call" | custom-call | flops 2147483648 | bytes 16777216 | tf_op jit(solution)/shard_map/last/pallas_call | solution.py:31
  58.1 1.5 %collective-permute-start.14 = (bf16[4,2,128,128]{3,2,1,0:T(8,128)(2,1)S(1)}, bf16[4,2,128,128]{3,2,1,0:T(8,128)(2,1)S(1)}, u32[]{:S(2)}, u32[]{:S(2)}) collective-permute-start(bf16[4,2,128,128]{3,2,1,0:T(8,128)(2,1)S(1)} %get-tuple-element.61), channel_id=1, source_target_pairs={{0,8},{8,0},{16,24},{24,16},{1,9},{9,1},{17,25},{25,17},{2,10},{10... | collective-permute-start | bytes 786440 | tf_op jit(solution)/shard_map/ppermute | solution.py:235
  59.5 1.5 %collective-permute-start.15 = (bf16[4,2,128,128]{3,2,1,0:T(8,128)(2,1)S(1)}, bf16[4,2,128,128]{3,2,1,0:T(8,128)(2,1)S(1)}, u32[]{:S(2)}, u32[]{:S(2)}) collective-permute-start(bf16[4,2,128,128]{3,2,1,0:T(8,128)(2,1)S(1)} %get-tuple-element.63), channel_id=1, source_target_pairs={{0,16},{8,24},{16,0},{24,8},{1,17},{9,25},{17,1},{25,9},{2,18},{10... | collective-permute-start | bytes 786440 | tf_op jit(solution)/shard_map/ppermute | solution.py:235
  61.1 3.8 %parts.1 = (bf16[4,2,128,128]{3,2,1,0:T(8,128)(2,1)S(1)}, bf16[4,2,128,128]{3,2,1,0:T(8,128)(2,1)S(1)}, bf16[4,2,128,128]{3,2,1,0:T(8,128)(2,1)S(1)}, bf16[4,2,128,128]{3,2,1,0:T(8,128)(2,1)S(1)}) custom-call(s32[4,8,128]{2,1,0:T(8,128)S(1)} %get-tuple-element.43.table.refs_0_, bf16[512,1024]{1,0:T(8,128)(2,1)S(1)} %get-tuple-element.56.turned, ...), custom_call_target="tpu_custom_call" | custom-call | flops 2147483648 | bytes 16777216 | tf_op jit(solution)/shard_map/parts/pallas_call | solution.py:31
  64.9 0.6 collective-permute-start.13
  65.5 0.6 collective-permute-start.18
  66.1 4.0 %base.1 = (bf16[8,4,128,128]{3,2,1,0:T(8,128)(2,1)}, f32[8,2,128,128]{3,2,1,0:T(8,128)S(1)}) custom-call(s32[4,8,128]{2,1,0:T(8,128)S(1)} %get-tuple-element.43.table.refs_0_, s32[4,8]{1,0:T(4,128)S(1)} %bitcast.12, f32[1024,512]{1,0:T(8,128)S(1)} %get-tuple-element.55.total, bf16[512,1024]{1,0:T(8,128)(2,1)S(1)} %get-tuple-element.56.turned, ...), custom_call_target="tpu_custom_call" | custom-call | flops 1073741824 | bytes 16777216 | tf_op jit(solution)/shard_map/base/pallas_call | solution.py:31
  70.1 1.7 %collective-permute-done.14.x_1 = bf16[4,2,128,128]{3,2,1,0:T(8,128)(2,1)S(1)} collective-permute-done((bf16[4,2,128,128]{3,2,1,0:T(8,128)(2,1)S(1)}, bf16[4,2,128,128]{3,2,1,0:T(8,128)(2,1)S(1)}, u32[]{:S(2)}, u32[]{:S(2)}) %collective-permute-start.14) | collective-permute-done | bytes 262176 | tf_op jit(solution)/shard_map/ppermute | solution.py:235
  72.0 1.4 %collective-permute-start.16 = (bf16[4,2,128,128]{3,2,1,0:T(8,128)(2,1)S(1)}, bf16[4,2,128,128]{3,2,1,0:T(8,128)(2,1)S(1)}, u32[]{:S(2)}, u32[]{:S(2)}) collective-permute-start(bf16[4,2,128,128]{3,2,1,0:T(8,128)(2,1)S(1)} %get-tuple-element.64), channel_id=1, source_target_pairs={{0,8},{8,0},{16,24},{24,16},{1,9},{9,1},{17,25},{25,17},{2,10},{10... | collective-permute-start | bytes 786440 | tf_op jit(solution)/shard_map/ppermute | solution.py:235
  73.4 1.6 %collective-permute-start.17 = (bf16[4,2,128,128]{3,2,1,0:T(8,128)(2,1)S(1)}, bf16[4,2,128,128]{3,2,1,0:T(8,128)(2,1)S(1)}, u32[]{:S(2)}, u32[]{:S(2)}) collective-permute-start(bf16[4,2,128,128]{3,2,1,0:T(8,128)(2,1)S(1)} %get-tuple-element.65), channel_id=1, source_target_pairs={{0,16},{8,24},{16,0},{24,8},{1,17},{9,25},{17,1},{25,9},{2,18},{10... | collective-permute-start | bytes 786440 | tf_op jit(solution)/shard_map/ppermute | solution.py:235
  74.9 7.4 %squared.1 = bf16[8,4,128,128]{3,2,1,0:T(8,128)(2,1)} custom-call(s32[4,8,128]{2,1,0:T(8,128)S(1)} %get-tuple-element.43.table.refs_0_, s32[4,8]{1,0:T(4,128)S(1)} %bitcast.13, bf16[1024,3072]{1,0:T(8,128)(2,1)S(1)} %get-tuple-element.44.panel.refs_2_, bf16[1024,1024]{1,0:T(8,128)(2,1)S(1)} %get-tuple-element.51.refs_3_.panel_last, ...), custom_call_target="tpu_custom_call" | custom-call | flops 4294967296 | bytes 16777216 | tf_op jit(solution)/shard_map/squared/pallas_call | solution.py:31
  82.6 1.1 %gradient.1 = bf16[8,2,128,128]{3,2,1,0:T(8,128)(2,1)} custom-call(f32[8,2,128,128]{3,2,1,0:T(8,128)S(1)} %get-tuple-element.58.base, bf16[4,2,128,128]{3,2,1,0:T(8,128)(2,1)S(1)} %collective-permute-done.13.refs_0_, bf16[4,2,128,128]{3,2,1,0:T(8,128)(2,1)S(1)} %collective-permute-done.16.refs_1_, ...), custom_call_target="tpu_custom_call" | custom-call | bytes 16777216 | tf_op jit(solution)/shard_map/gradient/pallas_call | solution.py:31
  (27 shorter events, 0.6 us)
Async XLA Ops:
  0.6 1.0 %copy-start = (bf16[8,2,128,128]{3,2,1,0:T(8,128)(2,1)S(1)}, bf16[8,2,128,128]{3,2,1,0:T(8,128)(2,1)}, u32[]{:S(2)}) copy-start(bf16[8,2,128,128]{3,2,1,0:T(8,128)(2,1)} %param.5) | copy-start | bytes 1572868
  1.7 0.7 copy-start.3
  2.4 22.5 %copy-start.1 = (bf16[8,2,128,128]{3,2,1,0:T(8,128)(2,1)S(1)}, bf16[8,2,128,128]{3,2,1,0:T(8,128)(2,1)}, u32[]{:S(2)}) copy-start(bf16[8,2,128,128]{3,2,1,0:T(8,128)(2,1)} %param.5) | copy-start | bytes 1572868
  2.4 17.3 %collective-permute-start.1 = (bf16[2064,128]{1,0:T(8,128)(2,1)S(1)}, bf16[2064,128]{1,0:T(8,128)(2,1)S(1)}, u32[]{:S(2)}, u32[]{:S(2)}) collective-permute-start(bf16[2064,128]{1,0:T(8,128)(2,1)S(1)} %pack_d.1.refs_0_), channel_id=1, source_target_pairs={{0,2},{2,4},{4,6},{6,0},{1,7},{3,1},{5,3},{7,5},{8,10},{10,12},{12... | collective-permute-start | bytes 1585160 | tf_op jit(solution)/shard_map/ppermute | solution.py:240
  5.5 1.0 %copy-start.2 = (bf16[8,2,128,128]{3,2,1,0:T(8,128)(2,1)S(1)}, bf16[8,2,128,128]{3,2,1,0:T(8,128)(2,1)}, u32[]{:S(2)}) copy-start(bf16[8,2,128,128]{3,2,1,0:T(8,128)(2,1)} %param.7) | copy-start | bytes 1572868
  6.5 0.7 copy-start.5
  7.2 14.4 %collective-permute-start.5 = (bf16[2064,128]{1,0:T(8,128)(2,1)S(1)}, bf16[2064,128]{1,0:T(8,128)(2,1)S(1)}, u32[]{:S(2)}, u32[]{:S(2)}) collective-permute-start(bf16[2064,128]{1,0:T(8,128)(2,1)S(1)} %pack_h.1.refs_6_), channel_id=1, source_target_pairs={{0,8},{8,0},{16,24},{24,16},{1,9},{9,1},{17,25},{25,17},{2,10},{10... | collective-permute-start | bytes 1585160 | tf_op jit(solution)/shard_map/ppermute | solution.py:235
  8.8 14.6 %collective-permute-start.6 = (bf16[2064,128]{1,0:T(8,128)(2,1)S(1)}, bf16[2064,128]{1,0:T(8,128)(2,1)S(1)}, u32[]{:S(2)}, u32[]{:S(2)}) collective-permute-start(bf16[2064,128]{1,0:T(8,128)(2,1)S(1)} %pack_h.1.refs_6_), channel_id=1, source_target_pairs={{0,16},{8,24},{16,0},{24,8},{1,17},{9,25},{17,1},{25,9},{2,18},{10... | collective-permute-start | bytes 1585160 | tf_op jit(solution)/shard_map/ppermute | solution.py:235
  19.7 14.6 %collective-permute-start.3 = (bf16[2064,128]{1,0:T(8,128)(2,1)S(1)}, bf16[2064,128]{1,0:T(8,128)(2,1)S(1)}, u32[]{:S(2)}, u32[]{:S(2)}) collective-permute-start(bf16[2064,128]{1,0:T(8,128)(2,1)S(1)} %collective-permute-done.1.refs_2_), channel_id=1, source_target_pairs={{0,2},{2,4},{4,6},{6,0},{1,7},{3,1},{5,3},{7,5},{8,10},{10,12},{12... | collective-permute-start | bytes 1585160 | tf_op jit(solution)/shard_map/ppermute | solution.py:240
  23.3 15.2 %collective-permute-start.8 = (bf16[2064,128]{1,0:T(8,128)(2,1)S(1)}, bf16[2064,128]{1,0:T(8,128)(2,1)S(1)}, u32[]{:S(2)}, u32[]{:S(2)}) collective-permute-start(bf16[2064,128]{1,0:T(8,128)(2,1)S(1)} %collective-permute-done.5.refs_7_), channel_id=1, source_target_pairs={{0,16},{8,24},{16,0},{24,8},{1,17},{9,25},{17,1},{25,9},{2,18},{10... | collective-permute-start | bytes 1585160 | tf_op jit(solution)/shard_map/ppermute | solution.py:235
  24.9 13.7 %collective-permute-start.7 = (bf16[2048,128]{1,0:T(8,128)(2,1)S(1)}, bf16[2048,128]{1,0:T(8,128)(2,1)S(1)}, u32[]{:S(2)}, u32[]{:S(2)}) collective-permute-start(bf16[2048,128]{1,0:T(8,128)(2,1)S(1)} %bitcast.6), channel_id=1, source_target_pairs={{0,8},{8,0},{16,24},{24,16},{1,9},{9,1},{17,25},{25,17},{2,10},{10... | collective-permute-start | bytes 1572872 | tf_op jit(solution)/shard_map/ppermute | solution.py:235
  25.4 13.7 %collective-permute-start = (bf16[2064,128]{1,0:T(8,128)(2,1)S(1)}, bf16[2064,128]{1,0:T(8,128)(2,1)S(1)}, u32[]{:S(2)}, u32[]{:S(2)}) collective-permute-start(bf16[2064,128]{1,0:T(8,128)(2,1)S(1)} %pack_d.1.refs_0_), channel_id=1, source_target_pairs={{0,1},{1,0},{2,3},{3,2},{4,5},{5,4},{6,7},{7,6},{8,9},{9,8},{10,11... | collective-permute-start | bytes 1585160 | tf_op jit(solution)/shard_map/ppermute | solution.py:243
  25.4 13.7 %collective-permute-start.2 = (bf16[2064,128]{1,0:T(8,128)(2,1)S(1)}, bf16[2064,128]{1,0:T(8,128)(2,1)S(1)}, u32[]{:S(2)}, u32[]{:S(2)}) collective-permute-start(bf16[2064,128]{1,0:T(8,128)(2,1)S(1)} %collective-permute-done.1.refs_2_), channel_id=1, source_target_pairs={{0,1},{1,0},{2,3},{3,2},{4,5},{5,4},{6,7},{7,6},{8,9},{9,8},{10,11... | collective-permute-start | bytes 1585160 | tf_op jit(solution)/shard_map/ppermute | solution.py:243
  34.3 4.8 %collective-permute-start.4 = (bf16[2064,128]{1,0:T(8,128)(2,1)S(1)}, bf16[2064,128]{1,0:T(8,128)(2,1)S(1)}, u32[]{:S(2)}, u32[]{:S(2)}) collective-permute-start(bf16[2064,128]{1,0:T(8,128)(2,1)S(1)} %collective-permute-done.3.refs_4_), channel_id=1, source_target_pairs={{0,1},{1,0},{2,3},{3,2},{4,5},{5,4},{6,7},{7,6},{8,9},{9,8},{10,11... | collective-permute-start | bytes 1585160 | tf_op jit(solution)/shard_map/ppermute | solution.py:243
  38.6 12.8 %collective-permute-start.9 = (bf16[2064,128]{1,0:T(8,128)(2,1)S(1)}, bf16[2064,128]{1,0:T(8,128)(2,1)S(1)}, u32[]{:S(2)}, u32[]{:S(2)}) collective-permute-start(bf16[2064,128]{1,0:T(8,128)(2,1)S(1)} %collective-permute-done.3.refs_4_), channel_id=1, source_target_pairs={{0,2},{2,4},{4,6},{6,0},{1,7},{3,1},{5,3},{7,5},{8,10},{10,12},{12... | collective-permute-start | bytes 1585160 | tf_op jit(solution)/shard_map/ppermute | solution.py:240
  38.6 12.8 %collective-permute-start.10 = (bf16[2048,128]{1,0:T(8,128)(2,1)S(1)}, bf16[2048,128]{1,0:T(8,128)(2,1)S(1)}, u32[]{:S(2)}, u32[]{:S(2)}) collective-permute-start(bf16[2048,128]{1,0:T(8,128)(2,1)S(1)} %bitcast.7), channel_id=1, source_target_pairs={{0,16},{8,24},{16,0},{24,8},{1,17},{9,25},{17,1},{25,9},{2,18},{10... | collective-permute-start | bytes 1572872 | tf_op jit(solution)/shard_map/ppermute | solution.py:235
  51.4 1.9 %collective-permute-start.11 = (bf16[2064,128]{1,0:T(8,128)(2,1)S(1)}, bf16[2064,128]{1,0:T(8,128)(2,1)S(1)}, u32[]{:S(2)}, u32[]{:S(2)}) collective-permute-start(bf16[2064,128]{1,0:T(8,128)(2,1)S(1)} %collective-permute-done.9.last_0), channel_id=1, source_target_pairs={{0,1},{1,0},{2,3},{3,2},{4,5},{5,4},{6,7},{7,6},{8,9},{9,8},{10,11... | collective-permute-start | bytes 1585160 | tf_op jit(solution)/shard_map/ppermute | solution.py:243
  51.5 23.4 %collective-permute-start.12 = (bf16[2048,128]{1,0:T(8,128)(2,1)S(1)}, bf16[2048,128]{1,0:T(8,128)(2,1)S(1)}, u32[]{:S(2)}, u32[]{:S(2)}) collective-permute-start(bf16[2048,128]{1,0:T(8,128)(2,1)S(1)} %collective-permute-done.10.refs_6_), channel_id=1, source_target_pairs={{0,8},{8,0},{16,24},{24,16},{1,9},{9,1},{17,25},{25,17},{2,10},{10... | collective-permute-start | bytes 1572872 | tf_op jit(solution)/shard_map/ppermute | solution.py:235
  58.1 13.8 %collective-permute-start.14 = (bf16[4,2,128,128]{3,2,1,0:T(8,128)(2,1)S(1)}, bf16[4,2,128,128]{3,2,1,0:T(8,128)(2,1)S(1)}, u32[]{:S(2)}, u32[]{:S(2)}) collective-permute-start(bf16[4,2,128,128]{3,2,1,0:T(8,128)(2,1)S(1)} %get-tuple-element.61), channel_id=1, source_target_pairs={{0,8},{8,0},{16,24},{24,16},{1,9},{9,1},{17,25},{25,17},{2,10},{10... | collective-permute-start | bytes 786440 | tf_op jit(solution)/shard_map/ppermute | solution.py:235
  59.5 12.3 %collective-permute-start.15 = (bf16[4,2,128,128]{3,2,1,0:T(8,128)(2,1)S(1)}, bf16[4,2,128,128]{3,2,1,0:T(8,128)(2,1)S(1)}, u32[]{:S(2)}, u32[]{:S(2)}) collective-permute-start(bf16[4,2,128,128]{3,2,1,0:T(8,128)(2,1)S(1)} %get-tuple-element.63), channel_id=1, source_target_pairs={{0,16},{8,24},{16,0},{24,8},{1,17},{9,25},{17,1},{25,9},{2,18},{10... | collective-permute-start | bytes 786440 | tf_op jit(solution)/shard_map/ppermute | solution.py:235
  61.1 5.0 %copy-start.4 = (s32[8,4]{0,1:T(4,128)S(1)}, s32[8,4]{0,1:T(4,128)}, u32[]{:S(2)}) copy-start(s32[8,4]{0,1:T(4,128)} %param.9) | copy-start | bytes 388
  64.9 17.5 %collective-permute-start.13 = (bf16[4,2,128,128]{3,2,1,0:T(8,128)(2,1)S(1)}, bf16[4,2,128,128]{3,2,1,0:T(8,128)(2,1)S(1)}, u32[]{:S(2)}, u32[]{:S(2)}) collective-permute-start(bf16[4,2,128,128]{3,2,1,0:T(8,128)(2,1)S(1)} %get-tuple-element.59), channel_id=1, source_target_pairs={{0,8},{8,0},{16,24},{24,16},{1,9},{9,1},{17,25},{25,17},{2,10},{10... | collective-permute-start | bytes 786440 | tf_op jit(solution)/shard_map/ppermute | solution.py:235
  65.5 16.9 %collective-permute-start.18 = (bf16[4,2,128,128]{3,2,1,0:T(8,128)(2,1)S(1)}, bf16[4,2,128,128]{3,2,1,0:T(8,128)(2,1)S(1)}, u32[]{:S(2)}, u32[]{:S(2)}) collective-permute-start(bf16[4,2,128,128]{3,2,1,0:T(8,128)(2,1)S(1)} %get-tuple-element.66), channel_id=1, source_target_pairs={{0,16},{8,24},{16,0},{24,8},{1,17},{9,25},{17,1},{25,9},{2,18},{10... | collective-permute-start | bytes 786440 | tf_op jit(solution)/shard_map/ppermute | solution.py:235
  72.0 10.6 %collective-permute-start.16 = (bf16[4,2,128,128]{3,2,1,0:T(8,128)(2,1)S(1)}, bf16[4,2,128,128]{3,2,1,0:T(8,128)(2,1)S(1)}, u32[]{:S(2)}, u32[]{:S(2)}) collective-permute-start(bf16[4,2,128,128]{3,2,1,0:T(8,128)(2,1)S(1)} %get-tuple-element.64), channel_id=1, source_target_pairs={{0,8},{8,0},{16,24},{24,16},{1,9},{9,1},{17,25},{25,17},{2,10},{10... | collective-permute-start | bytes 786440 | tf_op jit(solution)/shard_map/ppermute | solution.py:235
  73.4 9.3 %collective-permute-start.17 = (bf16[4,2,128,128]{3,2,1,0:T(8,128)(2,1)S(1)}, bf16[4,2,128,128]{3,2,1,0:T(8,128)(2,1)S(1)}, u32[]{:S(2)}, u32[]{:S(2)}) collective-permute-start(bf16[4,2,128,128]{3,2,1,0:T(8,128)(2,1)S(1)} %get-tuple-element.65), channel_id=1, source_target_pairs={{0,16},{8,24},{16,0},{24,8},{1,17},{9,25},{17,1},{25,9},{2,18},{10... | collective-permute-start | bytes 786440 | tf_op jit(solution)/shard_map/ppermute | solution.py:235

commit v5 on v4

--- a/solution.py
+++ b/solution.py
@@ -21,21 +21,21 @@
         self.nb = self.rows * n_row
         self.bc = self.nb // n_col
         self.tall, self.wide = self.rows * self.bs, self.bc * self.bs
-        self.n_first = n_col - 2
-
-
-def call(kernel, z, ins, outs, scratch, in_specs, out_specs, flops, name):
+        self.n_first, self.n_last = n_col - 3, 3
+
+
+def call(kernel, ins, outs, scratch, in_specs, out_specs, flops, name):
     held = [x for x in scratch if getattr(x, "memory_space", None) == pltpu.VMEM]
     held += [x for x, spec in zip(list(ins) + outs, in_specs + out_specs) if spec.memory_space == pltpu.VMEM]
     size = sum(math.prod(x.shape) * jnp.dtype(x.dtype).itemsize for x in held)
     return pl.pallas_call(
-        functools.partial(kernel, z),
+        kernel,
         out_shape=outs,
         in_specs=in_specs,
         out_specs=out_specs,
         scratch_shapes=scratch,
         compiler_params=pltpu.CompilerParams(vmem_limit_bytes=size + VMEM_ROOM),
-        cost_estimate=pl.CostEstimate(flops=flops, bytes_accessed=16 << 20, transcendentals=0),
+        cost_estimate=pl.CostEstimate(flops=flops, bytes_accessed=1024, transcendentals=0),
         name=name,
     )(*ins)
 
@@ -97,29 +97,41 @@
             dense[rows, at] = blocks[block_rows(z, i, s, z.ka), :]
 
 
-def fill_right(z, first_slot, slots, idx, payloads, dense):
+def fill_right(z, first_slot, slots, idx, payloads, flips, place, dense):
     dense[...] = jnp.zeros_like(dense)
     me = lax.axis_index("col")
-    for p, payload in enumerate(payloads):
+    for flip, payload in zip(flips, payloads):
         for i in range(z.rows):
-            k = (lax.axis_index("row") ^ p) * z.rows + i
-            n = piece_of(z, k // z.bc)
-            at = pl.ds(pl.multiple_of((n * z.bc + lax.rem(k, z.bc)) * z.bs, z.bs), z.bs)
+            at = pl.ds(pl.multiple_of(place(flip, i) * z.bs, z.bs), z.bs)
             for s in range(slots):
-                j = idx[p, first_slot + s, i] - me * z.bc
-                dense[at, lanes(z, j)] = payload[block_rows(z, i, s, slots), :]
+                j = idx[flip, first_slot + s, i] - me * z.bc
+                row, part = (i * slots + s) * z.bs, 0
+                while row >= payload[part].shape[0]:
+                    row -= payload[part].shape[0]
+                    part += 1
+                dense[at, lanes(z, j)] = payload[part][row:row + z.bs, :]
+
+
+def by_piece(z, flip, i):
+    k = (lax.axis_index("row") ^ flip) * z.rows + i
+    return piece_of(z, k // z.bc) * z.bc + lax.rem(k, z.bc)
+
+
+def group(refs, counts):
+    refs = iter(refs)
+    return [[next(refs) for _ in range(count)] for count in counts]
 
 
 def halves(n):
     return [slice(0, n // 2), slice(n // 2, n)]
 
 
-def first_kernel(z, *refs):
-    left_in, right_in = refs[:z.n_first], refs[z.n_first:z.n_first + z.n_row]
-    total, panel, right_last, table, right, ints, idx, sem = refs[z.n_first + z.n_row:]
-    read_tails(right_in + left_in, ints, idx, sem)
+def first_kernel(z, counts, *refs):
+    left_in, right_in = refs[:z.n_first], group(refs[z.n_first:], counts)
+    total, panel, right_last, table, right, ints, idx, sem = refs[z.n_first + sum(counts):]
+    read_tails([x[-1] for x in right_in] + list(left_in), ints, idx, sem)
     table[...] = ints[0:z.n_row]
-    fill_right(z, z.ka, z.kh, idx, right_in, right)
+    fill_right(z, z.ka, z.kh, idx, right_in, range(z.n_row), functools.partial(by_piece, z), right)
     for n in range(z.n_first):
         fill_left(z, idx, z.n_row + n, piece_col(z, n), left_in[n], panel, n * z.wide)
     deep = z.n_first * z.wide
@@ -128,10 +140,10 @@
     right_last[...] = right[deep:, :]
 
 
-def last_kernel(z, table, last_0, last_1, right, total_in, panel, *refs):
-    total, turned, panel_last, *part, columns, ints, idx, sem = refs
-    read_tails([last_0, last_1], ints, idx, sem)
-    for n, payload in enumerate((last_0, last_1)):
+def last_kernel(z, table, right, total_in, panel, *refs):
+    payloads, (total, turned, panel_last, *part, columns, ints, idx, sem) = refs[:z.n_last], refs[z.n_last:]
+    read_tails(payloads, ints, idx, sem)
+    for n, payload in enumerate(payloads):
         fill_left(z, idx, n, piece_col(z, z.n_first + n), payload, panel_last, n * z.wide)
     for rows in halves(z.tall):
         total[rows, :] = total_in[rows, :] + jnp.dot(panel_last[rows, :], right[...], preferred_element_type=F32)
@@ -186,11 +198,10 @@
             base[i, s] = 3.0 * direct - 2.0 * own[i, s].T
 
 
-def square_kernel(z, *refs):
-    table, filt, panel, panel_last = refs[:4]
-    squared, right, total = refs[4 + z.n_row:]
-    me = lax.axis_index("col")
-    fill_right(z, 0, z.ka, table, refs[4:4 + z.n_row], right)
+def square_kernel(z, counts, table, filt, panel, panel_last, *refs):
+    squared, right, total = refs[sum(counts):]
+    me = lax.axis_index("col")
+    fill_right(z, 0, z.ka, table, group(refs, counts), range(z.n_row), functools.partial(by_piece, z), right)
     deep = z.n_first * z.wide
     for rows in halves(z.tall):
         total[rows, :] = jnp.dot(panel[rows, :], right[0:deep, :], preferred_element_type=F32)
@@ -248,48 +259,48 @@
         rows = vals.shape[0]
         outs = [shape((rows + TAIL, z.bs), BF16)]
         scratch = [pltpu.VMEM((TAIL, z.bs), F32)]
-        return call(pack_kernel, z, [vals, *cols], outs, scratch, [vmem] * (1 + len(cols)), [vmem], 0, name)[0]
+        return call(functools.partial(pack_kernel, z), [vals, *cols], outs, scratch, [vmem] * (1 + len(cols)), [vmem], 0, name)[0]
 
     d_pay = pack(flat, [density_cols.T], "pack_d")
     h_pay = pack(hamilton.reshape(h_rows, z.bs), [density_cols.T, hamilton_cols.T], "pack_h")
 
-    def high(flip):
-        return 1 << (flip.bit_length() - 1)
-
-    def low(flip):
-        return flip & -flip
-
-    d_right, h_right = {0: flat}, {0: h_pay}
-    for flip in range(1, n_row):
-        if flip.bit_count() == 1:
-            h_right[flip] = over_row(h_pay, flip)
-    d_right, h_right = lax.optimization_barrier((d_right, h_right))
-    d_right[1] = over_row(d_right[0], 1)
-    for flip in sorted(range(1, n_row), key=int.bit_count):
-        if flip not in h_right:
-            h_right[flip] = over_row(h_right[flip - high(flip)], high(flip))
-    d_right, h_right = lax.optimization_barrier((d_right, h_right))
-    for flip in range(2, n_row):
-        if flip.bit_count() == 1:
-            d_right[flip] = over_row(d_right[0], flip)
-    h_right = [h_right[flip] for flip in range(n_row)]
-
-    left, piece = [], d_pay
-    for step in range(z.n_chip):
-        if step:
-            piece = next_chip(piece)
+    flips = sorted(range(1, n_row), key=int.bit_count)
+    single = [flip for flip in flips if flip.bit_count() == 1]
+    h_half, d_half = h_rows // 2, d_rows // 2
+
+    def forward(blocks):
+        for flip in flips:
+            if flip not in blocks:
+                blocks[flip] = [over_row(blocks[flip & (flip - 1)][0], flip & -flip)]
+
+    left, piece = [d_pay, other_core(d_pay)], d_pay
+    h_right, d_0 = {0: [h_pay]}, d_pay
+    for step in range(1, z.n_chip):
+        piece = next_chip(piece)
+        if step == 1:
+            for flip in single:
+                h_right[flip] = [over_row(h_pay, flip)]
+        if step == 2:
+            if n_row == 4:
+                h_right[3] = [over_row(h_right[1][0][:h_half], 2), over_row(h_right[2][0][h_half:], 1)]
+            forward(h_right)
+            piece, h_right, d_0 = lax.optimization_barrier((piece, h_right, d_0))
+            d_right = {0: [d_0]}
+            for flip in single:
+                d_right[flip] = [over_row(d_0, flip)]
         left.append(piece)
         if step < z.n_chip - 1:
             left.append(other_core(piece))
+    h_right = [h_right[flip] for flip in range(n_row)]
 
     n_pay = z.n_first + n_row
     total, panel, right_last, table = call(
-        first_kernel, z,
-        [*left[:z.n_first], *h_right],
+        functools.partial(first_kernel, z, [len(x) for x in h_right]),
+        [*left[:z.n_first], *sum(h_right, [])],
         [
             shape((z.tall, z.wide), F32),
             shape((z.tall, z.n_first * z.wide), BF16),
-            shape((2 * z.wide, z.wide), BF16),
+            shape((z.n_last * z.wide, z.wide), BF16),
             shape((n_row, 8, z.bs), jnp.int32),
         ],
         [
@@ -298,33 +309,33 @@
             pltpu.SMEM((n_pay, 8, z.bs), jnp.int32),
             dma,
         ],
-        [vmem] * n_pay, [vmem] * 4, panel_flops, "first",
+        [vmem] * (z.n_first + sum(map(len, h_right))), [vmem] * 4, 0, "first",
     )
     last, total, d_right = lax.optimization_barrier((left[-1], total, d_right))
-    for flip in range(1, n_row):
-        if flip not in d_right:
-            d_right[flip] = over_row(d_right[flip - low(flip)], low(flip))
+    if n_row == 4:
+        d_right[3] = [over_row(d_right[1][0][:d_half], 2), over_row(d_right[2][0][d_half:d_rows], 1)]
+    forward(d_right)
     d_right = [d_right[flip] for flip in range(n_row)]
-
     part = shape((z.rows, z.ka) + block, BF16)
     columns = pltpu.VMEM((2, z.wide, z.wide), F32)
     cuts = 2 if n_row == 4 and z.rows % 2 == 0 else 1
     cut_part = shape((z.rows // cuts, z.ka) + block, BF16)
     total, turned, panel_last, *far = call(
-        last_kernel, z,
-        [table, last, other_core(last), right_last, total, panel],
-        [shape((z.tall, z.wide), F32), shape((z.wide, z.tall), BF16), shape((z.tall, 2 * z.wide), BF16)]
+        functools.partial(last_kernel, z),
+        [table, right_last, total, panel, *left[z.n_first:-1], last, other_core(last)],
+        [shape((z.tall, z.wide), F32), shape((z.wide, z.tall), BF16), shape((z.tall, z.n_last * z.wide), BF16)]
         + [cut_part] * cuts,
         [
             columns,
-            pltpu.VMEM((2, 8, z.bs), jnp.int32),
-            pltpu.SMEM((2, 8, z.bs), jnp.int32),
+            pltpu.VMEM((z.n_last, 8, z.bs), jnp.int32),
+            pltpu.SMEM((z.n_last, 8, z.bs), jnp.int32),
             dma,
         ],
-        [smem] + [vmem] * 5, [vmem] * (3 + cuts), panel_flops // 4 + part_flops, "last",
-    )
+        [smem] + [vmem] * (3 + z.n_last), [vmem] * (3 + cuts), panel_flops // 4 + part_flops, "last",
+    )
+    far, d_right = lax.optimization_barrier((far, d_right))
     near = call(
-        parts_kernel, z, [table, turned, panel, panel_last], [cut_part] * (cuts * (n_row - 2)), [columns],
+        functools.partial(parts_kernel, z), [table, turned, panel, panel_last], [cut_part] * (cuts * (n_row - 2)), [columns],
         [smem] + [vmem] * 3, [vmem] * (cuts * (n_row - 2)), part_flops * (n_row - 2), "parts",
     )
     if cuts == 2:
@@ -333,7 +344,7 @@
     else:
         received = [over_row(term, n + 1) for n, term in enumerate([*near, *far])]
     mixed, base = call(
-        base_kernel, z,
+        functools.partial(base_kernel, z),
         [table, filter_cols.T, total, turned, panel, panel_last],
         [shape((z.rows, z.kf) + block, BF16), shape((z.rows, z.ka) + block, F32)],
         [columns, pltpu.VMEM((z.rows, z.ka) + block, F32)],
@@ -341,19 +352,19 @@
     )
     if cuts == 2:
         y_0, x_1 = call(
-            add_kernel, z, [near[2], far[0], near[1], far[1]], [cut_part] * 2, [],
+            functools.partial(add_kernel, z), [near[2], far[0], near[1], far[1]], [cut_part] * 2, [],
             [vmem] * 4, [vmem] * 2, 0, "add",
         )
         received = [x_0, over_row(x_1, 1), over_row(y_0, 2), y_1]
     squared, = call(
-        square_kernel, z,
-        [table, filter_cols.T, panel, panel_last, *d_right],
+        functools.partial(square_kernel, z, [len(x) for x in d_right]),
+        [table, filter_cols.T, panel, panel_last, *sum(d_right, [])],
         [shape((z.rows, z.kf) + block, BF16)],
         [pltpu.VMEM((z.nb * z.bs, z.wide), BF16), pltpu.VMEM((z.tall, z.wide), F32)],
-        [smem] * 2 + [vmem] * (n_row + 2), [vmem], panel_flops, "squared",
+        [smem] * 2 + [vmem] * (2 + sum(map(len, d_right))), [vmem], panel_flops, "squared",
     )
     gradient, = call(
-        gradient_kernel, z, [base, *received], [part], [],
+        functools.partial(gradient_kernel, z), [base, *received], [part], [],
         [vmem] * (1 + len(received)), [vmem], 0, "gradient",
     )
     return squared, mixed, gradient

time: 84 us -> 83.6 us (level)
  waiting for transfers between devices: 33.8 us -> 27.3 us
  starting transfers between devices: 17.8 us -> 23.4 us
    ppermute x12 -> x14, starting transfers between devices: 14.1 us -> 18.4 us  [over_row(): return lax.ppermute(x, 'row', [(r, r ^ flip) for r in range(n_row)])]
    ppermute x3, waiting for transfers between devices: 17.7 us -> 13.9 us  [next_chip(): return lax.ppermute(x, 'col', pairs)]
    ppermute x12 -> x14, waiting for transfers between devices: 15.6 us -> 13.3 us  [over_row(): return lax.ppermute(x, 'row', [(r, r ^ flip) for r in range(n_row)])]
    ppermute x4, starting transfers between devices: 0.62 us -> 1.88 us  [other_core(): return lax.ppermute(x, 'col', [(c, c ^ 1) for c in range(n_col)])]
  transfers between devices with their start and end apart: 19 -> 21, of which waited for: 9 -> 10; matrix products, arithmetic and copies ran while one was open for 0% -> 0% of each run, Pallas kernels for 32% -> 32%
where the time goes in v5:
time: 83.6 us; the launch traced here: 83.3 us
  Pallas kernels  27.7 us (33%)
  waiting for transfers between devices  27.3 us (33%)
  starting transfers between devices  23.4 us (28%)
  local copies, waits for them, and re-layouts  4.19 us (5%)
    pallas_call x9, Pallas kernels, call(): pl.pallas_call(kernel, out_shape=outs, in_specs=in_specs, out_specs=out_s...  27.7 us
    ppermute x14, starting transfers between devices, over_row(): return lax.ppermute(x, 'row', [(r, r ^ flip) for r in range(n_row)])  18.4 us
    ppermute x3, waiting for transfers between devices, next_chip(): return lax.ppermute(x, 'col', pairs)  13.9 us
    ppermute x14, waiting for transfers between devices, over_row(): return lax.ppermute(x, 'row', [(r, r ^ flip) for r in range(n_row)])  13.3 us
    unnamed x12, local copies, waits for them, and re-layouts  4.11 us
    ppermute x3, starting transfers between devices, next_chip(): return lax.ppermute(x, 'col', pairs)  3.12 us
    ppermute x4, starting transfers between devices, other_core(): return lax.ppermute(x, 'col', [(c, c ^ 1) for c in range(n_col)])  1.88 us
  transfers between devices with their start and end apart: 21, of which 10 were waited for; matrix products, arithmetic and copies ran while one was open for 0% of the time, Pallas kernels for 32%

profile of v5, /device:TPU:0, one launch (start us, length us, event | category | flops | bytes accessed | tf_op | source)
XLA Modules:
  0.0 83.3 jit_solution(2614179581103743305)
XLA Ops:
  0.6 1.0 %copy-done = bf16[8,2,128,128]{3,2,1,0:T(8,128)(2,1)S(1)} copy-done((bf16[8,2,128,128]{3,2,1,0:T(8,128)(2,1)S(1)}, bf16[8,2,128,128]{3,2,1,0:T(8,128)(2,1)}, u32[]{:S(2)}) %copy-start) | copy-done | bytes 524312
  1.7 0.7 copy-done.2
  2.4 3.1 %collective-permute-start.1 = (bf16[2064,128]{1,0:T(8,128)(2,1)S(1)}, bf16[2064,128]{1,0:T(8,128)(2,1)S(1)}, u32[]{:S(2)}, u32[]{:S(2)}) collective-permute-start(bf16[2064,128]{1,0:T(8,128)(2,1)S(1)} %pack_d.1.refs_0_), channel_id=1, source_target_pairs={{0,2},{2,4},{4,6},{6,0},{1,7},{3,1},{5,3},{7,5},{8,10},{10,12},{12... | collective-permute-start | bytes 1585160 | tf_op jit(solution)/shard_map/ppermute | solution.py:251
  5.5 1.0 %copy-done.1 = bf16[8,2,128,128]{3,2,1,0:T(8,128)(2,1)S(1)} copy-done((bf16[8,2,128,128]{3,2,1,0:T(8,128)(2,1)S(1)}, bf16[8,2,128,128]{3,2,1,0:T(8,128)(2,1)}, u32[]{:S(2)}) %copy-start.1) | copy-done | bytes 524312
  6.5 0.7 copy-done.3
  7.2 0.7 copy-done.5
  7.9 1.6 %collective-permute-start.5 = (bf16[2064,128]{1,0:T(8,128)(2,1)S(1)}, bf16[2064,128]{1,0:T(8,128)(2,1)S(1)}, u32[]{:S(2)}, u32[]{:S(2)}) collective-permute-start(bf16[2064,128]{1,0:T(8,128)(2,1)S(1)} %pack_h.1.refs_5_), channel_id=1, source_target_pairs={{0,16},{8,24},{16,0},{24,8},{1,17},{9,25},{17,1},{25,9},{2,18},{10... | collective-permute-start | bytes 1585160 | tf_op jit(solution)/shard_map/ppermute | solution.py:246
  9.5 1.5 %collective-permute-start.4 = (bf16[2064,128]{1,0:T(8,128)(2,1)S(1)}, bf16[2064,128]{1,0:T(8,128)(2,1)S(1)}, u32[]{:S(2)}, u32[]{:S(2)}) collective-permute-start(bf16[2064,128]{1,0:T(8,128)(2,1)S(1)} %pack_h.1.refs_5_), channel_id=1, source_target_pairs={{0,8},{8,0},{16,24},{24,16},{1,9},{9,1},{17,25},{25,17},{2,10},{10... | collective-permute-start | bytes 1585160 | tf_op jit(solution)/shard_map/ppermute | solution.py:246
  11.0 8.7 %collective-permute-done.1.refs_2_ = bf16[2064,128]{1,0:T(8,128)(2,1)S(1)} collective-permute-done((bf16[2064,128]{1,0:T(8,128)(2,1)S(1)}, bf16[2064,128]{1,0:T(8,128)(2,1)S(1)}, u32[]{:S(2)}, u32[]{:S(2)}) %collective-permute-start.1) | collective-permute-done | bytes 528416 | tf_op jit(solution)/shard_map/ppermute | solution.py:251
  19.7 2.6 %collective-permute-done.5.refs_7_ = bf16[2064,128]{1,0:T(8,128)(2,1)S(1)} collective-permute-done((bf16[2064,128]{1,0:T(8,128)(2,1)S(1)}, bf16[2064,128]{1,0:T(8,128)(2,1)S(1)}, u32[]{:S(2)}, u32[]{:S(2)}) %collective-permute-start.5) | collective-permute-done | bytes 528416 | tf_op jit(solution)/shard_map/ppermute | solution.py:246
  22.3 1.6 %collective-permute-start.7 = (bf16[1040,128]{1,0:T(8,128)(2,1)S(1)}, bf16[1040,128]{1,0:T(8,128)(2,1)S(1)}, u32[]{:S(2)}, u32[]{:S(2)}) collective-permute-start(bf16[1040,128]{1,0:T(8,128)(2,1)S(1)} %slice.17), channel_id=1, source_target_pairs={{0,8},{8,0},{16,24},{24,16},{1,9},{9,1},{17,25},{25,17},{2,10},{10... | collective-permute-start | bytes 798728 | tf_op jit(solution)/shard_map/ppermute | solution.py:246
  24.1 1.4 %collective-permute-start.6 = (bf16[1024,128]{1,0:T(8,128)(2,1)S(1)}, bf16[1024,128]{1,0:T(8,128)(2,1)S(1)}, u32[]{:S(2)}, u32[]{:S(2)}) collective-permute-start(bf16[1024,128]{1,0:T(8,128)(2,1)S(1)} %slice.16), channel_id=1, source_target_pairs={{0,16},{8,24},{16,0},{24,8},{1,17},{9,25},{17,1},{25,9},{2,18},{10... | collective-permute-start | bytes 786440 | tf_op jit(solution)/shard_map/ppermute | solution.py:246
  26.0 6.6 %collective-permute-done.6.refs_8_ = bf16[1024,128]{1,0:T(8,128)(2,1)S(1)} collective-permute-done((bf16[1024,128]{1,0:T(8,128)(2,1)S(1)}, bf16[1024,128]{1,0:T(8,128)(2,1)S(1)}, u32[]{:S(2)}, u32[]{:S(2)}) %collective-permute-start.6) | collective-permute-done | bytes 262176 | tf_op jit(solution)/shard_map/ppermute | solution.py:246
  32.6 1.7 %collective-permute-done.3.refs_4_ = bf16[2064,128]{1,0:T(8,128)(2,1)S(1)} collective-permute-done((bf16[2064,128]{1,0:T(8,128)(2,1)S(1)}, bf16[2064,128]{1,0:T(8,128)(2,1)S(1)}, u32[]{:S(2)}, u32[]{:S(2)}) %collective-permute-start.3) | collective-permute-done | bytes 528416 | tf_op jit(solution)/shard_map/ppermute | solution.py:251
  34.2 1.6 %collective-permute-start.10 = (bf16[2064,128]{1,0:T(8,128)(2,1)S(1)}, bf16[2064,128]{1,0:T(8,128)(2,1)S(1)}, u32[]{:S(2)}, u32[]{:S(2)}) collective-permute-start(bf16[2064,128]{1,0:T(8,128)(2,1)S(1)} %pack_d.1.refs_0_), channel_id=1, source_target_pairs={{0,16},{8,24},{16,0},{24,8},{1,17},{9,25},{17,1},{25,9},{2,18},{10... | collective-permute-start | bytes 1585160 | tf_op jit(solution)/shard_map/ppermute | solution.py:246
  35.9 1.5 %collective-permute-start.9 = (bf16[2064,128]{1,0:T(8,128)(2,1)S(1)}, bf16[2064,128]{1,0:T(8,128)(2,1)S(1)}, u32[]{:S(2)}, u32[]{:S(2)}) collective-permute-start(bf16[2064,128]{1,0:T(8,128)(2,1)S(1)} %pack_d.1.refs_0_), channel_id=1, source_target_pairs={{0,8},{8,0},{16,24},{24,16},{1,9},{9,1},{17,25},{25,17},{2,10},{10... | collective-permute-start | bytes 1585160 | tf_op jit(solution)/shard_map/ppermute | solution.py:246
  37.4 1.2 %collective-permute-start.11 = (bf16[2064,128]{1,0:T(8,128)(2,1)S(1)}, bf16[2064,128]{1,0:T(8,128)(2,1)S(1)}, u32[]{:S(2)}, u32[]{:S(2)}) collective-permute-start(bf16[2064,128]{1,0:T(8,128)(2,1)S(1)} %collective-permute-done.3.refs_4_), channel_id=1, source_target_pairs={{0,1},{1,0},{2,3},{3,2},{4,5},{5,4},{6,7},{7,6},{8,9},{9,8},{10,11... | collective-permute-start | bytes 1585160 | tf_op jit(solution)/shard_map/ppermute | solution.py:254
  38.5 5.7 %first.1 = (f32[1024,512]{1,0:T(8,128)S(1)}, bf16[1024,2560]{1,0:T(8,128)(2,1)S(1)}, bf16[1536,512]{1,0:T(8,128)(2,1)S(1)}, s32[4,8,128]{2,1,0:T(8,128)S(1)}) custom-call(bf16[2064,128]{1,0:T(8,128)(2,1)S(1)} %pack_d.1.refs_0_, bf16[2064,128]{1,0:T(8,128)(2,1)S(1)} %collective-permute-done.refs_1_, bf16[2064,128]{1,0:T(8,128)(2,1)S(1)} %collective-permute-done.1.refs_2_, ...), custom_call_target="tpu_custom_call" | custom-call | bytes 1024 | tf_op jit(solution)/shard_map/first/pallas_call | solution.py:31
  44.2 2.0 %collective-permute-done.10.refs_2_ = bf16[2064,128]{1,0:T(8,128)(2,1)S(1)} collective-permute-done((bf16[2064,128]{1,0:T(8,128)(2,1)S(1)}, bf16[2064,128]{1,0:T(8,128)(2,1)S(1)}, u32[]{:S(2)}, u32[]{:S(2)}) %collective-permute-start.10) | collective-permute-done | bytes 528416 | tf_op jit(solution)/shard_map/ppermute | solution.py:246
  46.2 3.6 %collective-permute-done.8.refs_1_ = bf16[2064,128]{1,0:T(8,128)(2,1)S(1)} collective-permute-done((bf16[2064,128]{1,0:T(8,128)(2,1)S(1)}, bf16[2064,128]{1,0:T(8,128)(2,1)S(1)}, u32[]{:S(2)}, u32[]{:S(2)}) %collective-permute-start.8) | collective-permute-done | bytes 528416 | tf_op jit(solution)/shard_map/ppermute | solution.py:251
  49.8 0.6 collective-permute-done.9.refs_1_
  51.2 1.6 %collective-permute-start.14 = (bf16[1024,128]{1,0:T(8,128)(2,1)S(1)}, bf16[1024,128]{1,0:T(8,128)(2,1)S(1)}, u32[]{:S(2)}, u32[]{:S(2)}) collective-permute-start(bf16[1024,128]{1,0:T(8,128)(2,1)S(1)} %slice.15), channel_id=1, source_target_pairs={{0,8},{8,0},{16,24},{24,16},{1,9},{9,1},{17,25},{25,17},{2,10},{10... | collective-permute-start | bytes 786440 | tf_op jit(solution)/shard_map/ppermute | solution.py:246
  52.7 5.4 %last.1 = (f32[1024,512]{1,0:T(8,128)S(1)}, bf16[512,1024]{1,0:T(8,128)(2,1)S(1)}, bf16[1024,1536]{1,0:T(8,128)(2,1)S(1)}, bf16[4,2,128,128]{3,2,1,0:T(8,128)(2,1)S(1)}, bf16[4,2,128,128]{3,2,1,0:T(8,128)(2,1)S(1)}) custom-call(s32[4,8,128]{2,1,0:T(8,128)S(1)} %get-tuple-element.45.table, bf16[1536,512]{1,0:T(8,128)(2,1)S(1)} %get-tuple-element.47.right, ...), custom_call_target="tpu_custom_call" | custom-call | flops 2147483648 | bytes 1024 | tf_op jit(solution)/shard_map/last/pallas_call | solution.py:31
  58.1 1.0 %collective-permute-done.13.refs_3_ = bf16[1024,128]{1,0:T(8,128)(2,1)S(1)} collective-permute-done((bf16[1024,128]{1,0:T(8,128)(2,1)S(1)}, bf16[1024,128]{1,0:T(8,128)(2,1)S(1)}, u32[]{:S(2)}, u32[]{:S(2)}) %collective-permute-start.13) | collective-permute-done | bytes 262176 | tf_op jit(solution)/shard_map/ppermute | solution.py:246
  59.5 1.5 %collective-permute-start.16 = (bf16[4,2,128,128]{3,2,1,0:T(8,128)(2,1)S(1)}, bf16[4,2,128,128]{3,2,1,0:T(8,128)(2,1)S(1)}, u32[]{:S(2)}, u32[]{:S(2)}) collective-permute-start(bf16[4,2,128,128]{3,2,1,0:T(8,128)(2,1)S(1)} %get-tuple-element.69), channel_id=1, source_target_pairs={{0,8},{8,0},{16,24},{24,16},{1,9},{9,1},{17,25},{25,17},{2,10},{10... | collective-permute-start | bytes 786440 | tf_op jit(solution)/shard_map/ppermute | solution.py:246
  61.0 1.5 %collective-permute-start.17 = (bf16[4,2,128,128]{3,2,1,0:T(8,128)(2,1)S(1)}, bf16[4,2,128,128]{3,2,1,0:T(8,128)(2,1)S(1)}, u32[]{:S(2)}, u32[]{:S(2)}) collective-permute-start(bf16[4,2,128,128]{3,2,1,0:T(8,128)(2,1)S(1)} %get-tuple-element.71), channel_id=1, source_target_pairs={{0,16},{8,24},{16,0},{24,8},{1,17},{9,25},{17,1},{25,9},{2,18},{10... | collective-permute-start | bytes 786440 | tf_op jit(solution)/shard_map/ppermute | solution.py:246
  62.5 3.8 %parts.1 = (bf16[4,2,128,128]{3,2,1,0:T(8,128)(2,1)S(1)}, bf16[4,2,128,128]{3,2,1,0:T(8,128)(2,1)S(1)}, bf16[4,2,128,128]{3,2,1,0:T(8,128)(2,1)S(1)}, bf16[4,2,128,128]{3,2,1,0:T(8,128)(2,1)S(1)}) custom-call(s32[4,8,128]{2,1,0:T(8,128)S(1)} %get-tuple-element.45.table, bf16[512,1024]{1,0:T(8,128)(2,1)S(1)} %get-tuple-element.64.turned, ...), custom_call_target="tpu_custom_call" | custom-call | flops 2147483648 | bytes 1024 | tf_op jit(solution)/shard_map/parts/pallas_call | solution.py:31
  67.4 4.0 %base.1 = (bf16[8,4,128,128]{3,2,1,0:T(8,128)(2,1)}, f32[8,2,128,128]{3,2,1,0:T(8,128)S(1)}) custom-call(s32[4,8,128]{2,1,0:T(8,128)S(1)} %get-tuple-element.45.table, s32[4,8]{1,0:T(4,128)S(1)} %bitcast.9, f32[1024,512]{1,0:T(8,128)S(1)} %get-tuple-element.63.total, bf16[512,1024]{1,0:T(8,128)(2,1)S(1)} %get-tuple-element.64.turned, ...), custom_call_target="tpu_custom_call" | custom-call | flops 1073741824 | bytes 1024 | tf_op jit(solution)/shard_map/base/pallas_call | solution.py:31
  71.6 1.6 %collective-permute-start.18 = (bf16[4,2,128,128]{3,2,1,0:T(8,128)(2,1)S(1)}, bf16[4,2,128,128]{3,2,1,0:T(8,128)(2,1)S(1)}, u32[]{:S(2)}, u32[]{:S(2)}) collective-permute-start(bf16[4,2,128,128]{3,2,1,0:T(8,128)(2,1)S(1)} %get-tuple-element.72), channel_id=1, source_target_pairs={{0,8},{8,0},{16,24},{24,16},{1,9},{9,1},{17,25},{25,17},{2,10},{10... | collective-permute-start | bytes 786440 | tf_op jit(solution)/shard_map/ppermute | solution.py:246
  73.2 1.5 %collective-permute-start.19 = (bf16[4,2,128,128]{3,2,1,0:T(8,128)(2,1)S(1)}, bf16[4,2,128,128]{3,2,1,0:T(8,128)(2,1)S(1)}, u32[]{:S(2)}, u32[]{:S(2)}) collective-permute-start(bf16[4,2,128,128]{3,2,1,0:T(8,128)(2,1)S(1)} %get-tuple-element.73), channel_id=1, source_target_pairs={{0,16},{8,24},{16,0},{24,8},{1,17},{9,25},{17,1},{25,9},{2,18},{10... | collective-permute-start | bytes 786440 | tf_op jit(solution)/shard_map/ppermute | solution.py:246
  74.7 7.4 %squared.1 = bf16[8,4,128,128]{3,2,1,0:T(8,128)(2,1)} custom-call(s32[4,8,128]{2,1,0:T(8,128)S(1)} %get-tuple-element.45.table, s32[4,8]{1,0:T(4,128)S(1)} %bitcast.10, bf16[1024,2560]{1,0:T(8,128)(2,1)S(1)} %get-tuple-element.46.panel, bf16[1024,1536]{1,0:T(8,128)(2,1)S(1)} %get-tuple-element.52.panel_last, bf16[2064,128]{1,0:T(8,128)(2,1)S(1)} %pack_d.1.refs_0_, ...), custom_call_target="tpu_custom_call" | custom-call | flops 4294967296 | bytes 1024 | tf_op jit(solution)/shard_map/squared/pallas_call | solution.py:31
  82.1 1.1 %gradient.1 = bf16[8,2,128,128]{3,2,1,0:T(8,128)(2,1)} custom-call(f32[8,2,128,128]{3,2,1,0:T(8,128)S(1)} %get-tuple-element.66.base, bf16[4,2,128,128]{3,2,1,0:T(8,128)(2,1)S(1)} %collective-permute-done.15.refs_0_, bf16[4,2,128,128]{3,2,1,0:T(8,128)(2,1)S(1)} %collective-permute-done.18.refs_1_, ...), custom_call_target="tpu_custom_call" | custom-call | bytes 1024 | tf_op jit(solution)/shard_map/gradient/pallas_call | solution.py:31
  (35 shorter events, 3.2 us)
Async XLA Ops:
  0.6 1.0 %copy-start = (bf16[8,2,128,128]{3,2,1,0:T(8,128)(2,1)S(1)}, bf16[8,2,128,128]{3,2,1,0:T(8,128)(2,1)}, u32[]{:S(2)}) copy-start(bf16[8,2,128,128]{3,2,1,0:T(8,128)(2,1)} %param.5) | copy-start | bytes 1572868
  1.7 0.7 copy-start.2
  2.4 17.3 %collective-permute-start.1 = (bf16[2064,128]{1,0:T(8,128)(2,1)S(1)}, bf16[2064,128]{1,0:T(8,128)(2,1)S(1)}, u32[]{:S(2)}, u32[]{:S(2)}) collective-permute-start(bf16[2064,128]{1,0:T(8,128)(2,1)S(1)} %pack_d.1.refs_0_), channel_id=1, source_target_pairs={{0,2},{2,4},{4,6},{6,0},{1,7},{3,1},{5,3},{7,5},{8,10},{10,12},{12... | collective-permute-start | bytes 1585160 | tf_op jit(solution)/shard_map/ppermute | solution.py:251
  5.5 1.0 %copy-start.1 = (bf16[8,2,128,128]{3,2,1,0:T(8,128)(2,1)S(1)}, bf16[8,2,128,128]{3,2,1,0:T(8,128)(2,1)}, u32[]{:S(2)}) copy-start(bf16[8,2,128,128]{3,2,1,0:T(8,128)(2,1)} %param.7) | copy-start | bytes 1572868
  6.5 0.7 copy-start.3
  7.2 0.7 copy-start.5
  7.9 14.4 %collective-permute-start.5 = (bf16[2064,128]{1,0:T(8,128)(2,1)S(1)}, bf16[2064,128]{1,0:T(8,128)(2,1)S(1)}, u32[]{:S(2)}, u32[]{:S(2)}) collective-permute-start(bf16[2064,128]{1,0:T(8,128)(2,1)S(1)} %pack_h.1.refs_5_), channel_id=1, source_target_pairs={{0,16},{8,24},{16,0},{24,8},{1,17},{9,25},{17,1},{25,9},{2,18},{10... | collective-permute-start | bytes 1585160 | tf_op jit(solution)/shard_map/ppermute | solution.py:246
  9.5 14.6 %collective-permute-start.4 = (bf16[2064,128]{1,0:T(8,128)(2,1)S(1)}, bf16[2064,128]{1,0:T(8,128)(2,1)S(1)}, u32[]{:S(2)}, u32[]{:S(2)}) collective-permute-start(bf16[2064,128]{1,0:T(8,128)(2,1)S(1)} %pack_h.1.refs_5_), channel_id=1, source_target_pairs={{0,8},{8,0},{16,24},{24,16},{1,9},{9,1},{17,25},{25,17},{2,10},{10... | collective-permute-start | bytes 1585160 | tf_op jit(solution)/shard_map/ppermute | solution.py:246
  19.7 14.6 %collective-permute-start.3 = (bf16[2064,128]{1,0:T(8,128)(2,1)S(1)}, bf16[2064,128]{1,0:T(8,128)(2,1)S(1)}, u32[]{:S(2)}, u32[]{:S(2)}) collective-permute-start(bf16[2064,128]{1,0:T(8,128)(2,1)S(1)} %collective-permute-done.1.refs_2_), channel_id=1, source_target_pairs={{0,2},{2,4},{4,6},{6,0},{1,7},{3,1},{5,3},{7,5},{8,10},{10,12},{12... | collective-permute-start | bytes 1585160 | tf_op jit(solution)/shard_map/ppermute | solution.py:251
  22.3 10.3 %collective-permute-start.7 = (bf16[1040,128]{1,0:T(8,128)(2,1)S(1)}, bf16[1040,128]{1,0:T(8,128)(2,1)S(1)}, u32[]{:S(2)}, u32[]{:S(2)}) collective-permute-start(bf16[1040,128]{1,0:T(8,128)(2,1)S(1)} %slice.17), channel_id=1, source_target_pairs={{0,8},{8,0},{16,24},{24,16},{1,9},{9,1},{17,25},{25,17},{2,10},{10... | collective-permute-start | bytes 798728 | tf_op jit(solution)/shard_map/ppermute | solution.py:246
  24.1 8.5 %collective-permute-start.6 = (bf16[1024,128]{1,0:T(8,128)(2,1)S(1)}, bf16[1024,128]{1,0:T(8,128)(2,1)S(1)}, u32[]{:S(2)}, u32[]{:S(2)}) collective-permute-start(bf16[1024,128]{1,0:T(8,128)(2,1)S(1)} %slice.16), channel_id=1, source_target_pairs={{0,16},{8,24},{16,0},{24,8},{1,17},{9,25},{17,1},{25,9},{2,18},{10... | collective-permute-start | bytes 786440 | tf_op jit(solution)/shard_map/ppermute | solution.py:246
  25.5 11.9 %collective-permute-start = (bf16[2064,128]{1,0:T(8,128)(2,1)S(1)}, bf16[2064,128]{1,0:T(8,128)(2,1)S(1)}, u32[]{:S(2)}, u32[]{:S(2)}) collective-permute-start(bf16[2064,128]{1,0:T(8,128)(2,1)S(1)} %pack_d.1.refs_0_), channel_id=1, source_target_pairs={{0,1},{1,0},{2,3},{3,2},{4,5},{5,4},{6,7},{7,6},{8,9},{9,8},{10,11... | collective-permute-start | bytes 1585160 | tf_op jit(solution)/shard_map/ppermute | solution.py:254
  25.6 12.9 %collective-permute-start.2 = (bf16[2064,128]{1,0:T(8,128)(2,1)S(1)}, bf16[2064,128]{1,0:T(8,128)(2,1)S(1)}, u32[]{:S(2)}, u32[]{:S(2)}) collective-permute-start(bf16[2064,128]{1,0:T(8,128)(2,1)S(1)} %collective-permute-done.1.refs_2_), channel_id=1, source_target_pairs={{0,1},{1,0},{2,3},{3,2},{4,5},{5,4},{6,7},{7,6},{8,9},{9,8},{10,11... | collective-permute-start | bytes 1585160 | tf_op jit(solution)/shard_map/ppermute | solution.py:254
  34.2 11.9 %collective-permute-start.10 = (bf16[2064,128]{1,0:T(8,128)(2,1)S(1)}, bf16[2064,128]{1,0:T(8,128)(2,1)S(1)}, u32[]{:S(2)}, u32[]{:S(2)}) collective-permute-start(bf16[2064,128]{1,0:T(8,128)(2,1)S(1)} %pack_d.1.refs_0_), channel_id=1, source_target_pairs={{0,16},{8,24},{16,0},{24,8},{1,17},{9,25},{17,1},{25,9},{2,18},{10... | collective-permute-start | bytes 1585160 | tf_op jit(solution)/shard_map/ppermute | solution.py:246
  35.8 13.9 %collective-permute-start.8 = (bf16[2064,128]{1,0:T(8,128)(2,1)S(1)}, bf16[2064,128]{1,0:T(8,128)(2,1)S(1)}, u32[]{:S(2)}, u32[]{:S(2)}) collective-permute-start(bf16[2064,128]{1,0:T(8,128)(2,1)S(1)} %collective-permute-done.3.refs_4_), channel_id=1, source_target_pairs={{0,2},{2,4},{4,6},{6,0},{1,7},{3,1},{5,3},{7,5},{8,10},{10,12},{12... | collective-permute-start | bytes 1585160 | tf_op jit(solution)/shard_map/ppermute | solution.py:251
  35.9 14.5 %collective-permute-start.9 = (bf16[2064,128]{1,0:T(8,128)(2,1)S(1)}, bf16[2064,128]{1,0:T(8,128)(2,1)S(1)}, u32[]{:S(2)}, u32[]{:S(2)}) collective-permute-start(bf16[2064,128]{1,0:T(8,128)(2,1)S(1)} %pack_d.1.refs_0_), channel_id=1, source_target_pairs={{0,8},{8,0},{16,24},{24,16},{1,9},{9,1},{17,25},{25,17},{2,10},{10... | collective-permute-start | bytes 1585160 | tf_op jit(solution)/shard_map/ppermute | solution.py:246
  37.4 15.4 %collective-permute-start.11 = (bf16[2064,128]{1,0:T(8,128)(2,1)S(1)}, bf16[2064,128]{1,0:T(8,128)(2,1)S(1)}, u32[]{:S(2)}, u32[]{:S(2)}) collective-permute-start(bf16[2064,128]{1,0:T(8,128)(2,1)S(1)} %collective-permute-done.3.refs_4_), channel_id=1, source_target_pairs={{0,1},{1,0},{2,3},{3,2},{4,5},{5,4},{6,7},{7,6},{8,9},{9,8},{10,11... | collective-permute-start | bytes 1585160 | tf_op jit(solution)/shard_map/ppermute | solution.py:254
  50.4 2.4 %collective-permute-start.12 = (bf16[2064,128]{1,0:T(8,128)(2,1)S(1)}, bf16[2064,128]{1,0:T(8,128)(2,1)S(1)}, u32[]{:S(2)}, u32[]{:S(2)}) collective-permute-start(bf16[2064,128]{1,0:T(8,128)(2,1)S(1)} %collective-permute-done.8.refs_1_), channel_id=1, source_target_pairs={{0,1},{1,0},{2,3},{3,2},{4,5},{5,4},{6,7},{7,6},{8,9},{9,8},{10,11... | collective-permute-start | bytes 1585160 | tf_op jit(solution)/shard_map/ppermute | solution.py:254
  50.6 8.6 %collective-permute-start.13 = (bf16[1024,128]{1,0:T(8,128)(2,1)S(1)}, bf16[1024,128]{1,0:T(8,128)(2,1)S(1)}, u32[]{:S(2)}, u32[]{:S(2)}) collective-permute-start(bf16[1024,128]{1,0:T(8,128)(2,1)S(1)} %slice.14), channel_id=1, source_target_pairs={{0,16},{8,24},{16,0},{24,8},{1,17},{9,25},{17,1},{25,9},{2,18},{10... | collective-permute-start | bytes 786440 | tf_op jit(solution)/shard_map/ppermute | solution.py:246
  51.2 8.3 %collective-permute-start.14 = (bf16[1024,128]{1,0:T(8,128)(2,1)S(1)}, bf16[1024,128]{1,0:T(8,128)(2,1)S(1)}, u32[]{:S(2)}, u32[]{:S(2)}) collective-permute-start(bf16[1024,128]{1,0:T(8,128)(2,1)S(1)} %slice.15), channel_id=1, source_target_pairs={{0,8},{8,0},{16,24},{24,16},{1,9},{9,1},{17,25},{25,17},{2,10},{10... | collective-permute-start | bytes 786440 | tf_op jit(solution)/shard_map/ppermute | solution.py:246
  59.5 12.0 %collective-permute-start.16 = (bf16[4,2,128,128]{3,2,1,0:T(8,128)(2,1)S(1)}, bf16[4,2,128,128]{3,2,1,0:T(8,128)(2,1)S(1)}, u32[]{:S(2)}, u32[]{:S(2)}) collective-permute-start(bf16[4,2,128,128]{3,2,1,0:T(8,128)(2,1)S(1)} %get-tuple-element.69), channel_id=1, source_target_pairs={{0,8},{8,0},{16,24},{24,16},{1,9},{9,1},{17,25},{25,17},{2,10},{10... | collective-permute-start | bytes 786440 | tf_op jit(solution)/shard_map/ppermute | solution.py:246
  61.0 10.5 %collective-permute-start.17 = (bf16[4,2,128,128]{3,2,1,0:T(8,128)(2,1)S(1)}, bf16[4,2,128,128]{3,2,1,0:T(8,128)(2,1)S(1)}, u32[]{:S(2)}, u32[]{:S(2)}) collective-permute-start(bf16[4,2,128,128]{3,2,1,0:T(8,128)(2,1)S(1)} %get-tuple-element.71), channel_id=1, source_target_pairs={{0,16},{8,24},{16,0},{24,8},{1,17},{9,25},{17,1},{25,9},{2,18},{10... | collective-permute-start | bytes 786440 | tf_op jit(solution)/shard_map/ppermute | solution.py:246
  62.5 4.9 %copy-start.4 = (s32[8,4]{0,1:T(4,128)S(1)}, s32[8,4]{0,1:T(4,128)}, u32[]{:S(2)}) copy-start(s32[8,4]{0,1:T(4,128)} %param.9) | copy-start | bytes 388
  66.3 15.8 %collective-permute-start.15 = (bf16[4,2,128,128]{3,2,1,0:T(8,128)(2,1)S(1)}, bf16[4,2,128,128]{3,2,1,0:T(8,128)(2,1)S(1)}, u32[]{:S(2)}, u32[]{:S(2)}) collective-permute-start(bf16[4,2,128,128]{3,2,1,0:T(8,128)(2,1)S(1)} %get-tuple-element.67), channel_id=1, source_target_pairs={{0,8},{8,0},{16,24},{24,16},{1,9},{9,1},{17,25},{25,17},{2,10},{10... | collective-permute-start | bytes 786440 | tf_op jit(solution)/shard_map/ppermute | solution.py:246
  66.9 15.2 %collective-permute-start.20 = (bf16[4,2,128,128]{3,2,1,0:T(8,128)(2,1)S(1)}, bf16[4,2,128,128]{3,2,1,0:T(8,128)(2,1)S(1)}, u32[]{:S(2)}, u32[]{:S(2)}) collective-permute-start(bf16[4,2,128,128]{3,2,1,0:T(8,128)(2,1)S(1)} %get-tuple-element.74), channel_id=1, source_target_pairs={{0,16},{8,24},{16,0},{24,8},{1,17},{9,25},{17,1},{25,9},{2,18},{10... | collective-permute-start | bytes 786440 | tf_op jit(solution)/shard_map/ppermute | solution.py:246
  71.6 10.5 %collective-permute-start.18 = (bf16[4,2,128,128]{3,2,1,0:T(8,128)(2,1)S(1)}, bf16[4,2,128,128]{3,2,1,0:T(8,128)(2,1)S(1)}, u32[]{:S(2)}, u32[]{:S(2)}) collective-permute-start(bf16[4,2,128,128]{3,2,1,0:T(8,128)(2,1)S(1)} %get-tuple-element.72), channel_id=1, source_target_pairs={{0,8},{8,0},{16,24},{24,16},{1,9},{9,1},{17,25},{25,17},{2,10},{10... | collective-permute-start | bytes 786440 | tf_op jit(solution)/shard_map/ppermute | solution.py:246
  73.2 9.0 %collective-permute-start.19 = (bf16[4,2,128,128]{3,2,1,0:T(8,128)(2,1)S(1)}, bf16[4,2,128,128]{3,2,1,0:T(8,128)(2,1)S(1)}, u32[]{:S(2)}, u32[]{:S(2)}) collective-permute-start(bf16[4,2,128,128]{3,2,1,0:T(8,128)(2,1)S(1)} %get-tuple-element.73), channel_id=1, source_target_pairs={{0,16},{8,24},{16,0},{24,8},{1,17},{9,25},{17,1},{25,9},{2,18},{10... | collective-permute-start | bytes 786440 | tf_op jit(solution)/shard_map/ppermute | solution.py:246

commit v6 on v5

--- a/solution.py
+++ b/solution.py
@@ -141,7 +141,7 @@
 
 
 def last_kernel(z, table, right, total_in, panel, *refs):
-    payloads, (total, turned, panel_last, *part, columns, ints, idx, sem) = refs[:z.n_last], refs[z.n_last:]
+    payloads, (total, turned, panel_last, *part, ints, idx, sem) = refs[:z.n_last], refs[z.n_last:]
     read_tails(payloads, ints, idx, sem)
     for n, payload in enumerate(payloads):
         fill_left(z, idx, n, piece_col(z, z.n_first + n), payload, panel_last, n * z.wide)
@@ -152,64 +152,71 @@
         for j in range(z.bc):
             cols = slice(j * z.bs, (j + 1) * z.bs)
             turned[cols, rows] = total[rows, cols].T.astype(BF16)
-    one_part(z, table, z.n_row - 1, turned, panel, panel_last, columns, part)
+    one_part(z, table, z.n_row - 1, turned, panel, panel_last, part)
 
 
 def parts_kernel(z, table, turned, panel, panel_last, *refs):
-    cuts = (len(refs) - 1) // (z.n_row - 2)
+    cuts = len(refs) // (z.n_row - 2)
     for n in range(1, z.n_row - 1):
-        one_part(z, table, n, turned, panel, panel_last, refs[-1], refs[(n - 1) * cuts:n * cuts])
-
-
-def one_part(z, table, n, turned, panel, panel_last, columns, out):
-    per_out = z.rows // len(out)
+        one_part(z, table, n, turned, panel, panel_last, refs[(n - 1) * cuts:n * cuts])
+
+
+def one_part(z, table, n, turned, panel, panel_last, out):
     row = lax.axis_index("row") ^ n
-    per = z.n_col // z.n_row
-    for t in range(per):
-        column = columns.at[t % 2]
-        piece = piece_of(z, row * per + t)
-
-        @pl.when(piece < z.n_first)
-        def _():
-            at = pl.ds(pl.multiple_of(piece * z.wide, z.wide), z.wide)
-            column[...] = jnp.dot(turned[...], panel[:, at], preferred_element_type=F32)
-
-        @pl.when(piece >= z.n_first)
-        def _():
-            at = pl.ds(pl.multiple_of((piece - z.n_first) * z.wide, z.wide), z.wide)
-            column[...] = jnp.dot(turned[...], panel_last[:, at], preferred_element_type=F32)
-
+    per, per_out = z.n_col // z.n_row, z.rows // len(out)
+    me = lax.axis_index("col")
+
+    def blocks(t, source, first):
         for b in range(z.bc):
             i = t * z.bc + b
+            wanted = [turned[lanes(z, table[n, s, i] - me * z.bc), :] for s in range(z.ka)]
+            column = source[:, lanes(z, first * z.bc + b)]
+            terms = jnp.dot(jnp.concatenate(wanted, axis=0), column, preferred_element_type=F32)
             for s in range(z.ka):
-                j = table[n, s, i] - lax.axis_index("col") * z.bc
-                out[i // per_out][i % per_out, s] = column[lanes(z, j), b * z.bs:(b + 1) * z.bs].astype(out[0].dtype)
-
-
-def base_kernel(z, table, filt, total, turned, panel, panel_last, mixed, base, columns, own):
-    me = lax.axis_index("col")
-    one_part(z, table, 0, turned, panel, panel_last, columns, [own])
-    for i in range(z.rows):
-        rows = slice(i * z.bs, (i + 1) * z.bs)
+                ref = out[i // per_out]
+                ref[i % per_out, s] = terms[s * z.bs:(s + 1) * z.bs, :].astype(ref.dtype)
+
+    for t in range(per):
+        piece = piece_of(z, row * per + t)
+        pl.when(piece < z.n_first)(functools.partial(blocks, t, panel, piece))
+        pl.when(piece >= z.n_first)(functools.partial(blocks, t, panel_last, piece - z.n_first))
+
+
+def filtered(z, filt, total, i, s):
+    me = lax.axis_index("col")
+    return total[i * z.bs:(i + 1) * z.bs, lanes(z, filt[s, i] - me * z.bc)].astype(BF16)
+
+
+def base_kernel(z, table, filt, total, turned, panel, panel_last, mixed, direct, own, held, sem):
+    me = lax.axis_index("col")
+    for i in range(z.rows):
         for s in range(z.kf):
-            mixed[i, s] = total[rows, lanes(z, filt[s, i] - me * z.bc)].astype(mixed.dtype)
+            held[i, s] = filtered(z, filt, total, i, s)
+    copy = pltpu.make_async_copy(held, mixed, sem)
+    copy.start()
+    for i in range(z.rows):
         for s in range(z.ka):
-            direct = total[rows, lanes(z, table[0, s, i] - me * z.bc)]
-            base[i, s] = 3.0 * direct - 2.0 * own[i, s].T
+            direct[i, s] = 3.0 * total[i * z.bs:(i + 1) * z.bs, lanes(z, table[0, s, i] - me * z.bc)]
+    one_part(z, table, 0, turned, panel, panel_last, [own])
+    copy.wait()
 
 
 def square_kernel(z, counts, table, filt, panel, panel_last, *refs):
-    squared, right, total = refs[sum(counts):]
-    me = lax.axis_index("col")
+    squared, right, total, held, sems = refs[sum(counts):]
     fill_right(z, 0, z.ka, table, group(refs, counts), range(z.n_row), functools.partial(by_piece, z), right)
     deep = z.n_first * z.wide
-    for rows in halves(z.tall):
+    copies = []
+    for n, rows in enumerate(halves(z.tall)):
         total[rows, :] = jnp.dot(panel[rows, :], right[0:deep, :], preferred_element_type=F32)
         total[rows, :] += jnp.dot(panel_last[rows, :], right[deep:, :], preferred_element_type=F32)
-    for i in range(z.rows):
-        rows = slice(i * z.bs, (i + 1) * z.bs)
-        for s in range(z.kf):
-            squared[i, s] = total[rows, lanes(z, filt[s, i] - me * z.bc)].astype(squared.dtype)
+        here = halves(z.rows)[n]
+        for i in range(here.start, here.stop):
+            for s in range(z.kf):
+                held[i, s] = filtered(z, filt, total, i, s)
+        copies.append(pltpu.make_async_copy(held.at[here], squared.at[here], sems.at[n]))
+        copies[-1].start()
+    for copy in copies:
+        copy.wait()
 
 
 def add_kernel(z, x_0, x_1, y_0, y_1, x_out, y_out):
@@ -217,18 +224,17 @@
     y_out[...] = (y_0[...].astype(F32) + y_1[...].astype(F32)).astype(y_out.dtype)
 
 
-def gradient_kernel(z, base, *refs):
+def gradient_kernel(z, direct, own, *refs):
     terms, out = refs[:-1], refs[-1]
+    half = z.rows // 2
+    here = [t for t in terms if t.shape[0] == z.rows]
+    cut = [t for t in terms if t.shape[0] < z.rows]
     for i in range(z.rows):
         for s in range(z.ka):
-            here = [t for t in terms if t.shape[0] == z.rows]
-            cut = [t for t in terms if t.shape[0] < z.rows]
-            half = z.rows // 2
-            blocks = [t[i, s] for t in here] + [t[i % half, s] for t in cut[i // half::2]]
-            cubic = blocks[0].astype(F32)
-            for other in blocks[1:]:
-                cubic += other.astype(F32)
-            out[i, s] = (base[i, s] - 2.0 * cubic.T).astype(out.dtype)
+            cubic = own[i, s]
+            for block in [t[i, s] for t in here] + [t[i % half, s] for t in cut[i // half::2]]:
+                cubic += block.astype(F32)
+            out[i, s] = (direct[i, s] - 2.0 * cubic.T).astype(out.dtype)
 
 
 def local(n_row, n_col, density, density_cols, hamilton, hamilton_cols, filter_cols):
@@ -237,6 +243,7 @@
     shape = jax.ShapeDtypeStruct
     smem = pl.BlockSpec(memory_space=pltpu.SMEM)
     vmem = pl.BlockSpec(memory_space=pltpu.VMEM)
+    anywhere = pl.BlockSpec(memory_space=pl.ANY)
     dma = pltpu.SemaphoreType.DMA
     d_rows, h_rows = z.rows * z.ka * z.bs, z.rows * z.kh * z.bs
     panel_flops = 2 * z.tall * z.wide * z.nb * z.bs
@@ -317,7 +324,6 @@
     forward(d_right)
     d_right = [d_right[flip] for flip in range(n_row)]
     part = shape((z.rows, z.ka) + block, BF16)
-    columns = pltpu.VMEM((2, z.wide, z.wide), F32)
     cuts = 2 if n_row == 4 and z.rows % 2 == 0 else 1
     cut_part = shape((z.rows // cuts, z.ka) + block, BF16)
     total, turned, panel_last, *far = call(
@@ -326,29 +332,29 @@
         [shape((z.tall, z.wide), F32), shape((z.wide, z.tall), BF16), shape((z.tall, z.n_last * z.wide), BF16)]
         + [cut_part] * cuts,
         [
-            columns,
             pltpu.VMEM((z.n_last, 8, z.bs), jnp.int32),
             pltpu.SMEM((z.n_last, 8, z.bs), jnp.int32),
             dma,
         ],
         [smem] + [vmem] * (3 + z.n_last), [vmem] * (3 + cuts), panel_flops // 4 + part_flops, "last",
     )
-    far, d_right = lax.optimization_barrier((far, d_right))
     near = call(
-        functools.partial(parts_kernel, z), [table, turned, panel, panel_last], [cut_part] * (cuts * (n_row - 2)), [columns],
+        functools.partial(parts_kernel, z), [table, turned, panel, panel_last], [cut_part] * (cuts * (n_row - 2)), [],
         [smem] + [vmem] * 3, [vmem] * (cuts * (n_row - 2)), part_flops * (n_row - 2), "parts",
     )
+    near, d_right = lax.optimization_barrier((near, d_right))
     if cuts == 2:
         far = over_row(far[0], 1), over_row(far[1], 2)
         x_0, y_1 = over_row(near[0], 1), over_row(near[3], 2)
     else:
         received = [over_row(term, n + 1) for n, term in enumerate([*near, *far])]
-    mixed, base = call(
+    whole_part = shape((z.rows, z.ka) + block, F32)
+    mixed, direct, own = call(
         functools.partial(base_kernel, z),
         [table, filter_cols.T, total, turned, panel, panel_last],
-        [shape((z.rows, z.kf) + block, BF16), shape((z.rows, z.ka) + block, F32)],
-        [columns, pltpu.VMEM((z.rows, z.ka) + block, F32)],
-        [smem] * 2 + [vmem] * 4, [vmem] * 2, part_flops, "base",
+        [shape((z.rows, z.kf) + block, BF16), whole_part, whole_part],
+        [pltpu.VMEM((z.rows, z.kf) + block, BF16), dma],
+        [smem] * 2 + [vmem] * 4, [anywhere, vmem, vmem], part_flops, "base",
     )
     if cuts == 2:
         y_0, x_1 = call(
@@ -360,12 +366,15 @@
         functools.partial(square_kernel, z, [len(x) for x in d_right]),
         [table, filter_cols.T, panel, panel_last, *sum(d_right, [])],
         [shape((z.rows, z.kf) + block, BF16)],
-        [pltpu.VMEM((z.nb * z.bs, z.wide), BF16), pltpu.VMEM((z.tall, z.wide), F32)],
-        [smem] * 2 + [vmem] * (2 + sum(map(len, d_right))), [vmem], panel_flops, "squared",
+        [
+            pltpu.VMEM((z.nb * z.bs, z.wide), BF16), pltpu.VMEM((z.tall, z.wide), F32),
+            pltpu.VMEM((z.rows, z.kf) + block, BF16), dma((2,)),
+        ],
+        [smem] * 2 + [vmem] * (2 + sum(map(len, d_right))), [anywhere], panel_flops, "squared",
     )
     gradient, = call(
-        functools.partial(gradient_kernel, z), [base, *received], [part], [],
-        [vmem] * (1 + len(received)), [vmem], 0, "gradient",
+        functools.partial(gradient_kernel, z), [direct, own, *received], [part], [],
+        [vmem] * (2 + len(received)), [vmem], 0, "gradient",
     )
     return squared, mixed, gradient
 

time: 83.6 us -> 80 us (0.957)
  waiting for transfers between devices: 27.3 us -> 25.9 us
  Pallas kernels: 27.7 us -> 26.3 us
  starting transfers between devices: 23.4 us -> 22.5 us
    pallas_call x9, Pallas kernels: 27.7 us -> 26.3 us  [call(): pl.pallas_call(kernel, out_shape=outs, in_specs=in_specs, out_specs=out_s...]
    ppermute x14, waiting for transfers between devices: 13.3 us -> 12 us  [over_row(): return lax.ppermute(x, 'row', [(r, r ^ flip) for r in range(n_row)])]
    ppermute x14, starting transfers between devices: 18.4 us -> 17.5 us  [over_row(): return lax.ppermute(x, 'row', [(r, r ^ flip) for r in range(n_row)])]
  transfers between devices with their start and end apart: 21 -> 21, of which waited for: 10 -> 8; matrix products, arithmetic and copies ran while one was open for 0% -> 0% of each run, Pallas kernels for 32% -> 31%
where the time goes in v6:
time: 80 us; the launch traced here: 79.8 us
  Pallas kernels  26.3 us (33%)
  waiting for transfers between devices  25.9 us (32%)
  starting transfers between devices  22.5 us (28%)
  local copies, waits for them, and re-layouts  4.19 us (5%)
    pallas_call x9, Pallas kernels, call(): pl.pallas_call(kernel, out_shape=outs, in_specs=in_specs, out_specs=out_s...  26.3 us
    ppermute x14, starting transfers between devices, over_row(): return lax.ppermute(x, 'row', [(r, r ^ flip) for r in range(n_row)])  17.5 us
    ppermute x3, waiting for transfers between devices, next_chip(): return lax.ppermute(x, 'col', pairs)  13.9 us
    ppermute x14, waiting for transfers between devices, over_row(): return lax.ppermute(x, 'row', [(r, r ^ flip) for r in range(n_row)])  12 us
    unnamed x12, local copies, waits for them, and re-layouts  4.11 us
    ppermute x3, starting transfers between devices, next_chip(): return lax.ppermute(x, 'col', pairs)  3.12 us
    ppermute x4, starting transfers between devices, other_core(): return lax.ppermute(x, 'col', [(c, c ^ 1) for c in range(n_col)])  1.88 us
  transfers between devices with their start and end apart: 21, of which 8 were waited for; matrix products, arithmetic and copies ran while one was open for 0% of the time, Pallas kernels for 31%

profile of v6, /device:TPU:0, one launch (start us, length us, event | category | flops | bytes accessed | tf_op | source)
XLA Modules:
  0.0 79.8 jit_solution(6748794019272457048)
XLA Ops:
  0.6 1.0 %copy-done = bf16[8,2,128,128]{3,2,1,0:T(8,128)(2,1)S(1)} copy-done((bf16[8,2,128,128]{3,2,1,0:T(8,128)(2,1)S(1)}, bf16[8,2,128,128]{3,2,1,0:T(8,128)(2,1)}, u32[]{:S(2)}) %copy-start) | copy-done | bytes 524312
  1.7 0.7 copy-done.2
  2.4 3.1 %collective-permute-start.1 = (bf16[2064,128]{1,0:T(8,128)(2,1)S(1)}, bf16[2064,128]{1,0:T(8,128)(2,1)S(1)}, u32[]{:S(2)}, u32[]{:S(2)}) collective-permute-start(bf16[2064,128]{1,0:T(8,128)(2,1)S(1)} %pack_d.1.refs_0_), channel_id=1, source_target_pairs={{0,2},{2,4},{4,6},{6,0},{1,7},{3,1},{5,3},{7,5},{8,10},{10,12},{12... | collective-permute-start | bytes 1585160 | tf_op jit(solution)/shard_map/ppermute | solution.py:258
  5.5 1.0 %copy-done.1 = bf16[8,2,128,128]{3,2,1,0:T(8,128)(2,1)S(1)} copy-done((bf16[8,2,128,128]{3,2,1,0:T(8,128)(2,1)S(1)}, bf16[8,2,128,128]{3,2,1,0:T(8,128)(2,1)}, u32[]{:S(2)}) %copy-start.1) | copy-done | bytes 524312
  6.5 0.7 copy-done.3
  7.2 0.7 copy-done.5
  7.9 1.6 %collective-permute-start.5 = (bf16[2064,128]{1,0:T(8,128)(2,1)S(1)}, bf16[2064,128]{1,0:T(8,128)(2,1)S(1)}, u32[]{:S(2)}, u32[]{:S(2)}) collective-permute-start(bf16[2064,128]{1,0:T(8,128)(2,1)S(1)} %pack_h.1.refs_5_), channel_id=1, source_target_pairs={{0,16},{8,24},{16,0},{24,8},{1,17},{9,25},{17,1},{25,9},{2,18},{10... | collective-permute-start | bytes 1585160 | tf_op jit(solution)/shard_map/ppermute | solution.py:253
  9.5 1.5 %collective-permute-start.4 = (bf16[2064,128]{1,0:T(8,128)(2,1)S(1)}, bf16[2064,128]{1,0:T(8,128)(2,1)S(1)}, u32[]{:S(2)}, u32[]{:S(2)}) collective-permute-start(bf16[2064,128]{1,0:T(8,128)(2,1)S(1)} %pack_h.1.refs_5_), channel_id=1, source_target_pairs={{0,8},{8,0},{16,24},{24,16},{1,9},{9,1},{17,25},{25,17},{2,10},{10... | collective-permute-start | bytes 1585160 | tf_op jit(solution)/shard_map/ppermute | solution.py:253
  11.0 8.7 %collective-permute-done.1.refs_2_ = bf16[2064,128]{1,0:T(8,128)(2,1)S(1)} collective-permute-done((bf16[2064,128]{1,0:T(8,128)(2,1)S(1)}, bf16[2064,128]{1,0:T(8,128)(2,1)S(1)}, u32[]{:S(2)}, u32[]{:S(2)}) %collective-permute-start.1) | collective-permute-done | bytes 528416 | tf_op jit(solution)/shard_map/ppermute | solution.py:258
  19.7 2.6 %collective-permute-done.5.refs_7_ = bf16[2064,128]{1,0:T(8,128)(2,1)S(1)} collective-permute-done((bf16[2064,128]{1,0:T(8,128)(2,1)S(1)}, bf16[2064,128]{1,0:T(8,128)(2,1)S(1)}, u32[]{:S(2)}, u32[]{:S(2)}) %collective-permute-start.5) | collective-permute-done | bytes 528416 | tf_op jit(solution)/shard_map/ppermute | solution.py:253
  22.3 1.6 %collective-permute-start.7 = (bf16[1040,128]{1,0:T(8,128)(2,1)S(1)}, bf16[1040,128]{1,0:T(8,128)(2,1)S(1)}, u32[]{:S(2)}, u32[]{:S(2)}) collective-permute-start(bf16[1040,128]{1,0:T(8,128)(2,1)S(1)} %slice.17), channel_id=1, source_target_pairs={{0,8},{8,0},{16,24},{24,16},{1,9},{9,1},{17,25},{25,17},{2,10},{10... | collective-permute-start | bytes 798728 | tf_op jit(solution)/shard_map/ppermute | solution.py:253
  24.1 1.4 %collective-permute-start.6 = (bf16[1024,128]{1,0:T(8,128)(2,1)S(1)}, bf16[1024,128]{1,0:T(8,128)(2,1)S(1)}, u32[]{:S(2)}, u32[]{:S(2)}) collective-permute-start(bf16[1024,128]{1,0:T(8,128)(2,1)S(1)} %slice.16), channel_id=1, source_target_pairs={{0,16},{8,24},{16,0},{24,8},{1,17},{9,25},{17,1},{25,9},{2,18},{10... | collective-permute-start | bytes 786440 | tf_op jit(solution)/shard_map/ppermute | solution.py:253
  26.0 6.6 %collective-permute-done.6.refs_8_ = bf16[1024,128]{1,0:T(8,128)(2,1)S(1)} collective-permute-done((bf16[1024,128]{1,0:T(8,128)(2,1)S(1)}, bf16[1024,128]{1,0:T(8,128)(2,1)S(1)}, u32[]{:S(2)}, u32[]{:S(2)}) %collective-permute-start.6) | collective-permute-done | bytes 262176 | tf_op jit(solution)/shard_map/ppermute | solution.py:253
  32.6 1.7 %collective-permute-done.3.refs_4_ = bf16[2064,128]{1,0:T(8,128)(2,1)S(1)} collective-permute-done((bf16[2064,128]{1,0:T(8,128)(2,1)S(1)}, bf16[2064,128]{1,0:T(8,128)(2,1)S(1)}, u32[]{:S(2)}, u32[]{:S(2)}) %collective-permute-start.3) | collective-permute-done | bytes 528416 | tf_op jit(solution)/shard_map/ppermute | solution.py:258
  34.2 1.6 %collective-permute-start.10 = (bf16[2064,128]{1,0:T(8,128)(2,1)S(1)}, bf16[2064,128]{1,0:T(8,128)(2,1)S(1)}, u32[]{:S(2)}, u32[]{:S(2)}) collective-permute-start(bf16[2064,128]{1,0:T(8,128)(2,1)S(1)} %pack_d.1.refs_0_), channel_id=1, source_target_pairs={{0,16},{8,24},{16,0},{24,8},{1,17},{9,25},{17,1},{25,9},{2,18},{10... | collective-permute-start | bytes 1585160 | tf_op jit(solution)/shard_map/ppermute | solution.py:253
  35.9 1.5 %collective-permute-start.9 = (bf16[2064,128]{1,0:T(8,128)(2,1)S(1)}, bf16[2064,128]{1,0:T(8,128)(2,1)S(1)}, u32[]{:S(2)}, u32[]{:S(2)}) collective-permute-start(bf16[2064,128]{1,0:T(8,128)(2,1)S(1)} %pack_d.1.refs_0_), channel_id=1, source_target_pairs={{0,8},{8,0},{16,24},{24,16},{1,9},{9,1},{17,25},{25,17},{2,10},{10... | collective-permute-start | bytes 1585160 | tf_op jit(solution)/shard_map/ppermute | solution.py:253
  37.4 1.2 %collective-permute-start.11 = (bf16[2064,128]{1,0:T(8,128)(2,1)S(1)}, bf16[2064,128]{1,0:T(8,128)(2,1)S(1)}, u32[]{:S(2)}, u32[]{:S(2)}) collective-permute-start(bf16[2064,128]{1,0:T(8,128)(2,1)S(1)} %collective-permute-done.3.refs_4_), channel_id=1, source_target_pairs={{0,1},{1,0},{2,3},{3,2},{4,5},{5,4},{6,7},{7,6},{8,9},{9,8},{10,11... | collective-permute-start | bytes 1585160 | tf_op jit(solution)/shard_map/ppermute | solution.py:261
  38.5 5.7 %first.1 = (f32[1024,512]{1,0:T(8,128)S(1)}, bf16[1024,2560]{1,0:T(8,128)(2,1)S(1)}, bf16[1536,512]{1,0:T(8,128)(2,1)S(1)}, s32[4,8,128]{2,1,0:T(8,128)S(1)}) custom-call(bf16[2064,128]{1,0:T(8,128)(2,1)S(1)} %pack_d.1.refs_0_, bf16[2064,128]{1,0:T(8,128)(2,1)S(1)} %collective-permute-done.refs_1_, bf16[2064,128]{1,0:T(8,128)(2,1)S(1)} %collective-permute-done.1.refs_2_, ...), custom_call_target="tpu_custom_call" | custom-call | bytes 1024 | tf_op jit(solution)/shard_map/first/pallas_call | solution.py:31
  44.2 2.0 %collective-permute-done.10.refs_2_ = bf16[2064,128]{1,0:T(8,128)(2,1)S(1)} collective-permute-done((bf16[2064,128]{1,0:T(8,128)(2,1)S(1)}, bf16[2064,128]{1,0:T(8,128)(2,1)S(1)}, u32[]{:S(2)}, u32[]{:S(2)}) %collective-permute-start.10) | collective-permute-done | bytes 528416 | tf_op jit(solution)/shard_map/ppermute | solution.py:253
  46.2 3.6 %collective-permute-done.8.refs_1_ = bf16[2064,128]{1,0:T(8,128)(2,1)S(1)} collective-permute-done((bf16[2064,128]{1,0:T(8,128)(2,1)S(1)}, bf16[2064,128]{1,0:T(8,128)(2,1)S(1)}, u32[]{:S(2)}, u32[]{:S(2)}) %collective-permute-start.8) | collective-permute-done | bytes 528416 | tf_op jit(solution)/shard_map/ppermute | solution.py:258
  49.8 0.6 collective-permute-done.9.refs_1_
  51.2 1.6 %collective-permute-start.14 = (bf16[1024,128]{1,0:T(8,128)(2,1)S(1)}, bf16[1024,128]{1,0:T(8,128)(2,1)S(1)}, u32[]{:S(2)}, u32[]{:S(2)}) collective-permute-start(bf16[1024,128]{1,0:T(8,128)(2,1)S(1)} %slice.15), channel_id=1, source_target_pairs={{0,8},{8,0},{16,24},{24,16},{1,9},{9,1},{17,25},{25,17},{2,10},{10... | collective-permute-start | bytes 786440 | tf_op jit(solution)/shard_map/ppermute | solution.py:253
  52.7 5.3 %last.1 = (f32[1024,512]{1,0:T(8,128)S(1)}, bf16[512,1024]{1,0:T(8,128)(2,1)S(1)}, bf16[1024,1536]{1,0:T(8,128)(2,1)S(1)}, bf16[4,2,128,128]{3,2,1,0:T(8,128)(2,1)S(1)}, bf16[4,2,128,128]{3,2,1,0:T(8,128)(2,1)S(1)}) custom-call(s32[4,8,128]{2,1,0:T(8,128)S(1)} %get-tuple-element.48.table, bf16[1536,512]{1,0:T(8,128)(2,1)S(1)} %get-tuple-element.50.right, ...), custom_call_target="tpu_custom_call" | custom-call | flops 2147483648 | bytes 1024 | tf_op jit(solution)/shard_map/last/pallas_call | solution.py:31
  58.1 1.1 %collective-permute-start.16 = (bf16[4,2,128,128]{3,2,1,0:T(8,128)(2,1)S(1)}, bf16[4,2,128,128]{3,2,1,0:T(8,128)(2,1)S(1)}, u32[]{:S(2)}, u32[]{:S(2)}) collective-permute-start(bf16[4,2,128,128]{3,2,1,0:T(8,128)(2,1)S(1)} %get-tuple-element.75), channel_id=1, source_target_pairs={{0,8},{8,0},{16,24},{24,16},{1,9},{9,1},{17,25},{25,17},{2,10},{10... | collective-permute-start | bytes 786440 | tf_op jit(solution)/shard_map/ppermute | solution.py:253
  59.2 1.0 %collective-permute-start.17 = (bf16[4,2,128,128]{3,2,1,0:T(8,128)(2,1)S(1)}, bf16[4,2,128,128]{3,2,1,0:T(8,128)(2,1)S(1)}, u32[]{:S(2)}, u32[]{:S(2)}) collective-permute-start(bf16[4,2,128,128]{3,2,1,0:T(8,128)(2,1)S(1)} %get-tuple-element.77), channel_id=1, source_target_pairs={{0,16},{8,24},{16,0},{24,8},{1,17},{9,25},{17,1},{25,9},{2,18},{10... | collective-permute-start | bytes 786440 | tf_op jit(solution)/shard_map/ppermute | solution.py:253
  60.2 4.0 %parts.1 = (bf16[4,2,128,128]{3,2,1,0:T(8,128)(2,1)S(1)}, bf16[4,2,128,128]{3,2,1,0:T(8,128)(2,1)S(1)}, bf16[4,2,128,128]{3,2,1,0:T(8,128)(2,1)S(1)}, bf16[4,2,128,128]{3,2,1,0:T(8,128)(2,1)S(1)}) custom-call(s32[4,8,128]{2,1,0:T(8,128)S(1)} %get-tuple-element.48.table, bf16[512,1024]{1,0:T(8,128)(2,1)S(1)} %get-tuple-element.56.turned, ...), custom_call_target="tpu_custom_call" | custom-call | flops 2147483648 | bytes 1024 | tf_op jit(solution)/shard_map/parts/pallas_call | solution.py:31
  64.2 1.6 %collective-permute-start.15 = (bf16[4,2,128,128]{3,2,1,0:T(8,128)(2,1)S(1)}, bf16[4,2,128,128]{3,2,1,0:T(8,128)(2,1)S(1)}, u32[]{:S(2)}, u32[]{:S(2)}) collective-permute-start(bf16[4,2,128,128]{3,2,1,0:T(8,128)(2,1)S(1)} %get-tuple-element.73), channel_id=1, source_target_pairs={{0,8},{8,0},{16,24},{24,16},{1,9},{9,1},{17,25},{25,17},{2,10},{10... | collective-permute-start | bytes 786440 | tf_op jit(solution)/shard_map/ppermute | solution.py:253
  66.2 2.7 %base.1 = (bf16[8,4,128,128]{3,2,1,0:T(8,128)(2,1)}, f32[8,2,128,128]{3,2,1,0:T(8,128)S(1)}, f32[8,2,128,128]{3,2,1,0:T(8,128)S(1)}) custom-call(s32[4,8,128]{2,1,0:T(8,128)S(1)} %get-tuple-element.48.table, s32[4,8]{1,0:T(4,128)S(1)} %bitcast.9, f32[1024,512]{1,0:T(8,128)S(1)} %get-tuple-element.69.total, bf16[512,1024]{1,0:T(8,128)(2,1)S(1)} %get-tuple-element.56.turned, ...), custom_call_target="tpu_custom_call" | custom-call | flops 1073741824 | bytes 1024 | tf_op jit(solution)/shard_map/base/pallas_call | solution.py:31
  69.1 1.1 %collective-permute-start.18 = (bf16[4,2,128,128]{3,2,1,0:T(8,128)(2,1)S(1)}, bf16[4,2,128,128]{3,2,1,0:T(8,128)(2,1)S(1)}, u32[]{:S(2)}, u32[]{:S(2)}) collective-permute-start(bf16[4,2,128,128]{3,2,1,0:T(8,128)(2,1)S(1)} %get-tuple-element.78), channel_id=1, source_target_pairs={{0,8},{8,0},{16,24},{24,16},{1,9},{9,1},{17,25},{25,17},{2,10},{10... | collective-permute-start | bytes 786440 | tf_op jit(solution)/shard_map/ppermute | solution.py:253
  70.2 1.0 %collective-permute-start.19 = (bf16[4,2,128,128]{3,2,1,0:T(8,128)(2,1)S(1)}, bf16[4,2,128,128]{3,2,1,0:T(8,128)(2,1)S(1)}, u32[]{:S(2)}, u32[]{:S(2)}) collective-permute-start(bf16[4,2,128,128]{3,2,1,0:T(8,128)(2,1)S(1)} %get-tuple-element.79), channel_id=1, source_target_pairs={{0,16},{8,24},{16,0},{24,8},{1,17},{9,25},{17,1},{25,9},{2,18},{10... | collective-permute-start | bytes 786440 | tf_op jit(solution)/shard_map/ppermute | solution.py:253
  71.3 7.3 %squared.1 = bf16[8,4,128,128]{3,2,1,0:T(8,128)(2,1)} custom-call(s32[4,8,128]{2,1,0:T(8,128)S(1)} %get-tuple-element.48.table, s32[4,8]{1,0:T(4,128)S(1)} %bitcast.10, bf16[1024,2560]{1,0:T(8,128)(2,1)S(1)} %get-tuple-element.49.panel, bf16[1024,1536]{1,0:T(8,128)(2,1)S(1)} %get-tuple-element.55.panel_last, bf16[2064,128]{1,0:T(8,128)(2,1)S(1)} %pack_d.1.refs_0_, ...), custom_call_target="tpu_custom_call" | custom-call | flops 4294967296 | bytes 1024 | tf_op jit(solution)/shard_map/squared/pallas_call | solution.py:31
  78.6 1.2 %gradient.1 = bf16[8,2,128,128]{3,2,1,0:T(8,128)(2,1)} custom-call(f32[8,2,128,128]{3,2,1,0:T(8,128)S(1)} %get-tuple-element.71.direct, f32[8,2,128,128]{3,2,1,0:T(8,128)S(1)} %get-tuple-element.72.own, bf16[4,2,128,128]{3,2,1,0:T(8,128)(2,1)S(1)} %collective-permute-done.15.refs_0_, bf16[4,2,128,128]{3,2,1,0:T(8,128)(2,1)S(1)} %collective-permute-done.18.refs_1_, ...), custom_call_target="tpu_custom_call" | custom-call | bytes 1024 | tf_op jit(solution)/shard_map/gradient/pallas_call | solution.py:31
  (35 shorter events, 2.3 us)
Async XLA Ops:
  0.6 1.0 %copy-start = (bf16[8,2,128,128]{3,2,1,0:T(8,128)(2,1)S(1)}, bf16[8,2,128,128]{3,2,1,0:T(8,128)(2,1)}, u32[]{:S(2)}) copy-start(bf16[8,2,128,128]{3,2,1,0:T(8,128)(2,1)} %param.5) | copy-start | bytes 1572868
  1.7 0.7 copy-start.2
  2.4 17.3 %collective-permute-start.1 = (bf16[2064,128]{1,0:T(8,128)(2,1)S(1)}, bf16[2064,128]{1,0:T(8,128)(2,1)S(1)}, u32[]{:S(2)}, u32[]{:S(2)}) collective-permute-start(bf16[2064,128]{1,0:T(8,128)(2,1)S(1)} %pack_d.1.refs_0_), channel_id=1, source_target_pairs={{0,2},{2,4},{4,6},{6,0},{1,7},{3,1},{5,3},{7,5},{8,10},{10,12},{12... | collective-permute-start | bytes 1585160 | tf_op jit(solution)/shard_map/ppermute | solution.py:258
  5.5 1.0 %copy-start.1 = (bf16[8,2,128,128]{3,2,1,0:T(8,128)(2,1)S(1)}, bf16[8,2,128,128]{3,2,1,0:T(8,128)(2,1)}, u32[]{:S(2)}) copy-start(bf16[8,2,128,128]{3,2,1,0:T(8,128)(2,1)} %param.7) | copy-start | bytes 1572868
  6.5 0.7 copy-start.3
  7.2 0.7 copy-start.5
  7.9 14.4 %collective-permute-start.5 = (bf16[2064,128]{1,0:T(8,128)(2,1)S(1)}, bf16[2064,128]{1,0:T(8,128)(2,1)S(1)}, u32[]{:S(2)}, u32[]{:S(2)}) collective-permute-start(bf16[2064,128]{1,0:T(8,128)(2,1)S(1)} %pack_h.1.refs_5_), channel_id=1, source_target_pairs={{0,16},{8,24},{16,0},{24,8},{1,17},{9,25},{17,1},{25,9},{2,18},{10... | collective-permute-start | bytes 1585160 | tf_op jit(solution)/shard_map/ppermute | solution.py:253
  9.5 14.6 %collective-permute-start.4 = (bf16[2064,128]{1,0:T(8,128)(2,1)S(1)}, bf16[2064,128]{1,0:T(8,128)(2,1)S(1)}, u32[]{:S(2)}, u32[]{:S(2)}) collective-permute-start(bf16[2064,128]{1,0:T(8,128)(2,1)S(1)} %pack_h.1.refs_5_), channel_id=1, source_target_pairs={{0,8},{8,0},{16,24},{24,16},{1,9},{9,1},{17,25},{25,17},{2,10},{10... | collective-permute-start | bytes 1585160 | tf_op jit(solution)/shard_map/ppermute | solution.py:253
  19.7 14.6 %collective-permute-start.3 = (bf16[2064,128]{1,0:T(8,128)(2,1)S(1)}, bf16[2064,128]{1,0:T(8,128)(2,1)S(1)}, u32[]{:S(2)}, u32[]{:S(2)}) collective-permute-start(bf16[2064,128]{1,0:T(8,128)(2,1)S(1)} %collective-permute-done.1.refs_2_), channel_id=1, source_target_pairs={{0,2},{2,4},{4,6},{6,0},{1,7},{3,1},{5,3},{7,5},{8,10},{10,12},{12... | collective-permute-start | bytes 1585160 | tf_op jit(solution)/shard_map/ppermute | solution.py:258
  22.3 10.3 %collective-permute-start.7 = (bf16[1040,128]{1,0:T(8,128)(2,1)S(1)}, bf16[1040,128]{1,0:T(8,128)(2,1)S(1)}, u32[]{:S(2)}, u32[]{:S(2)}) collective-permute-start(bf16[1040,128]{1,0:T(8,128)(2,1)S(1)} %slice.17), channel_id=1, source_target_pairs={{0,8},{8,0},{16,24},{24,16},{1,9},{9,1},{17,25},{25,17},{2,10},{10... | collective-permute-start | bytes 798728 | tf_op jit(solution)/shard_map/ppermute | solution.py:253
  24.1 8.5 %collective-permute-start.6 = (bf16[1024,128]{1,0:T(8,128)(2,1)S(1)}, bf16[1024,128]{1,0:T(8,128)(2,1)S(1)}, u32[]{:S(2)}, u32[]{:S(2)}) collective-permute-start(bf16[1024,128]{1,0:T(8,128)(2,1)S(1)} %slice.16), channel_id=1, source_target_pairs={{0,16},{8,24},{16,0},{24,8},{1,17},{9,25},{17,1},{25,9},{2,18},{10... | collective-permute-start | bytes 786440 | tf_op jit(solution)/shard_map/ppermute | solution.py:253
  25.5 11.9 %collective-permute-start = (bf16[2064,128]{1,0:T(8,128)(2,1)S(1)}, bf16[2064,128]{1,0:T(8,128)(2,1)S(1)}, u32[]{:S(2)}, u32[]{:S(2)}) collective-permute-start(bf16[2064,128]{1,0:T(8,128)(2,1)S(1)} %pack_d.1.refs_0_), channel_id=1, source_target_pairs={{0,1},{1,0},{2,3},{3,2},{4,5},{5,4},{6,7},{7,6},{8,9},{9,8},{10,11... | collective-permute-start | bytes 1585160 | tf_op jit(solution)/shard_map/ppermute | solution.py:261
  25.6 12.9 %collective-permute-start.2 = (bf16[2064,128]{1,0:T(8,128)(2,1)S(1)}, bf16[2064,128]{1,0:T(8,128)(2,1)S(1)}, u32[]{:S(2)}, u32[]{:S(2)}) collective-permute-start(bf16[2064,128]{1,0:T(8,128)(2,1)S(1)} %collective-permute-done.1.refs_2_), channel_id=1, source_target_pairs={{0,1},{1,0},{2,3},{3,2},{4,5},{5,4},{6,7},{7,6},{8,9},{9,8},{10,11... | collective-permute-start | bytes 1585160 | tf_op jit(solution)/shard_map/ppermute | solution.py:261
  34.2 11.9 %collective-permute-start.10 = (bf16[2064,128]{1,0:T(8,128)(2,1)S(1)}, bf16[2064,128]{1,0:T(8,128)(2,1)S(1)}, u32[]{:S(2)}, u32[]{:S(2)}) collective-permute-start(bf16[2064,128]{1,0:T(8,128)(2,1)S(1)} %pack_d.1.refs_0_), channel_id=1, source_target_pairs={{0,16},{8,24},{16,0},{24,8},{1,17},{9,25},{17,1},{25,9},{2,18},{10... | collective-permute-start | bytes 1585160 | tf_op jit(solution)/shard_map/ppermute | solution.py:253
  35.8 13.9 %collective-permute-start.8 = (bf16[2064,128]{1,0:T(8,128)(2,1)S(1)}, bf16[2064,128]{1,0:T(8,128)(2,1)S(1)}, u32[]{:S(2)}, u32[]{:S(2)}) collective-permute-start(bf16[2064,128]{1,0:T(8,128)(2,1)S(1)} %collective-permute-done.3.refs_4_), channel_id=1, source_target_pairs={{0,2},{2,4},{4,6},{6,0},{1,7},{3,1},{5,3},{7,5},{8,10},{10,12},{12... | collective-permute-start | bytes 1585160 | tf_op jit(solution)/shard_map/ppermute | solution.py:258
  35.9 14.5 %collective-permute-start.9 = (bf16[2064,128]{1,0:T(8,128)(2,1)S(1)}, bf16[2064,128]{1,0:T(8,128)(2,1)S(1)}, u32[]{:S(2)}, u32[]{:S(2)}) collective-permute-start(bf16[2064,128]{1,0:T(8,128)(2,1)S(1)} %pack_d.1.refs_0_), channel_id=1, source_target_pairs={{0,8},{8,0},{16,24},{24,16},{1,9},{9,1},{17,25},{25,17},{2,10},{10... | collective-permute-start | bytes 1585160 | tf_op jit(solution)/shard_map/ppermute | solution.py:253
  37.4 15.4 %collective-permute-start.11 = (bf16[2064,128]{1,0:T(8,128)(2,1)S(1)}, bf16[2064,128]{1,0:T(8,128)(2,1)S(1)}, u32[]{:S(2)}, u32[]{:S(2)}) collective-permute-start(bf16[2064,128]{1,0:T(8,128)(2,1)S(1)} %collective-permute-done.3.refs_4_), channel_id=1, source_target_pairs={{0,1},{1,0},{2,3},{3,2},{4,5},{5,4},{6,7},{7,6},{8,9},{9,8},{10,11... | collective-permute-start | bytes 1585160 | tf_op jit(solution)/shard_map/ppermute | solution.py:261
  50.4 2.4 %collective-permute-start.12 = (bf16[2064,128]{1,0:T(8,128)(2,1)S(1)}, bf16[2064,128]{1,0:T(8,128)(2,1)S(1)}, u32[]{:S(2)}, u32[]{:S(2)}) collective-permute-start(bf16[2064,128]{1,0:T(8,128)(2,1)S(1)} %collective-permute-done.8.refs_1_), channel_id=1, source_target_pairs={{0,1},{1,0},{2,3},{3,2},{4,5},{5,4},{6,7},{7,6},{8,9},{9,8},{10,11... | collective-permute-start | bytes 1585160 | tf_op jit(solution)/shard_map/ppermute | solution.py:261
  50.6 13.6 %collective-permute-start.13 = (bf16[1024,128]{1,0:T(8,128)(2,1)S(1)}, bf16[1024,128]{1,0:T(8,128)(2,1)S(1)}, u32[]{:S(2)}, u32[]{:S(2)}) collective-permute-start(bf16[1024,128]{1,0:T(8,128)(2,1)S(1)} %slice.14), channel_id=1, source_target_pairs={{0,16},{8,24},{16,0},{24,8},{1,17},{9,25},{17,1},{25,9},{2,18},{10... | collective-permute-start | bytes 786440 | tf_op jit(solution)/shard_map/ppermute | solution.py:253
  51.2 13.0 %collective-permute-start.14 = (bf16[1024,128]{1,0:T(8,128)(2,1)S(1)}, bf16[1024,128]{1,0:T(8,128)(2,1)S(1)}, u32[]{:S(2)}, u32[]{:S(2)}) collective-permute-start(bf16[1024,128]{1,0:T(8,128)(2,1)S(1)} %slice.15), channel_id=1, source_target_pairs={{0,8},{8,0},{16,24},{24,16},{1,9},{9,1},{17,25},{25,17},{2,10},{10... | collective-permute-start | bytes 786440 | tf_op jit(solution)/shard_map/ppermute | solution.py:253
  58.1 10.9 %collective-permute-start.16 = (bf16[4,2,128,128]{3,2,1,0:T(8,128)(2,1)S(1)}, bf16[4,2,128,128]{3,2,1,0:T(8,128)(2,1)S(1)}, u32[]{:S(2)}, u32[]{:S(2)}) collective-permute-start(bf16[4,2,128,128]{3,2,1,0:T(8,128)(2,1)S(1)} %get-tuple-element.75), channel_id=1, source_target_pairs={{0,8},{8,0},{16,24},{24,16},{1,9},{9,1},{17,25},{25,17},{2,10},{10... | collective-permute-start | bytes 786440 | tf_op jit(solution)/shard_map/ppermute | solution.py:253
  59.2 9.8 %collective-permute-start.17 = (bf16[4,2,128,128]{3,2,1,0:T(8,128)(2,1)S(1)}, bf16[4,2,128,128]{3,2,1,0:T(8,128)(2,1)S(1)}, u32[]{:S(2)}, u32[]{:S(2)}) collective-permute-start(bf16[4,2,128,128]{3,2,1,0:T(8,128)(2,1)S(1)} %get-tuple-element.77), channel_id=1, source_target_pairs={{0,16},{8,24},{16,0},{24,8},{1,17},{9,25},{17,1},{25,9},{2,18},{10... | collective-permute-start | bytes 786440 | tf_op jit(solution)/shard_map/ppermute | solution.py:253
  60.2 6.1 %copy-start.4 = (s32[8,4]{0,1:T(4,128)S(1)}, s32[8,4]{0,1:T(4,128)}, u32[]{:S(2)}) copy-start(s32[8,4]{0,1:T(4,128)} %param.9) | copy-start | bytes 388
  64.2 14.4 %collective-permute-start.15 = (bf16[4,2,128,128]{3,2,1,0:T(8,128)(2,1)S(1)}, bf16[4,2,128,128]{3,2,1,0:T(8,128)(2,1)S(1)}, u32[]{:S(2)}, u32[]{:S(2)}) collective-permute-start(bf16[4,2,128,128]{3,2,1,0:T(8,128)(2,1)S(1)} %get-tuple-element.73), channel_id=1, source_target_pairs={{0,8},{8,0},{16,24},{24,16},{1,9},{9,1},{17,25},{25,17},{2,10},{10... | collective-permute-start | bytes 786440 | tf_op jit(solution)/shard_map/ppermute | solution.py:253
  65.7 12.8 %collective-permute-start.20 = (bf16[4,2,128,128]{3,2,1,0:T(8,128)(2,1)S(1)}, bf16[4,2,128,128]{3,2,1,0:T(8,128)(2,1)S(1)}, u32[]{:S(2)}, u32[]{:S(2)}) collective-permute-start(bf16[4,2,128,128]{3,2,1,0:T(8,128)(2,1)S(1)} %get-tuple-element.80), channel_id=1, source_target_pairs={{0,16},{8,24},{16,0},{24,8},{1,17},{9,25},{17,1},{25,9},{2,18},{10... | collective-permute-start | bytes 786440 | tf_op jit(solution)/shard_map/ppermute | solution.py:253
  69.1 9.4 %collective-permute-start.18 = (bf16[4,2,128,128]{3,2,1,0:T(8,128)(2,1)S(1)}, bf16[4,2,128,128]{3,2,1,0:T(8,128)(2,1)S(1)}, u32[]{:S(2)}, u32[]{:S(2)}) collective-permute-start(bf16[4,2,128,128]{3,2,1,0:T(8,128)(2,1)S(1)} %get-tuple-element.78), channel_id=1, source_target_pairs={{0,8},{8,0},{16,24},{24,16},{1,9},{9,1},{17,25},{25,17},{2,10},{10... | collective-permute-start | bytes 786440 | tf_op jit(solution)/shard_map/ppermute | solution.py:253
  70.2 8.4 %collective-permute-start.19 = (bf16[4,2,128,128]{3,2,1,0:T(8,128)(2,1)S(1)}, bf16[4,2,128,128]{3,2,1,0:T(8,128)(2,1)S(1)}, u32[]{:S(2)}, u32[]{:S(2)}) collective-permute-start(bf16[4,2,128,128]{3,2,1,0:T(8,128)(2,1)S(1)} %get-tuple-element.79), channel_id=1, source_target_pairs={{0,16},{8,24},{16,0},{24,8},{1,17},{9,25},{17,1},{25,9},{2,18},{10... | collective-permute-start | bytes 786440 | tf_op jit(solution)/shard_map/ppermute | solution.py:253

commit v7 on v6

--- a/solution.py
+++ b/solution.py
@@ -9,6 +9,7 @@
 from jax.sharding import PartitionSpec as P
 
 VMEM_ROOM = 6 * 1024 * 1024
+N_LAST = 3
 TAIL = 16
 BF16, F32 = jnp.bfloat16, jnp.float32
 
@@ -21,7 +22,7 @@
         self.nb = self.rows * n_row
         self.bc = self.nb // n_col
         self.tall, self.wide = self.rows * self.bs, self.bc * self.bs
-        self.n_first, self.n_last = n_col - 3, 3
+        self.n_first, self.n_last = n_col - N_LAST, N_LAST
 
 
 def call(kernel, ins, outs, scratch, in_specs, out_specs, flops, name):
@@ -50,18 +51,21 @@
 
 def piece_col(z, n):
     me = lax.axis_index("col")
-    step, core = n // 2, lax.rem(me, 2) ^ (n % 2)
-    up = lax.rem(me // 2 + step, z.n_chip)
-    down = lax.rem(me // 2 + z.n_chip - step, z.n_chip)
-    return jnp.where(core == 0, down, up) * 2 + core
+    hops, core = (n // 2 + 1) // 2, lax.rem(me, 2) ^ (n % 2)
+    up = lax.rem(me // 2 + hops, z.n_chip)
+    down = lax.rem(me // 2 + z.n_chip - hops, z.n_chip)
+    behind = 0 if n // 2 % 2 else 1
+    return jnp.where(core == behind, down, up) * 2 + core
 
 
 def piece_of(z, col):
     me = lax.axis_index("col")
     chip, core = col // 2, lax.rem(col, 2)
-    ahead = lax.rem(chip - me // 2 + z.n_chip, z.n_chip)
-    behind = lax.rem(me // 2 - chip + z.n_chip, z.n_chip)
-    return jnp.where(core == 0, behind, ahead) * 2 + (core ^ lax.rem(me, 2))
+    up = lax.rem(chip - me // 2 + z.n_chip, z.n_chip)
+    down = lax.rem(me // 2 - chip + z.n_chip, z.n_chip)
+    hops = jnp.where(core == 0, down, up)
+    step = jnp.where(2 * hops <= z.n_chip, jnp.maximum(2 * hops - 1, 0), 2 * (z.n_chip - hops))
+    return step * 2 + (core ^ lax.rem(me, 2))
 
 
 def pack_kernel(z, vals_in, *refs):
@@ -252,10 +256,9 @@
     def over_row(x, flip):
         return lax.ppermute(x, "row", [(r, r ^ flip) for r in range(n_row)])
 
-    def next_chip(x):
-        pairs = [(2 * p, 2 * ((p + 1) % z.n_chip)) for p in range(z.n_chip)]
-        pairs += [(2 * p + 1, 2 * ((p - 1) % z.n_chip) + 1) for p in range(z.n_chip)]
-        return lax.ppermute(x, "col", pairs)
+    def next_chip(x, up):
+        move = {0: up, 1: -up}
+        return lax.ppermute(x, "col", [(c, (c // 2 + move[c % 2]) % z.n_chip * 2 + c % 2) for c in range(n_col)])
 
     def other_core(x):
         return lax.ppermute(x, "col", [(c, c ^ 1) for c in range(n_col)])
@@ -280,24 +283,26 @@
             if flip not in blocks:
                 blocks[flip] = [over_row(blocks[flip & (flip - 1)][0], flip & -flip)]
 
-    left, piece = [d_pay, other_core(d_pay)], d_pay
-    h_right, d_0 = {0: [h_pay]}, d_pay
-    for step in range(1, z.n_chip):
-        piece = next_chip(piece)
-        if step == 1:
-            for flip in single:
-                h_right[flip] = [over_row(h_pay, flip)]
-        if step == 2:
-            if n_row == 4:
-                h_right[3] = [over_row(h_right[1][0][:h_half], 2), over_row(h_right[2][0][h_half:], 1)]
-            forward(h_right)
-            piece, h_right, d_0 = lax.optimization_barrier((piece, h_right, d_0))
-            d_right = {0: [d_0]}
-            for flip in single:
-                d_right[flip] = [over_row(d_0, flip)]
+    pieces = [d_pay, next_chip(d_pay, 1)]
+    h_right = {0: [h_pay]}
+    for flip in single:
+        h_right[flip] = [over_row(h_pay, flip)]
+    pieces.append(next_chip(d_pay, -1))
+    pieces[1], h_right, twin = lax.optimization_barrier((pieces[1], h_right, other_core(d_pay)))
+    if n_row == 4:
+        h_right[3] = [over_row(h_right[1][0][:h_half], 2), over_row(h_right[2][0][h_half:], 1)]
+    forward(h_right)
+    d_0, pieces[2] = lax.optimization_barrier((d_pay, pieces[2]))
+    for step in range(3, z.n_chip):
+        pieces.append(next_chip(pieces[step - 2], 1 if step % 2 else -1))
+    d_right = {0: [d_0]}
+    for flip in single:
+        d_right[flip] = [over_row(d_0, flip)]
+    left = []
+    for step, piece in enumerate(pieces):
         left.append(piece)
         if step < z.n_chip - 1:
-            left.append(other_core(piece))
+            left.append(other_core(piece) if step else twin)
     h_right = [h_right[flip] for flip in range(n_row)]
 
     n_pay = z.n_first + n_row
@@ -318,7 +323,7 @@
         ],
         [vmem] * (z.n_first + sum(map(len, h_right))), [vmem] * 4, 0, "first",
     )
-    last, total, d_right = lax.optimization_barrier((left[-1], total, d_right))
+    last, total = lax.optimization_barrier((left[-1], total))
     if n_row == 4:
         d_right[3] = [over_row(d_right[1][0][:d_half], 2), over_row(d_right[2][0][d_half:d_rows], 1)]
     forward(d_right)

time: 80 us -> 79.3 us (level)
  the two profiles are of different devices: /device:TPU:0 before, /device:TPU:24 now
where the time goes in v7:
time: 79.3 us; the launch traced here: 79.1 us
  Pallas kernels  26.5 us (33%)
  waiting for transfers between devices  24.8 us (31%)
  starting transfers between devices  22.7 us (29%)
  local copies, waits for them, and re-layouts  4.18 us (5%)
  between operations  0.87 us (1%)
    pallas_call x9, Pallas kernels, call(): pl.pallas_call(kernel, out_shape=outs, in_specs=in_specs, out_specs=out_s...  26.5 us
    ppermute x14, starting transfers between devices, over_row(): return lax.ppermute(x, 'row', [(r, r ^ flip) for r in range(n_row)])  20.1 us
    ppermute x3, waiting for transfers between devices, next_chip(): lax.ppermute(x, 'col', [(c, (c // 2 + move[c % 2]) % z.n_chip * 2 + c % 2...  14.2 us
    ppermute x14, waiting for transfers between devices, over_row(): return lax.ppermute(x, 'row', [(r, r ^ flip) for r in range(n_row)])  10.6 us
    unnamed x12, local copies, waits for them, and re-layouts  4.11 us
    ppermute x3, starting transfers between devices, next_chip(): lax.ppermute(x, 'col', [(c, (c // 2 + move[c % 2]) % z.n_chip * 2 + c % 2...  1.92 us
  transfers between devices with their start and end apart: 21, of which 4 were waited for; matrix products, arithmetic and copies ran while one was open for 0% of the time, Pallas kernels for 32%

profile of v7, /device:TPU:24, one launch (start us, length us, event | category | flops | bytes accessed | tf_op | source)
XLA Modules:
  0.0 79.1 jit_solution(17388473219660116859)
XLA Ops:
  0.6 1.0 %copy-done = bf16[8,2,128,128]{3,2,1,0:T(8,128)(2,1)S(1)} copy-done((bf16[8,2,128,128]{3,2,1,0:T(8,128)(2,1)S(1)}, bf16[8,2,128,128]{3,2,1,0:T(8,128)(2,1)}, u32[]{:S(2)}) %copy-start) | copy-done | bytes 524312
  1.7 0.7 copy-done.2
  2.5 1.0 %copy-done.1 = bf16[8,2,128,128]{3,2,1,0:T(8,128)(2,1)S(1)} copy-done((bf16[8,2,128,128]{3,2,1,0:T(8,128)(2,1)S(1)}, bf16[8,2,128,128]{3,2,1,0:T(8,128)(2,1)}, u32[]{:S(2)}) %copy-start.1) | copy-done | bytes 524312
  3.6 0.7 copy-done.3
  4.3 0.7 copy-done.5
  5.0 1.7 %collective-permute-start.1 = (bf16[2064,128]{1,0:T(8,128)(2,1)S(1)}, bf16[2064,128]{1,0:T(8,128)(2,1)S(1)}, u32[]{:S(2)}, u32[]{:S(2)}) collective-permute-start(bf16[2064,128]{1,0:T(8,128)(2,1)S(1)} %pack_h.1.refs_5_), channel_id=1, source_target_pairs={{0,8},{8,0},{16,24},{24,16},{1,9},{9,1},{17,25},{25,17},{2,10},{10... | collective-permute-start | bytes 1585160 | tf_op jit(solution)/shard_map/ppermute | solution.py:257
  6.7 1.5 %collective-permute-start.2 = (bf16[2064,128]{1,0:T(8,128)(2,1)S(1)}, bf16[2064,128]{1,0:T(8,128)(2,1)S(1)}, u32[]{:S(2)}, u32[]{:S(2)}) collective-permute-start(bf16[2064,128]{1,0:T(8,128)(2,1)S(1)} %pack_h.1.refs_5_), channel_id=1, source_target_pairs={{0,16},{8,24},{16,0},{24,8},{1,17},{9,25},{17,1},{25,9},{2,18},{10... | collective-permute-start | bytes 1585160 | tf_op jit(solution)/shard_map/ppermute | solution.py:257
  8.2 1.8 %collective-permute-start.5 = (bf16[2064,128]{1,0:T(8,128)(2,1)S(1)}, bf16[2064,128]{1,0:T(8,128)(2,1)S(1)}, u32[]{:S(2)}, u32[]{:S(2)}) collective-permute-start(bf16[2064,128]{1,0:T(8,128)(2,1)S(1)} %pack_d.1.refs_0_), channel_id=1, source_target_pairs={{0,6},{1,3},{2,0},{3,5},{4,2},{5,7},{6,4},{7,1},{8,14},{9,11},{10,... | collective-permute-start | bytes 1585160 | tf_op jit(solution)/shard_map/ppermute | solution.py:261
  10.0 14.2 %collective-permute-done.refs_2_ = bf16[2064,128]{1,0:T(8,128)(2,1)S(1)} collective-permute-done((bf16[2064,128]{1,0:T(8,128)(2,1)S(1)}, bf16[2064,128]{1,0:T(8,128)(2,1)S(1)}, u32[]{:S(2)}, u32[]{:S(2)}) %collective-permute-start) | collective-permute-done | bytes 528416 | tf_op jit(solution)/shard_map/ppermute | solution.py:261
  24.2 0.1 collective-permute-start.4
  24.4 2.5 %collective-permute-start.7 = (bf16[1040,128]{1,0:T(8,128)(2,1)S(1)}, bf16[1040,128]{1,0:T(8,128)(2,1)S(1)}, u32[]{:S(2)}, u32[]{:S(2)}) collective-permute-start(bf16[1040,128]{1,0:T(8,128)(2,1)S(1)} %slice.13), channel_id=1, source_target_pairs={{0,8},{8,0},{16,24},{24,16},{1,9},{9,1},{17,25},{25,17},{2,10},{10... | collective-permute-start | bytes 798728 | tf_op jit(solution)/shard_map/ppermute | solution.py:257
  26.9 2.6 %collective-permute-start.6 = (bf16[1024,128]{1,0:T(8,128)(2,1)S(1)}, bf16[1024,128]{1,0:T(8,128)(2,1)S(1)}, u32[]{:S(2)}, u32[]{:S(2)}) collective-permute-start(bf16[1024,128]{1,0:T(8,128)(2,1)S(1)} %slice.12), channel_id=1, source_target_pairs={{0,16},{8,24},{16,0},{24,8},{1,17},{9,25},{17,1},{25,9},{2,18},{10... | collective-permute-start | bytes 786440 | tf_op jit(solution)/shard_map/ppermute | solution.py:257
  29.5 6.6 %collective-permute-done.6.refs_8_ = bf16[1024,128]{1,0:T(8,128)(2,1)S(1)} collective-permute-done((bf16[1024,128]{1,0:T(8,128)(2,1)S(1)}, bf16[1024,128]{1,0:T(8,128)(2,1)S(1)}, u32[]{:S(2)}, u32[]{:S(2)}) %collective-permute-start.6) | collective-permute-done | bytes 262176 | tf_op jit(solution)/shard_map/ppermute | solution.py:257
  36.1 1.7 %collective-permute-start.12 = (bf16[2064,128]{1,0:T(8,128)(2,1)S(1)}, bf16[2064,128]{1,0:T(8,128)(2,1)S(1)}, u32[]{:S(2)}, u32[]{:S(2)}) collective-permute-start(bf16[2064,128]{1,0:T(8,128)(2,1)S(1)} %pack_d.1.refs_0_), channel_id=1, source_target_pairs={{0,16},{8,24},{16,0},{24,8},{1,17},{9,25},{17,1},{25,9},{2,18},{10... | collective-permute-start | bytes 1585160 | tf_op jit(solution)/shard_map/ppermute | solution.py:257
  37.9 5.7 %first.1 = (f32[1024,512]{1,0:T(8,128)S(1)}, bf16[1024,2560]{1,0:T(8,128)(2,1)S(1)}, bf16[1536,512]{1,0:T(8,128)(2,1)S(1)}, s32[4,8,128]{2,1,0:T(8,128)S(1)}) custom-call(bf16[2064,128]{1,0:T(8,128)(2,1)S(1)} %pack_d.1.refs_0_, bf16[2064,128]{1,0:T(8,128)(2,1)S(1)} %collective-permute-done.3.refs_1_, bf16[2064,128]{1,0:T(8,128)(2,1)S(1)} %collective-permute-done.refs_2_, ...), custom_call_target="tpu_custom_call" | custom-call | bytes 1024 | tf_op jit(solution)/shard_map/first/pallas_call | solution.py:32
  43.6 0.6 collective-permute-start.10
  44.2 1.0 %collective-permute-done.11.refs_1_ = bf16[2064,128]{1,0:T(8,128)(2,1)S(1)} collective-permute-done((bf16[2064,128]{1,0:T(8,128)(2,1)S(1)}, bf16[2064,128]{1,0:T(8,128)(2,1)S(1)}, u32[]{:S(2)}, u32[]{:S(2)}) %collective-permute-start.11) | collective-permute-done | bytes 528416 | tf_op jit(solution)/shard_map/ppermute | solution.py:257
  45.2 2.6 %collective-permute-start.13 = (bf16[1024,128]{1,0:T(8,128)(2,1)S(1)}, bf16[1024,128]{1,0:T(8,128)(2,1)S(1)}, u32[]{:S(2)}, u32[]{:S(2)}) collective-permute-start(bf16[1024,128]{1,0:T(8,128)(2,1)S(1)} %slice.16), channel_id=1, source_target_pairs={{0,16},{8,24},{16,0},{24,8},{1,17},{9,25},{17,1},{25,9},{2,18},{10... | collective-permute-start | bytes 786440 | tf_op jit(solution)/shard_map/ppermute | solution.py:257
  47.8 3.0 %collective-permute-done.12.refs_2_ = bf16[2064,128]{1,0:T(8,128)(2,1)S(1)} collective-permute-done((bf16[2064,128]{1,0:T(8,128)(2,1)S(1)}, bf16[2064,128]{1,0:T(8,128)(2,1)S(1)}, u32[]{:S(2)}, u32[]{:S(2)}) %collective-permute-start.12) | collective-permute-done | bytes 528416 | tf_op jit(solution)/shard_map/ppermute | solution.py:257
  50.8 0.1 collective-permute-start.14
  50.9 5.3 %last.1 = (f32[1024,512]{1,0:T(8,128)S(1)}, bf16[512,1024]{1,0:T(8,128)(2,1)S(1)}, bf16[1024,1536]{1,0:T(8,128)(2,1)S(1)}, bf16[4,2,128,128]{3,2,1,0:T(8,128)(2,1)S(1)}, bf16[4,2,128,128]{3,2,1,0:T(8,128)(2,1)S(1)}) custom-call(s32[4,8,128]{2,1,0:T(8,128)S(1)} %get-tuple-element.45.table, bf16[1536,512]{1,0:T(8,128)(2,1)S(1)} %get-tuple-element.47.right, ...), custom_call_target="tpu_custom_call" | custom-call | flops 2147483648 | bytes 1024 | tf_op jit(solution)/shard_map/last/pallas_call | solution.py:32
  56.3 2.1 %collective-permute-start.16 = (bf16[4,2,128,128]{3,2,1,0:T(8,128)(2,1)S(1)}, bf16[4,2,128,128]{3,2,1,0:T(8,128)(2,1)S(1)}, u32[]{:S(2)}, u32[]{:S(2)}) collective-permute-start(bf16[4,2,128,128]{3,2,1,0:T(8,128)(2,1)S(1)} %get-tuple-element.69), channel_id=1, source_target_pairs={{0,8},{8,0},{16,24},{24,16},{1,9},{9,1},{17,25},{25,17},{2,10},{10... | collective-permute-start | bytes 786440 | tf_op jit(solution)/shard_map/ppermute | solution.py:257
  58.3 1.1 %collective-permute-start.17 = (bf16[4,2,128,128]{3,2,1,0:T(8,128)(2,1)S(1)}, bf16[4,2,128,128]{3,2,1,0:T(8,128)(2,1)S(1)}, u32[]{:S(2)}, u32[]{:S(2)}) collective-permute-start(bf16[4,2,128,128]{3,2,1,0:T(8,128)(2,1)S(1)} %get-tuple-element.71), channel_id=1, source_target_pairs={{0,16},{8,24},{16,0},{24,8},{1,17},{9,25},{17,1},{25,9},{2,18},{10... | collective-permute-start | bytes 786440 | tf_op jit(solution)/shard_map/ppermute | solution.py:257
  59.4 4.0 %parts.1 = (bf16[4,2,128,128]{3,2,1,0:T(8,128)(2,1)S(1)}, bf16[4,2,128,128]{3,2,1,0:T(8,128)(2,1)S(1)}, bf16[4,2,128,128]{3,2,1,0:T(8,128)(2,1)S(1)}, bf16[4,2,128,128]{3,2,1,0:T(8,128)(2,1)S(1)}) custom-call(s32[4,8,128]{2,1,0:T(8,128)S(1)} %get-tuple-element.45.table, bf16[512,1024]{1,0:T(8,128)(2,1)S(1)} %get-tuple-element.52.turned, ...), custom_call_target="tpu_custom_call" | custom-call | flops 2147483648 | bytes 1024 | tf_op jit(solution)/shard_map/parts/pallas_call | solution.py:32
  63.4 0.1 collective-permute-start.15
  63.6 0.9 %collective-permute-start.20 = (bf16[4,2,128,128]{3,2,1,0:T(8,128)(2,1)S(1)}, bf16[4,2,128,128]{3,2,1,0:T(8,128)(2,1)S(1)}, u32[]{:S(2)}, u32[]{:S(2)}) collective-permute-start(bf16[4,2,128,128]{3,2,1,0:T(8,128)(2,1)S(1)} %get-tuple-element.74), channel_id=1, source_target_pairs={{0,16},{8,24},{16,0},{24,8},{1,17},{9,25},{17,1},{25,9},{2,18},{10... | collective-permute-start | bytes 786440 | tf_op jit(solution)/shard_map/ppermute | solution.py:257
  64.5 2.7 %base.1 = (bf16[8,4,128,128]{3,2,1,0:T(8,128)(2,1)}, f32[8,2,128,128]{3,2,1,0:T(8,128)S(1)}, f32[8,2,128,128]{3,2,1,0:T(8,128)S(1)}) custom-call(s32[4,8,128]{2,1,0:T(8,128)S(1)} %get-tuple-element.45.table, s32[4,8]{1,0:T(4,128)S(1)} %bitcast.9, f32[1024,512]{1,0:T(8,128)S(1)} %get-tuple-element.63.total, bf16[512,1024]{1,0:T(8,128)(2,1)S(1)} %get-tuple-element.52.turned, ...), custom_call_target="tpu_custom_call" | custom-call | flops 1073741824 | bytes 1024 | tf_op jit(solution)/shard_map/base/pallas_call | solution.py:32
  67.3 0.1 add.1
  67.4 2.0 %collective-permute-start.18 = (bf16[4,2,128,128]{3,2,1,0:T(8,128)(2,1)S(1)}, bf16[4,2,128,128]{3,2,1,0:T(8,128)(2,1)S(1)}, u32[]{:S(2)}, u32[]{:S(2)}) collective-permute-start(bf16[4,2,128,128]{3,2,1,0:T(8,128)(2,1)S(1)} %get-tuple-element.72), channel_id=1, source_target_pairs={{0,8},{8,0},{16,24},{24,16},{1,9},{9,1},{17,25},{25,17},{2,10},{10... | collective-permute-start | bytes 786440 | tf_op jit(solution)/shard_map/ppermute | solution.py:257
  69.4 1.1 %collective-permute-start.19 = (bf16[4,2,128,128]{3,2,1,0:T(8,128)(2,1)S(1)}, bf16[4,2,128,128]{3,2,1,0:T(8,128)(2,1)S(1)}, u32[]{:S(2)}, u32[]{:S(2)}) collective-permute-start(bf16[4,2,128,128]{3,2,1,0:T(8,128)(2,1)S(1)} %get-tuple-element.73), channel_id=1, source_target_pairs={{0,16},{8,24},{16,0},{24,8},{1,17},{9,25},{17,1},{25,9},{2,18},{10... | collective-permute-start | bytes 786440 | tf_op jit(solution)/shard_map/ppermute | solution.py:257
  70.5 7.3 %squared.1 = bf16[8,4,128,128]{3,2,1,0:T(8,128)(2,1)} custom-call(s32[4,8,128]{2,1,0:T(8,128)S(1)} %get-tuple-element.45.table, s32[4,8]{1,0:T(4,128)S(1)} %bitcast.10, bf16[1024,2560]{1,0:T(8,128)(2,1)S(1)} %get-tuple-element.46.panel, bf16[1024,1536]{1,0:T(8,128)(2,1)S(1)} %get-tuple-element.51.panel_last, bf16[2064,128]{1,0:T(8,128)(2,1)S(1)} %pack_d.1.refs_0_, ...), custom_call_target="tpu_custom_call" | custom-call | flops 4294967296 | bytes 1024 | tf_op jit(solution)/shard_map/squared/pallas_call | solution.py:32
  77.9 1.2 %gradient.1 = bf16[8,2,128,128]{3,2,1,0:T(8,128)(2,1)} custom-call(f32[8,2,128,128]{3,2,1,0:T(8,128)S(1)} %get-tuple-element.65.direct, f32[8,2,128,128]{3,2,1,0:T(8,128)S(1)} %get-tuple-element.66.own, bf16[4,2,128,128]{3,2,1,0:T(8,128)(2,1)S(1)} %collective-permute-done.15.refs_0_, bf16[4,2,128,128]{3,2,1,0:T(8,128)(2,1)S(1)} %collective-permute-done.18.refs_1_, ...), custom_call_target="tpu_custom_call" | custom-call | bytes 1024 | tf_op jit(solution)/shard_map/gradient/pallas_call | solution.py:32
  (35 shorter events, 0.4 us)
Async XLA Ops:
  0.6 1.0 %copy-start = (bf16[8,2,128,128]{3,2,1,0:T(8,128)(2,1)S(1)}, bf16[8,2,128,128]{3,2,1,0:T(8,128)(2,1)}, u32[]{:S(2)}) copy-start(bf16[8,2,128,128]{3,2,1,0:T(8,128)(2,1)} %param.5) | copy-start | bytes 1572868
  1.7 0.7 copy-start.2
  2.4 21.8 %collective-permute-start = (bf16[2064,128]{1,0:T(8,128)(2,1)S(1)}, bf16[2064,128]{1,0:T(8,128)(2,1)S(1)}, u32[]{:S(2)}, u32[]{:S(2)}) collective-permute-start(bf16[2064,128]{1,0:T(8,128)(2,1)S(1)} %pack_d.1.refs_0_), channel_id=1, source_target_pairs={{0,2},{1,7},{2,4},{3,1},{4,6},{5,3},{6,0},{7,5},{8,10},{9,15},{10,... | collective-permute-start | bytes 1585160 | tf_op jit(solution)/shard_map/ppermute | solution.py:261
  2.5 21.7 %collective-permute-start.3 = (bf16[2064,128]{1,0:T(8,128)(2,1)S(1)}, bf16[2064,128]{1,0:T(8,128)(2,1)S(1)}, u32[]{:S(2)}, u32[]{:S(2)}) collective-permute-start(bf16[2064,128]{1,0:T(8,128)(2,1)S(1)} %pack_d.1.refs_0_), channel_id=1, source_target_pairs={{0,1},{1,0},{2,3},{3,2},{4,5},{5,4},{6,7},{7,6},{8,9},{9,8},{10,11... | collective-permute-start | bytes 1585160 | tf_op jit(solution)/shard_map/ppermute | solution.py:264
  2.5 1.0 %copy-start.1 = (bf16[8,2,128,128]{3,2,1,0:T(8,128)(2,1)S(1)}, bf16[8,2,128,128]{3,2,1,0:T(8,128)(2,1)}, u32[]{:S(2)}) copy-start(bf16[8,2,128,128]{3,2,1,0:T(8,128)(2,1)} %param.7) | copy-start | bytes 1572868
  3.6 0.7 copy-start.3
  4.3 0.7 copy-start.5
  5.0 19.2 %collective-permute-start.1 = (bf16[2064,128]{1,0:T(8,128)(2,1)S(1)}, bf16[2064,128]{1,0:T(8,128)(2,1)S(1)}, u32[]{:S(2)}, u32[]{:S(2)}) collective-permute-start(bf16[2064,128]{1,0:T(8,128)(2,1)S(1)} %pack_h.1.refs_5_), channel_id=1, source_target_pairs={{0,8},{8,0},{16,24},{24,16},{1,9},{9,1},{17,25},{25,17},{2,10},{10... | collective-permute-start | bytes 1585160 | tf_op jit(solution)/shard_map/ppermute | solution.py:257
  6.7 17.5 %collective-permute-start.2 = (bf16[2064,128]{1,0:T(8,128)(2,1)S(1)}, bf16[2064,128]{1,0:T(8,128)(2,1)S(1)}, u32[]{:S(2)}, u32[]{:S(2)}) collective-permute-start(bf16[2064,128]{1,0:T(8,128)(2,1)S(1)} %pack_h.1.refs_5_), channel_id=1, source_target_pairs={{0,16},{8,24},{16,0},{24,8},{1,17},{9,25},{17,1},{25,9},{2,18},{10... | collective-permute-start | bytes 1585160 | tf_op jit(solution)/shard_map/ppermute | solution.py:257
  8.2 21.3 %collective-permute-start.5 = (bf16[2064,128]{1,0:T(8,128)(2,1)S(1)}, bf16[2064,128]{1,0:T(8,128)(2,1)S(1)}, u32[]{:S(2)}, u32[]{:S(2)}) collective-permute-start(bf16[2064,128]{1,0:T(8,128)(2,1)S(1)} %pack_d.1.refs_0_), channel_id=1, source_target_pairs={{0,6},{1,3},{2,0},{3,5},{4,2},{5,7},{6,4},{7,1},{8,14},{9,11},{10,... | collective-permute-start | bytes 1585160 | tf_op jit(solution)/shard_map/ppermute | solution.py:261
  24.2 13.7 %collective-permute-start.4 = (bf16[2064,128]{1,0:T(8,128)(2,1)S(1)}, bf16[2064,128]{1,0:T(8,128)(2,1)S(1)}, u32[]{:S(2)}, u32[]{:S(2)}) collective-permute-start(bf16[2064,128]{1,0:T(8,128)(2,1)S(1)} %collective-permute-done.refs_2_), channel_id=1, source_target_pairs={{0,1},{1,0},{2,3},{3,2},{4,5},{5,4},{6,7},{7,6},{8,9},{9,8},{10,11... | collective-permute-start | bytes 1585160 | tf_op jit(solution)/shard_map/ppermute | solution.py:264
  24.3 19.4 %collective-permute-start.8 = (bf16[2064,128]{1,0:T(8,128)(2,1)S(1)}, bf16[2064,128]{1,0:T(8,128)(2,1)S(1)}, u32[]{:S(2)}, u32[]{:S(2)}) collective-permute-start(bf16[2064,128]{1,0:T(8,128)(2,1)S(1)} %collective-permute-done.refs_2_), channel_id=1, source_target_pairs={{0,2},{1,7},{2,4},{3,1},{4,6},{5,3},{6,0},{7,5},{8,10},{9,15},{10,... | collective-permute-start | bytes 1585160 | tf_op jit(solution)/shard_map/ppermute | solution.py:261
  24.4 13.5 %collective-permute-start.7 = (bf16[1040,128]{1,0:T(8,128)(2,1)S(1)}, bf16[1040,128]{1,0:T(8,128)(2,1)S(1)}, u32[]{:S(2)}, u32[]{:S(2)}) collective-permute-start(bf16[1040,128]{1,0:T(8,128)(2,1)S(1)} %slice.13), channel_id=1, source_target_pairs={{0,8},{8,0},{16,24},{24,16},{1,9},{9,1},{17,25},{25,17},{2,10},{10... | collective-permute-start | bytes 798728 | tf_op jit(solution)/shard_map/ppermute | solution.py:257
  26.9 9.2 %collective-permute-start.6 = (bf16[1024,128]{1,0:T(8,128)(2,1)S(1)}, bf16[1024,128]{1,0:T(8,128)(2,1)S(1)}, u32[]{:S(2)}, u32[]{:S(2)}) collective-permute-start(bf16[1024,128]{1,0:T(8,128)(2,1)S(1)} %slice.12), channel_id=1, source_target_pairs={{0,16},{8,24},{16,0},{24,8},{1,17},{9,25},{17,1},{25,9},{2,18},{10... | collective-permute-start | bytes 786440 | tf_op jit(solution)/shard_map/ppermute | solution.py:257
  29.5 15.7 %collective-permute-start.11 = (bf16[2064,128]{1,0:T(8,128)(2,1)S(1)}, bf16[2064,128]{1,0:T(8,128)(2,1)S(1)}, u32[]{:S(2)}, u32[]{:S(2)}) collective-permute-start(bf16[2064,128]{1,0:T(8,128)(2,1)S(1)} %pack_d.1.refs_0_), channel_id=1, source_target_pairs={{0,8},{8,0},{16,24},{24,16},{1,9},{9,1},{17,25},{25,17},{2,10},{10... | collective-permute-start | bytes 1585160 | tf_op jit(solution)/shard_map/ppermute | solution.py:257
  36.1 14.7 %collective-permute-start.12 = (bf16[2064,128]{1,0:T(8,128)(2,1)S(1)}, bf16[2064,128]{1,0:T(8,128)(2,1)S(1)}, u32[]{:S(2)}, u32[]{:S(2)}) collective-permute-start(bf16[2064,128]{1,0:T(8,128)(2,1)S(1)} %pack_d.1.refs_0_), channel_id=1, source_target_pairs={{0,16},{8,24},{16,0},{24,8},{1,17},{9,25},{17,1},{25,9},{2,18},{10... | collective-permute-start | bytes 1585160 | tf_op jit(solution)/shard_map/ppermute | solution.py:257
  37.9 13.0 %collective-permute-start.9 = (bf16[2064,128]{1,0:T(8,128)(2,1)S(1)}, bf16[2064,128]{1,0:T(8,128)(2,1)S(1)}, u32[]{:S(2)}, u32[]{:S(2)}) collective-permute-start(bf16[2064,128]{1,0:T(8,128)(2,1)S(1)} %collective-permute-done.5.refs_4_), channel_id=1, source_target_pairs={{0,1},{1,0},{2,3},{3,2},{4,5},{5,4},{6,7},{7,6},{8,9},{9,8},{10,11... | collective-permute-start | bytes 1585160 | tf_op jit(solution)/shard_map/ppermute | solution.py:264
  43.6 7.3 %collective-permute-start.10 = (bf16[2064,128]{1,0:T(8,128)(2,1)S(1)}, bf16[2064,128]{1,0:T(8,128)(2,1)S(1)}, u32[]{:S(2)}, u32[]{:S(2)}) collective-permute-start(bf16[2064,128]{1,0:T(8,128)(2,1)S(1)} %collective-permute-done.8.refs_1_), channel_id=1, source_target_pairs={{0,1},{1,0},{2,3},{3,2},{4,5},{5,4},{6,7},{7,6},{8,9},{9,8},{10,11... | collective-permute-start | bytes 1585160 | tf_op jit(solution)/shard_map/ppermute | solution.py:264
  45.2 18.2 %collective-permute-start.13 = (bf16[1024,128]{1,0:T(8,128)(2,1)S(1)}, bf16[1024,128]{1,0:T(8,128)(2,1)S(1)}, u32[]{:S(2)}, u32[]{:S(2)}) collective-permute-start(bf16[1024,128]{1,0:T(8,128)(2,1)S(1)} %slice.16), channel_id=1, source_target_pairs={{0,16},{8,24},{16,0},{24,8},{1,17},{9,25},{17,1},{25,9},{2,18},{10... | collective-permute-start | bytes 786440 | tf_op jit(solution)/shard_map/ppermute | solution.py:257
  50.8 12.6 %collective-permute-start.14 = (bf16[1024,128]{1,0:T(8,128)(2,1)S(1)}, bf16[1024,128]{1,0:T(8,128)(2,1)S(1)}, u32[]{:S(2)}, u32[]{:S(2)}) collective-permute-start(bf16[1024,128]{1,0:T(8,128)(2,1)S(1)} %slice.17), channel_id=1, source_target_pairs={{0,8},{8,0},{16,24},{24,16},{1,9},{9,1},{17,25},{25,17},{2,10},{10... | collective-permute-start | bytes 786440 | tf_op jit(solution)/shard_map/ppermute | solution.py:257
  56.3 11.0 %collective-permute-start.16 = (bf16[4,2,128,128]{3,2,1,0:T(8,128)(2,1)S(1)}, bf16[4,2,128,128]{3,2,1,0:T(8,128)(2,1)S(1)}, u32[]{:S(2)}, u32[]{:S(2)}) collective-permute-start(bf16[4,2,128,128]{3,2,1,0:T(8,128)(2,1)S(1)} %get-tuple-element.69), channel_id=1, source_target_pairs={{0,8},{8,0},{16,24},{24,16},{1,9},{9,1},{17,25},{25,17},{2,10},{10... | collective-permute-start | bytes 786440 | tf_op jit(solution)/shard_map/ppermute | solution.py:257
  58.3 8.9 %collective-permute-start.17 = (bf16[4,2,128,128]{3,2,1,0:T(8,128)(2,1)S(1)}, bf16[4,2,128,128]{3,2,1,0:T(8,128)(2,1)S(1)}, u32[]{:S(2)}, u32[]{:S(2)}) collective-permute-start(bf16[4,2,128,128]{3,2,1,0:T(8,128)(2,1)S(1)} %get-tuple-element.71), channel_id=1, source_target_pairs={{0,16},{8,24},{16,0},{24,8},{1,17},{9,25},{17,1},{25,9},{2,18},{10... | collective-permute-start | bytes 786440 | tf_op jit(solution)/shard_map/ppermute | solution.py:257
  59.4 5.1 %copy-start.4 = (s32[8,4]{0,1:T(4,128)S(1)}, s32[8,4]{0,1:T(4,128)}, u32[]{:S(2)}) copy-start(s32[8,4]{0,1:T(4,128)} %param.9) | copy-start | bytes 388
  63.4 14.4 %collective-permute-start.15 = (bf16[4,2,128,128]{3,2,1,0:T(8,128)(2,1)S(1)}, bf16[4,2,128,128]{3,2,1,0:T(8,128)(2,1)S(1)}, u32[]{:S(2)}, u32[]{:S(2)}) collective-permute-start(bf16[4,2,128,128]{3,2,1,0:T(8,128)(2,1)S(1)} %get-tuple-element.67), channel_id=1, source_target_pairs={{0,8},{8,0},{16,24},{24,16},{1,9},{9,1},{17,25},{25,17},{2,10},{10... | collective-permute-start | bytes 786440 | tf_op jit(solution)/shard_map/ppermute | solution.py:257
  63.6 14.3 %collective-permute-start.20 = (bf16[4,2,128,128]{3,2,1,0:T(8,128)(2,1)S(1)}, bf16[4,2,128,128]{3,2,1,0:T(8,128)(2,1)S(1)}, u32[]{:S(2)}, u32[]{:S(2)}) collective-permute-start(bf16[4,2,128,128]{3,2,1,0:T(8,128)(2,1)S(1)} %get-tuple-element.74), channel_id=1, source_target_pairs={{0,16},{8,24},{16,0},{24,8},{1,17},{9,25},{17,1},{25,9},{2,18},{10... | collective-permute-start | bytes 786440 | tf_op jit(solution)/shard_map/ppermute | solution.py:257
  67.4 10.5 %collective-permute-start.18 = (bf16[4,2,128,128]{3,2,1,0:T(8,128)(2,1)S(1)}, bf16[4,2,128,128]{3,2,1,0:T(8,128)(2,1)S(1)}, u32[]{:S(2)}, u32[]{:S(2)}) collective-permute-start(bf16[4,2,128,128]{3,2,1,0:T(8,128)(2,1)S(1)} %get-tuple-element.72), channel_id=1, source_target_pairs={{0,8},{8,0},{16,24},{24,16},{1,9},{9,1},{17,25},{25,17},{2,10},{10... | collective-permute-start | bytes 786440 | tf_op jit(solution)/shard_map/ppermute | solution.py:257
  69.4 8.5 %collective-permute-start.19 = (bf16[4,2,128,128]{3,2,1,0:T(8,128)(2,1)S(1)}, bf16[4,2,128,128]{3,2,1,0:T(8,128)(2,1)S(1)}, u32[]{:S(2)}, u32[]{:S(2)}) collective-permute-start(bf16[4,2,128,128]{3,2,1,0:T(8,128)(2,1)S(1)} %get-tuple-element.73), channel_id=1, source_target_pairs={{0,16},{8,24},{16,0},{24,8},{1,17},{9,25},{17,1},{25,9},{2,18},{10... | collective-permute-start | bytes 786440 | tf_op jit(solution)/shard_map/ppermute | solution.py:257

commit v8 on v7

--- a/solution.py
+++ b/solution.py
@@ -9,7 +9,7 @@
 from jax.sharding import PartitionSpec as P
 
 VMEM_ROOM = 6 * 1024 * 1024
-N_LAST = 3
+N_LAST = 2
 TAIL = 16
 BF16, F32 = jnp.bfloat16, jnp.float32
 
@@ -68,23 +68,22 @@
     return step * 2 + (core ^ lax.rem(me, 2))
 
 
-def pack_kernel(z, vals_in, *refs):
-    cols_in, (out, tail) = refs[:-2], refs[-2:]
+def pack_kernel(z, slots, first, last, *refs):
+    cols_in, vals_in, (out, tail) = refs[:len(slots)], refs[len(slots):-2], refs[-2:]
     tail[...] = jnp.zeros_like(tail)
-    first = 0
-    for cols in cols_in:
-        count = cols.shape[0]
-        tail[first:first + count, 0:z.rows] = cols[...].astype(F32)
-        first += count
-    rows = vals_in.shape[0]
-    out[rows:rows + TAIL, :] = tail[...].astype(BF16)
-    out[0:rows, :] = vals_in[...]
+    at = 0
+    for cols, count in zip(cols_in, slots):
+        tail[at:at + count, 0:z.rows] = cols[...].astype(F32)
+        at += count
+    out[0:first, :] = vals_in[0][...]
+    out[first:first + TAIL, :] = tail[...].astype(BF16)
+    if last:
+        out[first + TAIL:, :] = vals_in[1][...]
 
 
 def read_tails(payloads, ints, idx, sem):
-    for n, ref in enumerate(payloads):
-        rows = ref.shape[0] - TAIL
-        ints[n] = ref[rows:rows + TAIL, :].astype(F32).astype(jnp.int32)[0:8, :]
+    for n, (ref, row) in enumerate(payloads):
+        ints[n] = ref[row:row + TAIL, :].astype(F32).astype(jnp.int32)[0:8, :]
     copy = pltpu.make_async_copy(ints, idx, sem)
     copy.start()
     copy.wait()
@@ -101,19 +100,16 @@
             dense[rows, at] = blocks[block_rows(z, i, s, z.ka), :]
 
 
-def fill_right(z, first_slot, slots, idx, payloads, flips, place, dense):
+def fill_right(z, first_slot, slots, idx, payloads, place, dense):
     dense[...] = jnp.zeros_like(dense)
     me = lax.axis_index("col")
-    for flip, payload in zip(flips, payloads):
+    for flip, n, ref, row in payloads:
         for i in range(z.rows):
             at = pl.ds(pl.multiple_of(place(flip, i) * z.bs, z.bs), z.bs)
             for s in range(slots):
-                j = idx[flip, first_slot + s, i] - me * z.bc
-                row, part = (i * slots + s) * z.bs, 0
-                while row >= payload[part].shape[0]:
-                    row -= payload[part].shape[0]
-                    part += 1
-                dense[at, lanes(z, j)] = payload[part][row:row + z.bs, :]
+                j = idx[n, first_slot + s, i] - me * z.bc
+                here = row + (i * slots + s) * z.bs
+                dense[at, lanes(z, j)] = ref[here:here + z.bs, :]
 
 
 def by_piece(z, flip, i):
@@ -121,32 +117,67 @@
     return piece_of(z, k // z.bc) * z.bc + lax.rem(k, z.bc)
 
 
-def group(refs, counts):
-    refs = iter(refs)
-    return [[next(refs) for _ in range(count)] for count in counts]
+def panel_at(z, piece):
+    return pl.ds(pl.multiple_of(piece * z.wide, z.wide), z.wide)
+
+
+def each_group(z, flips):
+    per = z.n_col // z.n_row
+    for n, flip in enumerate(flips):
+        for t in range(per):
+            rows = slice((n * per + t) * z.wide, (n * per + t + 1) * z.wide)
+            yield piece_of(z, (lax.axis_index("row") ^ flip) * per + t), rows
+
+
+def in_order(z, flips):
+    return lambda flip, i: flips.index(flip) * z.rows + i
 
 
 def halves(n):
     return [slice(0, n // 2), slice(n // 2, n)]
 
 
-def first_kernel(z, counts, *refs):
-    left_in, right_in = refs[:z.n_first], group(refs[z.n_first:], counts)
-    total, panel, right_last, table, right, ints, idx, sem = refs[z.n_first + sum(counts):]
-    read_tails([x[-1] for x in right_in] + list(left_in), ints, idx, sem)
-    table[...] = ints[0:z.n_row]
-    fill_right(z, z.ka, z.kh, idx, right_in, range(z.n_row), functools.partial(by_piece, z), right)
+def first_kernel(z, near, *refs):
+    left_in, right_in = refs[:z.n_first], refs[z.n_first:z.n_first + len(near)]
+    total, panel, right_last, table, right, ints, idx, sem = refs[z.n_first + len(near):]
+    h_rows, d_rows = z.rows * z.kh * z.bs, z.rows * z.ka * z.bs
+    read_tails([(x, h_rows) for x in right_in] + [(x, d_rows) for x in left_in], ints, idx, sem)
+    for n, flip in enumerate(near):
+        table[flip] = ints[n]
+    payloads = [(flip, n, x, 0) for n, (flip, x) in enumerate(zip(near, right_in))]
+    fill_right(z, z.ka, z.kh, idx, payloads, functools.partial(by_piece, z), right)
     for n in range(z.n_first):
-        fill_left(z, idx, z.n_row + n, piece_col(z, n), left_in[n], panel, n * z.wide)
+        fill_left(z, idx, len(near) + n, piece_col(z, n), left_in[n], panel, n * z.wide)
     deep = z.n_first * z.wide
     for rows in halves(z.tall):
         total[rows, :] = jnp.dot(panel[rows, :], right[0:deep, :], preferred_element_type=F32)
     right_last[...] = right[deep:, :]
 
 
+def mid_kernel(z, near, far, table_in, total_in, panel, right_in, *refs):
+    payloads, (table, total, right_last, right, ints, idx, sem) = refs[:len(far)], refs[len(far):]
+    read_tails([(x, z.rows * z.kh * z.bs) for x in payloads], ints, idx, sem)
+    for flip in near:
+        table[flip] = table_in[flip]
+    for n, flip in enumerate(far):
+        table[flip] = ints[n]
+    payloads = [(flip, n, x, 0) for n, (flip, x) in enumerate(zip(far, payloads))]
+    fill_right(z, z.ka, z.kh, idx, payloads, in_order(z, far), right)
+    total[...] = total_in[...]
+    right_last[...] = right_in[...]
+    for piece, rows in each_group(z, far):
+        @pl.when(piece < z.n_first)
+        def _():
+            total[...] += jnp.dot(panel[:, panel_at(z, piece)], right[rows, :], preferred_element_type=F32)
+
+        @pl.when(piece >= z.n_first)
+        def _():
+            right_last[panel_at(z, piece - z.n_first), :] = right[rows, :]
+
+
 def last_kernel(z, table, right, total_in, panel, *refs):
     payloads, (total, turned, panel_last, *part, ints, idx, sem) = refs[:z.n_last], refs[z.n_last:]
-    read_tails(payloads, ints, idx, sem)
+    read_tails([(x, z.rows * z.ka * z.bs) for x in payloads], ints, idx, sem)
     for n, payload in enumerate(payloads):
         fill_left(z, idx, n, piece_col(z, z.n_first + n), payload, panel_last, n * z.wide)
     for rows in halves(z.tall):
@@ -205,22 +236,42 @@
     copy.wait()
 
 
-def square_kernel(z, counts, table, filt, panel, panel_last, *refs):
-    squared, right, total, held, sems = refs[sum(counts):]
-    fill_right(z, 0, z.ka, table, group(refs, counts), range(z.n_row), functools.partial(by_piece, z), right)
-    deep = z.n_first * z.wide
-    copies = []
-    for n, rows in enumerate(halves(z.tall)):
-        total[rows, :] = jnp.dot(panel[rows, :], right[0:deep, :], preferred_element_type=F32)
-        total[rows, :] += jnp.dot(panel_last[rows, :], right[deep:, :], preferred_element_type=F32)
-        here = halves(z.rows)[n]
-        for i in range(here.start, here.stop):
-            for s in range(z.kf):
-                held[i, s] = filtered(z, filt, total, i, s)
-        copies.append(pltpu.make_async_copy(held.at[here], squared.at[here], sems.at[n]))
-        copies[-1].start()
-    for copy in copies:
-        copy.wait()
+def early_kernel(z, near, table, panel, *refs):
+    payloads, (total, right) = refs[:-2], refs[-2:]
+    payloads = [(flip, flip, x, z.rows * z.kh * z.bs + TAIL) for flip, x in zip(near, payloads)]
+    fill_right(z, 0, z.ka, table, payloads, in_order(z, near), right)
+    total[...] = jnp.zeros_like(total)
+    for piece, rows in each_group(z, near):
+        @pl.when(piece < z.n_first)
+        def _():
+            total[...] += jnp.dot(panel[:, panel_at(z, piece)], right[rows, :], preferred_element_type=F32)
+
+
+def square_kernel(z, near, far, starts, table, filt, panel, panel_last, total_in, right_near, *refs):
+    payloads, (squared, right, total, held, sem) = refs[:len(far)], refs[len(far):]
+    payloads = [(flip, flip, x, start) for flip, x, start in zip(far, payloads, starts)]
+    fill_right(z, 0, z.ka, table, payloads, in_order(z, far), right)
+    total[...] = total_in[...]
+    for piece, rows in each_group(z, near):
+        @pl.when(piece >= z.n_first)
+        def _():
+            at = panel_at(z, piece - z.n_first)
+            total[...] += jnp.dot(panel_last[:, at], right_near[rows, :], preferred_element_type=F32)
+    for piece, rows in each_group(z, far):
+        @pl.when(piece < z.n_first)
+        def _():
+            total[...] += jnp.dot(panel[:, panel_at(z, piece)], right[rows, :], preferred_element_type=F32)
+
+        @pl.when(piece >= z.n_first)
+        def _():
+            at = panel_at(z, piece - z.n_first)
+            total[...] += jnp.dot(panel_last[:, at], right[rows, :], preferred_element_type=F32)
+    for i in range(z.rows):
+        for s in range(z.kf):
+            held[i, s] = filtered(z, filt, total, i, s)
+    copy = pltpu.make_async_copy(held, squared, sem)
+    copy.start()
+    copy.wait()
 
 
 def add_kernel(z, x_0, x_1, y_0, y_1, x_out, y_out):
@@ -263,75 +314,77 @@
     def other_core(x):
         return lax.ppermute(x, "col", [(c, c ^ 1) for c in range(n_col)])
 
-    flat = density.reshape(d_rows, z.bs)
+    flat_d, flat_h = density.reshape(d_rows, z.bs), hamilton.reshape(h_rows, z.bs)
 
     def pack(vals, cols, name):
-        rows = vals.shape[0]
-        outs = [shape((rows + TAIL, z.bs), BF16)]
-        scratch = [pltpu.VMEM((TAIL, z.bs), F32)]
-        return call(functools.partial(pack_kernel, z), [vals, *cols], outs, scratch, [vmem] * (1 + len(cols)), [vmem], 0, name)[0]
-
-    d_pay = pack(flat, [density_cols.T], "pack_d")
-    h_pay = pack(hamilton.reshape(h_rows, z.bs), [density_cols.T, hamilton_cols.T], "pack_h")
-
-    flips = sorted(range(1, n_row), key=int.bit_count)
-    single = [flip for flip in flips if flip.bit_count() == 1]
-    h_half, d_half = h_rows // 2, d_rows // 2
-
-    def forward(blocks):
-        for flip in flips:
-            if flip not in blocks:
-                blocks[flip] = [over_row(blocks[flip & (flip - 1)][0], flip & -flip)]
-
+        first, last = vals[0].shape[0], sum(x.shape[0] for x in vals[1:])
+        outs = [shape((first + TAIL + last, z.bs), BF16)]
+        kernel = functools.partial(pack_kernel, z, [x.shape[0] for x in cols], first, last)
+        ins = [*cols, *vals]
+        return call(kernel, ins, outs, [pltpu.VMEM((TAIL, z.bs), F32)], [vmem] * len(ins), [vmem], 0, name)[0]
+
+    d_pay = pack([flat_d], [density_cols.T], "pack_d")
+    dh_pay = pack([flat_h, flat_d], [density_cols.T, hamilton_cols.T], "pack_dh")
+
+    near = [0] + [1 << bit for bit in range(n_row.bit_length() - 1)]
+    far = sorted(set(range(n_row)) - set(near), key=int.bit_count)
     pieces = [d_pay, next_chip(d_pay, 1)]
-    h_right = {0: [h_pay]}
-    for flip in single:
-        h_right[flip] = [over_row(h_pay, flip)]
-    pieces.append(next_chip(d_pay, -1))
-    pieces[1], h_right, twin = lax.optimization_barrier((pieces[1], h_right, other_core(d_pay)))
-    if n_row == 4:
-        h_right[3] = [over_row(h_right[1][0][:h_half], 2), over_row(h_right[2][0][h_half:], 1)]
-    forward(h_right)
-    d_0, pieces[2] = lax.optimization_barrier((d_pay, pieces[2]))
+    dh = {0: dh_pay}
+    for flip in near[1:]:
+        dh[flip] = over_row(dh_pay, flip)
+    later, dh_pay = lax.optimization_barrier((d_pay, dh_pay))
+    pieces.append(next_chip(later, -1))
     for step in range(3, z.n_chip):
         pieces.append(next_chip(pieces[step - 2], 1 if step % 2 else -1))
-    d_right = {0: [d_0]}
-    for flip in single:
-        d_right[flip] = [over_row(d_0, flip)]
+    if n_row == 4:
+        h_far, d_far = [over_row(dh[2][:h_rows + TAIL], 1)], [over_row(dh[1][h_rows + TAIL:], 2)]
+        d_starts = [0]
+    else:
+        for flip in far:
+            dh[flip] = over_row(dh[flip & (flip - 1)], flip & -flip)
+        h_far = d_far = [dh[flip] for flip in far]
+        d_starts = [h_rows + TAIL] * len(far)
+    dh_near = [dh[flip] for flip in near]
     left = []
     for step, piece in enumerate(pieces):
         left.append(piece)
         if step < z.n_chip - 1:
-            left.append(other_core(piece) if step else twin)
-    h_right = [h_right[flip] for flip in range(n_row)]
-
-    n_pay = z.n_first + n_row
+            left.append(other_core(piece))
+
+    table_shape = shape((n_row, 8, z.bs), jnp.int32)
+    total_shape = shape((z.tall, z.wide), F32)
+    last_shape = shape((z.n_last * z.wide, z.wide), BF16)
+
+    def scalars(count):
+        return [pltpu.VMEM((count, 8, z.bs), jnp.int32), pltpu.SMEM((count, 8, z.bs), jnp.int32), dma]
+
+    n_pay = z.n_first + len(near)
     total, panel, right_last, table = call(
-        functools.partial(first_kernel, z, [len(x) for x in h_right]),
-        [*left[:z.n_first], *sum(h_right, [])],
-        [
-            shape((z.tall, z.wide), F32),
-            shape((z.tall, z.n_first * z.wide), BF16),
-            shape((z.n_last * z.wide, z.wide), BF16),
-            shape((n_row, 8, z.bs), jnp.int32),
-        ],
-        [
-            pltpu.VMEM((z.nb * z.bs, z.wide), BF16),
-            pltpu.VMEM((n_pay, 8, z.bs), jnp.int32),
-            pltpu.SMEM((n_pay, 8, z.bs), jnp.int32),
-            dma,
-        ],
-        [vmem] * (z.n_first + sum(map(len, h_right))), [vmem] * 4, 0, "first",
-    )
-    last, total = lax.optimization_barrier((left[-1], total))
-    if n_row == 4:
-        d_right[3] = [over_row(d_right[1][0][:d_half], 2), over_row(d_right[2][0][d_half:d_rows], 1)]
-    forward(d_right)
-    d_right = [d_right[flip] for flip in range(n_row)]
+        functools.partial(first_kernel, z, near),
+        [*left[:z.n_first], *dh_near],
+        [total_shape, shape((z.tall, z.n_first * z.wide), BF16), last_shape, table_shape],
+        [pltpu.VMEM((z.nb * z.bs, z.wide), BF16)] + scalars(n_pay),
+        [vmem] * n_pay, [vmem] * 4, 0, "first",
+    )
+    total_early, right_near = call(
+        functools.partial(early_kernel, z, near),
+        [table, panel, *dh_near],
+        [total_shape, shape((len(near) * z.tall, z.wide), BF16)],
+        [], [smem] + [vmem] * (1 + len(near)), [vmem] * 2, 0, "early",
+    )
+    last, total, total_early = lax.optimization_barrier((left[-1], total, total_early))
+    h_far, d_far = lax.optimization_barrier((h_far, d_far))
+    table, total, right_last = call(
+        functools.partial(mid_kernel, z, near, far),
+        [table, total, panel, right_last, *h_far],
+        [table_shape, total_shape, last_shape],
+        [pltpu.VMEM((len(far) * z.tall, z.wide), BF16)] + scalars(len(far)),
+        [vmem] * (4 + len(far)), [vmem] * 3, 1 * panel_flops, "mid",
+    )
     part = shape((z.rows, z.ka) + block, BF16)
     cuts = 2 if n_row == 4 and z.rows % 2 == 0 else 1
     cut_part = shape((z.rows // cuts, z.ka) + block, BF16)
-    total, turned, panel_last, *far = call(
+    total, turned, panel_last, *ends = call(
         functools.partial(last_kernel, z),
         [table, right_last, total, panel, *left[z.n_first:-1], last, other_core(last)],
         [shape((z.tall, z.wide), F32), shape((z.wide, z.tall), BF16), shape((z.tall, z.n_last * z.wide), BF16)]
@@ -343,16 +396,15 @@
         ],
         [smem] + [vmem] * (3 + z.n_last), [vmem] * (3 + cuts), panel_flops // 4 + part_flops, "last",
     )
-    near = call(
+    sums = call(
         functools.partial(parts_kernel, z), [table, turned, panel, panel_last], [cut_part] * (cuts * (n_row - 2)), [],
         [smem] + [vmem] * 3, [vmem] * (cuts * (n_row - 2)), part_flops * (n_row - 2), "parts",
     )
-    near, d_right = lax.optimization_barrier((near, d_right))
     if cuts == 2:
-        far = over_row(far[0], 1), over_row(far[1], 2)
-        x_0, y_1 = over_row(near[0], 1), over_row(near[3], 2)
+        ends = over_row(ends[0], 1), over_row(ends[1], 2)
+        x_0, y_1 = over_row(sums[0], 1), over_row(sums[3], 2)
     else:
-        received = [over_row(term, n + 1) for n, term in enumerate([*near, *far])]
+        received = [over_row(term, n + 1) for n, term in enumerate([*sums, *ends])]
     whole_part = shape((z.rows, z.ka) + block, F32)
     mixed, direct, own = call(
         functools.partial(base_kernel, z),
@@ -363,19 +415,19 @@
     )
     if cuts == 2:
         y_0, x_1 = call(
-            functools.partial(add_kernel, z), [near[2], far[0], near[1], far[1]], [cut_part] * 2, [],
+            functools.partial(add_kernel, z), [sums[2], ends[0], sums[1], ends[1]], [cut_part] * 2, [],
             [vmem] * 4, [vmem] * 2, 0, "add",
         )
         received = [x_0, over_row(x_1, 1), over_row(y_0, 2), y_1]
     squared, = call(
-        functools.partial(square_kernel, z, [len(x) for x in d_right]),
-        [table, filter_cols.T, panel, panel_last, *sum(d_right, [])],
+        functools.partial(square_kernel, z, near, far, d_starts),
+        [table, filter_cols.T, panel, panel_last, total_early, right_near, *d_far],
         [shape((z.rows, z.kf) + block, BF16)],
         [
-            pltpu.VMEM((z.nb * z.bs, z.wide), BF16), pltpu.VMEM((z.tall, z.wide), F32),
-            pltpu.VMEM((z.rows, z.kf) + block, BF16), dma((2,)),
+            pltpu.VMEM((len(far) * z.tall, z.wide), BF16), pltpu.VMEM((z.tall, z.wide), F32),
+            pltpu.VMEM((z.rows, z.kf) + block, BF16), dma,
         ],
-        [smem] * 2 + [vmem] * (2 + sum(map(len, d_right))), [anywhere], panel_flops, "squared",
+        [smem] * 2 + [vmem] * (4 + len(far)), [anywhere], panel_flops, "squared",
     )
     gradient, = call(
         functools.partial(gradient_kernel, z), [direct, own, *received], [part], [],

time: 79.3 us -> 80.4 us (1.014)
  the two profiles are of different devices: /device:TPU:24 before, /device:TPU:0 now
where the time goes in v8:
time: 80.4 us; the launch traced here: 80.1 us
  Pallas kernels  31.9 us (40%)
  waiting for transfers between devices  25 us (31%)
  starting transfers between devices  19 us (24%)
  local copies, waits for them, and re-layouts  3.51 us (4%)
    pallas_call x11, Pallas kernels, call(): pl.pallas_call(kernel, out_shape=outs, in_specs=in_specs, out_specs=out_s...  31.9 us
    ppermute x3, waiting for transfers between devices, next_chip(): lax.ppermute(x, 'col', [(c, (c // 2 + move[c % 2]) % z.n_chip * 2 + c % 2...  22.8 us
    ppermute x10, starting transfers between devices, over_row(): return lax.ppermute(x, 'row', [(r, r ^ flip) for r in range(n_row)])  12 us
    ppermute x3, starting transfers between devices, next_chip(): lax.ppermute(x, 'col', [(c, (c // 2 + move[c % 2]) % z.n_chip * 2 + c % 2...  6.06 us
    unnamed x10, local copies, waits for them, and re-layouts  3.44 us
    ppermute x10, waiting for transfers between devices, over_row(): return lax.ppermute(x, 'row', [(r, r ^ flip) for r in range(n_row)])  2.18 us
  transfers between devices with their start and end apart: 17, of which 6 were waited for; matrix products, arithmetic and copies ran while one was open for 0% of the time, Pallas kernels for 32%

profile of v8, /device:TPU:0, one launch (start us, length us, event | category | flops | bytes accessed | tf_op | source)
XLA Modules:
  0.0 80.1 jit_solution(5533228680893406160)
XLA Ops:
  0.6 1.0 %copy-done = bf16[8,2,128,128]{3,2,1,0:T(8,128)(2,1)S(1)} copy-done((bf16[8,2,128,128]{3,2,1,0:T(8,128)(2,1)S(1)}, bf16[8,2,128,128]{3,2,1,0:T(8,128)(2,1)}, u32[]{:S(2)}) %copy-start) | copy-done | bytes 524312
  1.7 1.0 %copy-done.1 = bf16[8,2,128,128]{3,2,1,0:T(8,128)(2,1)S(1)} copy-done((bf16[8,2,128,128]{3,2,1,0:T(8,128)(2,1)S(1)}, bf16[8,2,128,128]{3,2,1,0:T(8,128)(2,1)}, u32[]{:S(2)}) %copy-start.1) | copy-done | bytes 524312
  2.7 0.7 copy-done.2
  3.4 0.7 copy-done.4
  4.1 3.0 %collective-permute-start.6 = (bf16[4112,128]{1,0:T(8,128)(2,1)S(1)}, bf16[4112,128]{1,0:T(8,128)(2,1)S(1)}, u32[]{:S(2)}, u32[]{:S(2)}) collective-permute-start(bf16[4112,128]{1,0:T(8,128)(2,1)S(1)} %pack_dh.1.refs_6_.refs_0_), channel_id=1, source_target_pairs={{0,16},{8,24},{16,0},{24,8},{1,17},{9,25},{17,1},{25,9},{2,18},{10... | collective-permute-start | bytes 3158024 | tf_op jit(solution)/shard_map/ppermute | solution.py:308
  7.2 1.5 %collective-permute-start.5 = (bf16[4112,128]{1,0:T(8,128)(2,1)S(1)}, bf16[4112,128]{1,0:T(8,128)(2,1)S(1)}, u32[]{:S(2)}, u32[]{:S(2)}) collective-permute-start(bf16[4112,128]{1,0:T(8,128)(2,1)S(1)} %pack_dh.1.refs_6_.refs_0_), channel_id=1, source_target_pairs={{0,8},{8,0},{16,24},{24,16},{1,9},{9,1},{17,25},{25,17},{2,10},{10... | collective-permute-start | bytes 3158024 | tf_op jit(solution)/shard_map/ppermute | solution.py:308
  8.7 1.6 %collective-permute-start.1 = (bf16[2064,128]{1,0:T(8,128)(2,1)S(1)}, bf16[2064,128]{1,0:T(8,128)(2,1)S(1)}, u32[]{:S(2)}, u32[]{:S(2)}) collective-permute-start(bf16[2064,128]{1,0:T(8,128)(2,1)S(1)} %pack_d.1.refs_0_), channel_id=1, source_target_pairs={{0,2},{1,7},{2,4},{3,1},{4,6},{5,3},{6,0},{7,5},{8,10},{9,15},{10,... | collective-permute-start | bytes 1585160 | tf_op jit(solution)/shard_map/ppermute | solution.py:312
  10.3 2.2 %collective-permute-start.3 = (bf16[2064,128]{1,0:T(8,128)(2,1)S(1)}, bf16[2064,128]{1,0:T(8,128)(2,1)S(1)}, u32[]{:S(2)}, u32[]{:S(2)}) collective-permute-start(bf16[2064,128]{1,0:T(8,128)(2,1)S(1)} %pack_d.1.refs_0_), channel_id=1, source_target_pairs={{0,6},{1,3},{2,0},{3,5},{4,2},{5,7},{6,4},{7,1},{8,14},{9,11},{10,... | collective-permute-start | bytes 1585160 | tf_op jit(solution)/shard_map/ppermute | solution.py:312
  12.6 13.1 %collective-permute-done.1.refs_2_ = bf16[2064,128]{1,0:T(8,128)(2,1)S(1)} collective-permute-done((bf16[2064,128]{1,0:T(8,128)(2,1)S(1)}, bf16[2064,128]{1,0:T(8,128)(2,1)S(1)}, u32[]{:S(2)}, u32[]{:S(2)}) %collective-permute-start.1) | collective-permute-done | bytes 528416 | tf_op jit(solution)/shard_map/ppermute | solution.py:312
  25.7 0.5 collective-permute-start.2
  26.2 7.6 %collective-permute-done.3.refs_4_ = bf16[2064,128]{1,0:T(8,128)(2,1)S(1)} collective-permute-done((bf16[2064,128]{1,0:T(8,128)(2,1)S(1)}, bf16[2064,128]{1,0:T(8,128)(2,1)S(1)}, u32[]{:S(2)}, u32[]{:S(2)}) %collective-permute-start.3) | collective-permute-done | bytes 528416 | tf_op jit(solution)/shard_map/ppermute | solution.py:312
  33.7 0.5 collective-permute-start.4
  34.2 2.2 %collective-permute-start.7 = (bf16[2064,128]{1,0:T(8,128)(2,1)S(1)}, bf16[2064,128]{1,0:T(8,128)(2,1)S(1)}, u32[]{:S(2)}, u32[]{:S(2)}) collective-permute-start(bf16[2064,128]{1,0:T(8,128)(2,1)S(1)} %collective-permute-done.1.refs_2_), channel_id=1, source_target_pairs={{0,2},{1,7},{2,4},{3,1},{4,6},{5,3},{6,0},{7,5},{8,10},{9,15},{10,... | collective-permute-start | bytes 1585160 | tf_op jit(solution)/shard_map/ppermute | solution.py:312
  36.4 0.6 collective-permute-start.8
  37.1 0.6 collective-permute-start.9
  37.7 6.6 %first.1 = (f32[1024,512]{1,0:T(8,128)S(1)}, bf16[1024,3072]{1,0:T(8,128)(2,1)S(1)}, bf16[1024,512]{1,0:T(8,128)(2,1)S(1)}, s32[4,8,128]{2,1,0:T(8,128)S(1)}) custom-call(bf16[2064,128]{1,0:T(8,128)(2,1)S(1)} %pack_d.1.refs_0_, bf16[2064,128]{1,0:T(8,128)(2,1)S(1)} %collective-permute-done.refs_1_, bf16[2064,128]{1,0:T(8,128)(2,1)S(1)} %collective-permute-done.1.refs_2_, ...), custom_call_target="tpu_custom_call" | custom-call | bytes 1024 | tf_op jit(solution)/shard_map/first/pallas_call | solution.py:32
  44.2 4.3 %early.1 = (f32[1024,512]{1,0:T(8,128)S(1)}, bf16[3072,512]{1,0:T(8,128)(2,1)S(1)}) custom-call(s32[4,8,128]{2,1,0:T(8,128)S(1)} %get-tuple-element.33.table.table_in, bf16[1024,3072]{1,0:T(8,128)(2,1)S(1)} %get-tuple-element.35.panel, bf16[4112,128]{1,0:T(8,128)(2,1)S(1)} %pack_dh.1.refs_6_.refs_0_, ...), custom_call_target="tpu_custom_call" | custom-call | bytes 1024 | tf_op jit(solution)/shard_map/early/pallas_call | solution.py:32
  48.6 2.1 %collective-permute-done.7.refs_0_ = bf16[2064,128]{1,0:T(8,128)(2,1)S(1)} collective-permute-done((bf16[2064,128]{1,0:T(8,128)(2,1)S(1)}, bf16[2064,128]{1,0:T(8,128)(2,1)S(1)}, u32[]{:S(2)}, u32[]{:S(2)}) %collective-permute-start.7) | collective-permute-done | bytes 528416 | tf_op jit(solution)/shard_map/ppermute | solution.py:312
  50.7 0.7 collective-permute-done.9.refs_0_
  51.4 2.4 %mid.1 = (s32[4,8,128]{2,1,0:T(8,128)S(1)}, f32[1024,512]{1,0:T(8,128)S(1)}, bf16[1024,512]{1,0:T(8,128)(2,1)S(1)}) custom-call(s32[4,8,128]{2,1,0:T(8,128)S(1)} %get-tuple-element.33.table.table_in, f32[1024,512]{1,0:T(8,128)S(1)} %get-tuple-element.37.total_in, bf16[1024,3072]{1,0:T(8,128)(2,1)S(1)} %get-tuple-element.35.panel, ...), custom_call_target="tpu_custom_call" | custom-call | flops 4294967296 | bytes 1024 | tf_op jit(solution)/shard_map/mid/pallas_call | solution.py:32
  53.8 5.0 %last.1 = (f32[1024,512]{1,0:T(8,128)S(1)}, bf16[512,1024]{1,0:T(8,128)(2,1)S(1)}, bf16[1024,1024]{1,0:T(8,128)(2,1)S(1)}, bf16[4,2,128,128]{3,2,1,0:T(8,128)(2,1)S(1)}, bf16[4,2,128,128]{3,2,1,0:T(8,128)(2,1)S(1)}) custom-call(s32[4,8,128]{2,1,0:T(8,128)S(1)} %get-tuple-element.40.table, bf16[1024,512]{1,0:T(8,128)(2,1)S(1)} %get-tuple-element.41.right, ...), custom_call_target="tpu_custom_call" | custom-call | flops 2147483648 | bytes 1024 | tf_op jit(solution)/shard_map/last/pallas_call | solution.py:32
  58.8 0.7 collective-permute-start.12
  59.4 1.4 %collective-permute-start.13 = (bf16[4,2,128,128]{3,2,1,0:T(8,128)(2,1)S(1)}, bf16[4,2,128,128]{3,2,1,0:T(8,128)(2,1)S(1)}, u32[]{:S(2)}, u32[]{:S(2)}) collective-permute-start(bf16[4,2,128,128]{3,2,1,0:T(8,128)(2,1)S(1)} %get-tuple-element.57), channel_id=1, source_target_pairs={{0,16},{8,24},{16,0},{24,8},{1,17},{9,25},{17,1},{25,9},{2,18},{10... | collective-permute-start | bytes 786440 | tf_op jit(solution)/shard_map/ppermute | solution.py:308
  60.9 3.9 %parts.1 = (bf16[4,2,128,128]{3,2,1,0:T(8,128)(2,1)S(1)}, bf16[4,2,128,128]{3,2,1,0:T(8,128)(2,1)S(1)}, bf16[4,2,128,128]{3,2,1,0:T(8,128)(2,1)S(1)}, bf16[4,2,128,128]{3,2,1,0:T(8,128)(2,1)S(1)}) custom-call(s32[4,8,128]{2,1,0:T(8,128)S(1)} %get-tuple-element.40.table, bf16[512,1024]{1,0:T(8,128)(2,1)S(1)} %get-tuple-element.49.turned, ...), custom_call_target="tpu_custom_call" | custom-call | flops 2147483648 | bytes 1024 | tf_op jit(solution)/shard_map/parts/pallas_call | solution.py:32
  64.8 0.6 collective-permute-start.11
  65.4 1.5 %collective-permute-start.16 = (bf16[4,2,128,128]{3,2,1,0:T(8,128)(2,1)S(1)}, bf16[4,2,128,128]{3,2,1,0:T(8,128)(2,1)S(1)}, u32[]{:S(2)}, u32[]{:S(2)}) collective-permute-start(bf16[4,2,128,128]{3,2,1,0:T(8,128)(2,1)S(1)} %get-tuple-element.60), channel_id=1, source_target_pairs={{0,16},{8,24},{16,0},{24,8},{1,17},{9,25},{17,1},{25,9},{2,18},{10... | collective-permute-start | bytes 786440 | tf_op jit(solution)/shard_map/ppermute | solution.py:308
  66.9 3.0 %base.1 = (bf16[8,4,128,128]{3,2,1,0:T(8,128)(2,1)}, f32[8,2,128,128]{3,2,1,0:T(8,128)S(1)}, f32[8,2,128,128]{3,2,1,0:T(8,128)S(1)}) custom-call(s32[4,8,128]{2,1,0:T(8,128)S(1)} %get-tuple-element.40.table, s32[4,8]{1,0:T(4,128)S(1)} %bitcast.10, f32[1024,512]{1,0:T(8,128)S(1)} %get-tuple-element.48.total, bf16[512,1024]{1,0:T(8,128)(2,1)S(1)} %get-tuple-element.49.turned, ...), custom_call_target="tpu_custom_call" | custom-call | flops 1073741824 | bytes 1024 | tf_op jit(solution)/shard_map/base/pallas_call | solution.py:32
  70.1 0.6 collective-permute-start.14
  70.7 1.4 %collective-permute-start.15 = (bf16[4,2,128,128]{3,2,1,0:T(8,128)(2,1)S(1)}, bf16[4,2,128,128]{3,2,1,0:T(8,128)(2,1)S(1)}, u32[]{:S(2)}, u32[]{:S(2)}) collective-permute-start(bf16[4,2,128,128]{3,2,1,0:T(8,128)(2,1)S(1)} %get-tuple-element.59), channel_id=1, source_target_pairs={{0,16},{8,24},{16,0},{24,8},{1,17},{9,25},{17,1},{25,9},{2,18},{10... | collective-permute-start | bytes 786440 | tf_op jit(solution)/shard_map/ppermute | solution.py:308
  72.1 5.3 %squared.1 = bf16[8,4,128,128]{3,2,1,0:T(8,128)(2,1)} custom-call(s32[4,8,128]{2,1,0:T(8,128)S(1)} %get-tuple-element.40.table, s32[4,8]{1,0:T(4,128)S(1)} %bitcast.11, bf16[1024,3072]{1,0:T(8,128)(2,1)S(1)} %get-tuple-element.35.panel, bf16[1024,1024]{1,0:T(8,128)(2,1)S(1)} %get-tuple-element.44.panel_last, f32[1024,512]{1,0:T(8,128)S(1)} %get-tuple-element.45.total_in, ...), custom_call_target="tpu_custom_call" | custom-call | flops 4294967296 | bytes 1024 | tf_op jit(solution)/shard_map/squared/pallas_call | solution.py:32
  77.5 1.2 %collective-permute-done.14.refs_1_ = bf16[4,2,128,128]{3,2,1,0:T(8,128)(2,1)S(1)} collective-permute-done((bf16[4,2,128,128]{3,2,1,0:T(8,128)(2,1)S(1)}, bf16[4,2,128,128]{3,2,1,0:T(8,128)(2,1)S(1)}, u32[]{:S(2)}, u32[]{:S(2)}) %collective-permute-start.14) | collective-permute-done | bytes 262176 | tf_op jit(solution)/shard_map/ppermute | solution.py:308
  79.0 1.1 %gradient.1 = bf16[8,2,128,128]{3,2,1,0:T(8,128)(2,1)} custom-call(f32[8,2,128,128]{3,2,1,0:T(8,128)S(1)} %get-tuple-element.51.direct, f32[8,2,128,128]{3,2,1,0:T(8,128)S(1)} %get-tuple-element.52.own, bf16[4,2,128,128]{3,2,1,0:T(8,128)(2,1)S(1)} %collective-permute-done.11.refs_0_, bf16[4,2,128,128]{3,2,1,0:T(8,128)(2,1)S(1)} %collective-permute-done.14.refs_1_, ...), custom_call_target="tpu_custom_call" | custom-call | bytes 1024 | tf_op jit(solution)/shard_map/gradient/pallas_call | solution.py:32
  (25 shorter events, 0.6 us)
Async XLA Ops:
  0.6 1.0 %copy-start = (bf16[8,2,128,128]{3,2,1,0:T(8,128)(2,1)S(1)}, bf16[8,2,128,128]{3,2,1,0:T(8,128)(2,1)}, u32[]{:S(2)}) copy-start(bf16[8,2,128,128]{3,2,1,0:T(8,128)(2,1)} %param.5) | copy-start | bytes 1572868
  1.7 1.0 %copy-start.1 = (bf16[8,2,128,128]{3,2,1,0:T(8,128)(2,1)S(1)}, bf16[8,2,128,128]{3,2,1,0:T(8,128)(2,1)}, u32[]{:S(2)}) copy-start(bf16[8,2,128,128]{3,2,1,0:T(8,128)(2,1)} %param.7) | copy-start | bytes 1572868
  2.7 0.7 copy-start.2
  3.4 0.7 copy-start.4
  4.1 30.0 %collective-permute-start.6 = (bf16[4112,128]{1,0:T(8,128)(2,1)S(1)}, bf16[4112,128]{1,0:T(8,128)(2,1)S(1)}, u32[]{:S(2)}, u32[]{:S(2)}) collective-permute-start(bf16[4112,128]{1,0:T(8,128)(2,1)S(1)} %pack_dh.1.refs_6_.refs_0_), channel_id=1, source_target_pairs={{0,16},{8,24},{16,0},{24,8},{1,17},{9,25},{17,1},{25,9},{2,18},{10... | collective-permute-start | bytes 3158024 | tf_op jit(solution)/shard_map/ppermute | solution.py:308
  7.2 29.2 %collective-permute-start.5 = (bf16[4112,128]{1,0:T(8,128)(2,1)S(1)}, bf16[4112,128]{1,0:T(8,128)(2,1)S(1)}, u32[]{:S(2)}, u32[]{:S(2)}) collective-permute-start(bf16[4112,128]{1,0:T(8,128)(2,1)S(1)} %pack_dh.1.refs_6_.refs_0_), channel_id=1, source_target_pairs={{0,8},{8,0},{16,24},{24,16},{1,9},{9,1},{17,25},{25,17},{2,10},{10... | collective-permute-start | bytes 3158024 | tf_op jit(solution)/shard_map/ppermute | solution.py:308
  8.7 17.0 %collective-permute-start.1 = (bf16[2064,128]{1,0:T(8,128)(2,1)S(1)}, bf16[2064,128]{1,0:T(8,128)(2,1)S(1)}, u32[]{:S(2)}, u32[]{:S(2)}) collective-permute-start(bf16[2064,128]{1,0:T(8,128)(2,1)S(1)} %pack_d.1.refs_0_), channel_id=1, source_target_pairs={{0,2},{1,7},{2,4},{3,1},{4,6},{5,3},{6,0},{7,5},{8,10},{9,15},{10,... | collective-permute-start | bytes 1585160 | tf_op jit(solution)/shard_map/ppermute | solution.py:312
  10.3 23.4 %collective-permute-start.3 = (bf16[2064,128]{1,0:T(8,128)(2,1)S(1)}, bf16[2064,128]{1,0:T(8,128)(2,1)S(1)}, u32[]{:S(2)}, u32[]{:S(2)}) collective-permute-start(bf16[2064,128]{1,0:T(8,128)(2,1)S(1)} %pack_d.1.refs_0_), channel_id=1, source_target_pairs={{0,6},{1,3},{2,0},{3,5},{4,2},{5,7},{6,4},{7,1},{8,14},{9,11},{10,... | collective-permute-start | bytes 1585160 | tf_op jit(solution)/shard_map/ppermute | solution.py:312
  12.6 24.5 %collective-permute-start = (bf16[2064,128]{1,0:T(8,128)(2,1)S(1)}, bf16[2064,128]{1,0:T(8,128)(2,1)S(1)}, u32[]{:S(2)}, u32[]{:S(2)}) collective-permute-start(bf16[2064,128]{1,0:T(8,128)(2,1)S(1)} %pack_d.1.refs_0_), channel_id=1, source_target_pairs={{0,1},{1,0},{2,3},{3,2},{4,5},{5,4},{6,7},{7,6},{8,9},{9,8},{10,11... | collective-permute-start | bytes 1585160 | tf_op jit(solution)/shard_map/ppermute | solution.py:315
  25.7 12.0 %collective-permute-start.2 = (bf16[2064,128]{1,0:T(8,128)(2,1)S(1)}, bf16[2064,128]{1,0:T(8,128)(2,1)S(1)}, u32[]{:S(2)}, u32[]{:S(2)}) collective-permute-start(bf16[2064,128]{1,0:T(8,128)(2,1)S(1)} %collective-permute-done.1.refs_2_), channel_id=1, source_target_pairs={{0,1},{1,0},{2,3},{3,2},{4,5},{5,4},{6,7},{7,6},{8,9},{9,8},{10,11... | collective-permute-start | bytes 1585160 | tf_op jit(solution)/shard_map/ppermute | solution.py:315
  33.7 3.9 %collective-permute-start.4 = (bf16[2064,128]{1,0:T(8,128)(2,1)S(1)}, bf16[2064,128]{1,0:T(8,128)(2,1)S(1)}, u32[]{:S(2)}, u32[]{:S(2)}) collective-permute-start(bf16[2064,128]{1,0:T(8,128)(2,1)S(1)} %collective-permute-done.3.refs_4_), channel_id=1, source_target_pairs={{0,1},{1,0},{2,3},{3,2},{4,5},{5,4},{6,7},{7,6},{8,9},{9,8},{10,11... | collective-permute-start | bytes 1585160 | tf_op jit(solution)/shard_map/ppermute | solution.py:315
  34.2 16.5 %collective-permute-start.7 = (bf16[2064,128]{1,0:T(8,128)(2,1)S(1)}, bf16[2064,128]{1,0:T(8,128)(2,1)S(1)}, u32[]{:S(2)}, u32[]{:S(2)}) collective-permute-start(bf16[2064,128]{1,0:T(8,128)(2,1)S(1)} %collective-permute-done.1.refs_2_), channel_id=1, source_target_pairs={{0,2},{1,7},{2,4},{3,1},{4,6},{5,3},{6,0},{7,5},{8,10},{9,15},{10,... | collective-permute-start | bytes 1585160 | tf_op jit(solution)/shard_map/ppermute | solution.py:312
  36.4 14.9 %collective-permute-start.8 = (bf16[2064,128]{1,0:T(8,128)(2,1)S(1)}, bf16[2064,128]{1,0:T(8,128)(2,1)S(1)}, u32[]{:S(2)}, u32[]{:S(2)}) collective-permute-start(bf16[2064,128]{1,0:T(8,128)(2,1)S(1)} %slice.8), channel_id=1, source_target_pairs={{0,8},{8,0},{16,24},{24,16},{1,9},{9,1},{17,25},{25,17},{2,10},{10... | collective-permute-start | bytes 1585160 | tf_op jit(solution)/shard_map/ppermute | solution.py:308
  37.1 14.3 %collective-permute-start.9 = (bf16[2048,128]{1,0:T(8,128)(2,1)S(1)}, bf16[2048,128]{1,0:T(8,128)(2,1)S(1)}, u32[]{:S(2)}, u32[]{:S(2)}) collective-permute-start(bf16[2048,128]{1,0:T(8,128)(2,1)S(1)} %slice.9), channel_id=1, source_target_pairs={{0,16},{8,24},{16,0},{24,8},{1,17},{9,25},{17,1},{25,9},{2,18},{10... | collective-permute-start | bytes 1572872 | tf_op jit(solution)/shard_map/ppermute | solution.py:308
  50.7 3.1 %collective-permute-start.10 = (bf16[2064,128]{1,0:T(8,128)(2,1)S(1)}, bf16[2064,128]{1,0:T(8,128)(2,1)S(1)}, u32[]{:S(2)}, u32[]{:S(2)}) collective-permute-start(bf16[2064,128]{1,0:T(8,128)(2,1)S(1)} %collective-permute-done.7.refs_0_), channel_id=1, source_target_pairs={{0,1},{1,0},{2,3},{3,2},{4,5},{5,4},{6,7},{7,6},{8,9},{9,8},{10,11... | collective-permute-start | bytes 1585160 | tf_op jit(solution)/shard_map/ppermute | solution.py:315
  58.8 11.1 %collective-permute-start.12 = (bf16[4,2,128,128]{3,2,1,0:T(8,128)(2,1)S(1)}, bf16[4,2,128,128]{3,2,1,0:T(8,128)(2,1)S(1)}, u32[]{:S(2)}, u32[]{:S(2)}) collective-permute-start(bf16[4,2,128,128]{3,2,1,0:T(8,128)(2,1)S(1)} %get-tuple-element.55), channel_id=1, source_target_pairs={{0,8},{8,0},{16,24},{24,16},{1,9},{9,1},{17,25},{25,17},{2,10},{10... | collective-permute-start | bytes 786440 | tf_op jit(solution)/shard_map/ppermute | solution.py:308
  59.4 10.5 %collective-permute-start.13 = (bf16[4,2,128,128]{3,2,1,0:T(8,128)(2,1)S(1)}, bf16[4,2,128,128]{3,2,1,0:T(8,128)(2,1)S(1)}, u32[]{:S(2)}, u32[]{:S(2)}) collective-permute-start(bf16[4,2,128,128]{3,2,1,0:T(8,128)(2,1)S(1)} %get-tuple-element.57), channel_id=1, source_target_pairs={{0,16},{8,24},{16,0},{24,8},{1,17},{9,25},{17,1},{25,9},{2,18},{10... | collective-permute-start | bytes 786440 | tf_op jit(solution)/shard_map/ppermute | solution.py:308
  60.9 6.0 %copy-start.3 = (s32[8,4]{0,1:T(4,128)S(1)}, s32[8,4]{0,1:T(4,128)}, u32[]{:S(2)}) copy-start(s32[8,4]{0,1:T(4,128)} %param.9) | copy-start | bytes 388
  64.8 12.7 %collective-permute-start.11 = (bf16[4,2,128,128]{3,2,1,0:T(8,128)(2,1)S(1)}, bf16[4,2,128,128]{3,2,1,0:T(8,128)(2,1)S(1)}, u32[]{:S(2)}, u32[]{:S(2)}) collective-permute-start(bf16[4,2,128,128]{3,2,1,0:T(8,128)(2,1)S(1)} %get-tuple-element.53), channel_id=1, source_target_pairs={{0,8},{8,0},{16,24},{24,16},{1,9},{9,1},{17,25},{25,17},{2,10},{10... | collective-permute-start | bytes 786440 | tf_op jit(solution)/shard_map/ppermute | solution.py:308
  65.4 12.1 %collective-permute-start.16 = (bf16[4,2,128,128]{3,2,1,0:T(8,128)(2,1)S(1)}, bf16[4,2,128,128]{3,2,1,0:T(8,128)(2,1)S(1)}, u32[]{:S(2)}, u32[]{:S(2)}) collective-permute-start(bf16[4,2,128,128]{3,2,1,0:T(8,128)(2,1)S(1)} %get-tuple-element.60), channel_id=1, source_target_pairs={{0,16},{8,24},{16,0},{24,8},{1,17},{9,25},{17,1},{25,9},{2,18},{10... | collective-permute-start | bytes 786440 | tf_op jit(solution)/shard_map/ppermute | solution.py:308
  70.1 8.6 %collective-permute-start.14 = (bf16[4,2,128,128]{3,2,1,0:T(8,128)(2,1)S(1)}, bf16[4,2,128,128]{3,2,1,0:T(8,128)(2,1)S(1)}, u32[]{:S(2)}, u32[]{:S(2)}) collective-permute-start(bf16[4,2,128,128]{3,2,1,0:T(8,128)(2,1)S(1)} %get-tuple-element.58), channel_id=1, source_target_pairs={{0,8},{8,0},{16,24},{24,16},{1,9},{9,1},{17,25},{25,17},{2,10},{10... | collective-permute-start | bytes 786440 | tf_op jit(solution)/shard_map/ppermute | solution.py:308
  70.7 8.3 %collective-permute-start.15 = (bf16[4,2,128,128]{3,2,1,0:T(8,128)(2,1)S(1)}, bf16[4,2,128,128]{3,2,1,0:T(8,128)(2,1)S(1)}, u32[]{:S(2)}, u32[]{:S(2)}) collective-permute-start(bf16[4,2,128,128]{3,2,1,0:T(8,128)(2,1)S(1)} %get-tuple-element.59), channel_id=1, source_target_pairs={{0,16},{8,24},{16,0},{24,8},{1,17},{9,25},{17,1},{25,9},{2,18},{10... | collective-permute-start | bytes 786440 | tf_op jit(solution)/shard_map/ppermute | solution.py:308

commit v9 on v7

--- a/solution.py
+++ b/solution.py
@@ -90,15 +90,20 @@
     copy.wait()
 
 
-def fill_left(z, idx, n, col, blocks, dense, first):
-    zero = jnp.zeros((z.bs, z.wide), BF16)
+def fill_left(z, idx, n, col, blocks, dense, dense_t, first):
+    zero, zero_t = jnp.zeros((z.bs, z.wide), BF16), jnp.zeros((z.wide, z.bs), BF16)
     for i in range(z.rows):
         rows = slice(i * z.bs, (i + 1) * z.bs)
         dense[rows, first:first + z.wide] = zero
+        if dense_t is not None:
+            dense_t[first:first + z.wide, rows] = zero_t
         for s in range(z.ka):
             k = idx[n, s, i] - col * z.bc
             at = pl.ds(pl.multiple_of(first + k * z.bs, z.bs), z.bs)
-            dense[rows, at] = blocks[block_rows(z, i, s, z.ka), :]
+            block = blocks[block_rows(z, i, s, z.ka), :]
+            dense[rows, at] = block
+            if dense_t is not None:
+                dense_t[at, rows] = block.T
 
 
 def fill_right(z, first_slot, slots, idx, payloads, flips, place, dense):
@@ -132,40 +137,45 @@
 
 def first_kernel(z, counts, *refs):
     left_in, right_in = refs[:z.n_first], group(refs[z.n_first:], counts)
-    total, panel, right_last, table, right, ints, idx, sem = refs[z.n_first + sum(counts):]
+    total, panel, panel_t, right_last, table, right, ints, idx, sem = refs[z.n_first + sum(counts):]
     read_tails([x[-1] for x in right_in] + list(left_in), ints, idx, sem)
     table[...] = ints[0:z.n_row]
     fill_right(z, z.ka, z.kh, idx, right_in, range(z.n_row), functools.partial(by_piece, z), right)
     for n in range(z.n_first):
-        fill_left(z, idx, z.n_row + n, piece_col(z, n), left_in[n], panel, n * z.wide)
+        fill_left(z, idx, z.n_row + n, piece_col(z, n), left_in[n], panel, None, n * z.wide)
     deep = z.n_first * z.wide
     for rows in halves(z.tall):
         total[rows, :] = jnp.dot(panel[rows, :], right[0:deep, :], preferred_element_type=F32)
+
+    def turn(n, _):
+        for i in range(z.rows):
+            rows = slice(i * z.bs, (i + 1) * z.bs)
+            at = pl.ds(pl.multiple_of(n * z.wide, z.wide), z.wide)
+            panel_t[at, rows] = panel[rows, at].T
+        return 0
+
+    lax.fori_loop(0, z.n_first, turn, 0)
     right_last[...] = right[deep:, :]
 
 
-def last_kernel(z, table, right, total_in, panel, *refs):
-    payloads, (total, turned, panel_last, *part, ints, idx, sem) = refs[:z.n_last], refs[z.n_last:]
+def last_kernel(z, table, right, total_in, panel_t, *refs):
+    payloads, (total, m16, panel_last, panel_last_t, *part, ints, idx, sem) = refs[:z.n_last], refs[z.n_last:]
     read_tails(payloads, ints, idx, sem)
     for n, payload in enumerate(payloads):
-        fill_left(z, idx, n, piece_col(z, z.n_first + n), payload, panel_last, n * z.wide)
+        fill_left(z, idx, n, piece_col(z, z.n_first + n), payload, panel_last, panel_last_t, n * z.wide)
     for rows in halves(z.tall):
         total[rows, :] = total_in[rows, :] + jnp.dot(panel_last[rows, :], right[...], preferred_element_type=F32)
-    for i in range(z.rows):
-        rows = slice(i * z.bs, (i + 1) * z.bs)
-        for j in range(z.bc):
-            cols = slice(j * z.bs, (j + 1) * z.bs)
-            turned[cols, rows] = total[rows, cols].T.astype(BF16)
-    one_part(z, table, z.n_row - 1, turned, panel, panel_last, part)
-
-
-def parts_kernel(z, table, turned, panel, panel_last, *refs):
+        m16[rows, :] = total[rows, :].astype(BF16)
+    one_part(z, table, z.n_row - 1, m16, panel_t, panel_last_t, part)
+
+
+def parts_kernel(z, table, m16, panel_t, panel_last_t, *refs):
     cuts = len(refs) // (z.n_row - 2)
     for n in range(1, z.n_row - 1):
-        one_part(z, table, n, turned, panel, panel_last, refs[(n - 1) * cuts:n * cuts])
-
-
-def one_part(z, table, n, turned, panel, panel_last, out):
+        one_part(z, table, n, m16, panel_t, panel_last_t, refs[(n - 1) * cuts:n * cuts])
+
+
+def one_part(z, table, n, m16, panel_t, panel_last_t, out):
     row = lax.axis_index("row") ^ n
     per, per_out = z.n_col // z.n_row, z.rows // len(out)
     me = lax.axis_index("col")
@@ -173,17 +183,18 @@
     def blocks(t, source, first):
         for b in range(z.bc):
             i = t * z.bc + b
-            wanted = [turned[lanes(z, table[n, s, i] - me * z.bc), :] for s in range(z.ka)]
-            column = source[:, lanes(z, first * z.bc + b)]
-            terms = jnp.dot(jnp.concatenate(wanted, axis=0), column, preferred_element_type=F32)
+            wanted = [m16[:, lanes(z, table[n, s, i] - me * z.bc)] for s in range(z.ka)]
+            terms = jnp.dot(
+                source[lanes(z, first * z.bc + b), :], jnp.concatenate(wanted, axis=1), preferred_element_type=F32
+            )
             for s in range(z.ka):
                 ref = out[i // per_out]
-                ref[i % per_out, s] = terms[s * z.bs:(s + 1) * z.bs, :].astype(ref.dtype)
+                ref[i % per_out, s] = terms[:, s * z.bs:(s + 1) * z.bs].astype(ref.dtype)
 
     for t in range(per):
         piece = piece_of(z, row * per + t)
-        pl.when(piece < z.n_first)(functools.partial(blocks, t, panel, piece))
-        pl.when(piece >= z.n_first)(functools.partial(blocks, t, panel_last, piece - z.n_first))
+        pl.when(piece < z.n_first)(functools.partial(blocks, t, panel_t, piece))
+        pl.when(piece >= z.n_first)(functools.partial(blocks, t, panel_last_t, piece - z.n_first))
 
 
 def filtered(z, filt, total, i, s):
@@ -191,17 +202,18 @@
     return total[i * z.bs:(i + 1) * z.bs, lanes(z, filt[s, i] - me * z.bc)].astype(BF16)
 
 
-def base_kernel(z, table, filt, total, turned, panel, panel_last, mixed, direct, own, held, sem):
+def base_kernel(z, table, filt, total, m16, panel_t, panel_last_t, mixed, base, held, sem):
     me = lax.axis_index("col")
     for i in range(z.rows):
         for s in range(z.kf):
             held[i, s] = filtered(z, filt, total, i, s)
     copy = pltpu.make_async_copy(held, mixed, sem)
     copy.start()
+    one_part(z, table, 0, m16, panel_t, panel_last_t, [base])
     for i in range(z.rows):
         for s in range(z.ka):
-            direct[i, s] = 3.0 * total[i * z.bs:(i + 1) * z.bs, lanes(z, table[0, s, i] - me * z.bc)]
-    one_part(z, table, 0, turned, panel, panel_last, [own])
+            direct = total[i * z.bs:(i + 1) * z.bs, lanes(z, table[0, s, i] - me * z.bc)]
+            base[i, s] = 3.0 * direct - 2.0 * base[i, s]
     copy.wait()
 
 
@@ -228,17 +240,16 @@
     y_out[...] = (y_0[...].astype(F32) + y_1[...].astype(F32)).astype(y_out.dtype)
 
 
-def gradient_kernel(z, direct, own, *refs):
+def gradient_kernel(z, base, *refs):
     terms, out = refs[:-1], refs[-1]
     half = z.rows // 2
     here = [t for t in terms if t.shape[0] == z.rows]
     cut = [t for t in terms if t.shape[0] < z.rows]
     for i in range(z.rows):
         for s in range(z.ka):
-            cubic = own[i, s]
-            for block in [t[i, s] for t in here] + [t[i % half, s] for t in cut[i // half::2]]:
-                cubic += block.astype(F32)
-            out[i, s] = (direct[i, s] - 2.0 * cubic.T).astype(out.dtype)
+            blocks = [t[i, s] for t in here] + [t[i % half, s] for t in cut[i // half::2]]
+            cubic = sum(block.astype(F32) for block in blocks)
+            out[i, s] = (base[i, s] - 2.0 * cubic).astype(out.dtype)
 
 
 def local(n_row, n_col, density, density_cols, hamilton, hamilton_cols, filter_cols):
@@ -306,12 +317,13 @@
     h_right = [h_right[flip] for flip in range(n_row)]
 
     n_pay = z.n_first + n_row
-    total, panel, right_last, table = call(
+    total, panel, panel_t, right_last, table = call(
         functools.partial(first_kernel, z, [len(x) for x in h_right]),
         [*left[:z.n_first], *sum(h_right, [])],
         [
             shape((z.tall, z.wide), F32),
             shape((z.tall, z.n_first * z.wide), BF16),
+            shape((z.n_first * z.wide, z.tall), BF16),
             shape((z.n_last * z.wide, z.wide), BF16),
             shape((n_row, 8, z.bs), jnp.int32),
         ],
@@ -321,7 +333,7 @@
             pltpu.SMEM((n_pay, 8, z.bs), jnp.int32),
             dma,
         ],
-        [vmem] * (z.n_first + sum(map(len, h_right))), [vmem] * 4, 0, "first",
+        [vmem] * (z.n_first + sum(map(len, h_right))), [vmem] * 5, 0, "first",
     )
     last, total = lax.optimization_barrier((left[-1], total))
     if n_row == 4:
@@ -331,20 +343,22 @@
     part = shape((z.rows, z.ka) + block, BF16)
     cuts = 2 if n_row == 4 and z.rows % 2 == 0 else 1
     cut_part = shape((z.rows // cuts, z.ka) + block, BF16)
-    total, turned, panel_last, *far = call(
+    total, m16, panel_last, panel_last_t, *far = call(
         functools.partial(last_kernel, z),
-        [table, right_last, total, panel, *left[z.n_first:-1], last, other_core(last)],
-        [shape((z.tall, z.wide), F32), shape((z.wide, z.tall), BF16), shape((z.tall, z.n_last * z.wide), BF16)]
-        + [cut_part] * cuts,
+        [table, right_last, total, panel_t, *left[z.n_first:-1], last, other_core(last)],
+        [
+            shape((z.tall, z.wide), F32), shape((z.tall, z.wide), BF16),
+            shape((z.tall, z.n_last * z.wide), BF16), shape((z.n_last * z.wide, z.tall), BF16),
+        ] + [cut_part] * cuts,
         [
             pltpu.VMEM((z.n_last, 8, z.bs), jnp.int32),
             pltpu.SMEM((z.n_last, 8, z.bs), jnp.int32),
             dma,
         ],
-        [smem] + [vmem] * (3 + z.n_last), [vmem] * (3 + cuts), panel_flops // 4 + part_flops, "last",
+        [smem] + [vmem] * (3 + z.n_last), [vmem] * (4 + cuts), panel_flops // 4 + part_flops, "last",
     )
     near = call(
-        functools.partial(parts_kernel, z), [table, turned, panel, panel_last], [cut_part] * (cuts * (n_row - 2)), [],
+        functools.partial(parts_kernel, z), [table, m16, panel_t, panel_last_t], [cut_part] * (cuts * (n_row - 2)), [],
         [smem] + [vmem] * 3, [vmem] * (cuts * (n_row - 2)), part_flops * (n_row - 2), "parts",
     )
     near, d_right = lax.optimization_barrier((near, d_right))
@@ -353,13 +367,12 @@
         x_0, y_1 = over_row(near[0], 1), over_row(near[3], 2)
     else:
         received = [over_row(term, n + 1) for n, term in enumerate([*near, *far])]
-    whole_part = shape((z.rows, z.ka) + block, F32)
-    mixed, direct, own = call(
+    mixed, base = call(
         functools.partial(base_kernel, z),
-        [table, filter_cols.T, total, turned, panel, panel_last],
-        [shape((z.rows, z.kf) + block, BF16), whole_part, whole_part],
+        [table, filter_cols.T, total, m16, panel_t, panel_last_t],
+        [shape((z.rows, z.kf) + block, BF16), shape((z.rows, z.ka) + block, F32)],
         [pltpu.VMEM((z.rows, z.kf) + block, BF16), dma],
-        [smem] * 2 + [vmem] * 4, [anywhere, vmem, vmem], part_flops, "base",
+        [smem] * 2 + [vmem] * 4, [anywhere, vmem], part_flops, "base",
     )
     if cuts == 2:
         y_0, x_1 = call(
@@ -378,8 +391,8 @@
         [smem] * 2 + [vmem] * (2 + sum(map(len, d_right))), [anywhere], panel_flops, "squared",
     )
     gradient, = call(
-        functools.partial(gradient_kernel, z), [direct, own, *received], [part], [],
-        [vmem] * (2 + len(received)), [vmem], 0, "gradient",
+        functools.partial(gradient_kernel, z), [base, *received], [part], [],
+        [vmem] * (1 + len(received)), [vmem], 0, "gradient",
     )
     return squared, mixed, gradient
 

time: 79.3 us -> 78.2 us (0.986)
  the two profiles are of different devices: /device:TPU:24 before, /device:TPU:0 now
where the time goes in v9:
time: 78.2 us; the launch traced here: 76.9 us
  starting transfers between devices  30.4 us (39%)
  Pallas kernels  27.7 us (35%)
  waiting for transfers between devices  13.8 us (18%)
  local copies, waits for them, and re-layouts  4.19 us (5%)
  between operations  0.8 us (1%)
    pallas_call x9, Pallas kernels, call(): pl.pallas_call(kernel, out_shape=outs, in_specs=in_specs, out_specs=out_s...  27.7 us
    ppermute x14, starting transfers between devices, over_row(): return lax.ppermute(x, 'row', [(r, r ^ flip) for r in range(n_row)])  20.6 us
    ppermute x3, waiting for transfers between devices, next_chip(): lax.ppermute(x, 'col', [(c, (c // 2 + move[c % 2]) % z.n_chip * 2 + c % 2...  7.28 us
    ppermute x14, waiting for transfers between devices, over_row(): return lax.ppermute(x, 'row', [(r, r ^ flip) for r in range(n_row)])  6.55 us
    ppermute x4, starting transfers between devices, other_core(): return lax.ppermute(x, 'col', [(c, c ^ 1) for c in range(n_col)])  5.45 us
    ppermute x3, starting transfers between devices, next_chip(): lax.ppermute(x, 'col', [(c, (c // 2 + move[c % 2]) % z.n_chip * 2 + c % 2...  4.31 us
    unnamed x12, local copies, waits for them, and re-layouts  4.11 us
  transfers between devices with their start and end apart: 21, of which 7 were waited for; matrix products, arithmetic and copies ran while one was open for 0% of the time, Pallas kernels for 35%

profile of v9, /device:TPU:0, one launch (start us, length us, event | category | flops | bytes accessed | tf_op | source)
XLA Modules:
  0.0 76.9 jit_solution(14125139307378320010)
XLA Ops:
  0.6 1.0 %copy-done = bf16[8,2,128,128]{3,2,1,0:T(8,128)(2,1)S(1)} copy-done((bf16[8,2,128,128]{3,2,1,0:T(8,128)(2,1)S(1)}, bf16[8,2,128,128]{3,2,1,0:T(8,128)(2,1)}, u32[]{:S(2)}) %copy-start) | copy-done | bytes 524312
  1.7 0.7 copy-done.2
  2.4 3.1 %collective-permute-start = (bf16[2064,128]{1,0:T(8,128)(2,1)S(1)}, bf16[2064,128]{1,0:T(8,128)(2,1)S(1)}, u32[]{:S(2)}, u32[]{:S(2)}) collective-permute-start(bf16[2064,128]{1,0:T(8,128)(2,1)S(1)} %pack_d.1.refs_0_), channel_id=1, source_target_pairs={{0,2},{1,7},{2,4},{3,1},{4,6},{5,3},{6,0},{7,5},{8,10},{9,15},{10,... | collective-permute-start | bytes 1585160 | tf_op jit(solution)/shard_map/ppermute | solution.py:272
  5.5 1.0 %copy-done.1 = bf16[8,2,128,128]{3,2,1,0:T(8,128)(2,1)S(1)} copy-done((bf16[8,2,128,128]{3,2,1,0:T(8,128)(2,1)S(1)}, bf16[8,2,128,128]{3,2,1,0:T(8,128)(2,1)}, u32[]{:S(2)}) %copy-start.1) | copy-done | bytes 524312
  6.5 0.7 copy-done.3
  7.2 0.7 copy-done.5
  7.9 1.6 %collective-permute-start.1 = (bf16[2064,128]{1,0:T(8,128)(2,1)S(1)}, bf16[2064,128]{1,0:T(8,128)(2,1)S(1)}, u32[]{:S(2)}, u32[]{:S(2)}) collective-permute-start(bf16[2064,128]{1,0:T(8,128)(2,1)S(1)} %pack_h.1.refs_5_), channel_id=1, source_target_pairs={{0,8},{8,0},{16,24},{24,16},{1,9},{9,1},{17,25},{25,17},{2,10},{10... | collective-permute-start | bytes 1585160 | tf_op jit(solution)/shard_map/ppermute | solution.py:268
  9.5 1.5 %collective-permute-start.2 = (bf16[2064,128]{1,0:T(8,128)(2,1)S(1)}, bf16[2064,128]{1,0:T(8,128)(2,1)S(1)}, u32[]{:S(2)}, u32[]{:S(2)}) collective-permute-start(bf16[2064,128]{1,0:T(8,128)(2,1)S(1)} %pack_h.1.refs_5_), channel_id=1, source_target_pairs={{0,16},{8,24},{16,0},{24,8},{1,17},{9,25},{17,1},{25,9},{2,18},{10... | collective-permute-start | bytes 1585160 | tf_op jit(solution)/shard_map/ppermute | solution.py:268
  11.0 1.0 %collective-permute-start.3 = (bf16[2064,128]{1,0:T(8,128)(2,1)S(1)}, bf16[2064,128]{1,0:T(8,128)(2,1)S(1)}, u32[]{:S(2)}, u32[]{:S(2)}) collective-permute-start(bf16[2064,128]{1,0:T(8,128)(2,1)S(1)} %pack_d.1.refs_0_), channel_id=1, source_target_pairs={{0,1},{1,0},{2,3},{3,2},{4,5},{5,4},{6,7},{7,6},{8,9},{9,8},{10,11... | collective-permute-start | bytes 1585160 | tf_op jit(solution)/shard_map/ppermute | solution.py:275
  12.0 1.2 %collective-permute-start.5 = (bf16[2064,128]{1,0:T(8,128)(2,1)S(1)}, bf16[2064,128]{1,0:T(8,128)(2,1)S(1)}, u32[]{:S(2)}, u32[]{:S(2)}) collective-permute-start(bf16[2064,128]{1,0:T(8,128)(2,1)S(1)} %pack_d.1.refs_0_), channel_id=1, source_target_pairs={{0,6},{1,3},{2,0},{3,5},{4,2},{5,7},{6,4},{7,1},{8,14},{9,11},{10,... | collective-permute-start | bytes 1585160 | tf_op jit(solution)/shard_map/ppermute | solution.py:272
  13.2 7.2 %collective-permute-done.refs_2_ = bf16[2064,128]{1,0:T(8,128)(2,1)S(1)} collective-permute-done((bf16[2064,128]{1,0:T(8,128)(2,1)S(1)}, bf16[2064,128]{1,0:T(8,128)(2,1)S(1)}, u32[]{:S(2)}, u32[]{:S(2)}) %collective-permute-start) | collective-permute-done | bytes 528416 | tf_op jit(solution)/shard_map/ppermute | solution.py:272
  20.4 1.9 %collective-permute-done.1.refs_6_ = bf16[2064,128]{1,0:T(8,128)(2,1)S(1)} collective-permute-done((bf16[2064,128]{1,0:T(8,128)(2,1)S(1)}, bf16[2064,128]{1,0:T(8,128)(2,1)S(1)}, u32[]{:S(2)}, u32[]{:S(2)}) %collective-permute-start.1) | collective-permute-done | bytes 528416 | tf_op jit(solution)/shard_map/ppermute | solution.py:268
  22.3 1.7 %collective-permute-done.2.refs_7_ = bf16[2064,128]{1,0:T(8,128)(2,1)S(1)} collective-permute-done((bf16[2064,128]{1,0:T(8,128)(2,1)S(1)}, bf16[2064,128]{1,0:T(8,128)(2,1)S(1)}, u32[]{:S(2)}, u32[]{:S(2)}) %collective-permute-start.2) | collective-permute-done | bytes 528416 | tf_op jit(solution)/shard_map/ppermute | solution.py:268
  24.0 0.5 collective-permute-start.4
  24.5 1.9 %collective-permute-start.7 = (bf16[1040,128]{1,0:T(8,128)(2,1)S(1)}, bf16[1040,128]{1,0:T(8,128)(2,1)S(1)}, u32[]{:S(2)}, u32[]{:S(2)}) collective-permute-start(bf16[1040,128]{1,0:T(8,128)(2,1)S(1)} %slice.13), channel_id=1, source_target_pairs={{0,8},{8,0},{16,24},{24,16},{1,9},{9,1},{17,25},{25,17},{2,10},{10... | collective-permute-start | bytes 798728 | tf_op jit(solution)/shard_map/ppermute | solution.py:268
  26.4 2.6 %collective-permute-start.6 = (bf16[1024,128]{1,0:T(8,128)(2,1)S(1)}, bf16[1024,128]{1,0:T(8,128)(2,1)S(1)}, u32[]{:S(2)}, u32[]{:S(2)}) collective-permute-start(bf16[1024,128]{1,0:T(8,128)(2,1)S(1)} %slice.12), channel_id=1, source_target_pairs={{0,16},{8,24},{16,0},{24,8},{1,17},{9,25},{17,1},{25,9},{2,18},{10... | collective-permute-start | bytes 786440 | tf_op jit(solution)/shard_map/ppermute | solution.py:268
  29.1 1.7 %collective-permute-start.11 = (bf16[2064,128]{1,0:T(8,128)(2,1)S(1)}, bf16[2064,128]{1,0:T(8,128)(2,1)S(1)}, u32[]{:S(2)}, u32[]{:S(2)}) collective-permute-start(bf16[2064,128]{1,0:T(8,128)(2,1)S(1)} %pack_d.1.refs_0_), channel_id=1, source_target_pairs={{0,8},{8,0},{16,24},{24,16},{1,9},{9,1},{17,25},{25,17},{2,10},{10... | collective-permute-start | bytes 1585160 | tf_op jit(solution)/shard_map/ppermute | solution.py:268
  30.8 2.5 %collective-permute-done.6.refs_8_ = bf16[1024,128]{1,0:T(8,128)(2,1)S(1)} collective-permute-done((bf16[1024,128]{1,0:T(8,128)(2,1)S(1)}, bf16[1024,128]{1,0:T(8,128)(2,1)S(1)}, u32[]{:S(2)}, u32[]{:S(2)}) %collective-permute-start.6) | collective-permute-done | bytes 262176 | tf_op jit(solution)/shard_map/ppermute | solution.py:268
  33.4 2.0 %collective-permute-start.12 = (bf16[2064,128]{1,0:T(8,128)(2,1)S(1)}, bf16[2064,128]{1,0:T(8,128)(2,1)S(1)}, u32[]{:S(2)}, u32[]{:S(2)}) collective-permute-start(bf16[2064,128]{1,0:T(8,128)(2,1)S(1)} %pack_d.1.refs_0_), channel_id=1, source_target_pairs={{0,16},{8,24},{16,0},{24,8},{1,17},{9,25},{17,1},{25,9},{2,18},{10... | collective-permute-start | bytes 1585160 | tf_op jit(solution)/shard_map/ppermute | solution.py:268
  35.4 3.9 %collective-permute-start.9 = (bf16[2064,128]{1,0:T(8,128)(2,1)S(1)}, bf16[2064,128]{1,0:T(8,128)(2,1)S(1)}, u32[]{:S(2)}, u32[]{:S(2)}) collective-permute-start(bf16[2064,128]{1,0:T(8,128)(2,1)S(1)} %collective-permute-done.5.refs_4_), channel_id=1, source_target_pairs={{0,1},{1,0},{2,3},{3,2},{4,5},{5,4},{6,7},{7,6},{8,9},{9,8},{10,11... | collective-permute-start | bytes 1585160 | tf_op jit(solution)/shard_map/ppermute | solution.py:275
  39.3 7.6 %first.1 = (f32[1024,512]{1,0:T(8,128)S(1)}, bf16[1024,2560]{1,0:T(8,128)(2,1)S(1)}, bf16[2560,1024]{1,0:T(8,128)(2,1)S(1)}, bf16[1536,512]{1,0:T(8,128)(2,1)S(1)}, s32[4,8,128]{2,1,0:T(8,128)S(1)}) custom-call(bf16[2064,128]{1,0:T(8,128)(2,1)S(1)} %pack_d.1.refs_0_, bf16[2064,128]{1,0:T(8,128)(2,1)S(1)} %collective-permute-done.3.refs_1_, ...), custom_call_target="tpu_custom_call" | custom-call | bytes 1024 | tf_op jit(solution)/shard_map/first/pallas_call | solution.py:32
  47.1 1.5 %collective-permute-start.13 = (bf16[1024,128]{1,0:T(8,128)(2,1)S(1)}, bf16[1024,128]{1,0:T(8,128)(2,1)S(1)}, u32[]{:S(2)}, u32[]{:S(2)}) collective-permute-start(bf16[1024,128]{1,0:T(8,128)(2,1)S(1)} %slice.16), channel_id=1, source_target_pairs={{0,16},{8,24},{16,0},{24,8},{1,17},{9,25},{17,1},{25,9},{2,18},{10... | collective-permute-start | bytes 786440 | tf_op jit(solution)/shard_map/ppermute | solution.py:268
  48.6 1.8 %collective-permute-start.14 = (bf16[1024,128]{1,0:T(8,128)(2,1)S(1)}, bf16[1024,128]{1,0:T(8,128)(2,1)S(1)}, u32[]{:S(2)}, u32[]{:S(2)}) collective-permute-start(bf16[1024,128]{1,0:T(8,128)(2,1)S(1)} %slice.17), channel_id=1, source_target_pairs={{0,8},{8,0},{16,24},{24,16},{1,9},{9,1},{17,25},{25,17},{2,10},{10... | collective-permute-start | bytes 786440 | tf_op jit(solution)/shard_map/ppermute | solution.py:268
  50.4 6.0 %last.1 = (f32[1024,512]{1,0:T(8,128)S(1)}, bf16[1024,512]{1,0:T(8,128)(2,1)S(1)}, bf16[1024,1536]{1,0:T(8,128)(2,1)S(1)}, bf16[1536,1024]{1,0:T(8,128)(2,1)S(1)...) custom-call(s32[4,8,128]{2,1,0:T(8,128)S(1)} %get-tuple-element.46.table, ...), custom_call_target="tpu_custom_call" | custom-call | flops 2147483648 | bytes 1024 | tf_op jit(solution)/shard_map/last/pallas_call | solution.py:32
  56.8 1.4 %collective-permute-start.17 = (bf16[4,2,128,128]{3,2,1,0:T(8,128)(2,1)S(1)}, bf16[4,2,128,128]{3,2,1,0:T(8,128)(2,1)S(1)}, u32[]{:S(2)}, u32[]{:S(2)}) collective-permute-start(bf16[4,2,128,128]{3,2,1,0:T(8,128)(2,1)S(1)} %get-tuple-element.73), channel_id=1, source_target_pairs={{0,16},{8,24},{16,0},{24,8},{1,17},{9,25},{17,1},{25,9},{2,18},{10... | collective-permute-start | bytes 786440 | tf_op jit(solution)/shard_map/ppermute | solution.py:268
  58.2 3.2 %parts.1 = (bf16[4,2,128,128]{3,2,1,0:T(8,128)(2,1)S(1)}, bf16[4,2,128,128]{3,2,1,0:T(8,128)(2,1)S(1)}, bf16[4,2,128,128]{3,2,1,0:T(8,128)(2,1)S(1)}, bf16[4,2,128,128]{3,2,1,0:T(8,128)(2,1)S(1)}) custom-call(s32[4,8,128]{2,1,0:T(8,128)S(1)} %get-tuple-element.46.table, bf16[1024,512]{1,0:T(8,128)(2,1)S(1)} %get-tuple-element.54.m16, ...), custom_call_target="tpu_custom_call" | custom-call | flops 2147483648 | bytes 1024 | tf_op jit(solution)/shard_map/parts/pallas_call | solution.py:32
  61.8 2.0 %collective-permute-start.20 = (bf16[4,2,128,128]{3,2,1,0:T(8,128)(2,1)S(1)}, bf16[4,2,128,128]{3,2,1,0:T(8,128)(2,1)S(1)}, u32[]{:S(2)}, u32[]{:S(2)}) collective-permute-start(bf16[4,2,128,128]{3,2,1,0:T(8,128)(2,1)S(1)} %get-tuple-element.76), channel_id=1, source_target_pairs={{0,16},{8,24},{16,0},{24,8},{1,17},{9,25},{17,1},{25,9},{2,18},{10... | collective-permute-start | bytes 786440 | tf_op jit(solution)/shard_map/ppermute | solution.py:268
  63.9 2.4 %base.1 = (bf16[8,4,128,128]{3,2,1,0:T(8,128)(2,1)}, f32[8,2,128,128]{3,2,1,0:T(8,128)S(1)}) custom-call(s32[4,8,128]{2,1,0:T(8,128)S(1)} %get-tuple-element.46.table, s32[4,8]{1,0:T(4,128)S(1)} %bitcast.9, f32[1024,512]{1,0:T(8,128)S(1)} %get-tuple-element.66.total, bf16[1024,512]{1,0:T(8,128)(2,1)S(1)} %get-tuple-element.54.m16, ...), custom_call_target="tpu_custom_call" | custom-call | flops 1073741824 | bytes 1024 | tf_op jit(solution)/shard_map/base/pallas_call | solution.py:32
  66.4 1.0 %collective-permute-start.18 = (bf16[4,2,128,128]{3,2,1,0:T(8,128)(2,1)S(1)}, bf16[4,2,128,128]{3,2,1,0:T(8,128)(2,1)S(1)}, u32[]{:S(2)}, u32[]{:S(2)}) collective-permute-start(bf16[4,2,128,128]{3,2,1,0:T(8,128)(2,1)S(1)} %get-tuple-element.74), channel_id=1, source_target_pairs={{0,8},{8,0},{16,24},{24,16},{1,9},{9,1},{17,25},{25,17},{2,10},{10... | collective-permute-start | bytes 786440 | tf_op jit(solution)/shard_map/ppermute | solution.py:268
  67.4 0.7 collective-permute-start.19
  68.2 7.3 %squared.1 = bf16[8,4,128,128]{3,2,1,0:T(8,128)(2,1)} custom-call(s32[4,8,128]{2,1,0:T(8,128)S(1)} %get-tuple-element.46.table, s32[4,8]{1,0:T(4,128)S(1)} %bitcast.10, bf16[1024,2560]{1,0:T(8,128)(2,1)S(1)} %get-tuple-element.47.panel, bf16[1024,1536]{1,0:T(8,128)(2,1)S(1)} %get-tuple-element.53.panel_last, bf16[2064,128]{1,0:T(8,128)(2,1)S(1)} %pack_d.1.refs_0_, ...), custom_call_target="tpu_custom_call" | custom-call | flops 4294967296 | bytes 1024 | tf_op jit(solution)/shard_map/squared/pallas_call | solution.py:32
  75.9 1.0 %gradient.1 = bf16[8,2,128,128]{3,2,1,0:T(8,128)(2,1)} custom-call(f32[8,2,128,128]{3,2,1,0:T(8,128)S(1)} %get-tuple-element.68.base, bf16[4,2,128,128]{3,2,1,0:T(8,128)(2,1)S(1)} %collective-permute-done.15.refs_0_, bf16[4,2,128,128]{3,2,1,0:T(8,128)(2,1)S(1)} %collective-permute-done.18.refs_1_, ...), custom_call_target="tpu_custom_call" | custom-call | bytes 1024 | tf_op jit(solution)/shard_map/gradient/pallas_call | solution.py:32
  (35 shorter events, 1.6 us)
Async XLA Ops:
  0.6 1.0 %copy-start = (bf16[8,2,128,128]{3,2,1,0:T(8,128)(2,1)S(1)}, bf16[8,2,128,128]{3,2,1,0:T(8,128)(2,1)}, u32[]{:S(2)}) copy-start(bf16[8,2,128,128]{3,2,1,0:T(8,128)(2,1)} %param.5) | copy-start | bytes 1572868
  1.7 0.7 copy-start.2
  2.4 18.0 %collective-permute-start = (bf16[2064,128]{1,0:T(8,128)(2,1)S(1)}, bf16[2064,128]{1,0:T(8,128)(2,1)S(1)}, u32[]{:S(2)}, u32[]{:S(2)}) collective-permute-start(bf16[2064,128]{1,0:T(8,128)(2,1)S(1)} %pack_d.1.refs_0_), channel_id=1, source_target_pairs={{0,2},{1,7},{2,4},{3,1},{4,6},{5,3},{6,0},{7,5},{8,10},{9,15},{10,... | collective-permute-start | bytes 1585160 | tf_op jit(solution)/shard_map/ppermute | solution.py:272
  5.5 1.0 %copy-start.1 = (bf16[8,2,128,128]{3,2,1,0:T(8,128)(2,1)S(1)}, bf16[8,2,128,128]{3,2,1,0:T(8,128)(2,1)}, u32[]{:S(2)}) copy-start(bf16[8,2,128,128]{3,2,1,0:T(8,128)(2,1)} %param.7) | copy-start | bytes 1572868
  6.5 0.7 copy-start.3
  7.2 0.7 copy-start.5
  7.9 14.4 %collective-permute-start.1 = (bf16[2064,128]{1,0:T(8,128)(2,1)S(1)}, bf16[2064,128]{1,0:T(8,128)(2,1)S(1)}, u32[]{:S(2)}, u32[]{:S(2)}) collective-permute-start(bf16[2064,128]{1,0:T(8,128)(2,1)S(1)} %pack_h.1.refs_5_), channel_id=1, source_target_pairs={{0,8},{8,0},{16,24},{24,16},{1,9},{9,1},{17,25},{25,17},{2,10},{10... | collective-permute-start | bytes 1585160 | tf_op jit(solution)/shard_map/ppermute | solution.py:268
  9.5 14.6 %collective-permute-start.2 = (bf16[2064,128]{1,0:T(8,128)(2,1)S(1)}, bf16[2064,128]{1,0:T(8,128)(2,1)S(1)}, u32[]{:S(2)}, u32[]{:S(2)}) collective-permute-start(bf16[2064,128]{1,0:T(8,128)(2,1)S(1)} %pack_h.1.refs_5_), channel_id=1, source_target_pairs={{0,16},{8,24},{16,0},{24,8},{1,17},{9,25},{17,1},{25,9},{2,18},{10... | collective-permute-start | bytes 1585160 | tf_op jit(solution)/shard_map/ppermute | solution.py:268
  11.0 13.0 %collective-permute-start.3 = (bf16[2064,128]{1,0:T(8,128)(2,1)S(1)}, bf16[2064,128]{1,0:T(8,128)(2,1)S(1)}, u32[]{:S(2)}, u32[]{:S(2)}) collective-permute-start(bf16[2064,128]{1,0:T(8,128)(2,1)S(1)} %pack_d.1.refs_0_), channel_id=1, source_target_pairs={{0,1},{1,0},{2,3},{3,2},{4,5},{5,4},{6,7},{7,6},{8,9},{9,8},{10,11... | collective-permute-start | bytes 1585160 | tf_op jit(solution)/shard_map/ppermute | solution.py:275
  12.0 17.1 %collective-permute-start.5 = (bf16[2064,128]{1,0:T(8,128)(2,1)S(1)}, bf16[2064,128]{1,0:T(8,128)(2,1)S(1)}, u32[]{:S(2)}, u32[]{:S(2)}) collective-permute-start(bf16[2064,128]{1,0:T(8,128)(2,1)S(1)} %pack_d.1.refs_0_), channel_id=1, source_target_pairs={{0,6},{1,3},{2,0},{3,5},{4,2},{5,7},{6,4},{7,1},{8,14},{9,11},{10,... | collective-permute-start | bytes 1585160 | tf_op jit(solution)/shard_map/ppermute | solution.py:272
  24.0 15.3 %collective-permute-start.4 = (bf16[2064,128]{1,0:T(8,128)(2,1)S(1)}, bf16[2064,128]{1,0:T(8,128)(2,1)S(1)}, u32[]{:S(2)}, u32[]{:S(2)}) collective-permute-start(bf16[2064,128]{1,0:T(8,128)(2,1)S(1)} %collective-permute-done.refs_2_), channel_id=1, source_target_pairs={{0,1},{1,0},{2,3},{3,2},{4,5},{5,4},{6,7},{7,6},{8,9},{9,8},{10,11... | collective-permute-start | bytes 1585160 | tf_op jit(solution)/shard_map/ppermute | solution.py:275
  24.5 22.5 %collective-permute-start.8 = (bf16[2064,128]{1,0:T(8,128)(2,1)S(1)}, bf16[2064,128]{1,0:T(8,128)(2,1)S(1)}, u32[]{:S(2)}, u32[]{:S(2)}) collective-permute-start(bf16[2064,128]{1,0:T(8,128)(2,1)S(1)} %collective-permute-done.refs_2_), channel_id=1, source_target_pairs={{0,2},{1,7},{2,4},{3,1},{4,6},{5,3},{6,0},{7,5},{8,10},{9,15},{10,... | collective-permute-start | bytes 1585160 | tf_op jit(solution)/shard_map/ppermute | solution.py:272
  24.5 10.9 %collective-permute-start.7 = (bf16[1040,128]{1,0:T(8,128)(2,1)S(1)}, bf16[1040,128]{1,0:T(8,128)(2,1)S(1)}, u32[]{:S(2)}, u32[]{:S(2)}) collective-permute-start(bf16[1040,128]{1,0:T(8,128)(2,1)S(1)} %slice.13), channel_id=1, source_target_pairs={{0,8},{8,0},{16,24},{24,16},{1,9},{9,1},{17,25},{25,17},{2,10},{10... | collective-permute-start | bytes 798728 | tf_op jit(solution)/shard_map/ppermute | solution.py:268
  26.4 7.0 %collective-permute-start.6 = (bf16[1024,128]{1,0:T(8,128)(2,1)S(1)}, bf16[1024,128]{1,0:T(8,128)(2,1)S(1)}, u32[]{:S(2)}, u32[]{:S(2)}) collective-permute-start(bf16[1024,128]{1,0:T(8,128)(2,1)S(1)} %slice.12), channel_id=1, source_target_pairs={{0,16},{8,24},{16,0},{24,8},{1,17},{9,25},{17,1},{25,9},{2,18},{10... | collective-permute-start | bytes 786440 | tf_op jit(solution)/shard_map/ppermute | solution.py:268
  29.1 17.9 %collective-permute-start.11 = (bf16[2064,128]{1,0:T(8,128)(2,1)S(1)}, bf16[2064,128]{1,0:T(8,128)(2,1)S(1)}, u32[]{:S(2)}, u32[]{:S(2)}) collective-permute-start(bf16[2064,128]{1,0:T(8,128)(2,1)S(1)} %pack_d.1.refs_0_), channel_id=1, source_target_pairs={{0,8},{8,0},{16,24},{24,16},{1,9},{9,1},{17,25},{25,17},{2,10},{10... | collective-permute-start | bytes 1585160 | tf_op jit(solution)/shard_map/ppermute | solution.py:268
  33.4 15.2 %collective-permute-start.12 = (bf16[2064,128]{1,0:T(8,128)(2,1)S(1)}, bf16[2064,128]{1,0:T(8,128)(2,1)S(1)}, u32[]{:S(2)}, u32[]{:S(2)}) collective-permute-start(bf16[2064,128]{1,0:T(8,128)(2,1)S(1)} %pack_d.1.refs_0_), channel_id=1, source_target_pairs={{0,16},{8,24},{16,0},{24,8},{1,17},{9,25},{17,1},{25,9},{2,18},{10... | collective-permute-start | bytes 1585160 | tf_op jit(solution)/shard_map/ppermute | solution.py:268
  35.4 15.0 %collective-permute-start.9 = (bf16[2064,128]{1,0:T(8,128)(2,1)S(1)}, bf16[2064,128]{1,0:T(8,128)(2,1)S(1)}, u32[]{:S(2)}, u32[]{:S(2)}) collective-permute-start(bf16[2064,128]{1,0:T(8,128)(2,1)S(1)} %collective-permute-done.5.refs_4_), channel_id=1, source_target_pairs={{0,1},{1,0},{2,3},{3,2},{4,5},{5,4},{6,7},{7,6},{8,9},{9,8},{10,11... | collective-permute-start | bytes 1585160 | tf_op jit(solution)/shard_map/ppermute | solution.py:275
  46.9 3.5 %collective-permute-start.10 = (bf16[2064,128]{1,0:T(8,128)(2,1)S(1)}, bf16[2064,128]{1,0:T(8,128)(2,1)S(1)}, u32[]{:S(2)}, u32[]{:S(2)}) collective-permute-start(bf16[2064,128]{1,0:T(8,128)(2,1)S(1)} %collective-permute-done.8.refs_1_), channel_id=1, source_target_pairs={{0,1},{1,0},{2,3},{3,2},{4,5},{5,4},{6,7},{7,6},{8,9},{9,8},{10,11... | collective-permute-start | bytes 1585160 | tf_op jit(solution)/shard_map/ppermute | solution.py:275
  47.1 14.4 %collective-permute-start.13 = (bf16[1024,128]{1,0:T(8,128)(2,1)S(1)}, bf16[1024,128]{1,0:T(8,128)(2,1)S(1)}, u32[]{:S(2)}, u32[]{:S(2)}) collective-permute-start(bf16[1024,128]{1,0:T(8,128)(2,1)S(1)} %slice.16), channel_id=1, source_target_pairs={{0,16},{8,24},{16,0},{24,8},{1,17},{9,25},{17,1},{25,9},{2,18},{10... | collective-permute-start | bytes 786440 | tf_op jit(solution)/shard_map/ppermute | solution.py:268
  48.6 12.8 %collective-permute-start.14 = (bf16[1024,128]{1,0:T(8,128)(2,1)S(1)}, bf16[1024,128]{1,0:T(8,128)(2,1)S(1)}, u32[]{:S(2)}, u32[]{:S(2)}) collective-permute-start(bf16[1024,128]{1,0:T(8,128)(2,1)S(1)} %slice.17), channel_id=1, source_target_pairs={{0,8},{8,0},{16,24},{24,16},{1,9},{9,1},{17,25},{25,17},{2,10},{10... | collective-permute-start | bytes 786440 | tf_op jit(solution)/shard_map/ppermute | solution.py:268
  56.4 9.8 %collective-permute-start.16 = (bf16[4,2,128,128]{3,2,1,0:T(8,128)(2,1)S(1)}, bf16[4,2,128,128]{3,2,1,0:T(8,128)(2,1)S(1)}, u32[]{:S(2)}, u32[]{:S(2)}) collective-permute-start(bf16[4,2,128,128]{3,2,1,0:T(8,128)(2,1)S(1)} %get-tuple-element.71), channel_id=1, source_target_pairs={{0,8},{8,0},{16,24},{24,16},{1,9},{9,1},{17,25},{25,17},{2,10},{10... | collective-permute-start | bytes 786440 | tf_op jit(solution)/shard_map/ppermute | solution.py:268
  56.8 9.5 %collective-permute-start.17 = (bf16[4,2,128,128]{3,2,1,0:T(8,128)(2,1)S(1)}, bf16[4,2,128,128]{3,2,1,0:T(8,128)(2,1)S(1)}, u32[]{:S(2)}, u32[]{:S(2)}) collective-permute-start(bf16[4,2,128,128]{3,2,1,0:T(8,128)(2,1)S(1)} %get-tuple-element.73), channel_id=1, source_target_pairs={{0,16},{8,24},{16,0},{24,8},{1,17},{9,25},{17,1},{25,9},{2,18},{10... | collective-permute-start | bytes 786440 | tf_op jit(solution)/shard_map/ppermute | solution.py:268
  58.2 5.7 %copy-start.4 = (s32[8,4]{0,1:T(4,128)S(1)}, s32[8,4]{0,1:T(4,128)}, u32[]{:S(2)}) copy-start(s32[8,4]{0,1:T(4,128)} %param.9) | copy-start | bytes 388
  61.4 14.1 %collective-permute-start.15 = (bf16[4,2,128,128]{3,2,1,0:T(8,128)(2,1)S(1)}, bf16[4,2,128,128]{3,2,1,0:T(8,128)(2,1)S(1)}, u32[]{:S(2)}, u32[]{:S(2)}) collective-permute-start(bf16[4,2,128,128]{3,2,1,0:T(8,128)(2,1)S(1)} %get-tuple-element.69), channel_id=1, source_target_pairs={{0,8},{8,0},{16,24},{24,16},{1,9},{9,1},{17,25},{25,17},{2,10},{10... | collective-permute-start | bytes 786440 | tf_op jit(solution)/shard_map/ppermute | solution.py:268
  61.8 13.7 %collective-permute-start.20 = (bf16[4,2,128,128]{3,2,1,0:T(8,128)(2,1)S(1)}, bf16[4,2,128,128]{3,2,1,0:T(8,128)(2,1)S(1)}, u32[]{:S(2)}, u32[]{:S(2)}) collective-permute-start(bf16[4,2,128,128]{3,2,1,0:T(8,128)(2,1)S(1)} %get-tuple-element.76), channel_id=1, source_target_pairs={{0,16},{8,24},{16,0},{24,8},{1,17},{9,25},{17,1},{25,9},{2,18},{10... | collective-permute-start | bytes 786440 | tf_op jit(solution)/shard_map/ppermute | solution.py:268
  66.4 9.5 %collective-permute-start.18 = (bf16[4,2,128,128]{3,2,1,0:T(8,128)(2,1)S(1)}, bf16[4,2,128,128]{3,2,1,0:T(8,128)(2,1)S(1)}, u32[]{:S(2)}, u32[]{:S(2)}) collective-permute-start(bf16[4,2,128,128]{3,2,1,0:T(8,128)(2,1)S(1)} %get-tuple-element.74), channel_id=1, source_target_pairs={{0,8},{8,0},{16,24},{24,16},{1,9},{9,1},{17,25},{25,17},{2,10},{10... | collective-permute-start | bytes 786440 | tf_op jit(solution)/shard_map/ppermute | solution.py:268
  67.4 8.5 %collective-permute-start.19 = (bf16[4,2,128,128]{3,2,1,0:T(8,128)(2,1)S(1)}, bf16[4,2,128,128]{3,2,1,0:T(8,128)(2,1)S(1)}, u32[]{:S(2)}, u32[]{:S(2)}) collective-permute-start(bf16[4,2,128,128]{3,2,1,0:T(8,128)(2,1)S(1)} %get-tuple-element.75), channel_id=1, source_target_pairs={{0,16},{8,24},{16,0},{24,8},{1,17},{9,25},{17,1},{25,9},{2,18},{10... | collective-permute-start | bytes 786440 | tf_op jit(solution)/shard_map/ppermute | solution.py:268

commit v10 on v9

--- a/solution.py
+++ b/solution.py
@@ -303,7 +303,8 @@
     if n_row == 4:
         h_right[3] = [over_row(h_right[1][0][:h_half], 2), over_row(h_right[2][0][h_half:], 1)]
     forward(h_right)
-    d_0, pieces[2] = lax.optimization_barrier((d_pay, pieces[2]))
+    twins = [twin, other_core(pieces[1])]
+    d_0, pieces[2], twins[1] = lax.optimization_barrier((d_pay, pieces[2], twins[1]))
     for step in range(3, z.n_chip):
         pieces.append(next_chip(pieces[step - 2], 1 if step % 2 else -1))
     d_right = {0: [d_0]}
@@ -313,7 +314,7 @@
     for step, piece in enumerate(pieces):
         left.append(piece)
         if step < z.n_chip - 1:
-            left.append(other_core(piece) if step else twin)
+            left.append(twins[step] if step < 2 else other_core(piece))
     h_right = [h_right[flip] for flip in range(n_row)]
 
     n_pay = z.n_first + n_row

time: 78.2 us -> 80.5 us (1.029); the launches traced: 76.9 us -> 80.2 us
  waiting for transfers between devices: 13.8 us -> 16.5 us
    ppermute x4, starting transfers between devices: 5.45 us -> 8.6 us  [other_core(): return lax.ppermute(x, 'col', [(c, c ^ 1) for c in range(n_col)])]
    ppermute x14, waiting for transfers between devices: 6.55 us -> 9.18 us  [over_row(): return lax.ppermute(x, 'row', [(r, r ^ flip) for r in range(n_row)])]
    ppermute x14, starting transfers between devices: 20.6 us -> 18.1 us  [over_row(): return lax.ppermute(x, 'row', [(r, r ^ flip) for r in range(n_row)])]
  transfers between devices with their start and end apart: 21 -> 21, of which waited for: 7 -> 8; matrix products, arithmetic and copies ran while one was open for 0% -> 0% of each run, Pallas kernels for 35% -> 33%
where the time goes in v10:
time: 80.5 us; the launch traced here: 80.2 us
  starting transfers between devices  31 us (39%)
  Pallas kernels  27.8 us (35%)
  waiting for transfers between devices  16.5 us (20%)
  local copies, waits for them, and re-layouts  4.19 us (5%)
    pallas_call x9, Pallas kernels, call(): pl.pallas_call(kernel, out_shape=outs, in_specs=in_specs, out_specs=out_s...  27.8 us
    ppermute x14, starting transfers between devices, over_row(): return lax.ppermute(x, 'row', [(r, r ^ flip) for r in range(n_row)])  18.1 us
    ppermute x14, waiting for transfers between devices, over_row(): return lax.ppermute(x, 'row', [(r, r ^ flip) for r in range(n_row)])  9.18 us
    ppermute x4, starting transfers between devices, other_core(): return lax.ppermute(x, 'col', [(c, c ^ 1) for c in range(n_col)])  8.6 us
    ppermute x3, waiting for transfers between devices, next_chip(): lax.ppermute(x, 'col', [(c, (c // 2 + move[c % 2]) % z.n_chip * 2 + c % 2...  7.28 us
    ppermute x3, starting transfers between devices, next_chip(): lax.ppermute(x, 'col', [(c, (c // 2 + move[c % 2]) % z.n_chip * 2 + c % 2...  4.31 us
    unnamed x12, local copies, waits for them, and re-layouts  4.11 us
  transfers between devices with their start and end apart: 21, of which 8 were waited for; matrix products, arithmetic and copies ran while one was open for 0% of the time, Pallas kernels for 33%

profile of v10, /device:TPU:0, one launch (start us, length us, event | category | flops | bytes accessed | tf_op | source)
XLA Modules:
  0.0 80.2 jit_solution(12796499373944323162)
XLA Ops:
  0.6 1.0 %copy-done = bf16[8,2,128,128]{3,2,1,0:T(8,128)(2,1)S(1)} copy-done((bf16[8,2,128,128]{3,2,1,0:T(8,128)(2,1)S(1)}, bf16[8,2,128,128]{3,2,1,0:T(8,128)(2,1)}, u32[]{:S(2)}) %copy-start) | copy-done | bytes 524312
  1.7 0.7 copy-done.2
  2.4 3.1 %collective-permute-start = (bf16[2064,128]{1,0:T(8,128)(2,1)S(1)}, bf16[2064,128]{1,0:T(8,128)(2,1)S(1)}, u32[]{:S(2)}, u32[]{:S(2)}) collective-permute-start(bf16[2064,128]{1,0:T(8,128)(2,1)S(1)} %pack_d.1.refs_0_), channel_id=1, source_target_pairs={{0,2},{1,7},{2,4},{3,1},{4,6},{5,3},{6,0},{7,5},{8,10},{9,15},{10,... | collective-permute-start | bytes 1585160 | tf_op jit(solution)/shard_map/ppermute | solution.py:272
  5.5 1.0 %copy-done.1 = bf16[8,2,128,128]{3,2,1,0:T(8,128)(2,1)S(1)} copy-done((bf16[8,2,128,128]{3,2,1,0:T(8,128)(2,1)S(1)}, bf16[8,2,128,128]{3,2,1,0:T(8,128)(2,1)}, u32[]{:S(2)}) %copy-start.1) | copy-done | bytes 524312
  6.5 0.7 copy-done.3
  7.2 0.7 copy-done.5
  7.9 1.6 %collective-permute-start.1 = (bf16[2064,128]{1,0:T(8,128)(2,1)S(1)}, bf16[2064,128]{1,0:T(8,128)(2,1)S(1)}, u32[]{:S(2)}, u32[]{:S(2)}) collective-permute-start(bf16[2064,128]{1,0:T(8,128)(2,1)S(1)} %pack_h.1.refs_5_), channel_id=1, source_target_pairs={{0,8},{8,0},{16,24},{24,16},{1,9},{9,1},{17,25},{25,17},{2,10},{10... | collective-permute-start | bytes 1585160 | tf_op jit(solution)/shard_map/ppermute | solution.py:268
  9.5 1.5 %collective-permute-start.2 = (bf16[2064,128]{1,0:T(8,128)(2,1)S(1)}, bf16[2064,128]{1,0:T(8,128)(2,1)S(1)}, u32[]{:S(2)}, u32[]{:S(2)}) collective-permute-start(bf16[2064,128]{1,0:T(8,128)(2,1)S(1)} %pack_h.1.refs_5_), channel_id=1, source_target_pairs={{0,16},{8,24},{16,0},{24,8},{1,17},{9,25},{17,1},{25,9},{2,18},{10... | collective-permute-start | bytes 1585160 | tf_op jit(solution)/shard_map/ppermute | solution.py:268
  11.0 1.0 %collective-permute-start.3 = (bf16[2064,128]{1,0:T(8,128)(2,1)S(1)}, bf16[2064,128]{1,0:T(8,128)(2,1)S(1)}, u32[]{:S(2)}, u32[]{:S(2)}) collective-permute-start(bf16[2064,128]{1,0:T(8,128)(2,1)S(1)} %pack_d.1.refs_0_), channel_id=1, source_target_pairs={{0,1},{1,0},{2,3},{3,2},{4,5},{5,4},{6,7},{7,6},{8,9},{9,8},{10,11... | collective-permute-start | bytes 1585160 | tf_op jit(solution)/shard_map/ppermute | solution.py:275
  12.0 1.2 %collective-permute-start.4 = (bf16[2064,128]{1,0:T(8,128)(2,1)S(1)}, bf16[2064,128]{1,0:T(8,128)(2,1)S(1)}, u32[]{:S(2)}, u32[]{:S(2)}) collective-permute-start(bf16[2064,128]{1,0:T(8,128)(2,1)S(1)} %pack_d.1.refs_0_), channel_id=1, source_target_pairs={{0,6},{1,3},{2,0},{3,5},{4,2},{5,7},{6,4},{7,1},{8,14},{9,11},{10,... | collective-permute-start | bytes 1585160 | tf_op jit(solution)/shard_map/ppermute | solution.py:272
  13.2 7.2 %collective-permute-done.refs_2_ = bf16[2064,128]{1,0:T(8,128)(2,1)S(1)} collective-permute-done((bf16[2064,128]{1,0:T(8,128)(2,1)S(1)}, bf16[2064,128]{1,0:T(8,128)(2,1)S(1)}, u32[]{:S(2)}, u32[]{:S(2)}) %collective-permute-start) | collective-permute-done | bytes 528416 | tf_op jit(solution)/shard_map/ppermute | solution.py:272
  20.4 1.9 %collective-permute-done.1.refs_6_ = bf16[2064,128]{1,0:T(8,128)(2,1)S(1)} collective-permute-done((bf16[2064,128]{1,0:T(8,128)(2,1)S(1)}, bf16[2064,128]{1,0:T(8,128)(2,1)S(1)}, u32[]{:S(2)}, u32[]{:S(2)}) %collective-permute-start.1) | collective-permute-done | bytes 528416 | tf_op jit(solution)/shard_map/ppermute | solution.py:268
  22.3 1.7 %collective-permute-done.2.refs_7_ = bf16[2064,128]{1,0:T(8,128)(2,1)S(1)} collective-permute-done((bf16[2064,128]{1,0:T(8,128)(2,1)S(1)}, bf16[2064,128]{1,0:T(8,128)(2,1)S(1)}, u32[]{:S(2)}, u32[]{:S(2)}) %collective-permute-start.2) | collective-permute-done | bytes 528416 | tf_op jit(solution)/shard_map/ppermute | solution.py:268
  24.0 0.5 collective-permute-start.5
  24.5 1.9 %collective-permute-start.7 = (bf16[1040,128]{1,0:T(8,128)(2,1)S(1)}, bf16[1040,128]{1,0:T(8,128)(2,1)S(1)}, u32[]{:S(2)}, u32[]{:S(2)}) collective-permute-start(bf16[1040,128]{1,0:T(8,128)(2,1)S(1)} %slice.13), channel_id=1, source_target_pairs={{0,8},{8,0},{16,24},{24,16},{1,9},{9,1},{17,25},{25,17},{2,10},{10... | collective-permute-start | bytes 798728 | tf_op jit(solution)/shard_map/ppermute | solution.py:268
  26.4 2.6 %collective-permute-start.6 = (bf16[1024,128]{1,0:T(8,128)(2,1)S(1)}, bf16[1024,128]{1,0:T(8,128)(2,1)S(1)}, u32[]{:S(2)}, u32[]{:S(2)}) collective-permute-start(bf16[1024,128]{1,0:T(8,128)(2,1)S(1)} %slice.12), channel_id=1, source_target_pairs={{0,16},{8,24},{16,0},{24,8},{1,17},{9,25},{17,1},{25,9},{2,18},{10... | collective-permute-start | bytes 786440 | tf_op jit(solution)/shard_map/ppermute | solution.py:268
  29.1 1.7 %collective-permute-start.11 = (bf16[2064,128]{1,0:T(8,128)(2,1)S(1)}, bf16[2064,128]{1,0:T(8,128)(2,1)S(1)}, u32[]{:S(2)}, u32[]{:S(2)}) collective-permute-start(bf16[2064,128]{1,0:T(8,128)(2,1)S(1)} %pack_d.1.refs_0_), channel_id=1, source_target_pairs={{0,8},{8,0},{16,24},{24,16},{1,9},{9,1},{17,25},{25,17},{2,10},{10... | collective-permute-start | bytes 1585160 | tf_op jit(solution)/shard_map/ppermute | solution.py:268
  30.8 0.6 collective-permute-start.12
  31.4 2.0 %collective-permute-done.6.refs_8_ = bf16[1024,128]{1,0:T(8,128)(2,1)S(1)} collective-permute-done((bf16[1024,128]{1,0:T(8,128)(2,1)S(1)}, bf16[1024,128]{1,0:T(8,128)(2,1)S(1)}, u32[]{:S(2)}, u32[]{:S(2)}) %collective-permute-start.6) | collective-permute-done | bytes 262176 | tf_op jit(solution)/shard_map/ppermute | solution.py:268
  33.4 7.1 %collective-permute-start.9 = (bf16[2064,128]{1,0:T(8,128)(2,1)S(1)}, bf16[2064,128]{1,0:T(8,128)(2,1)S(1)}, u32[]{:S(2)}, u32[]{:S(2)}) collective-permute-start(bf16[2064,128]{1,0:T(8,128)(2,1)S(1)} %collective-permute-done.4.refs_4_), channel_id=1, source_target_pairs={{0,1},{1,0},{2,3},{3,2},{4,5},{5,4},{6,7},{7,6},{8,9},{9,8},{10,11... | collective-permute-start | bytes 1585160 | tf_op jit(solution)/shard_map/ppermute | solution.py:275
  40.4 7.6 %first.1 = (f32[1024,512]{1,0:T(8,128)S(1)}, bf16[1024,2560]{1,0:T(8,128)(2,1)S(1)}, bf16[2560,1024]{1,0:T(8,128)(2,1)S(1)}, bf16[1536,512]{1,0:T(8,128)(2,1)S(1)}, s32[4,8,128]{2,1,0:T(8,128)S(1)}) custom-call(bf16[2064,128]{1,0:T(8,128)(2,1)S(1)} %pack_d.1.refs_0_, bf16[2064,128]{1,0:T(8,128)(2,1)S(1)} %collective-permute-done.3.refs_1_, ...), custom_call_target="tpu_custom_call" | custom-call | bytes 1024 | tf_op jit(solution)/shard_map/first/pallas_call | solution.py:32
  48.2 1.9 %collective-permute-start.13 = (bf16[1024,128]{1,0:T(8,128)(2,1)S(1)}, bf16[1024,128]{1,0:T(8,128)(2,1)S(1)}, u32[]{:S(2)}, u32[]{:S(2)}) collective-permute-start(bf16[1024,128]{1,0:T(8,128)(2,1)S(1)} %slice.16), channel_id=1, source_target_pairs={{0,16},{8,24},{16,0},{24,8},{1,17},{9,25},{17,1},{25,9},{2,18},{10... | collective-permute-start | bytes 786440 | tf_op jit(solution)/shard_map/ppermute | solution.py:268
  50.4 6.0 %last.1 = (f32[1024,512]{1,0:T(8,128)S(1)}, bf16[1024,512]{1,0:T(8,128)(2,1)S(1)}, bf16[1024,1536]{1,0:T(8,128)(2,1)S(1)}, bf16[1536,1024]{1,0:T(8,128)(2,1)S(1)...) custom-call(s32[4,8,128]{2,1,0:T(8,128)S(1)} %get-tuple-element.48.table, ...), custom_call_target="tpu_custom_call" | custom-call | flops 2147483648 | bytes 1024 | tf_op jit(solution)/shard_map/last/pallas_call | solution.py:32
  56.4 1.8 %collective-permute-start.16 = (bf16[4,2,128,128]{3,2,1,0:T(8,128)(2,1)S(1)}, bf16[4,2,128,128]{3,2,1,0:T(8,128)(2,1)S(1)}, u32[]{:S(2)}, u32[]{:S(2)}) collective-permute-start(bf16[4,2,128,128]{3,2,1,0:T(8,128)(2,1)S(1)} %get-tuple-element.73), channel_id=1, source_target_pairs={{0,8},{8,0},{16,24},{24,16},{1,9},{9,1},{17,25},{25,17},{2,10},{10... | collective-permute-start | bytes 786440 | tf_op jit(solution)/shard_map/ppermute | solution.py:268
  58.5 2.4 %base.1 = (bf16[8,4,128,128]{3,2,1,0:T(8,128)(2,1)}, f32[8,2,128,128]{3,2,1,0:T(8,128)S(1)}) custom-call(s32[4,8,128]{2,1,0:T(8,128)S(1)} %get-tuple-element.48.table, s32[4,8]{1,0:T(4,128)S(1)} %bitcast.9, f32[1024,512]{1,0:T(8,128)S(1)} %get-tuple-element.68.total, bf16[1024,512]{1,0:T(8,128)(2,1)S(1)} %get-tuple-element.56.m16, ...), custom_call_target="tpu_custom_call" | custom-call | flops 1073741824 | bytes 1024 | tf_op jit(solution)/shard_map/base/pallas_call | solution.py:32
  60.9 3.2 %parts.1 = (bf16[4,2,128,128]{3,2,1,0:T(8,128)(2,1)S(1)}, bf16[4,2,128,128]{3,2,1,0:T(8,128)(2,1)S(1)}, bf16[4,2,128,128]{3,2,1,0:T(8,128)(2,1)S(1)}, bf16[4,2,128,128]{3,2,1,0:T(8,128)(2,1)S(1)}) custom-call(s32[4,8,128]{2,1,0:T(8,128)S(1)} %get-tuple-element.48.table, bf16[1024,512]{1,0:T(8,128)(2,1)S(1)} %get-tuple-element.56.m16, ...), custom_call_target="tpu_custom_call" | custom-call | flops 2147483648 | bytes 1024 | tf_op jit(solution)/shard_map/parts/pallas_call | solution.py:32
  64.1 1.5 %collective-permute-start.15 = (bf16[4,2,128,128]{3,2,1,0:T(8,128)(2,1)S(1)}, bf16[4,2,128,128]{3,2,1,0:T(8,128)(2,1)S(1)}, u32[]{:S(2)}, u32[]{:S(2)}) collective-permute-start(bf16[4,2,128,128]{3,2,1,0:T(8,128)(2,1)S(1)} %get-tuple-element.71), channel_id=1, source_target_pairs={{0,8},{8,0},{16,24},{24,16},{1,9},{9,1},{17,25},{25,17},{2,10},{10... | collective-permute-start | bytes 786440 | tf_op jit(solution)/shard_map/ppermute | solution.py:268
  66.7 1.6 %collective-permute-start.19 = (bf16[4,2,128,128]{3,2,1,0:T(8,128)(2,1)S(1)}, bf16[4,2,128,128]{3,2,1,0:T(8,128)(2,1)S(1)}, u32[]{:S(2)}, u32[]{:S(2)}) collective-permute-start(bf16[4,2,128,128]{3,2,1,0:T(8,128)(2,1)S(1)} %get-tuple-element.77), channel_id=1, source_target_pairs={{0,16},{8,24},{16,0},{24,8},{1,17},{9,25},{17,1},{25,9},{2,18},{10... | collective-permute-start | bytes 786440 | tf_op jit(solution)/shard_map/ppermute | solution.py:268
  68.7 7.3 %squared.1 = bf16[8,4,128,128]{3,2,1,0:T(8,128)(2,1)} custom-call(s32[4,8,128]{2,1,0:T(8,128)S(1)} %get-tuple-element.48.table, s32[4,8]{1,0:T(4,128)S(1)} %bitcast.10, bf16[1024,2560]{1,0:T(8,128)(2,1)S(1)} %get-tuple-element.49.panel, bf16[1024,1536]{1,0:T(8,128)(2,1)S(1)} %get-tuple-element.55.panel_last, bf16[2064,128]{1,0:T(8,128)(2,1)S(1)} %pack_d.1.refs_0_, ...), custom_call_target="tpu_custom_call" | custom-call | flops 4294967296 | bytes 1024 | tf_op jit(solution)/shard_map/squared/pallas_call | solution.py:32
  76.1 1.4 %collective-permute-done.18.refs_1_ = bf16[4,2,128,128]{3,2,1,0:T(8,128)(2,1)S(1)} collective-permute-done((bf16[4,2,128,128]{3,2,1,0:T(8,128)(2,1)S(1)}, bf16[4,2,128,128]{3,2,1,0:T(8,128)(2,1)S(1)}, u32[]{:S(2)}, u32[]{:S(2)}) %collective-permute-start.18) | collective-permute-done | bytes 262176 | tf_op jit(solution)/shard_map/ppermute | solution.py:268
  77.5 1.7 %collective-permute-done.20.refs_3_ = bf16[4,2,128,128]{3,2,1,0:T(8,128)(2,1)S(1)} collective-permute-done((bf16[4,2,128,128]{3,2,1,0:T(8,128)(2,1)S(1)}, bf16[4,2,128,128]{3,2,1,0:T(8,128)(2,1)S(1)}, u32[]{:S(2)}, u32[]{:S(2)}) %collective-permute-start.20) | collective-permute-done | bytes 262176 | tf_op jit(solution)/shard_map/ppermute | solution.py:268
  79.2 1.0 %gradient.1 = bf16[8,2,128,128]{3,2,1,0:T(8,128)(2,1)} custom-call(f32[8,2,128,128]{3,2,1,0:T(8,128)S(1)} %get-tuple-element.70.base, bf16[4,2,128,128]{3,2,1,0:T(8,128)(2,1)S(1)} %collective-permute-done.15.refs_0_, bf16[4,2,128,128]{3,2,1,0:T(8,128)(2,1)S(1)} %collective-permute-done.18.refs_1_, ...), custom_call_target="tpu_custom_call" | custom-call | bytes 1024 | tf_op jit(solution)/shard_map/gradient/pallas_call | solution.py:32
  (35 shorter events, 2.3 us)
Async XLA Ops:
  0.6 1.0 %copy-start = (bf16[8,2,128,128]{3,2,1,0:T(8,128)(2,1)S(1)}, bf16[8,2,128,128]{3,2,1,0:T(8,128)(2,1)}, u32[]{:S(2)}) copy-start(bf16[8,2,128,128]{3,2,1,0:T(8,128)(2,1)} %param.5) | copy-start | bytes 1572868
  1.7 0.7 copy-start.2
  2.4 18.0 %collective-permute-start = (bf16[2064,128]{1,0:T(8,128)(2,1)S(1)}, bf16[2064,128]{1,0:T(8,128)(2,1)S(1)}, u32[]{:S(2)}, u32[]{:S(2)}) collective-permute-start(bf16[2064,128]{1,0:T(8,128)(2,1)S(1)} %pack_d.1.refs_0_), channel_id=1, source_target_pairs={{0,2},{1,7},{2,4},{3,1},{4,6},{5,3},{6,0},{7,5},{8,10},{9,15},{10,... | collective-permute-start | bytes 1585160 | tf_op jit(solution)/shard_map/ppermute | solution.py:272
  5.5 1.0 %copy-start.1 = (bf16[8,2,128,128]{3,2,1,0:T(8,128)(2,1)S(1)}, bf16[8,2,128,128]{3,2,1,0:T(8,128)(2,1)}, u32[]{:S(2)}) copy-start(bf16[8,2,128,128]{3,2,1,0:T(8,128)(2,1)} %param.7) | copy-start | bytes 1572868
  6.5 0.7 copy-start.3
  7.2 0.7 copy-start.5
  7.9 14.4 %collective-permute-start.1 = (bf16[2064,128]{1,0:T(8,128)(2,1)S(1)}, bf16[2064,128]{1,0:T(8,128)(2,1)S(1)}, u32[]{:S(2)}, u32[]{:S(2)}) collective-permute-start(bf16[2064,128]{1,0:T(8,128)(2,1)S(1)} %pack_h.1.refs_5_), channel_id=1, source_target_pairs={{0,8},{8,0},{16,24},{24,16},{1,9},{9,1},{17,25},{25,17},{2,10},{10... | collective-permute-start | bytes 1585160 | tf_op jit(solution)/shard_map/ppermute | solution.py:268
  9.5 14.6 %collective-permute-start.2 = (bf16[2064,128]{1,0:T(8,128)(2,1)S(1)}, bf16[2064,128]{1,0:T(8,128)(2,1)S(1)}, u32[]{:S(2)}, u32[]{:S(2)}) collective-permute-start(bf16[2064,128]{1,0:T(8,128)(2,1)S(1)} %pack_h.1.refs_5_), channel_id=1, source_target_pairs={{0,16},{8,24},{16,0},{24,8},{1,17},{9,25},{17,1},{25,9},{2,18},{10... | collective-permute-start | bytes 1585160 | tf_op jit(solution)/shard_map/ppermute | solution.py:268
  11.0 13.0 %collective-permute-start.3 = (bf16[2064,128]{1,0:T(8,128)(2,1)S(1)}, bf16[2064,128]{1,0:T(8,128)(2,1)S(1)}, u32[]{:S(2)}, u32[]{:S(2)}) collective-permute-start(bf16[2064,128]{1,0:T(8,128)(2,1)S(1)} %pack_d.1.refs_0_), channel_id=1, source_target_pairs={{0,1},{1,0},{2,3},{3,2},{4,5},{5,4},{6,7},{7,6},{8,9},{9,8},{10,11... | collective-permute-start | bytes 1585160 | tf_op jit(solution)/shard_map/ppermute | solution.py:275
  12.0 17.1 %collective-permute-start.4 = (bf16[2064,128]{1,0:T(8,128)(2,1)S(1)}, bf16[2064,128]{1,0:T(8,128)(2,1)S(1)}, u32[]{:S(2)}, u32[]{:S(2)}) collective-permute-start(bf16[2064,128]{1,0:T(8,128)(2,1)S(1)} %pack_d.1.refs_0_), channel_id=1, source_target_pairs={{0,6},{1,3},{2,0},{3,5},{4,2},{5,7},{6,4},{7,1},{8,14},{9,11},{10,... | collective-permute-start | bytes 1585160 | tf_op jit(solution)/shard_map/ppermute | solution.py:272
  24.0 5.1 %collective-permute-start.5 = (bf16[2064,128]{1,0:T(8,128)(2,1)S(1)}, bf16[2064,128]{1,0:T(8,128)(2,1)S(1)}, u32[]{:S(2)}, u32[]{:S(2)}) collective-permute-start(bf16[2064,128]{1,0:T(8,128)(2,1)S(1)} %collective-permute-done.refs_2_), channel_id=1, source_target_pairs={{0,1},{1,0},{2,3},{3,2},{4,5},{5,4},{6,7},{7,6},{8,9},{9,8},{10,11... | collective-permute-start | bytes 1585160 | tf_op jit(solution)/shard_map/ppermute | solution.py:275
  24.5 23.6 %collective-permute-start.8 = (bf16[2064,128]{1,0:T(8,128)(2,1)S(1)}, bf16[2064,128]{1,0:T(8,128)(2,1)S(1)}, u32[]{:S(2)}, u32[]{:S(2)}) collective-permute-start(bf16[2064,128]{1,0:T(8,128)(2,1)S(1)} %collective-permute-done.refs_2_), channel_id=1, source_target_pairs={{0,2},{1,7},{2,4},{3,1},{4,6},{5,3},{6,0},{7,5},{8,10},{9,15},{10,... | collective-permute-start | bytes 1585160 | tf_op jit(solution)/shard_map/ppermute | solution.py:272
  24.5 15.9 %collective-permute-start.7 = (bf16[1040,128]{1,0:T(8,128)(2,1)S(1)}, bf16[1040,128]{1,0:T(8,128)(2,1)S(1)}, u32[]{:S(2)}, u32[]{:S(2)}) collective-permute-start(bf16[1040,128]{1,0:T(8,128)(2,1)S(1)} %slice.13), channel_id=1, source_target_pairs={{0,8},{8,0},{16,24},{24,16},{1,9},{9,1},{17,25},{25,17},{2,10},{10... | collective-permute-start | bytes 798728 | tf_op jit(solution)/shard_map/ppermute | solution.py:268
  26.4 7.0 %collective-permute-start.6 = (bf16[1024,128]{1,0:T(8,128)(2,1)S(1)}, bf16[1024,128]{1,0:T(8,128)(2,1)S(1)}, u32[]{:S(2)}, u32[]{:S(2)}) collective-permute-start(bf16[1024,128]{1,0:T(8,128)(2,1)S(1)} %slice.12), channel_id=1, source_target_pairs={{0,16},{8,24},{16,0},{24,8},{1,17},{9,25},{17,1},{25,9},{2,18},{10... | collective-permute-start | bytes 786440 | tf_op jit(solution)/shard_map/ppermute | solution.py:268
  29.1 19.0 %collective-permute-start.11 = (bf16[2064,128]{1,0:T(8,128)(2,1)S(1)}, bf16[2064,128]{1,0:T(8,128)(2,1)S(1)}, u32[]{:S(2)}, u32[]{:S(2)}) collective-permute-start(bf16[2064,128]{1,0:T(8,128)(2,1)S(1)} %pack_d.1.refs_0_), channel_id=1, source_target_pairs={{0,8},{8,0},{16,24},{24,16},{1,9},{9,1},{17,25},{25,17},{2,10},{10... | collective-permute-start | bytes 1585160 | tf_op jit(solution)/shard_map/ppermute | solution.py:268
  30.8 19.2 %collective-permute-start.12 = (bf16[2064,128]{1,0:T(8,128)(2,1)S(1)}, bf16[2064,128]{1,0:T(8,128)(2,1)S(1)}, u32[]{:S(2)}, u32[]{:S(2)}) collective-permute-start(bf16[2064,128]{1,0:T(8,128)(2,1)S(1)} %pack_d.1.refs_0_), channel_id=1, source_target_pairs={{0,16},{8,24},{16,0},{24,8},{1,17},{9,25},{17,1},{25,9},{2,18},{10... | collective-permute-start | bytes 1585160 | tf_op jit(solution)/shard_map/ppermute | solution.py:268
  33.4 17.0 %collective-permute-start.9 = (bf16[2064,128]{1,0:T(8,128)(2,1)S(1)}, bf16[2064,128]{1,0:T(8,128)(2,1)S(1)}, u32[]{:S(2)}, u32[]{:S(2)}) collective-permute-start(bf16[2064,128]{1,0:T(8,128)(2,1)S(1)} %collective-permute-done.4.refs_4_), channel_id=1, source_target_pairs={{0,1},{1,0},{2,3},{3,2},{4,5},{5,4},{6,7},{7,6},{8,9},{9,8},{10,11... | collective-permute-start | bytes 1585160 | tf_op jit(solution)/shard_map/ppermute | solution.py:275
  48.1 2.3 %collective-permute-start.10 = (bf16[2064,128]{1,0:T(8,128)(2,1)S(1)}, bf16[2064,128]{1,0:T(8,128)(2,1)S(1)}, u32[]{:S(2)}, u32[]{:S(2)}) collective-permute-start(bf16[2064,128]{1,0:T(8,128)(2,1)S(1)} %collective-permute-done.8.refs_1_), channel_id=1, source_target_pairs={{0,1},{1,0},{2,3},{3,2},{4,5},{5,4},{6,7},{7,6},{8,9},{9,8},{10,11... | collective-permute-start | bytes 1585160 | tf_op jit(solution)/shard_map/ppermute | solution.py:275
  48.2 15.9 %collective-permute-start.13 = (bf16[1024,128]{1,0:T(8,128)(2,1)S(1)}, bf16[1024,128]{1,0:T(8,128)(2,1)S(1)}, u32[]{:S(2)}, u32[]{:S(2)}) collective-permute-start(bf16[1024,128]{1,0:T(8,128)(2,1)S(1)} %slice.16), channel_id=1, source_target_pairs={{0,16},{8,24},{16,0},{24,8},{1,17},{9,25},{17,1},{25,9},{2,18},{10... | collective-permute-start | bytes 786440 | tf_op jit(solution)/shard_map/ppermute | solution.py:268
  50.1 14.0 %collective-permute-start.14 = (bf16[1024,128]{1,0:T(8,128)(2,1)S(1)}, bf16[1024,128]{1,0:T(8,128)(2,1)S(1)}, u32[]{:S(2)}, u32[]{:S(2)}) collective-permute-start(bf16[1024,128]{1,0:T(8,128)(2,1)S(1)} %slice.17), channel_id=1, source_target_pairs={{0,8},{8,0},{16,24},{24,16},{1,9},{9,1},{17,25},{25,17},{2,10},{10... | collective-permute-start | bytes 786440 | tf_op jit(solution)/shard_map/ppermute | solution.py:268
  50.4 8.1 %copy-start.4 = (s32[8,4]{0,1:T(4,128)S(1)}, s32[8,4]{0,1:T(4,128)}, u32[]{:S(2)}) copy-start(s32[8,4]{0,1:T(4,128)} %param.9) | copy-start | bytes 388
  56.4 9.3 %collective-permute-start.16 = (bf16[4,2,128,128]{3,2,1,0:T(8,128)(2,1)S(1)}, bf16[4,2,128,128]{3,2,1,0:T(8,128)(2,1)S(1)}, u32[]{:S(2)}, u32[]{:S(2)}) collective-permute-start(bf16[4,2,128,128]{3,2,1,0:T(8,128)(2,1)S(1)} %get-tuple-element.73), channel_id=1, source_target_pairs={{0,8},{8,0},{16,24},{24,16},{1,9},{9,1},{17,25},{25,17},{2,10},{10... | collective-permute-start | bytes 786440 | tf_op jit(solution)/shard_map/ppermute | solution.py:268
  58.2 7.9 %collective-permute-start.17 = (bf16[4,2,128,128]{3,2,1,0:T(8,128)(2,1)S(1)}, bf16[4,2,128,128]{3,2,1,0:T(8,128)(2,1)S(1)}, u32[]{:S(2)}, u32[]{:S(2)}) collective-permute-start(bf16[4,2,128,128]{3,2,1,0:T(8,128)(2,1)S(1)} %get-tuple-element.75), channel_id=1, source_target_pairs={{0,16},{8,24},{16,0},{24,8},{1,17},{9,25},{17,1},{25,9},{2,18},{10... | collective-permute-start | bytes 786440 | tf_op jit(solution)/shard_map/ppermute | solution.py:268
  64.1 11.9 %collective-permute-start.15 = (bf16[4,2,128,128]{3,2,1,0:T(8,128)(2,1)S(1)}, bf16[4,2,128,128]{3,2,1,0:T(8,128)(2,1)S(1)}, u32[]{:S(2)}, u32[]{:S(2)}) collective-permute-start(bf16[4,2,128,128]{3,2,1,0:T(8,128)(2,1)S(1)} %get-tuple-element.71), channel_id=1, source_target_pairs={{0,8},{8,0},{16,24},{24,16},{1,9},{9,1},{17,25},{25,17},{2,10},{10... | collective-permute-start | bytes 786440 | tf_op jit(solution)/shard_map/ppermute | solution.py:268
  66.2 11.2 %collective-permute-start.18 = (bf16[4,2,128,128]{3,2,1,0:T(8,128)(2,1)S(1)}, bf16[4,2,128,128]{3,2,1,0:T(8,128)(2,1)S(1)}, u32[]{:S(2)}, u32[]{:S(2)}) collective-permute-start(bf16[4,2,128,128]{3,2,1,0:T(8,128)(2,1)S(1)} %get-tuple-element.76), channel_id=1, source_target_pairs={{0,8},{8,0},{16,24},{24,16},{1,9},{9,1},{17,25},{25,17},{2,10},{10... | collective-permute-start | bytes 786440 | tf_op jit(solution)/shard_map/ppermute | solution.py:268
  66.7 10.8 %collective-permute-start.19 = (bf16[4,2,128,128]{3,2,1,0:T(8,128)(2,1)S(1)}, bf16[4,2,128,128]{3,2,1,0:T(8,128)(2,1)S(1)}, u32[]{:S(2)}, u32[]{:S(2)}) collective-permute-start(bf16[4,2,128,128]{3,2,1,0:T(8,128)(2,1)S(1)} %get-tuple-element.77), channel_id=1, source_target_pairs={{0,16},{8,24},{16,0},{24,8},{1,17},{9,25},{17,1},{25,9},{2,18},{10... | collective-permute-start | bytes 786440 | tf_op jit(solution)/shard_map/ppermute | solution.py:268
  68.3 11.0 %collective-permute-start.20 = (bf16[4,2,128,128]{3,2,1,0:T(8,128)(2,1)S(1)}, bf16[4,2,128,128]{3,2,1,0:T(8,128)(2,1)S(1)}, u32[]{:S(2)}, u32[]{:S(2)}) collective-permute-start(bf16[4,2,128,128]{3,2,1,0:T(8,128)(2,1)S(1)} %get-tuple-element.78), channel_id=1, source_target_pairs={{0,16},{8,24},{16,0},{24,8},{1,17},{9,25},{17,1},{25,9},{2,18},{10... | collective-permute-start | bytes 786440 | tf_op jit(solution)/shard_map/ppermute | solution.py:268

commit v11 on v9

--- a/solution.py
+++ b/solution.py
@@ -90,15 +90,25 @@
     copy.wait()
 
 
+def empty_places(z, wanted):
+    if z.bc != 4 or len(wanted) != 2:
+        return range(z.bc)
+    a, b = wanted
+    one = jnp.where((a != 0) & (b != 0), 0, jnp.where((a != 1) & (b != 1), 1, 2))
+    return one, 6 - a - b - one
+
+
 def fill_left(z, idx, n, col, blocks, dense, dense_t, first):
-    zero, zero_t = jnp.zeros((z.bs, z.wide), BF16), jnp.zeros((z.wide, z.bs), BF16)
+    zero = jnp.zeros((z.bs, z.bs), BF16)
     for i in range(z.rows):
         rows = slice(i * z.bs, (i + 1) * z.bs)
-        dense[rows, first:first + z.wide] = zero
-        if dense_t is not None:
-            dense_t[first:first + z.wide, rows] = zero_t
-        for s in range(z.ka):
-            k = idx[n, s, i] - col * z.bc
+        wanted = [idx[n, s, i] - col * z.bc for s in range(z.ka)]
+        for k in empty_places(z, wanted):
+            at = pl.ds(pl.multiple_of(first + k * z.bs, z.bs), z.bs)
+            dense[rows, at] = zero
+            if dense_t is not None:
+                dense_t[at, rows] = zero
+        for s, k in enumerate(wanted):
             at = pl.ds(pl.multiple_of(first + k * z.bs, z.bs), z.bs)
             block = blocks[block_rows(z, i, s, z.ka), :]
             dense[rows, at] = block
@@ -107,13 +117,15 @@
 
 
 def fill_right(z, first_slot, slots, idx, payloads, flips, place, dense):
-    dense[...] = jnp.zeros_like(dense)
+    zero = jnp.zeros((z.bs, z.bs), BF16)
     me = lax.axis_index("col")
     for flip, payload in zip(flips, payloads):
         for i in range(z.rows):
             at = pl.ds(pl.multiple_of(place(flip, i) * z.bs, z.bs), z.bs)
-            for s in range(slots):
-                j = idx[flip, first_slot + s, i] - me * z.bc
+            wanted = [idx[flip, first_slot + s, i] - me * z.bc for s in range(slots)]
+            for j in empty_places(z, wanted):
+                dense[at, lanes(z, j)] = zero
+            for s, j in enumerate(wanted):
                 row, part = (i * slots + s) * z.bs, 0
                 while row >= payload[part].shape[0]:
                     row -= payload[part].shape[0]
@@ -223,8 +235,8 @@
     deep = z.n_first * z.wide
     copies = []
     for n, rows in enumerate(halves(z.tall)):
-        total[rows, :] = jnp.dot(panel[rows, :], right[0:deep, :], preferred_element_type=F32)
-        total[rows, :] += jnp.dot(panel_last[rows, :], right[deep:, :], preferred_element_type=F32)
+        term = jnp.dot(panel[rows, :], right[0:deep, :], preferred_element_type=F32)
+        total[rows, :] = term + jnp.dot(panel_last[rows, :], right[deep:, :], preferred_element_type=F32)
         here = halves(z.rows)[n]
         for i in range(here.start, here.stop):
             for s in range(z.kf):

time: 78.2 us -> 77.7 us (level)
  transfers between devices with their start and end apart: 21 -> 21, of which waited for: 7 -> 7; matrix products, arithmetic and copies ran while one was open for 0% -> 0% of each run, Pallas kernels for 35% -> 34%
where the time goes in v11:
time: 77.7 us; the launch traced here: 76.6 us
  starting transfers between devices  30.4 us (39%)
  Pallas kernels  27.3 us (35%)
  waiting for transfers between devices  13.9 us (18%)
  local copies, waits for them, and re-layouts  4.19 us (5%)
  between operations  0.8 us (1%)
    pallas_call x9, Pallas kernels, call(): pl.pallas_call(kernel, out_shape=outs, in_specs=in_specs, out_specs=out_s...  27.3 us
    ppermute x14, starting transfers between devices, over_row(): return lax.ppermute(x, 'row', [(r, r ^ flip) for r in range(n_row)])  20.6 us
    ppermute x3, waiting for transfers between devices, next_chip(): lax.ppermute(x, 'col', [(c, (c // 2 + move[c % 2]) % z.n_chip * 2 + c % 2...  7.28 us
    ppermute x14, waiting for transfers between devices, over_row(): return lax.ppermute(x, 'row', [(r, r ^ flip) for r in range(n_row)])  6.56 us
    ppermute x4, starting transfers between devices, other_core(): return lax.ppermute(x, 'col', [(c, c ^ 1) for c in range(n_col)])  5.45 us
    ppermute x3, starting transfers between devices, next_chip(): lax.ppermute(x, 'col', [(c, (c // 2 + move[c % 2]) % z.n_chip * 2 + c % 2...  4.31 us
    unnamed x12, local copies, waits for them, and re-layouts  4.11 us
  transfers between devices with their start and end apart: 21, of which 7 were waited for; matrix products, arithmetic and copies ran while one was open for 0% of the time, Pallas kernels for 34%

profile of v11, /device:TPU:0, one launch (start us, length us, event | category | flops | bytes accessed | tf_op | source)
XLA Modules:
  0.0 76.6 jit_solution(11681655036857068334)
XLA Ops:
  0.6 1.0 %copy-done = bf16[8,2,128,128]{3,2,1,0:T(8,128)(2,1)S(1)} copy-done((bf16[8,2,128,128]{3,2,1,0:T(8,128)(2,1)S(1)}, bf16[8,2,128,128]{3,2,1,0:T(8,128)(2,1)}, u32[]{:S(2)}) %copy-start) | copy-done | bytes 524312
  1.7 0.7 copy-done.2
  2.4 3.1 %collective-permute-start = (bf16[2064,128]{1,0:T(8,128)(2,1)S(1)}, bf16[2064,128]{1,0:T(8,128)(2,1)S(1)}, u32[]{:S(2)}, u32[]{:S(2)}) collective-permute-start(bf16[2064,128]{1,0:T(8,128)(2,1)S(1)} %pack_d.1.refs_0_), channel_id=1, source_target_pairs={{0,2},{1,7},{2,4},{3,1},{4,6},{5,3},{6,0},{7,5},{8,10},{9,15},{10,... | collective-permute-start | bytes 1585160 | tf_op jit(solution)/shard_map/ppermute | solution.py:284
  5.5 1.0 %copy-done.1 = bf16[8,2,128,128]{3,2,1,0:T(8,128)(2,1)S(1)} copy-done((bf16[8,2,128,128]{3,2,1,0:T(8,128)(2,1)S(1)}, bf16[8,2,128,128]{3,2,1,0:T(8,128)(2,1)}, u32[]{:S(2)}) %copy-start.1) | copy-done | bytes 524312
  6.5 0.7 copy-done.3
  7.2 0.7 copy-done.5
  7.9 1.6 %collective-permute-start.1 = (bf16[2064,128]{1,0:T(8,128)(2,1)S(1)}, bf16[2064,128]{1,0:T(8,128)(2,1)S(1)}, u32[]{:S(2)}, u32[]{:S(2)}) collective-permute-start(bf16[2064,128]{1,0:T(8,128)(2,1)S(1)} %pack_h.1.refs_5_), channel_id=1, source_target_pairs={{0,8},{8,0},{16,24},{24,16},{1,9},{9,1},{17,25},{25,17},{2,10},{10... | collective-permute-start | bytes 1585160 | tf_op jit(solution)/shard_map/ppermute | solution.py:280
  9.5 1.5 %collective-permute-start.2 = (bf16[2064,128]{1,0:T(8,128)(2,1)S(1)}, bf16[2064,128]{1,0:T(8,128)(2,1)S(1)}, u32[]{:S(2)}, u32[]{:S(2)}) collective-permute-start(bf16[2064,128]{1,0:T(8,128)(2,1)S(1)} %pack_h.1.refs_5_), channel_id=1, source_target_pairs={{0,16},{8,24},{16,0},{24,8},{1,17},{9,25},{17,1},{25,9},{2,18},{10... | collective-permute-start | bytes 1585160 | tf_op jit(solution)/shard_map/ppermute | solution.py:280
  11.0 1.0 %collective-permute-start.3 = (bf16[2064,128]{1,0:T(8,128)(2,1)S(1)}, bf16[2064,128]{1,0:T(8,128)(2,1)S(1)}, u32[]{:S(2)}, u32[]{:S(2)}) collective-permute-start(bf16[2064,128]{1,0:T(8,128)(2,1)S(1)} %pack_d.1.refs_0_), channel_id=1, source_target_pairs={{0,1},{1,0},{2,3},{3,2},{4,5},{5,4},{6,7},{7,6},{8,9},{9,8},{10,11... | collective-permute-start | bytes 1585160 | tf_op jit(solution)/shard_map/ppermute | solution.py:287
  12.0 1.2 %collective-permute-start.5 = (bf16[2064,128]{1,0:T(8,128)(2,1)S(1)}, bf16[2064,128]{1,0:T(8,128)(2,1)S(1)}, u32[]{:S(2)}, u32[]{:S(2)}) collective-permute-start(bf16[2064,128]{1,0:T(8,128)(2,1)S(1)} %pack_d.1.refs_0_), channel_id=1, source_target_pairs={{0,6},{1,3},{2,0},{3,5},{4,2},{5,7},{6,4},{7,1},{8,14},{9,11},{10,... | collective-permute-start | bytes 1585160 | tf_op jit(solution)/shard_map/ppermute | solution.py:284
  13.2 7.2 %collective-permute-done.refs_2_ = bf16[2064,128]{1,0:T(8,128)(2,1)S(1)} collective-permute-done((bf16[2064,128]{1,0:T(8,128)(2,1)S(1)}, bf16[2064,128]{1,0:T(8,128)(2,1)S(1)}, u32[]{:S(2)}, u32[]{:S(2)}) %collective-permute-start) | collective-permute-done | bytes 528416 | tf_op jit(solution)/shard_map/ppermute | solution.py:284
  20.4 1.9 %collective-permute-done.1.refs_6_ = bf16[2064,128]{1,0:T(8,128)(2,1)S(1)} collective-permute-done((bf16[2064,128]{1,0:T(8,128)(2,1)S(1)}, bf16[2064,128]{1,0:T(8,128)(2,1)S(1)}, u32[]{:S(2)}, u32[]{:S(2)}) %collective-permute-start.1) | collective-permute-done | bytes 528416 | tf_op jit(solution)/shard_map/ppermute | solution.py:280
  22.3 1.7 %collective-permute-done.2.refs_7_ = bf16[2064,128]{1,0:T(8,128)(2,1)S(1)} collective-permute-done((bf16[2064,128]{1,0:T(8,128)(2,1)S(1)}, bf16[2064,128]{1,0:T(8,128)(2,1)S(1)}, u32[]{:S(2)}, u32[]{:S(2)}) %collective-permute-start.2) | collective-permute-done | bytes 528416 | tf_op jit(solution)/shard_map/ppermute | solution.py:280
  24.0 0.5 collective-permute-start.4
  24.5 1.9 %collective-permute-start.7 = (bf16[1040,128]{1,0:T(8,128)(2,1)S(1)}, bf16[1040,128]{1,0:T(8,128)(2,1)S(1)}, u32[]{:S(2)}, u32[]{:S(2)}) collective-permute-start(bf16[1040,128]{1,0:T(8,128)(2,1)S(1)} %slice.13), channel_id=1, source_target_pairs={{0,8},{8,0},{16,24},{24,16},{1,9},{9,1},{17,25},{25,17},{2,10},{10... | collective-permute-start | bytes 798728 | tf_op jit(solution)/shard_map/ppermute | solution.py:280
  26.4 2.6 %collective-permute-start.6 = (bf16[1024,128]{1,0:T(8,128)(2,1)S(1)}, bf16[1024,128]{1,0:T(8,128)(2,1)S(1)}, u32[]{:S(2)}, u32[]{:S(2)}) collective-permute-start(bf16[1024,128]{1,0:T(8,128)(2,1)S(1)} %slice.12), channel_id=1, source_target_pairs={{0,16},{8,24},{16,0},{24,8},{1,17},{9,25},{17,1},{25,9},{2,18},{10... | collective-permute-start | bytes 786440 | tf_op jit(solution)/shard_map/ppermute | solution.py:280
  29.1 1.7 %collective-permute-start.11 = (bf16[2064,128]{1,0:T(8,128)(2,1)S(1)}, bf16[2064,128]{1,0:T(8,128)(2,1)S(1)}, u32[]{:S(2)}, u32[]{:S(2)}) collective-permute-start(bf16[2064,128]{1,0:T(8,128)(2,1)S(1)} %pack_d.1.refs_0_), channel_id=1, source_target_pairs={{0,8},{8,0},{16,24},{24,16},{1,9},{9,1},{17,25},{25,17},{2,10},{10... | collective-permute-start | bytes 1585160 | tf_op jit(solution)/shard_map/ppermute | solution.py:280
  30.8 2.5 %collective-permute-done.6.refs_8_ = bf16[1024,128]{1,0:T(8,128)(2,1)S(1)} collective-permute-done((bf16[1024,128]{1,0:T(8,128)(2,1)S(1)}, bf16[1024,128]{1,0:T(8,128)(2,1)S(1)}, u32[]{:S(2)}, u32[]{:S(2)}) %collective-permute-start.6) | collective-permute-done | bytes 262176 | tf_op jit(solution)/shard_map/ppermute | solution.py:280
  33.4 2.0 %collective-permute-start.12 = (bf16[2064,128]{1,0:T(8,128)(2,1)S(1)}, bf16[2064,128]{1,0:T(8,128)(2,1)S(1)}, u32[]{:S(2)}, u32[]{:S(2)}) collective-permute-start(bf16[2064,128]{1,0:T(8,128)(2,1)S(1)} %pack_d.1.refs_0_), channel_id=1, source_target_pairs={{0,16},{8,24},{16,0},{24,8},{1,17},{9,25},{17,1},{25,9},{2,18},{10... | collective-permute-start | bytes 1585160 | tf_op jit(solution)/shard_map/ppermute | solution.py:280
  35.4 3.9 %collective-permute-start.9 = (bf16[2064,128]{1,0:T(8,128)(2,1)S(1)}, bf16[2064,128]{1,0:T(8,128)(2,1)S(1)}, u32[]{:S(2)}, u32[]{:S(2)}) collective-permute-start(bf16[2064,128]{1,0:T(8,128)(2,1)S(1)} %collective-permute-done.5.refs_4_), channel_id=1, source_target_pairs={{0,1},{1,0},{2,3},{3,2},{4,5},{5,4},{6,7},{7,6},{8,9},{9,8},{10,11... | collective-permute-start | bytes 1585160 | tf_op jit(solution)/shard_map/ppermute | solution.py:287
  39.3 7.7 %first.1 = (f32[1024,512]{1,0:T(8,128)S(1)}, bf16[1024,2560]{1,0:T(8,128)(2,1)S(1)}, bf16[2560,1024]{1,0:T(8,128)(2,1)S(1)}, bf16[1536,512]{1,0:T(8,128)(2,1)S(1)}, s32[4,8,128]{2,1,0:T(8,128)S(1)}) custom-call(bf16[2064,128]{1,0:T(8,128)(2,1)S(1)} %pack_d.1.refs_0_, bf16[2064,128]{1,0:T(8,128)(2,1)S(1)} %collective-permute-done.3.refs_1_, ...), custom_call_target="tpu_custom_call" | custom-call | bytes 1024 | tf_op jit(solution)/shard_map/first/pallas_call | solution.py:32
  47.1 1.5 %collective-permute-start.13 = (bf16[1024,128]{1,0:T(8,128)(2,1)S(1)}, bf16[1024,128]{1,0:T(8,128)(2,1)S(1)}, u32[]{:S(2)}, u32[]{:S(2)}) collective-permute-start(bf16[1024,128]{1,0:T(8,128)(2,1)S(1)} %slice.16), channel_id=1, source_target_pairs={{0,16},{8,24},{16,0},{24,8},{1,17},{9,25},{17,1},{25,9},{2,18},{10... | collective-permute-start | bytes 786440 | tf_op jit(solution)/shard_map/ppermute | solution.py:280
  48.7 1.8 %collective-permute-start.14 = (bf16[1024,128]{1,0:T(8,128)(2,1)S(1)}, bf16[1024,128]{1,0:T(8,128)(2,1)S(1)}, u32[]{:S(2)}, u32[]{:S(2)}) collective-permute-start(bf16[1024,128]{1,0:T(8,128)(2,1)S(1)} %slice.17), channel_id=1, source_target_pairs={{0,8},{8,0},{16,24},{24,16},{1,9},{9,1},{17,25},{25,17},{2,10},{10... | collective-permute-start | bytes 786440 | tf_op jit(solution)/shard_map/ppermute | solution.py:280
  50.5 5.6 %last.1 = (f32[1024,512]{1,0:T(8,128)S(1)}, bf16[1024,512]{1,0:T(8,128)(2,1)S(1)}, bf16[1024,1536]{1,0:T(8,128)(2,1)S(1)}, bf16[1536,1024]{1,0:T(8,128)(2,1)S(1)...) custom-call(s32[4,8,128]{2,1,0:T(8,128)S(1)} %get-tuple-element.46.table, ...), custom_call_target="tpu_custom_call" | custom-call | flops 2147483648 | bytes 1024 | tf_op jit(solution)/shard_map/last/pallas_call | solution.py:32
  56.4 1.4 %collective-permute-start.17 = (bf16[4,2,128,128]{3,2,1,0:T(8,128)(2,1)S(1)}, bf16[4,2,128,128]{3,2,1,0:T(8,128)(2,1)S(1)}, u32[]{:S(2)}, u32[]{:S(2)}) collective-permute-start(bf16[4,2,128,128]{3,2,1,0:T(8,128)(2,1)S(1)} %get-tuple-element.73), channel_id=1, source_target_pairs={{0,16},{8,24},{16,0},{24,8},{1,17},{9,25},{17,1},{25,9},{2,18},{10... | collective-permute-start | bytes 786440 | tf_op jit(solution)/shard_map/ppermute | solution.py:280
  57.8 3.2 %parts.1 = (bf16[4,2,128,128]{3,2,1,0:T(8,128)(2,1)S(1)}, bf16[4,2,128,128]{3,2,1,0:T(8,128)(2,1)S(1)}, bf16[4,2,128,128]{3,2,1,0:T(8,128)(2,1)S(1)}, bf16[4,2,128,128]{3,2,1,0:T(8,128)(2,1)S(1)}) custom-call(s32[4,8,128]{2,1,0:T(8,128)S(1)} %get-tuple-element.46.table, bf16[1024,512]{1,0:T(8,128)(2,1)S(1)} %get-tuple-element.54.m16, ...), custom_call_target="tpu_custom_call" | custom-call | flops 2147483648 | bytes 1024 | tf_op jit(solution)/shard_map/parts/pallas_call | solution.py:32
  61.5 2.0 %collective-permute-start.20 = (bf16[4,2,128,128]{3,2,1,0:T(8,128)(2,1)S(1)}, bf16[4,2,128,128]{3,2,1,0:T(8,128)(2,1)S(1)}, u32[]{:S(2)}, u32[]{:S(2)}) collective-permute-start(bf16[4,2,128,128]{3,2,1,0:T(8,128)(2,1)S(1)} %get-tuple-element.76), channel_id=1, source_target_pairs={{0,16},{8,24},{16,0},{24,8},{1,17},{9,25},{17,1},{25,9},{2,18},{10... | collective-permute-start | bytes 786440 | tf_op jit(solution)/shard_map/ppermute | solution.py:280
  63.5 2.4 %base.1 = (bf16[8,4,128,128]{3,2,1,0:T(8,128)(2,1)}, f32[8,2,128,128]{3,2,1,0:T(8,128)S(1)}) custom-call(s32[4,8,128]{2,1,0:T(8,128)S(1)} %get-tuple-element.46.table, s32[4,8]{1,0:T(4,128)S(1)} %bitcast.9, f32[1024,512]{1,0:T(8,128)S(1)} %get-tuple-element.66.total, bf16[1024,512]{1,0:T(8,128)(2,1)S(1)} %get-tuple-element.54.m16, ...), custom_call_target="tpu_custom_call" | custom-call | flops 1073741824 | bytes 1024 | tf_op jit(solution)/shard_map/base/pallas_call | solution.py:32
  66.0 1.0 %collective-permute-start.18 = (bf16[4,2,128,128]{3,2,1,0:T(8,128)(2,1)S(1)}, bf16[4,2,128,128]{3,2,1,0:T(8,128)(2,1)S(1)}, u32[]{:S(2)}, u32[]{:S(2)}) collective-permute-start(bf16[4,2,128,128]{3,2,1,0:T(8,128)(2,1)S(1)} %get-tuple-element.74), channel_id=1, source_target_pairs={{0,8},{8,0},{16,24},{24,16},{1,9},{9,1},{17,25},{25,17},{2,10},{10... | collective-permute-start | bytes 786440 | tf_op jit(solution)/shard_map/ppermute | solution.py:280
  67.1 0.7 collective-permute-start.19
  67.8 7.3 %squared.1 = bf16[8,4,128,128]{3,2,1,0:T(8,128)(2,1)} custom-call(s32[4,8,128]{2,1,0:T(8,128)S(1)} %get-tuple-element.46.table, s32[4,8]{1,0:T(4,128)S(1)} %bitcast.10, bf16[1024,2560]{1,0:T(8,128)(2,1)S(1)} %get-tuple-element.47.panel, bf16[1024,1536]{1,0:T(8,128)(2,1)S(1)} %get-tuple-element.53.panel_last, bf16[2064,128]{1,0:T(8,128)(2,1)S(1)} %pack_d.1.refs_0_, ...), custom_call_target="tpu_custom_call" | custom-call | flops 4294967296 | bytes 1024 | tf_op jit(solution)/shard_map/squared/pallas_call | solution.py:32
  75.6 1.0 %gradient.1 = bf16[8,2,128,128]{3,2,1,0:T(8,128)(2,1)} custom-call(f32[8,2,128,128]{3,2,1,0:T(8,128)S(1)} %get-tuple-element.68.base, bf16[4,2,128,128]{3,2,1,0:T(8,128)(2,1)S(1)} %collective-permute-done.15.refs_0_, bf16[4,2,128,128]{3,2,1,0:T(8,128)(2,1)S(1)} %collective-permute-done.18.refs_1_, ...), custom_call_target="tpu_custom_call" | custom-call | bytes 1024 | tf_op jit(solution)/shard_map/gradient/pallas_call | solution.py:32
  (35 shorter events, 1.7 us)
Async XLA Ops:
  0.6 1.0 %copy-start = (bf16[8,2,128,128]{3,2,1,0:T(8,128)(2,1)S(1)}, bf16[8,2,128,128]{3,2,1,0:T(8,128)(2,1)}, u32[]{:S(2)}) copy-start(bf16[8,2,128,128]{3,2,1,0:T(8,128)(2,1)} %param.5) | copy-start | bytes 1572868
  1.7 0.7 copy-start.2
  2.4 18.0 %collective-permute-start = (bf16[2064,128]{1,0:T(8,128)(2,1)S(1)}, bf16[2064,128]{1,0:T(8,128)(2,1)S(1)}, u32[]{:S(2)}, u32[]{:S(2)}) collective-permute-start(bf16[2064,128]{1,0:T(8,128)(2,1)S(1)} %pack_d.1.refs_0_), channel_id=1, source_target_pairs={{0,2},{1,7},{2,4},{3,1},{4,6},{5,3},{6,0},{7,5},{8,10},{9,15},{10,... | collective-permute-start | bytes 1585160 | tf_op jit(solution)/shard_map/ppermute | solution.py:284
  5.5 1.0 %copy-start.1 = (bf16[8,2,128,128]{3,2,1,0:T(8,128)(2,1)S(1)}, bf16[8,2,128,128]{3,2,1,0:T(8,128)(2,1)}, u32[]{:S(2)}) copy-start(bf16[8,2,128,128]{3,2,1,0:T(8,128)(2,1)} %param.7) | copy-start | bytes 1572868
  6.5 0.7 copy-start.3
  7.2 0.7 copy-start.5
  7.9 14.4 %collective-permute-start.1 = (bf16[2064,128]{1,0:T(8,128)(2,1)S(1)}, bf16[2064,128]{1,0:T(8,128)(2,1)S(1)}, u32[]{:S(2)}, u32[]{:S(2)}) collective-permute-start(bf16[2064,128]{1,0:T(8,128)(2,1)S(1)} %pack_h.1.refs_5_), channel_id=1, source_target_pairs={{0,8},{8,0},{16,24},{24,16},{1,9},{9,1},{17,25},{25,17},{2,10},{10... | collective-permute-start | bytes 1585160 | tf_op jit(solution)/shard_map/ppermute | solution.py:280
  9.5 14.6 %collective-permute-start.2 = (bf16[2064,128]{1,0:T(8,128)(2,1)S(1)}, bf16[2064,128]{1,0:T(8,128)(2,1)S(1)}, u32[]{:S(2)}, u32[]{:S(2)}) collective-permute-start(bf16[2064,128]{1,0:T(8,128)(2,1)S(1)} %pack_h.1.refs_5_), channel_id=1, source_target_pairs={{0,16},{8,24},{16,0},{24,8},{1,17},{9,25},{17,1},{25,9},{2,18},{10... | collective-permute-start | bytes 1585160 | tf_op jit(solution)/shard_map/ppermute | solution.py:280
  11.0 13.0 %collective-permute-start.3 = (bf16[2064,128]{1,0:T(8,128)(2,1)S(1)}, bf16[2064,128]{1,0:T(8,128)(2,1)S(1)}, u32[]{:S(2)}, u32[]{:S(2)}) collective-permute-start(bf16[2064,128]{1,0:T(8,128)(2,1)S(1)} %pack_d.1.refs_0_), channel_id=1, source_target_pairs={{0,1},{1,0},{2,3},{3,2},{4,5},{5,4},{6,7},{7,6},{8,9},{9,8},{10,11... | collective-permute-start | bytes 1585160 | tf_op jit(solution)/shard_map/ppermute | solution.py:287
  12.0 17.1 %collective-permute-start.5 = (bf16[2064,128]{1,0:T(8,128)(2,1)S(1)}, bf16[2064,128]{1,0:T(8,128)(2,1)S(1)}, u32[]{:S(2)}, u32[]{:S(2)}) collective-permute-start(bf16[2064,128]{1,0:T(8,128)(2,1)S(1)} %pack_d.1.refs_0_), channel_id=1, source_target_pairs={{0,6},{1,3},{2,0},{3,5},{4,2},{5,7},{6,4},{7,1},{8,14},{9,11},{10,... | collective-permute-start | bytes 1585160 | tf_op jit(solution)/shard_map/ppermute | solution.py:284
  24.0 15.3 %collective-permute-start.4 = (bf16[2064,128]{1,0:T(8,128)(2,1)S(1)}, bf16[2064,128]{1,0:T(8,128)(2,1)S(1)}, u32[]{:S(2)}, u32[]{:S(2)}) collective-permute-start(bf16[2064,128]{1,0:T(8,128)(2,1)S(1)} %collective-permute-done.refs_2_), channel_id=1, source_target_pairs={{0,1},{1,0},{2,3},{3,2},{4,5},{5,4},{6,7},{7,6},{8,9},{9,8},{10,11... | collective-permute-start | bytes 1585160 | tf_op jit(solution)/shard_map/ppermute | solution.py:287
  24.5 22.5 %collective-permute-start.8 = (bf16[2064,128]{1,0:T(8,128)(2,1)S(1)}, bf16[2064,128]{1,0:T(8,128)(2,1)S(1)}, u32[]{:S(2)}, u32[]{:S(2)}) collective-permute-start(bf16[2064,128]{1,0:T(8,128)(2,1)S(1)} %collective-permute-done.refs_2_), channel_id=1, source_target_pairs={{0,2},{1,7},{2,4},{3,1},{4,6},{5,3},{6,0},{7,5},{8,10},{9,15},{10,... | collective-permute-start | bytes 1585160 | tf_op jit(solution)/shard_map/ppermute | solution.py:284
  24.5 10.9 %collective-permute-start.7 = (bf16[1040,128]{1,0:T(8,128)(2,1)S(1)}, bf16[1040,128]{1,0:T(8,128)(2,1)S(1)}, u32[]{:S(2)}, u32[]{:S(2)}) collective-permute-start(bf16[1040,128]{1,0:T(8,128)(2,1)S(1)} %slice.13), channel_id=1, source_target_pairs={{0,8},{8,0},{16,24},{24,16},{1,9},{9,1},{17,25},{25,17},{2,10},{10... | collective-permute-start | bytes 798728 | tf_op jit(solution)/shard_map/ppermute | solution.py:280
  26.4 7.0 %collective-permute-start.6 = (bf16[1024,128]{1,0:T(8,128)(2,1)S(1)}, bf16[1024,128]{1,0:T(8,128)(2,1)S(1)}, u32[]{:S(2)}, u32[]{:S(2)}) collective-permute-start(bf16[1024,128]{1,0:T(8,128)(2,1)S(1)} %slice.12), channel_id=1, source_target_pairs={{0,16},{8,24},{16,0},{24,8},{1,17},{9,25},{17,1},{25,9},{2,18},{10... | collective-permute-start | bytes 786440 | tf_op jit(solution)/shard_map/ppermute | solution.py:280
  29.1 18.0 %collective-permute-start.11 = (bf16[2064,128]{1,0:T(8,128)(2,1)S(1)}, bf16[2064,128]{1,0:T(8,128)(2,1)S(1)}, u32[]{:S(2)}, u32[]{:S(2)}) collective-permute-start(bf16[2064,128]{1,0:T(8,128)(2,1)S(1)} %pack_d.1.refs_0_), channel_id=1, source_target_pairs={{0,8},{8,0},{16,24},{24,16},{1,9},{9,1},{17,25},{25,17},{2,10},{10... | collective-permute-start | bytes 1585160 | tf_op jit(solution)/shard_map/ppermute | solution.py:280
  33.4 15.3 %collective-permute-start.12 = (bf16[2064,128]{1,0:T(8,128)(2,1)S(1)}, bf16[2064,128]{1,0:T(8,128)(2,1)S(1)}, u32[]{:S(2)}, u32[]{:S(2)}) collective-permute-start(bf16[2064,128]{1,0:T(8,128)(2,1)S(1)} %pack_d.1.refs_0_), channel_id=1, source_target_pairs={{0,16},{8,24},{16,0},{24,8},{1,17},{9,25},{17,1},{25,9},{2,18},{10... | collective-permute-start | bytes 1585160 | tf_op jit(solution)/shard_map/ppermute | solution.py:280
  35.4 15.1 %collective-permute-start.9 = (bf16[2064,128]{1,0:T(8,128)(2,1)S(1)}, bf16[2064,128]{1,0:T(8,128)(2,1)S(1)}, u32[]{:S(2)}, u32[]{:S(2)}) collective-permute-start(bf16[2064,128]{1,0:T(8,128)(2,1)S(1)} %collective-permute-done.5.refs_4_), channel_id=1, source_target_pairs={{0,1},{1,0},{2,3},{3,2},{4,5},{5,4},{6,7},{7,6},{8,9},{9,8},{10,11... | collective-permute-start | bytes 1585160 | tf_op jit(solution)/shard_map/ppermute | solution.py:287
  47.0 3.5 %collective-permute-start.10 = (bf16[2064,128]{1,0:T(8,128)(2,1)S(1)}, bf16[2064,128]{1,0:T(8,128)(2,1)S(1)}, u32[]{:S(2)}, u32[]{:S(2)}) collective-permute-start(bf16[2064,128]{1,0:T(8,128)(2,1)S(1)} %collective-permute-done.8.refs_1_), channel_id=1, source_target_pairs={{0,1},{1,0},{2,3},{3,2},{4,5},{5,4},{6,7},{7,6},{8,9},{9,8},{10,11... | collective-permute-start | bytes 1585160 | tf_op jit(solution)/shard_map/ppermute | solution.py:287
  47.1 13.9 %collective-permute-start.13 = (bf16[1024,128]{1,0:T(8,128)(2,1)S(1)}, bf16[1024,128]{1,0:T(8,128)(2,1)S(1)}, u32[]{:S(2)}, u32[]{:S(2)}) collective-permute-start(bf16[1024,128]{1,0:T(8,128)(2,1)S(1)} %slice.16), channel_id=1, source_target_pairs={{0,16},{8,24},{16,0},{24,8},{1,17},{9,25},{17,1},{25,9},{2,18},{10... | collective-permute-start | bytes 786440 | tf_op jit(solution)/shard_map/ppermute | solution.py:280
  48.7 12.4 %collective-permute-start.14 = (bf16[1024,128]{1,0:T(8,128)(2,1)S(1)}, bf16[1024,128]{1,0:T(8,128)(2,1)S(1)}, u32[]{:S(2)}, u32[]{:S(2)}) collective-permute-start(bf16[1024,128]{1,0:T(8,128)(2,1)S(1)} %slice.17), channel_id=1, source_target_pairs={{0,8},{8,0},{16,24},{24,16},{1,9},{9,1},{17,25},{25,17},{2,10},{10... | collective-permute-start | bytes 786440 | tf_op jit(solution)/shard_map/ppermute | solution.py:280
  56.1 9.8 %collective-permute-start.16 = (bf16[4,2,128,128]{3,2,1,0:T(8,128)(2,1)S(1)}, bf16[4,2,128,128]{3,2,1,0:T(8,128)(2,1)S(1)}, u32[]{:S(2)}, u32[]{:S(2)}) collective-permute-start(bf16[4,2,128,128]{3,2,1,0:T(8,128)(2,1)S(1)} %get-tuple-element.71), channel_id=1, source_target_pairs={{0,8},{8,0},{16,24},{24,16},{1,9},{9,1},{17,25},{25,17},{2,10},{10... | collective-permute-start | bytes 786440 | tf_op jit(solution)/shard_map/ppermute | solution.py:280
  56.4 9.5 %collective-permute-start.17 = (bf16[4,2,128,128]{3,2,1,0:T(8,128)(2,1)S(1)}, bf16[4,2,128,128]{3,2,1,0:T(8,128)(2,1)S(1)}, u32[]{:S(2)}, u32[]{:S(2)}) collective-permute-start(bf16[4,2,128,128]{3,2,1,0:T(8,128)(2,1)S(1)} %get-tuple-element.73), channel_id=1, source_target_pairs={{0,16},{8,24},{16,0},{24,8},{1,17},{9,25},{17,1},{25,9},{2,18},{10... | collective-permute-start | bytes 786440 | tf_op jit(solution)/shard_map/ppermute | solution.py:280
  57.8 5.7 %copy-start.4 = (s32[8,4]{0,1:T(4,128)S(1)}, s32[8,4]{0,1:T(4,128)}, u32[]{:S(2)}) copy-start(s32[8,4]{0,1:T(4,128)} %param.9) | copy-start | bytes 388
  61.1 14.1 %collective-permute-start.15 = (bf16[4,2,128,128]{3,2,1,0:T(8,128)(2,1)S(1)}, bf16[4,2,128,128]{3,2,1,0:T(8,128)(2,1)S(1)}, u32[]{:S(2)}, u32[]{:S(2)}) collective-permute-start(bf16[4,2,128,128]{3,2,1,0:T(8,128)(2,1)S(1)} %get-tuple-element.69), channel_id=1, source_target_pairs={{0,8},{8,0},{16,24},{24,16},{1,9},{9,1},{17,25},{25,17},{2,10},{10... | collective-permute-start | bytes 786440 | tf_op jit(solution)/shard_map/ppermute | solution.py:280
  61.5 13.7 %collective-permute-start.20 = (bf16[4,2,128,128]{3,2,1,0:T(8,128)(2,1)S(1)}, bf16[4,2,128,128]{3,2,1,0:T(8,128)(2,1)S(1)}, u32[]{:S(2)}, u32[]{:S(2)}) collective-permute-start(bf16[4,2,128,128]{3,2,1,0:T(8,128)(2,1)S(1)} %get-tuple-element.76), channel_id=1, source_target_pairs={{0,16},{8,24},{16,0},{24,8},{1,17},{9,25},{17,1},{25,9},{2,18},{10... | collective-permute-start | bytes 786440 | tf_op jit(solution)/shard_map/ppermute | solution.py:280
  66.0 9.4 %collective-permute-start.18 = (bf16[4,2,128,128]{3,2,1,0:T(8,128)(2,1)S(1)}, bf16[4,2,128,128]{3,2,1,0:T(8,128)(2,1)S(1)}, u32[]{:S(2)}, u32[]{:S(2)}) collective-permute-start(bf16[4,2,128,128]{3,2,1,0:T(8,128)(2,1)S(1)} %get-tuple-element.74), channel_id=1, source_target_pairs={{0,8},{8,0},{16,24},{24,16},{1,9},{9,1},{17,25},{25,17},{2,10},{10... | collective-permute-start | bytes 786440 | tf_op jit(solution)/shard_map/ppermute | solution.py:280
  67.1 8.5 %collective-permute-start.19 = (bf16[4,2,128,128]{3,2,1,0:T(8,128)(2,1)S(1)}, bf16[4,2,128,128]{3,2,1,0:T(8,128)(2,1)S(1)}, u32[]{:S(2)}, u32[]{:S(2)}) collective-permute-start(bf16[4,2,128,128]{3,2,1,0:T(8,128)(2,1)S(1)} %get-tuple-element.75), channel_id=1, source_target_pairs={{0,16},{8,24},{16,0},{24,8},{1,17},{9,25},{17,1},{25,9},{2,18},{10... | collective-permute-start | bytes 786440 | tf_op jit(solution)/shard_map/ppermute | solution.py:280
